TPU v7x, 32 devices: a whole 2x2x4 slice. The times are simulated.
32 devices in a mesh: groups: 2 (over y), dom: 4 (over z), pair: 2 (over x), sub: 2 (over core).
Axes of the slice: x: 2, y: 2, z: 4, core: 2. Of those that a mesh axis runs over, the one named last changes fastest.
Arguments:
- nodes: bfloat16 [16384, 128], P(('groups', 'dom', 'pair', 'sub')), parts along dimension 0, may hold values from -6 to 6
- cotangent: bfloat16 [16384, 128], P(('groups', 'dom', 'pair', 'sub')), parts along dimension 0, may hold values from -6 to 6
- send_blocks: int32 [32, 2, 1], P(('groups', 'dom', 'pair', 'sub')), parts along dimension 0, may hold values from 0 to 3
- neighbour_blocks: int32 [128, 4], P(('groups', 'dom', 'pair', 'sub')), parts along dimension 0, may hold values from 0 to 5
- neighbour_nodes: int32 [128, 4, 128], P(('groups', 'dom', 'pair', 'sub')), parts along dimension 0, may hold values from 0 to 127
- pool_map: int32 [128], P(('groups', 'dom', 'pair', 'sub')), parts along dimension 0, may hold values from 0 to 3
- coarse_blocks: int32 [32, 4], P(('groups', 'dom', 'pair', 'sub')), parts along dimension 0, may hold values from 0 to 2
- coarse_nodes: int32 [32, 4, 128], P(('groups', 'dom', 'pair', 'sub')), parts along dimension 0, may hold values from 0 to 127
- weights: bfloat16 [3, 6, 128, 128], replicated, may hold values from -0.5 to 0.5
- biases: float32 [3, 2, 128], replicated, may hold values from -3 to 3
Outputs:
- out_nodes: bfloat16 [16384, 128], P(('groups', 'dom', 'pair', 'sub')), parts along dimension 0
- grad_nodes: float32 [16384, 128], P(('groups', 'dom', 'pair', 'sub')), parts along dimension 0
There are 2 independent parts, one for each index of `groups`. A program takes and returns all parts, laid end to end along the dimension named above; an argument that names none is the same for every part. Nothing has to cross between parts.
Inputs may be any that keep to these rules, and one draw needn't show every extreme that they name: `send_blocks`: entries index a device's own blocks. `neighbour_blocks`: entries under 4 are own blocks, the rest received blocks in round order. `pool_map`: a coarse block of the pooling group, which may receive no fine block. `coarse_blocks`: entries under 1 are own coarse blocks, the rest received ones in round order.
All inputs are finite; a program needn't handle non-finite values.
Results may differ from a plain program's by a relative error of at most 0.013.
Values may be sent and summed in bfloat16 or wider, within the bound.
No kernel may reach another device: no remote copies, remote signals or barrier semaphores. Data moves between devices by JAX's collectives and lax.ppermute only.
A program may use at most 64 MiB of HBM per device.

v0:
```python
import jax
import jax.numpy as jnp
from jax import lax
from jax.sharding import PartitionSpec as P


def swapped(value, axis, stride):
    mask = 2**stride
    pairs = [(source, source ^ mask) for source in range(lax.axis_size(axis))]
    return lax.ppermute(value, axis, pairs)


def shortened(x):
    return jax.tree.map(lambda a: a.astype(jnp.bfloat16) if a.dtype == jnp.float32 else a, x)


def project(inputs, matrix):
    leading = inputs.shape[:-1]
    flat_inputs = inputs.reshape(-1, inputs.shape[-1])
    return jnp.dot(flat_inputs, matrix, preferred_element_type=jnp.float32).reshape(
        leading + (matrix.shape[1],)
    )


def message_layer(own_field, halo_field, near_blocks, near_nodes, weights, biases):
    own_state = own_field.astype(jnp.bfloat16)
    halo_state = halo_field.astype(jnp.bfloat16)
    blocks, block_size, features = own_state.shape
    degree = near_blocks.shape[1]
    everyone = jnp.concatenate([own_state, halo_state], axis=0)
    sender = project(everyone, weights[1]).reshape(-1, features)
    receiver = project(own_state, weights[0]) + biases[0]
    flat_index = (near_blocks[:, :, None] * block_size + near_nodes).reshape(-1)
    picked = jnp.take(sender, flat_index, axis=0).reshape(blocks, degree, block_size, features)
    active = jax.nn.silu(receiver[:, None] + picked).astype(jnp.bfloat16)
    message = project(active, weights[2])
    average = (jnp.sum(message, axis=1) / degree).astype(jnp.bfloat16)
    hidden = jax.nn.silu(
        project(own_state, weights[3]) + project(average, weights[4]) + biases[1]
    ).astype(jnp.bfloat16)
    return own_field + project(hidden, weights[5])


def rounded(values):
    return lax.optimization_barrier(values.astype(jnp.bfloat16)).astype(jnp.float32)


def per_device(
    nodes,
    cotangent,
    send_blocks,
    neighbour_blocks,
    neighbour_nodes,
    pool_map,
    coarse_blocks,
    coarse_nodes,
    weights,
    biases,
):
    features = nodes.shape[1]
    blocks = neighbour_blocks.shape[0]
    block_size = neighbour_nodes.shape[2]
    coarse = coarse_blocks.shape[0]
    send_lists = send_blocks[0]
    halo_count = send_lists.shape[1]
    xor_bits = (0, lax.axis_size("dom").bit_length() - 2)
    owner_index = lax.axis_index(("pair", "sub"))
    owned_slots = jnp.arange(coarse, dtype=jnp.int32) + owner_index * coarse

    def fine_halo(states):
        pieces = []
        for section in range(2):
            chosen = states[send_lists[section]].astype(jnp.bfloat16)
            pieces.append(swapped(chosen, "dom", xor_bits[section]))
        return jnp.concatenate(pieces, axis=0).astype(jnp.float32)

    def fine_return(halo_grad, grads):
        for section in range(2):
            arrived = swapped(
                halo_grad[section * halo_count : (section + 1) * halo_count].astype(jnp.bfloat16),
                "dom",
                xor_bits[section],
            ).astype(jnp.float32)
            grads = grads.at[send_lists[section]].add(arrived)
        return grads

    start_state = nodes.reshape(blocks, block_size, features).astype(jnp.float32)
    halo_first = fine_halo(start_state)
    after_first = rounded(
        message_layer(
            start_state, halo_first, neighbour_blocks, neighbour_nodes, weights[0], biases[0]
        )
    )
    first_rows = after_first.astype(jnp.bfloat16).reshape(blocks, -1)
    piece_rows = lax.all_gather(first_rows, ("pair", "sub"), axis=0, tiled=True)
    labels = lax.all_gather(pool_map, ("pair", "sub"), axis=0, tiled=True)
    matches = labels[None, :] == owned_slots[:, None]
    new_sums = jnp.dot(matches.astype(jnp.bfloat16), piece_rows, preferred_element_type=jnp.float32)
    new_counts = jnp.sum(matches.astype(jnp.float32), axis=1)
    divisor = jnp.maximum(new_counts, 1.0)
    coarse_start = rounded(new_sums / divisor[:, None]).reshape(coarse, block_size, features)
    pieces = []
    for section in range(2):
        pieces.append(swapped(coarse_start.astype(jnp.bfloat16), "dom", xor_bits[section]))
    coarse_in = jnp.concatenate(pieces, axis=0).astype(jnp.float32)
    coarse_end = rounded(
        message_layer(coarse_start, coarse_in, coarse_blocks, coarse_nodes, weights[1], biases[1])
    )
    coarse_every = lax.all_gather(
        coarse_end.astype(jnp.bfloat16).reshape(coarse, -1), ("pair", "sub"), axis=0, tiled=True
    )
    lifted = (
        jnp.take(coarse_every, pool_map, axis=0)
        .astype(jnp.float32)
        .reshape(blocks, block_size, features)
    )
    middle = rounded(after_first + lifted)
    halo_second = fine_halo(middle)
    final = message_layer(
        middle, halo_second, neighbour_blocks, neighbour_nodes, weights[2], biases[2]
    )
    out_nodes = final.astype(jnp.bfloat16).reshape(-1, features)
    grad_final = cotangent.reshape(blocks, block_size, features).astype(jnp.float32)
    _, pullback_second = jax.vjp(
        lambda first_in, second_in: message_layer(
            first_in, second_in, neighbour_blocks, neighbour_nodes, weights[2], biases[2]
        ),
        middle,
        halo_second,
    )
    grad_middle, grad_halo_second = pullback_second(grad_final)
    grad_middle = fine_return(grad_halo_second, grad_middle)
    flat_grad = grad_middle.reshape(blocks, -1)
    wanted = jnp.arange(lax.axis_size(("pair", "sub")) * coarse, dtype=jnp.int32)
    matches = (pool_map[None, :] == wanted[:, None]).astype(jnp.float32)
    grad_coarse_end = (
        lax.psum_scatter(
            jnp.dot(matches, flat_grad, precision=lax.Precision.HIGHEST).astype(jnp.bfloat16),
            ("pair", "sub"),
            scatter_dimension=0,
            tiled=True,
        )
        .astype(jnp.float32)
        .reshape(coarse, block_size, features)
    )
    _, pullback_coarse = jax.vjp(
        lambda first_in, second_in: message_layer(
            first_in, second_in, coarse_blocks, coarse_nodes, weights[1], biases[1]
        ),
        coarse_start,
        coarse_in,
    )
    grad_coarse, grad_coarse_halo = pullback_coarse(grad_coarse_end)
    grads = grad_coarse
    for section in range(2):
        grads = grads + swapped(
            grad_coarse_halo[section * coarse : (section + 1) * coarse].astype(jnp.bfloat16),
            "dom",
            xor_bits[section],
        ).astype(jnp.float32)
    grad_coarse = grads
    scaled = grad_coarse.reshape(coarse, -1) / divisor[:, None]
    scaled_every = lax.all_gather(shortened(scaled), ("pair", "sub"), axis=0, tiled=True).astype(
        scaled.dtype
    )
    grad_first = grad_middle + jnp.take(scaled_every, pool_map, axis=0).reshape(
        blocks, block_size, features
    )
    _, pullback_first = jax.vjp(
        lambda first_in, second_in: message_layer(
            first_in, second_in, neighbour_blocks, neighbour_nodes, weights[0], biases[0]
        ),
        start_state,
        halo_first,
    )
    grad_start, grad_halo_first = pullback_first(grad_first)
    grad_start = fine_return(grad_halo_first, grad_start)
    return (out_nodes, grad_start.reshape(-1, features))


def solution(mesh):
    placed = (
        P(("groups", "dom", "pair", "sub"), None),
        P(("groups", "dom", "pair", "sub"), None),
        P(("groups", "dom", "pair", "sub"), None, None),
        P(("groups", "dom", "pair", "sub"), None),
        P(("groups", "dom", "pair", "sub"), None, None),
        P(("groups", "dom", "pair", "sub")),
        P(("groups", "dom", "pair", "sub"), None),
        P(("groups", "dom", "pair", "sub"), None, None),
        P(),
        P(),
    )
    return jax.shard_map(
        per_device,
        mesh=mesh,
        in_specs=placed,
        out_specs=(
            P(("groups", "dom", "pair", "sub"), None),
            P(("groups", "dom", "pair", "sub"), None),
        ),
        check_vma=False,
    )
```

profile of v0, /device:TPU:0, one launch (start us, length us, event | category | flops | bytes accessed | tf_op | source)
XLA Modules:
  0.0 210.6 jit_solution(3608488233605412984)
XLA Ops:
  7.2 1.3 fusion.178
  13.2 3.0 %collective-permute-start = (bf16[1,128,128]{2,1,0:T(8,128)(2,1)S(1)}, bf16[1,128,128]{2,1,0:T(8,128)(2,1)S(1)}, u32[]{:S(2)}, u32[]{:S(2)}) collective-permute-start(bf16[1,128,128]{2,1,0:T(8,128)(2,1)S(1)} %get-tuple-element.121), channel_id=1, source_target_pairs={{0,4},{4,0},{8,12},{12,8},{1,5},{5,1},{9,13},{13,9},{2,6},{6,2},{1... | collective-permute-start | bytes 98312 | tf_op jit(solution)/shard_map/ppermute | solution.py:10
  16.3 2.6 %collective-permute-start.1 = (bf16[1,128,128]{2,1,0:T(8,128)(2,1)S(1)}, bf16[1,128,128]{2,1,0:T(8,128)(2,1)S(1)}, u32[]{:S(2)}, u32[]{:S(2)}) collective-permute-start(bf16[1,128,128]{2,1,0:T(8,128)(2,1)S(1)} %get-tuple-element.122), channel_id=1, source_target_pairs={{0,8},{4,12},{8,0},{12,4},{1,9},{5,13},{9,1},{13,5},{2,10},{6,14},... | collective-permute-start | bytes 98312 | tf_op jit(solution)/shard_map/ppermute | solution.py:10
  25.3 5.0 %all-reduce = s32[16]{0:T(128)S(1)} all-reduce(s32[16]{0:T(128)S(1)} %dynamic-update-slice.16), channel_id=1, replica_groups=mesh['groups'=2,'dom'=4,'pair'=2,'sub'=2] {'pair','sub'}, use_global_device_ids=true, to_apply=%add | all-reduce | flops 16 | bytes 128
  33.1 1.7 fusion.93
  34.7 1.6 convolution_convert_fusion.13
  36.3 0.9 convolution_add_fusion.5
  38.7 0.9 fusion.123
  39.7 5.5 %gather_fusion.3 = f32[2048,128]{1,0:T(8,128)S(1)} fusion(f32[768,128]{1,0:T(8,128)S(1)} %fusion.123, s32[2048]{0:T(1024)S(1)} %get-tuple-element.126), kind=kCustom, calls=%fused_computation.clone | custom fusion | bytes 2105344 | tf_op jit(solution)/shard_map/jit(_take)/gather | solution.py:34
  45.7 1.1 convolution_reduce_fusion.1
  47.5 0.9 fusion.3
  49.1 1.0 fusion.4
  50.1 6.5 %all-gather = bf16[4,4,16384]{2,1,0:T(4,128)(2,1)S(1)} all-gather(bf16[1,4,16384]{2,1,0:T(4,128)(2,1)S(1)} %reshape.969), channel_id=1, replica_groups=mesh['groups'=2,'dom'=4,'pair'=2,'sub'=2] {'pair','sub'}, dimensions={0}, use_global_device_ids=true | all-gather | bytes 655360 | tf_op jit(solution)/shard_map/all_gather | solution.py:95
  59.6 0.9 fusion.84
  60.5 2.5 %collective-permute-done.3 = bf16[1,128,128]{2,1,0:T(8,128)(2,1)S(1)} collective-permute-done((bf16[1,128,128]{2,1,0:T(8,128)(2,1)S(1)}, bf16[1,128,128]{2,1,0:T(8,128)(2,1)S(1)}, u32[]{:S(2)}, u32[]{:S(2)}) %collective-permute-start.3) | collective-permute-done | bytes 32800 | tf_op jit(solution)/shard_map/ppermute | solution.py:10
  63.0 0.9 fusion.113
  63.9 1.0 gather_fusion
  65.7 0.9 bitcast_add_fusion.2
  66.6 0.9 convolution_reduce_fusion.2
  68.1 0.9 fusion.17
  69.0 0.9 fusion.27
  69.9 5.8 %all-gather.1 = bf16[4,1,16384]{2,1,0:T(2,128)(2,1)S(1)} all-gather(bf16[1,1,16384]{2,1,0:T(2,128)(2,1)S(1)} %reshape.971), channel_id=1, replica_groups=mesh['groups'=2,'dom'=4,'pair'=2,'sub'=2] {'pair','sub'}, dimensions={0}, use_global_device_ids=true | all-gather | bytes 163840 | tf_op jit(solution)/shard_map/all_gather | solution.py:109
  77.7 2.0 collective-permute-start.5
  79.7 1.6 convolution_add_fusion.2
  81.4 1.6 fusion.88
  83.1 0.9 fusion.103
  84.0 5.5 %gather_fusion.4 = f32[2048,128]{1,0:T(8,128)S(1)} fusion(f32[768,128]{1,0:T(8,128)S(1)} %fusion.103, s32[2048]{0:T(1024)S(1)} %get-tuple-element.126), kind=kCustom, calls=%fused_computation.2.clone | custom fusion | bytes 2105344 | tf_op jit(solution)/shard_map/jit(_take)/gather | solution.py:34
  89.5 2.5 %multiply_convert_fusion = (bf16[2048,128]{1,0:T(8,128)(2,1)S(1)}, f32[2048,128]{1,0:T(8,128)}, f32[2048,128]{1,0:T(8,128)}) fusion(f32[4,128,128]{2,1,0:T(8,128)} %convolution_add_fusion.2, f32[2048,128]{1,0:T(8,128)S(1)} %gather_fusion.4, pred[2048]{0:T(1024)(128)(4,1)S(1)} %compare_and_fusion), kind=kLoop, calls=%fused_computation.91 | loop fusion | flops 1835008 | bytes 3934208 | tf_op jit(solution)/shard_map/convert_element_type | solution.py:35
  92.0 1.1 convolution_reduce_fusion
  93.7 1.7 fusion.48
  95.5 0.9 fusion.10
  96.5 1.1 fusion.1
  97.6 12.6 %scatter_custom_fusion = f32[768,128]{1,0:T(8,128)S(1)} fusion(s32[2048]{0:T(1024)} %get-tuple-element.125, f32[2048,128]{1,0:T(8,128)} %get-tuple-element.108, f32[2048,128]{1,0:T(8,128)S(1)} %fusion.1, f32[]{:T(128)} %constant.199.clone.1, f32[]{:T(128)} %constant.200.clone.1), kind=kCustom, calls=%fused_computation.78 | custom fusion | flops 2621440 | bytes 2491392 | tf_op jit(solution)/shard_map/transpose(jvp(jit(_take)))/scatter-add | solution.py:34
  110.2 1.0 convolution_convert_fusion.4
  111.2 1.7 fusion.30
  112.9 1.0 convolution_convert_fusion.10
  113.9 1.7 collective-permute-start.6
  115.6 1.0 fusion.14
  116.5 1.8 collective-permute-start.7
  119.1 2.7 %collective-permute-done.7 = bf16[1,128,128]{2,1,0:T(8,128)(2,1)S(1)} collective-permute-done((bf16[1,128,128]{2,1,0:T(8,128)(2,1)S(1)}, bf16[1,128,128]{2,1,0:T(8,128)(2,1)S(1)}, u32[]{:S(2)}, u32[]{:S(2)}) %collective-permute-start.7) | collective-permute-done | bytes 32800 | tf_op jit(solution)/shard_map/ppermute | solution.py:10
  123.1 1.2 convolution_convert_fusion
  125.1 1.6 fusion.5
  126.7 28.1 %all-reduce.4.cloned.1.call-done = bf16[4,16384]{1,0:T(4,128)(2,1)} async-done(((bf16[4,16384]{1,0:T(4,128)(2,1)}), bf16[4,16384]{1,0:T(4,128)(2,1)}) %all-reduce.4.cloned.1.call-update) | async-done | bytes 131088
  154.9 1.7 dynamic-slice_reduce_fusion
  156.5 0.9 fusion.79
  157.5 0.9 fusion.20
  158.4 1.0 fusion.8
  159.4 2.5 %scatter_custom_fusion.1 = f32[384,128]{1,0:T(8,128)S(1)} fusion(s32[512]{0:T(512)} %bitcast.327, f32[512,128]{1,0:T(8,128)S(1)} %copy-done.8, f32[512,128]{1,0:T(8,128)S(1)} %fusion.8, f32[]{:T(128)} %constant.199.clone.1, f32[]{:T(128)} %constant.200.clone.1), kind=kCustom, calls=%fused_computation.118 | custom fusion | flops 655360 | bytes 721920 | tf_op jit(solution)/shard_map/transpose(jvp(jit(_take)))/scatter-add | solution.py:34
  162.0 1.0 convolution_convert_fusion.14
  163.0 1.6 collective-permute-start.8
  164.5 2.4 %collective-permute-start.9 = (bf16[1,128,128]{2,1,0:T(8,128)(2,1)S(1)}, bf16[1,128,128]{2,1,0:T(8,128)(2,1)S(1)}, u32[]{:S(2)}, u32[]{:S(2)}) collective-permute-start(bf16[1,128,128]{2,1,0:T(8,128)(2,1)S(1)} %get-tuple-element.124), channel_id=1, source_target_pairs={{0,8},{4,12},{8,0},{12,4},{1,9},{5,13},{9,1},{13,5},{2,10},{6,14},... | collective-permute-start | bytes 98312 | tf_op jit(solution)/shard_map/ppermute | solution.py:10
  167.7 0.9 convolution_convert_fusion.15
  168.6 1.0 collective-permute-done.9
  169.7 0.9 divide_convert_fusion
  170.6 5.8 %all-gather.2 = bf16[4,1,16384]{2,1,0:T(2,128)(2,1)S(1)} all-gather(bf16[1,1,16384]{2,1,0:T(2,128)(2,1)S(1)} %reshape.973), channel_id=1, replica_groups=mesh['groups'=2,'dom'=4,'pair'=2,'sub'=2] {'pair','sub'}, dimensions={0}, use_global_device_ids=true | all-gather | bytes 163840 | tf_op jit(solution)/shard_map/all_gather | solution.py:163
  177.5 1.0 convolution_convert_fusion.8
  178.6 0.9 fusion.7
  179.7 1.1 fusion
  180.8 12.7 %scatter_custom_fusion.2 = f32[768,128]{1,0:T(8,128)} fusion(s32[2048]{0:T(1024)} %get-tuple-element.125, f32[2048,128]{1,0:T(8,128)S(1)} %get-tuple-element.111, f32[2048,128]{1,0:T(8,128)S(1)} %fusion, f32[]{:T(128)} %constant.199.clone.1, f32[]{:T(128)} %constant.200.clone.1), kind=kCustom, calls=%fused_computation.84 | custom fusion | flops 2621440 | bytes 2491392 | tf_op jit(solution)/shard_map/transpose(jvp(jit(_take)))/scatter-add | solution.py:34
  193.5 1.2 convolution_convert_fusion.3
  195.2 0.9 convolution_convert_fusion.5
  196.2 1.0 fusion.16
  197.5 2.4 %collective-permute-start.11 = (bf16[1,128,128]{2,1,0:T(8,128)(2,1)S(1)}, bf16[1,128,128]{2,1,0:T(8,128)(2,1)S(1)}, u32[]{:S(2)}, u32[]{:S(2)}) collective-permute-start(bf16[1,128,128]{2,1,0:T(8,128)(2,1)S(1)} %get-tuple-element.115), channel_id=1, source_target_pairs={{0,8},{4,12},{8,0},{12,4},{1,9},{5,13},{9,1},{13,5},{2,10},{6,14},... | collective-permute-start | bytes 98312 | tf_op jit(solution)/shard_map/ppermute | solution.py:10
  199.9 1.2 collective-permute-done.10
  (158 shorter events, 27.3 us)
Async XLA Ops:
  7.2 147.7 %all-reduce.4.cloned.1.call-start = ((), (), s32[]{:S(2)}) async-start(), calls=%async_computation | async-start | bytes 262144
  12.4 20.6 %copy-start.7 = (bf16[512,128]{1,0:T(8,128)(2,1)S(1)}, bf16[512,128]{1,0:T(8,128)(2,1)}, u32[]{:S(2)}) copy-start(bf16[512,128]{1,0:T(8,128)(2,1)} %param.22) | copy-start | bytes 393220
  13.2 25.4 %collective-permute-start = (bf16[1,128,128]{2,1,0:T(8,128)(2,1)S(1)}, bf16[1,128,128]{2,1,0:T(8,128)(2,1)S(1)}, u32[]{:S(2)}, u32[]{:S(2)}) collective-permute-start(bf16[1,128,128]{2,1,0:T(8,128)(2,1)S(1)} %get-tuple-element.121), channel_id=1, source_target_pairs={{0,4},{4,0},{8,12},{12,8},{1,5},{5,1},{9,13},{13,9},{2,6},{6,2},{1... | collective-permute-start | bytes 98312 | tf_op jit(solution)/shard_map/ppermute | solution.py:10
  16.3 22.4 %collective-permute-start.1 = (bf16[1,128,128]{2,1,0:T(8,128)(2,1)S(1)}, bf16[1,128,128]{2,1,0:T(8,128)(2,1)S(1)}, u32[]{:S(2)}, u32[]{:S(2)}) collective-permute-start(bf16[1,128,128]{2,1,0:T(8,128)(2,1)S(1)} %get-tuple-element.122), channel_id=1, source_target_pairs={{0,8},{4,12},{8,0},{12,4},{1,9},{5,13},{9,1},{13,5},{2,10},{6,14},... | collective-permute-start | bytes 98312 | tf_op jit(solution)/shard_map/ppermute | solution.py:10
  18.9 0.7 copy-start.37
  19.5 0.7 copy-start.43
  20.1 0.7 copy-start.30
  20.8 1.7 copy-start.24
  21.4 1.1 copy-start.31
  23.2 0.7 copy-start.29
  25.3 5.0 %copy-start.42 = (s32[3]{0:T(128)S(1)}, s32[3]{0:T(128)}, u32[]{:S(2)}) copy-start(s32[3]{0:T(128)} %constant.211.clone.1) | copy-start | bytes 40
  30.4 6.9 %copy-start.39 = (s32[16]{0:T(128)}, s32[16]{0:T(128)S(1)}, u32[]{:S(2)}) copy-start(s32[16]{0:T(128)S(1)} %all-reduce) | copy-start | bytes 196
  31.2 0.7 copy-start.25
  31.8 1.2 copy-start.23
  33.1 1.7 copy-start.15
  37.3 7.9 %copy-start.2 = (f32[4,128,128]{2,1,0:T(8,128)}, f32[4,128,128]{2,1,0:T(8,128)S(1)}, u32[]{:S(2)}) copy-start(f32[4,128,128]{2,1,0:T(8,128)S(1)} %convolution_add_fusion.5) | copy-start | bytes 786436
  45.7 1.1 copy-start.11
  46.8 0.7 copy-start.36
  48.4 0.7 copy-start.9
  56.7 0.7 copy-start.40
  57.8 0.9 copy-start.28
  57.8 5.2 %collective-permute-start.3 = (bf16[1,128,128]{2,1,0:T(8,128)(2,1)S(1)}, bf16[1,128,128]{2,1,0:T(8,128)(2,1)S(1)}, u32[]{:S(2)}, u32[]{:S(2)}) collective-permute-start(bf16[1,128,128]{2,1,0:T(8,128)(2,1)S(1)} %bitcast.317), channel_id=1, source_target_pairs={{0,8},{4,12},{8,0},{12,4},{1,9},{5,13},{9,1},{13,5},{2,10},{6,14},... | collective-permute-start | bytes 98312 | tf_op jit(solution)/shard_map/ppermute | solution.py:10
  58.2 4.8 %collective-permute-start.2 = (bf16[1,128,128]{2,1,0:T(8,128)(2,1)S(1)}, bf16[1,128,128]{2,1,0:T(8,128)(2,1)S(1)}, u32[]{:S(2)}, u32[]{:S(2)}) collective-permute-start(bf16[1,128,128]{2,1,0:T(8,128)(2,1)S(1)} %bitcast.318), channel_id=1, source_target_pairs={{0,4},{4,0},{8,12},{12,8},{1,5},{5,1},{9,13},{13,9},{2,6},{6,2},{1... | collective-permute-start | bytes 98312 | tf_op jit(solution)/shard_map/ppermute | solution.py:10
  59.6 5.4 %copy-start.13 = (f32[128,128]{1,0:T(8,128)}, f32[128,128]{1,0:T(8,128)S(1)}, u32[]{:S(2)}) copy-start(f32[128,128]{1,0:T(8,128)S(1)} %convolution_add_fusion.8) | copy-start | bytes 196612
  65.0 1.6 copy-start.5
  65.0 0.7 copy-start.34
  65.0 0.7 copy-start.35
  67.5 0.6 copy-start.27
  69.0 0.9 copy-start.21
  76.7 0.7 copy-start.32
  77.5 5.6 %copy-start = (bf16[4,128,128]{2,1,0:T(8,128)(2,1)}, bf16[4,128,128]{2,1,0:T(8,128)(2,1)S(1)}, u32[]{:S(2)}) copy-start(bf16[4,128,128]{2,1,0:T(8,128)(2,1)S(1)} %add_convert_fusion) | copy-start | bytes 393220
  77.5 5.5 %collective-permute-start.4 = (bf16[1,128,128]{2,1,0:T(8,128)(2,1)S(1)}, bf16[1,128,128]{2,1,0:T(8,128)(2,1)S(1)}, u32[]{:S(2)}, u32[]{:S(2)}) collective-permute-start(bf16[1,128,128]{2,1,0:T(8,128)(2,1)S(1)} %get-tuple-element.119), channel_id=1, source_target_pairs={{0,4},{4,0},{8,12},{12,8},{1,5},{5,1},{9,13},{13,9},{2,6},{6,2},{1... | collective-permute-start | bytes 98312 | tf_op jit(solution)/shard_map/ppermute | solution.py:10
  77.7 2.0 copy-start.26
  77.7 5.3 %collective-permute-start.5 = (bf16[1,128,128]{2,1,0:T(8,128)(2,1)S(1)}, bf16[1,128,128]{2,1,0:T(8,128)(2,1)S(1)}, u32[]{:S(2)}, u32[]{:S(2)}) collective-permute-start(bf16[1,128,128]{2,1,0:T(8,128)(2,1)S(1)} %get-tuple-element.120), channel_id=1, source_target_pairs={{0,8},{4,12},{8,0},{12,4},{1,9},{5,13},{9,1},{13,5},{2,10},{6,14},... | collective-permute-start | bytes 98312 | tf_op jit(solution)/shard_map/ppermute | solution.py:10
  92.0 1.1 copy-start.19
  92.0 1.1 copy-start.20
  93.1 0.7 copy-start.41
  95.5 1.0 copy-start.17
  110.2 1.0 copy-start.4
  112.9 2.7 %copy-start.18 = (bf16[4,128,128]{2,1,0:T(8,128)(2,1)S(1)}, bf16[4,128,128]{2,1,0:T(8,128)(2,1)}, u32[]{:S(2)}) copy-start(bf16[4,128,128]{2,1,0:T(8,128)(2,1)} %copy-done.17) | copy-start | bytes 393220
  113.9 1.7 copy-start.16
  113.9 4.4 %collective-permute-start.6 = (bf16[1,128,128]{2,1,0:T(8,128)(2,1)S(1)}, bf16[1,128,128]{2,1,0:T(8,128)(2,1)S(1)}, u32[]{:S(2)}, u32[]{:S(2)}) collective-permute-start(bf16[1,128,128]{2,1,0:T(8,128)(2,1)S(1)} %get-tuple-element.118), channel_id=1, source_target_pairs={{0,4},{4,0},{8,12},{12,8},{1,5},{5,1},{9,13},{13,9},{2,6},{6,2},{1... | collective-permute-start | bytes 98312 | tf_op jit(solution)/shard_map/ppermute | solution.py:10
  116.5 5.2 %collective-permute-start.7 = (bf16[1,128,128]{2,1,0:T(8,128)(2,1)S(1)}, bf16[1,128,128]{2,1,0:T(8,128)(2,1)S(1)}, u32[]{:S(2)}, u32[]{:S(2)}) collective-permute-start(bf16[1,128,128]{2,1,0:T(8,128)(2,1)S(1)} %get-tuple-element.117), channel_id=1, source_target_pairs={{0,8},{4,12},{8,0},{12,4},{1,9},{5,13},{9,1},{13,5},{2,10},{6,14},... | collective-permute-start | bytes 98312 | tf_op jit(solution)/shard_map/ppermute | solution.py:10
  122.4 0.7 copy-start.38
  123.1 1.2 copy-start.44
  124.2 0.9 copy-start.1
  126.7 29.8 %copy-start.22 = (f32[128,128]{1,0:T(8,128)S(1)}, f32[128,128]{1,0:T(8,128)}, u32[]{:S(2)}) copy-start(f32[128,128]{1,0:T(8,128)} %copy-done.21) | copy-start | bytes 196612
  158.4 1.0 copy-start.8
  161.9 5.0 %copy-start.6 = (f32[512,128]{1,0:T(8,128)S(1)}, f32[512,128]{1,0:T(8,128)}, u32[]{:S(2)}) copy-start(f32[512,128]{1,0:T(8,128)} %copy-done.5) | copy-start | bytes 786436
  162.9 4.0 %copy-start.14 = (f32[128,128]{1,0:T(8,128)S(1)}, f32[128,128]{1,0:T(8,128)}, u32[]{:S(2)}) copy-start(f32[128,128]{1,0:T(8,128)} %copy-done.13) | copy-start | bytes 196612
  163.0 5.7 %collective-permute-start.8 = (bf16[1,128,128]{2,1,0:T(8,128)(2,1)S(1)}, bf16[1,128,128]{2,1,0:T(8,128)(2,1)S(1)}, u32[]{:S(2)}, u32[]{:S(2)}) collective-permute-start(bf16[1,128,128]{2,1,0:T(8,128)(2,1)S(1)} %get-tuple-element.123), channel_id=1, source_target_pairs={{0,4},{4,0},{8,12},{12,8},{1,5},{5,1},{9,13},{13,9},{2,6},{6,2},{1... | collective-permute-start | bytes 98312 | tf_op jit(solution)/shard_map/ppermute | solution.py:10
  164.5 5.1 %collective-permute-start.9 = (bf16[1,128,128]{2,1,0:T(8,128)(2,1)S(1)}, bf16[1,128,128]{2,1,0:T(8,128)(2,1)S(1)}, u32[]{:S(2)}, u32[]{:S(2)}) collective-permute-start(bf16[1,128,128]{2,1,0:T(8,128)(2,1)S(1)} %get-tuple-element.124), channel_id=1, source_target_pairs={{0,8},{4,12},{8,0},{12,4},{1,9},{5,13},{9,1},{13,5},{2,10},{6,14},... | collective-permute-start | bytes 98312 | tf_op jit(solution)/shard_map/ppermute | solution.py:10
  166.9 0.6 copy-start.33
  177.5 1.0 copy-start.10
  193.5 1.3 copy-start.3
  197.1 4.0 %collective-permute-start.10 = (bf16[1,128,128]{2,1,0:T(8,128)(2,1)S(1)}, bf16[1,128,128]{2,1,0:T(8,128)(2,1)S(1)}, u32[]{:S(2)}, u32[]{:S(2)}) collective-permute-start(bf16[1,128,128]{2,1,0:T(8,128)(2,1)S(1)} %get-tuple-element.116), channel_id=1, source_target_pairs={{0,4},{4,0},{8,12},{12,8},{1,5},{5,1},{9,13},{13,9},{2,6},{6,2},{1... | collective-permute-start | bytes 98312 | tf_op jit(solution)/shard_map/ppermute | solution.py:10
  197.5 4.9 %collective-permute-start.11 = (bf16[1,128,128]{2,1,0:T(8,128)(2,1)S(1)}, bf16[1,128,128]{2,1,0:T(8,128)(2,1)S(1)}, u32[]{:S(2)}, u32[]{:S(2)}) collective-permute-start(bf16[1,128,128]{2,1,0:T(8,128)(2,1)S(1)} %get-tuple-element.115), channel_id=1, source_target_pairs={{0,8},{4,12},{8,0},{12,4},{1,9},{5,13},{9,1},{13,5},{2,10},{6,14},... | collective-permute-start | bytes 98312 | tf_op jit(solution)/shard_map/ppermute | solution.py:10
  203.0 0.7 copy-start.12
Sparse Core Ops, SparseCore 0:
  124.4 30.4 all-reduce.3
where the time goes:
time: 213 us; the launch traced here: 211 us
  other arithmetic  42.5 us (20%)
  matrix products  40.3 us (19%)
  waiting for transfers between devices  36.1 us (17%)
  local copies, waits for them, and re-layouts  29.4 us (14%)
  blocking collectives  23.2 us (11%)
  between operations  20.1 us (9%)
  starting transfers between devices  19 us (9%)
    dot_general x36, matrix products, project(): jnp.dot(flat_inputs, matrix, preferred_element_type=jnp.float32)  38.9 us
    unnamed x2, waiting for transfers between devices  28.1 us
    scatter-add x3, other arithmetic, message_layer(): jnp.take(sender, flat_index, axis=0)  27.9 us
    ppermute x12, starting transfers between devices, swapped(): return lax.ppermute(value, axis, pairs)  18.9 us
    unnamed x99, local copies, waits for them, and re-layouts  12.9 us
    gather x3, local copies, waits for them, and re-layouts, message_layer(): jnp.take(sender, flat_index, axis=0)  12 us
    ppermute x12, waiting for transfers between devices, swapped(): return lax.ppermute(value, axis, pairs)  7.97 us
    all_gather x1, blocking collectives, per_device(): piece_rows = lax.all_gather(first_rows, ('pair', 'sub'), axis=0, tiled=True)  6.54 us
  transfers between devices with their start and end apart: 13, of which 6 were waited for; matrix products, arithmetic and copies ran while one was open for 10% of the time, Pallas kernels for 0%

commit v1 on v0

v1 whole, which is shorter than its diff:
```python
import jax
import jax.numpy as jnp
from jax import lax
from jax.experimental import pallas as pl
from jax.experimental.pallas import tpu as pltpu
from jax.sharding import PartitionSpec as P

F32 = jnp.float32
BF16 = jnp.bfloat16
COUNT_ROWS = 16


def swapped(value, axis, mask):
    size = lax.axis_size(axis)
    return lax.ppermute(value, axis, [(source, source ^ mask) for source in range(size)])


def mm(a, b):
    return jnp.dot(a, b, preferred_element_type=F32)


def mm_t(a, b):
    return lax.dot_general(a, b, (((1,), (1,)), ((), ())), preferred_element_type=F32)


def sigmoid(x):
    return 0.5 * jnp.tanh(0.5 * x) + 0.5


def run(kernel, outs, scalars, *arrays, scratch=(), flops=0):
    in_specs = [pl.BlockSpec(memory_space=pltpu.SMEM)] + [pl.BlockSpec(memory_space=pltpu.VMEM)] * len(arrays)
    return pl.pallas_call(
        kernel,
        out_shape=[jax.ShapeDtypeStruct(shape, dtype) for shape, dtype in outs],
        in_specs=in_specs,
        out_specs=[pl.BlockSpec(memory_space=pltpu.VMEM)] * len(outs),
        scratch_shapes=list(scratch),
        compiler_params=pltpu.CompilerParams(vmem_limit_bytes=12 * 2**20),
        cost_estimate=pl.CostEstimate(flops=flops, bytes_accessed=2**20, transcendentals=0),
    )(scalars, *arrays)


def per_device(
    nodes,
    cotangent,
    send_blocks,
    neighbour_blocks,
    neighbour_nodes,
    pool_map,
    coarse_blocks,
    coarse_nodes,
    weights,
    biases,
):
    size, features = neighbour_nodes.shape[2], nodes.shape[1]
    blocks, degree = neighbour_blocks.shape
    xor_bits = (1, lax.axis_size("dom") // 2)
    rounds = len(xor_bits)
    group_axes = ("pair", "sub")
    slots = lax.axis_size(group_axes)
    edges = blocks * degree
    everyone = blocks + rounds
    tile = (size, features)

    at_near = rounds
    at_pool = at_near + edges
    at_coarse = at_pool + blocks
    at_me = at_coarse + degree
    scalars = jnp.concatenate(
        [
            send_blocks.reshape(-1),
            neighbour_blocks.reshape(-1),
            pool_map.reshape(-1),
            coarse_blocks.reshape(-1),
            lax.axis_index(group_axes).astype(jnp.int32)[None],
        ]
    )

    def exchange(pieces):
        return [swapped(piece, "dom", bit) for piece, bit in zip(pieces, xor_bits)]

    def spread(pieces):
        return [swapped(pieces[mask], group_axes, mask) for mask in range(1, slots)]

    def tables_into(ends_ref, count, pick_ref, put_ref):
        rows = lax.broadcasted_iota(jnp.int32, (size, size), 0)
        columns = lax.broadcasted_iota(jnp.int32, (size, size), 1)
        upright = jnp.transpose(ends_ref[...])
        for edge in range(count):
            put_ref[edge] = (rows == ends_ref[edge : edge + 1, :]).astype(BF16)
            pick_ref[edge] = (columns == upright[:, edge : edge + 1]).astype(BF16)

    def own_into(state, layer, w_ref, b_ref, recv_ref, node_ref, sender_ref):
        recv_ref[...] = mm(state, w_ref[layer, 0]) + b_ref[layer, 0:1, :]
        node_ref[...] = mm(state, w_ref[layer, 3]) + b_ref[layer, 1:2, :]
        sender_ref[...] = mm(state, w_ref[layer, 1]).astype(BF16)

    def forward_block(b, near_at, layer, s_ref, w_ref, recv_ref, node_ref, send_scr, pick_ref, slope_ref, node_slope_ref):
        rows = pl.ds(b * size, size)
        recv = recv_ref[rows, :]
        total = None
        for e in range(degree):
            edge = b * degree + e
            pre = recv + mm(pick_ref[edge], send_scr[s_ref[near_at + edge]])
            gate = sigmoid(pre)
            active = pre * gate
            slope_ref[edge] = (gate + active * (1.0 - gate)).astype(BF16)
            message = active.astype(BF16).astype(F32)
            total = message if total is None else total + message
        average = (mm(total.astype(BF16), w_ref[layer, 2]) * (1.0 / degree)).astype(BF16)
        hidden_pre = node_ref[rows, :] + mm(average, w_ref[layer, 4])
        gate = sigmoid(hidden_pre)
        hidden = hidden_pre * gate
        node_slope_ref[b] = (gate + hidden * (1.0 - gate)).astype(BF16)
        return mm(hidden.astype(BF16), w_ref[layer, 5])

    def backward_edges(grad, b, near_at, layer, s_ref, w_ref, put_ref, slope_ref, node_slope_ref, acc_scr):
        d_hidden = (mm_t(grad.astype(BF16), w_ref[layer, 5]) * node_slope_ref[b].astype(F32)).astype(BF16)
        d_average = (mm_t(d_hidden, w_ref[layer, 4]) * (1.0 / degree)).astype(BF16)
        d_active = mm_t(d_average, w_ref[layer, 2])
        total = None
        for e in range(degree):
            edge = b * degree + e
            d_pre = d_active * slope_ref[edge].astype(F32)
            total = d_pre if total is None else total + d_pre
            near = s_ref[near_at + edge]
            acc_scr[near] = acc_scr[near] + mm(put_ref[edge], d_pre.astype(BF16))
        return d_hidden, total.astype(BF16)

    def pooled_into(read, s_ref, out_refs, with_count):
        me = s_ref[at_me]
        for mask in range(slots):
            slot = me ^ mask
            total, count = None, None
            for b in range(blocks):
                hit = (s_ref[at_pool + b] == slot).astype(F32)
                part = read(b) * hit
                total = part if total is None else total + part
                count = hit if count is None else count + hit
            out_refs[mask][0:size, :] = total.astype(BF16)
            if with_count:
                out_refs[mask][size:, :] = jnp.full((COUNT_ROWS, features), count, F32).astype(BF16)

    def send_rows(b):
        return lax.dynamic_slice_in_dim(nodes, b * size, size, axis=0)

    halo = exchange([send_rows(send_blocks[0, r, 0]) for r in range(rounds)])

    def prepare(s_ref, ends_ref, coarse_ref, h_ref, w_ref, b_ref, pick, put, cpick, cput, recv, node, sender):
        tables_into(ends_ref, edges, pick, put)
        tables_into(coarse_ref, degree, cpick, cput)
        own_into(h_ref[...], 0, w_ref, b_ref, recv, node, sender)

    fine_own = [((blocks * size, features), F32), ((blocks * size, features), F32), ((blocks * size, features), BF16)]
    coarse_own = [(tile, F32), (tile, F32), (tile, BF16)]
    pick, put, coarse_pick, coarse_put, recv0, node0, sender0 = run(
        prepare,
        [((edges, size, size), BF16)] * 2 + [((degree, size, size), BF16)] * 2 + fine_own,
        scalars,
        neighbour_nodes.reshape(edges, size),
        coarse_nodes.reshape(degree, size),
        nodes,
        weights,
        biases,
    )

    slopes = [((edges,) + tile, BF16), ((blocks,) + tile, BF16)]
    pool_out = [((size + COUNT_ROWS, features), BF16)] * slots

    def first_layer(s_ref, g0, g1, h_ref, recv, node, sender, pick, w_ref, *rest):
        first_ref, slope_ref, node_slope_ref = rest[:3]
        sends, send_scr = rest[3:-1], rest[-1]
        for b in range(blocks):
            send_scr[b] = sender[pl.ds(b * size, size), :]
        for r, g in enumerate((g0, g1)):
            send_scr[blocks + r] = mm(g[...], w_ref[0, 1]).astype(BF16)
        for b in range(blocks):
            change = forward_block(b, at_near, 0, s_ref, w_ref, recv, node, send_scr, pick, slope_ref, node_slope_ref)
            first_ref[b] = (h_ref[pl.ds(b * size, size), :].astype(F32) + change).astype(BF16)
        pooled_into(lambda b: first_ref[b].astype(F32), s_ref, sends, True)

    first, slope0, node_slope0, *pool_sends = run(
        first_layer,
        [((blocks,) + tile, BF16)] + slopes + pool_out,
        scalars, halo[0], halo[1], nodes, recv0, node0, sender0, pick, weights,
        scratch=[pltpu.VMEM((everyone,) + tile, BF16)],
    )

    pool_in = spread(pool_sends)

    def coarse_begin(s_ref, *refs):
        parts, (start_ref, divisor_ref) = refs[:slots], refs[slots:]
        total = parts[0][...].astype(F32)
        for part in parts[1:]:
            total = total + part[...].astype(F32)
        divisor = jnp.maximum(total[size : size + 8, :], 1.0)
        divisor_ref[...] = divisor
        start_ref[...] = (total[:size, :] / divisor[0:1, :]).astype(BF16)

    coarse_start, divisor = run(
        coarse_begin, [(tile, BF16), ((8, features), F32)], scalars, pool_sends[0], *pool_in
    )
    coarse_halo = exchange([coarse_start] * rounds)

    def coarse_prepare(s_ref, h_ref, w_ref, b_ref, recv, node, sender):
        own_into(h_ref[...], 1, w_ref, b_ref, recv, node, sender)

    recv1, node1, sender1 = run(coarse_prepare, coarse_own, scalars, coarse_start, weights, biases)

    def coarse_layer(s_ref, g0, g1, h_ref, recv, node, sender, pick, w_ref, end_ref, slope_ref, node_slope_ref, send_scr):
        send_scr[0] = sender[...]
        for r, g in enumerate((g0, g1)):
            send_scr[1 + r] = mm(g[...], w_ref[1, 1]).astype(BF16)
        change = forward_block(0, at_coarse, 1, s_ref, w_ref, recv, node, send_scr, pick, slope_ref, node_slope_ref)
        end_ref[...] = (h_ref[...].astype(F32) + change).astype(BF16)

    coarse_end, slope1, node_slope1 = run(
        coarse_layer,
        [(tile, BF16), ((degree,) + tile, BF16), ((1,) + tile, BF16)],
        scalars, coarse_halo[0], coarse_halo[1], coarse_start, recv1, node1, sender1, coarse_pick, weights,
        scratch=[pltpu.VMEM((1 + rounds,) + tile, BF16)],
    )
    ends_in = spread([coarse_end] * slots)

    def lift(s_ref, *refs):
        parts, first_ref = refs[:slots], refs[slots]
        middle_ref, out0, out1, table = refs[slots + 1 :]
        me = s_ref[at_me]
        for mask in range(slots):
            table[me ^ mask] = parts[mask][...]
        for b in range(blocks):
            lifted = table[s_ref[at_pool + b]].astype(F32)
            middle_ref[b] = (first_ref[b].astype(F32) + lifted).astype(BF16)
        for r, out in enumerate((out0, out1)):
            out[...] = middle_ref[s_ref[r]]

    middle, *middle_sends = run(
        lift,
        [((blocks,) + tile, BF16)] + [(tile, BF16)] * rounds,
        scalars, coarse_end, *ends_in, first,
        scratch=[pltpu.VMEM((slots,) + tile, BF16)],
    )
    halo = exchange(middle_sends)

    def last_prepare(s_ref, h_ref, w_ref, b_ref, recv, node, sender):
        own_into(h_ref[...].reshape(blocks * size, features), 2, w_ref, b_ref, recv, node, sender)

    recv2, node2, sender2 = run(last_prepare, fine_own, scalars, middle, weights, biases)

    back_out = [(tile, BF16)] * rounds + [((blocks,) + tile, BF16)] * 3

    def backward_out(read, layer, s_ref, w_ref, put_ref, slope_ref, node_slope_ref, halo_refs, d_node, d_recv, d_send, acc_scr):
        acc_scr[...] = jnp.zeros_like(acc_scr)
        for b in range(blocks):
            d_node[b], d_recv[b] = backward_edges(
                read(b), b, at_near, layer, s_ref, w_ref, put_ref, slope_ref, node_slope_ref, acc_scr
            )
        for r, out in enumerate(halo_refs):
            out[...] = mm_t(acc_scr[blocks + r].astype(BF16), w_ref[layer, 1]).astype(BF16)
        d_send[...] = acc_scr[0:blocks].astype(BF16)

    def last_layer(s_ref, g0, g1, h_ref, recv, node, sender, pick, put, w_ref, cot_ref, out_ref, h0, h1, d_node, d_recv, d_send, send_scr, slope_scr, node_slope_scr, acc_scr):
        for b in range(blocks):
            send_scr[b] = sender[pl.ds(b * size, size), :]
        for r, g in enumerate((g0, g1)):
            send_scr[blocks + r] = mm(g[...], w_ref[2, 1]).astype(BF16)
        for b in range(blocks):
            change = forward_block(b, at_near, 2, s_ref, w_ref, recv, node, send_scr, pick, slope_scr, node_slope_scr)
            out_ref[pl.ds(b * size, size), :] = (h_ref[b].astype(F32) + change).astype(BF16)
        backward_out(
            lambda b: cot_ref[pl.ds(b * size, size), :],
            2, s_ref, w_ref, put, slope_scr, node_slope_scr, (h0, h1), d_node, d_recv, d_send, acc_scr,
        )

    out_nodes, *rest = run(
        last_layer,
        [((blocks * size, features), BF16)] + back_out,
        scalars, halo[0], halo[1], middle, recv2, node2, sender2, pick, put, weights, cotangent,
        scratch=[
            pltpu.VMEM((everyone,) + tile, BF16),
            pltpu.VMEM((edges,) + tile, BF16),
            pltpu.VMEM((blocks,) + tile, BF16),
            pltpu.VMEM((everyone,) + tile, F32),
        ],
    )
    halo_grads, (d_node, d_recv, d_send) = rest[:rounds], rest[rounds:]
    returned = exchange(halo_grads)

    def own_back(layer, b, grad, w_ref, d_node, d_recv, d_send):
        return (
            grad
            + mm_t(d_recv[b], w_ref[layer, 0])
            + mm_t(d_node[b], w_ref[layer, 3])
            + mm_t(d_send[b], w_ref[layer, 1])
        )

    def last_own(s_ref, cot_ref, d_node, d_recv, d_send, w_ref, grad_ref):
        for b in range(blocks):
            grad = cot_ref[pl.ds(b * size, size), :].astype(F32)
            grad_ref[b] = own_back(2, b, grad, w_ref, d_node, d_recv, d_send)

    (grad_own,) = run(
        last_own, [((blocks,) + tile, F32)], scalars, cotangent, d_node, d_recv, d_send, weights
    )

    def pool_grads(s_ref, r0, r1, own_ref, grad_ref, *sends):
        grad_ref[...] = own_ref[...]
        for r, arrived in enumerate((r0, r1)):
            grad_ref[s_ref[r]] = grad_ref[s_ref[r]] + arrived[...].astype(F32)
        pooled_into(lambda b: grad_ref[b], s_ref, sends, False)

    grad_middle, *grad_sends = run(
        pool_grads,
        [((blocks,) + tile, F32)] + [(tile, BF16)] * slots,
        scalars, returned[0], returned[1], grad_own,
    )
    grads_in = spread(grad_sends)

    def coarse_back(s_ref, *refs):
        parts = refs[:slots]
        put, slope_ref, node_slope_ref, w_ref, own_ref, h0, h1, acc_scr = refs[slots:]
        grad = parts[0][...].astype(F32)
        for part in parts[1:]:
            grad = grad + part[...].astype(F32)
        acc_scr[...] = jnp.zeros_like(acc_scr)
        d_node, d_recv = backward_edges(
            grad, 0, at_coarse, 1, s_ref, w_ref, put, slope_ref, node_slope_ref, acc_scr
        )
        for r, out in enumerate((h0, h1)):
            out[...] = mm_t(acc_scr[1 + r].astype(BF16), w_ref[1, 1]).astype(BF16)
        own_ref[...] = (
            grad
            + mm_t(d_recv, w_ref[1, 0])
            + mm_t(d_node, w_ref[1, 3])
            + mm_t(acc_scr[0].astype(BF16), w_ref[1, 1])
        )

    coarse_grad, *coarse_sends = run(
        coarse_back,
        [(tile, F32)] + [(tile, BF16)] * rounds,
        scalars, grad_sends[0], *grads_in, coarse_put, slope1, node_slope1, weights,
        scratch=[pltpu.VMEM((1 + rounds,) + tile, F32)],
    )
    coarse_returned = exchange(coarse_sends)

    def scale(s_ref, own_ref, r0, r1, divisor_ref, out_ref):
        total = own_ref[...] + r0[...].astype(F32) + r1[...].astype(F32)
        out_ref[...] = (total / divisor_ref[0:1, :]).astype(BF16)

    (scaled,) = run(scale, [(tile, BF16)], scalars, coarse_grad, *coarse_returned, divisor)
    scaled_in = spread([scaled] * slots)

    def first_back(s_ref, *refs):
        parts = refs[:slots]
        middle_ref, put, slope_ref, node_slope_ref, w_ref = refs[slots : slots + 5]
        grad_ref, h0, h1, d_node, d_recv, d_send, table, acc_scr = refs[slots + 5 :]
        me = s_ref[at_me]
        for mask in range(slots):
            table[me ^ mask] = parts[mask][...]
        for b in range(blocks):
            grad_ref[b] = middle_ref[b] + table[s_ref[at_pool + b]].astype(F32)
        backward_out(
            lambda b: grad_ref[b],
            0, s_ref, w_ref, put, slope_ref, node_slope_ref, (h0, h1), d_node, d_recv, d_send, acc_scr,
        )

    grad_first, *rest = run(
        first_back,
        [((blocks,) + tile, F32)] + back_out,
        scalars, scaled, *scaled_in, grad_middle, put, slope0, node_slope0, weights,
        scratch=[pltpu.VMEM((slots,) + tile, BF16), pltpu.VMEM((everyone,) + tile, F32)],
    )
    halo_grads, (d_node, d_recv, d_send) = rest[:rounds], rest[rounds:]
    returned = exchange(halo_grads)

    def first_own(s_ref, first_ref, d_node, d_recv, d_send, w_ref, grad_ref):
        for b in range(blocks):
            grad_ref[b] = own_back(0, b, first_ref[b], w_ref, d_node, d_recv, d_send)

    (grad_own,) = run(
        first_own, [((blocks,) + tile, F32)], scalars, grad_first, d_node, d_recv, d_send, weights
    )

    def finish(s_ref, r0, r1, own_ref, out_ref):
        out_ref[...] = own_ref[...]
        for r, arrived in enumerate((r0, r1)):
            out_ref[s_ref[r]] = out_ref[s_ref[r]] + arrived[...].astype(F32)

    (grad_nodes,) = run(finish, [((blocks,) + tile, F32)], scalars, returned[0], returned[1], grad_own)
    return (out_nodes, grad_nodes.reshape(-1, features))


def solution(mesh):
    split = ("groups", "dom", "pair", "sub")
    placed = (
        P(split, None),
        P(split, None),
        P(split, None, None),
        P(split, None),
        P(split, None, None),
        P(split),
        P(split, None),
        P(split, None, None),
        P(),
        P(),
    )
    return jax.shard_map(
        per_device,
        mesh=mesh,
        in_specs=placed,
        out_specs=(P(split, None), P(split, None)),
        check_vma=False,
    )
```

time: 213 us -> 78.3 us (0.37)
  other arithmetic: 42.5 us -> 0 us
  matrix products: 40.3 us -> 0 us
  local copies, waits for them, and re-layouts: 29.4 us -> 5.45 us
  blocking collectives: 23.2 us -> 0 us
  Pallas kernels: 0 us -> 20.7 us
  between operations: 20.1 us -> 2.1 us
  waiting for transfers between devices: 36.1 us -> 24.2 us
  starting transfers between devices: 19 us -> 25.5 us
    dot_general x38 -> x0, matrix products: 40.3 us -> none  [the longest x36 38.9 us: project(): jnp.dot(flat_inputs, matrix, preferred_element_type=jnp.float32)]
    scatter-add x7 -> x0, other arithmetic: 30.5 us -> none  [the longest x3 27.9 us: message_layer(): jnp.take(sender, flat_index, axis=0)]
    unnamed x2 -> x0, waiting for transfers between devices: 28.1 us -> none
    pallas_call x0 -> x15, Pallas kernels: none -> 20.7 us  [run(): pl.pallas_call(kernel, out_shape=[jax.ShapeDtypeStruct(shape, dtype) for...]
    all_gather x3 -> x0, blocking collectives: 18.1 us -> none  [the longest x1 6.54 us: per_device(): piece_rows = lax.all_gather(first_rows, ('pair', 'sub'), axis=0, tiled=True)]
    ppermute x12 -> x24, waiting for transfers between devices: 7.97 us -> 24.2 us  [swapped(): lax.ppermute(value, axis, [(source, source ^ mask) for source in range(si...]
    gather x5 -> x0, local copies, waits for them, and re-layouts: 13.6 us -> none  [the longest x3 12 us: message_layer(): jnp.take(sender, flat_index, axis=0)]
    unnamed x99 -> x22, local copies, waits for them, and re-layouts: 12.9 us -> 3.12 us
  transfers between devices with their start and end apart: 13 -> 24, of which waited for: 6 -> 15; matrix products, arithmetic and copies ran while one was open for 10% -> 0% of each run, Pallas kernels for 0% -> 6%
where the time goes in v1:
time: 78.3 us; the launch traced here: 78 us
  starting transfers between devices  25.5 us (33%)
  waiting for transfers between devices  24.2 us (31%)
  Pallas kernels  20.7 us (26%)
  local copies, waits for them, and re-layouts  5.45 us (7%)
  between operations  2.1 us (3%)
    ppermute x24, starting transfers between devices, swapped(): lax.ppermute(value, axis, [(source, source ^ mask) for source in range(si...  25.5 us
    ppermute x24, waiting for transfers between devices, swapped(): lax.ppermute(value, axis, [(source, source ^ mask) for source in range(si...  24.2 us
    pallas_call x15, Pallas kernels, run(): pl.pallas_call(kernel, out_shape=[jax.ShapeDtypeStruct(shape, dtype) for...  20.7 us
    unnamed x22, local copies, waits for them, and re-layouts  3.12 us
  transfers between devices with their start and end apart: 24, of which 15 were waited for; matrix products, arithmetic and copies ran while one was open for 0% of the time, Pallas kernels for 6%

profile of v1, /device:TPU:0, one launch (start us, length us, event | category | flops | bytes accessed | tf_op | source)
XLA Modules:
  0.0 78.0 jit_solution(18132699495017273112)
XLA Ops:
  0.6 1.3 %fusion = (s32[1,1,1]{1,2,0:T(1,128)}, s32[1,1,1]{1,2,0:T(1,128)}) fusion(s32[1,2,1]{1,2,0:T(1,128)} %param.12), kind=kLoop, calls=%fused_computation.2 | loop fusion | bytes 16 | tf_op jit(solution)/shard_map/slice | solution.py:147
  3.3 0.8 %constant_dynamic-slice_fusion = (bf16[128,128]{1,0:T(8,128)(2,1)S(1)}, bf16[128,128]{1,0:T(8,128)(2,1)S(1)}) fusion(bf16[512,128]{1,0:T(8,128)(2,1)} %h_ref.3, s32[]{:T(128)S(6)} %select_n.7, s32[]{:T(128)S(6)} %select_n.6), kind=kLoop, calls=%fused_computation | loop fusion | bytes 131080 | tf_op jit(solution)/shard_map/dynamic_slice | solution.py:145
  4.1 4.0 %collective-permute-start.1 = (bf16[128,128]{1,0:T(8,128)(2,1)S(1)}, bf16[128,128]{1,0:T(8,128)(2,1)S(1)}, u32[]{:S(2)}, u32[]{:S(2)}) collective-permute-start(bf16[128,128]{1,0:T(8,128)(2,1)S(1)} %get-tuple-element.98), channel_id=1, source_target_pairs={{0,8},{4,12},{8,0},{12,4},{1,9},{5,13},{9,1},{13,5},{2,10},{6,14},... | collective-permute-start | bytes 98312 | tf_op jit(solution)/shard_map/ppermute | solution.py:15
  8.1 1.5 %collective-permute-start = (bf16[128,128]{1,0:T(8,128)(2,1)S(1)}, bf16[128,128]{1,0:T(8,128)(2,1)S(1)}, u32[]{:S(2)}, u32[]{:S(2)}) collective-permute-start(bf16[128,128]{1,0:T(8,128)(2,1)S(1)} %get-tuple-element.99), channel_id=1, source_target_pairs={{0,4},{4,0},{8,12},{12,8},{1,5},{5,1},{9,13},{13,9},{2,6},{6,2},{1... | collective-permute-start | bytes 98312 | tf_op jit(solution)/shard_map/ppermute | solution.py:15
  9.7 0.7 copy-done.8
  10.3 0.1 reshape.27
  10.4 0.6 copy-done.10
  11.0 0.1 copy-done.7
  11.1 0.1 concatenate.3.s_ref
  11.2 0.6 copy-done.4
  11.8 0.1 copy-done.6
  11.9 1.1 %copy-done = bf16[3,6,128,128]{3,2,1,0:T(8,128)(2,1)S(1)} copy-done((bf16[3,6,128,128]{3,2,1,0:T(8,128)(2,1)S(1)}, bf16[3,6,128,128]{3,2,1,0:T(8,128)(2,1)}, u32[]{:S(2)}) %copy-start) | copy-done | bytes 589848
  13.0 1.1 %shard_map.113 = (bf16[16,128,128]{2,1,0:T(8,128)(2,1)S(1)}, bf16[16,128,128]{2,1,0:T(8,128)(2,1)S(1)}, bf16[4,128,128]{2,1,0:T(8,128)(2,1)S(1)}, bf16[4,128,128...) custom-call(s32[27]{0:T(128)S(1)} %concatenate.3.s_ref, ...), custom_call_target="tpu_custom_call" | custom-call | bytes 1048576 | tf_op jit(solution)/shard_map/pallas_call | solution.py:32
  14.1 2.7 %shard_map.114 = (bf16[4,128,128]{2,1,0:T(8,128)(2,1)S(1)}, bf16[16,128,128]{2,1,0:T(8,128)(2,1)S(1)}, bf16[4,128,128]{2,1,0:T(8,128)(2,1)S(1)}, bf16[144,128]{1...) custom-call(s32[27]{0:T(128)S(1)} %concatenate.3.s_ref, ...), custom_call_target="tpu_custom_call" | custom-call | bytes 1048576 | tf_op jit(solution)/shard_map/pallas_call | solution.py:32
  16.8 0.1 collective-permute-start.2
  16.9 1.6 %collective-permute-start.3 = (bf16[144,128]{1,0:T(8,128)(2,1)S(1)}, bf16[144,128]{1,0:T(8,128)(2,1)S(1)}, u32[]{:S(2)}, u32[]{:S(2)}) collective-permute-start(bf16[144,128]{1,0:T(8,128)(2,1)S(1)} %get-tuple-element.56), channel_id=1, source_target_pairs={{0,2},{1,3},{2,0},{3,1},{4,6},{5,7},{6,4},{7,5},{8,10},{9,11},{10,... | collective-permute-start | bytes 110600 | tf_op jit(solution)/shard_map/ppermute | solution.py:15
  18.4 0.3 collective-permute-start.4
  18.7 2.2 %collective-permute-done.3.refs_2_ = bf16[144,128]{1,0:T(8,128)(2,1)S(1)} collective-permute-done((bf16[144,128]{1,0:T(8,128)(2,1)S(1)}, bf16[144,128]{1,0:T(8,128)(2,1)S(1)}, u32[]{:S(2)}, u32[]{:S(2)}) %collective-permute-start.3) | collective-permute-done | bytes 36896 | tf_op jit(solution)/shard_map/ppermute | solution.py:15
  20.9 1.0 %collective-permute-done.4.refs_3_ = bf16[144,128]{1,0:T(8,128)(2,1)S(1)} collective-permute-done((bf16[144,128]{1,0:T(8,128)(2,1)S(1)}, bf16[144,128]{1,0:T(8,128)(2,1)S(1)}, u32[]{:S(2)}, u32[]{:S(2)}) %collective-permute-start.4) | collective-permute-done | bytes 36896 | tf_op jit(solution)/shard_map/ppermute | solution.py:15
  21.9 0.6 shard_map.115
  22.4 0.4 collective-permute-start.6
  22.9 0.4 collective-permute-start.5
  23.3 0.7 shard_map.116
  24.0 3.6 %collective-permute-done.6.g1 = bf16[128,128]{1,0:T(8,128)(2,1)S(1)} collective-permute-done((bf16[128,128]{1,0:T(8,128)(2,1)S(1)}, bf16[128,128]{1,0:T(8,128)(2,1)S(1)}, u32[]{:S(2)}, u32[]{:S(2)}) %collective-permute-start.6) | collective-permute-done | bytes 32800 | tf_op jit(solution)/shard_map/ppermute | solution.py:15
  27.6 1.3 %shard_map.117 = (bf16[128,128]{1,0:T(8,128)(2,1)S(1)}, bf16[4,128,128]{2,1,0:T(8,128)(2,1)S(1)}, bf16[1,128,128]{2,1,0:T(8,128)(2,1)S(1)}) custom-call(s32[27]{0:T(128)S(1)} %concatenate.3.s_ref, bf16[128,128]{1,0:T(8,128)(2,1)S(1)} %collective-permute-done.5.g0, bf16[128,128]{1,0:T(8,128)(2,1)S(1)} %collective-permute-done.6.g1, ...), custom_call_target="tpu_custom_call" | custom-call | bytes 1048576 | tf_op jit(solution)/shard_map/pallas_call | solution.py:32
  28.9 0.1 collective-permute-start.9
  29.0 1.0 %collective-permute-start.8 = (bf16[128,128]{1,0:T(8,128)(2,1)S(1)}, bf16[128,128]{1,0:T(8,128)(2,1)S(1)}, u32[]{:S(2)}, u32[]{:S(2)}) collective-permute-start(bf16[128,128]{1,0:T(8,128)(2,1)S(1)} %get-tuple-element.63.refs_0_), channel_id=1, source_target_pairs={{0,2},{1,3},{2,0},{3,1},{4,6},{5,7},{6,4},{7,5},{8,10},{9,11},{10,... | collective-permute-start | bytes 98312 | tf_op jit(solution)/shard_map/ppermute | solution.py:15
  30.0 0.8 %collective-permute-start.7 = (bf16[128,128]{1,0:T(8,128)(2,1)S(1)}, bf16[128,128]{1,0:T(8,128)(2,1)S(1)}, u32[]{:S(2)}, u32[]{:S(2)}) collective-permute-start(bf16[128,128]{1,0:T(8,128)(2,1)S(1)} %get-tuple-element.63.refs_0_), channel_id=1, source_target_pairs={{0,1},{1,0},{2,3},{3,2},{4,5},{5,4},{6,7},{7,6},{8,9},{9,8},{10,11... | collective-permute-start | bytes 98312 | tf_op jit(solution)/shard_map/ppermute | solution.py:15
  30.8 1.5 %collective-permute-done.9.refs_3_ = bf16[128,128]{1,0:T(8,128)(2,1)S(1)} collective-permute-done((bf16[128,128]{1,0:T(8,128)(2,1)S(1)}, bf16[128,128]{1,0:T(8,128)(2,1)S(1)}, u32[]{:S(2)}, u32[]{:S(2)}) %collective-permute-start.9) | collective-permute-done | bytes 32800 | tf_op jit(solution)/shard_map/ppermute | solution.py:15
  32.3 1.0 %collective-permute-done.8.refs_2_ = bf16[128,128]{1,0:T(8,128)(2,1)S(1)} collective-permute-done((bf16[128,128]{1,0:T(8,128)(2,1)S(1)}, bf16[128,128]{1,0:T(8,128)(2,1)S(1)}, u32[]{:S(2)}, u32[]{:S(2)}) %collective-permute-start.8) | collective-permute-done | bytes 32800 | tf_op jit(solution)/shard_map/ppermute | solution.py:15
  33.3 0.6 shard_map.118
  33.9 0.3 collective-permute-start.10
  34.2 2.0 %collective-permute-start.11 = (bf16[128,128]{1,0:T(8,128)(2,1)S(1)}, bf16[128,128]{1,0:T(8,128)(2,1)S(1)}, u32[]{:S(2)}, u32[]{:S(2)}) collective-permute-start(bf16[128,128]{1,0:T(8,128)(2,1)S(1)} %get-tuple-element.66), channel_id=1, source_target_pairs={{0,8},{4,12},{8,0},{12,4},{1,9},{5,13},{9,1},{13,5},{2,10},{6,14},... | collective-permute-start | bytes 98312 | tf_op jit(solution)/shard_map/ppermute | solution.py:15
  36.2 0.8 %shard_map.119 = (f32[512,128]{1,0:T(8,128)S(1)}, f32[512,128]{1,0:T(8,128)S(1)}, bf16[512,128]{1,0:T(8,128)(2,1)S(1)}) custom-call(s32[27]{0:T(128)S(1)} %concatenate.3.s_ref, bf16[4,128,128]{2,1,0:T(8,128)(2,1)S(1)} %get-tuple-element.67.h_ref, bf16[3,6,128,128]{3,2,1,0:T(8,128)(2,1)S(1)} %copy-done.1, f32[3,2,128]{2,1,0:T(2,128)S(1)} %copy-done.4), custom_call_target="tpu_custom_call" | custom-call | bytes 1048576 | tf_op jit(solution)/shard_map/pallas_call | solution.py:32
  37.0 1.2 %collective-permute-done.10.g0 = bf16[128,128]{1,0:T(8,128)(2,1)S(1)} collective-permute-done((bf16[128,128]{1,0:T(8,128)(2,1)S(1)}, bf16[128,128]{1,0:T(8,128)(2,1)S(1)}, u32[]{:S(2)}, u32[]{:S(2)}) %collective-permute-start.10) | collective-permute-done | bytes 32800 | tf_op jit(solution)/shard_map/ppermute | solution.py:15
  38.2 1.0 %collective-permute-done.11.g1 = bf16[128,128]{1,0:T(8,128)(2,1)S(1)} collective-permute-done((bf16[128,128]{1,0:T(8,128)(2,1)S(1)}, bf16[128,128]{1,0:T(8,128)(2,1)S(1)}, u32[]{:S(2)}, u32[]{:S(2)}) %collective-permute-start.11) | collective-permute-done | bytes 32800 | tf_op jit(solution)/shard_map/ppermute | solution.py:15
  39.2 4.7 %shard_map.120 = (bf16[512,128]{1,0:T(8,128)(2,1)}, bf16[128,128]{1,0:T(8,128)(2,1)S(1)}, bf16[128,128]{1,0:T(8,128)(2,1)S(1)}, bf16[4,128,128]{2,1,0:T(8,128)(2...) custom-call(s32[27]{0:T(128)S(1)} %concatenate.3.s_ref, ...), custom_call_target="tpu_custom_call" | custom-call | bytes 1048576 | tf_op jit(solution)/shard_map/pallas_call | solution.py:32
  43.9 1.6 %collective-permute-start.12 = (bf16[128,128]{1,0:T(8,128)(2,1)S(1)}, bf16[128,128]{1,0:T(8,128)(2,1)S(1)}, u32[]{:S(2)}, u32[]{:S(2)}) collective-permute-start(bf16[128,128]{1,0:T(8,128)(2,1)S(1)} %get-tuple-element.73), channel_id=1, source_target_pairs={{0,4},{4,0},{8,12},{12,8},{1,5},{5,1},{9,13},{13,9},{2,6},{6,2},{1... | collective-permute-start | bytes 98312 | tf_op jit(solution)/shard_map/ppermute | solution.py:15
  45.5 2.0 %collective-permute-start.13 = (bf16[128,128]{1,0:T(8,128)(2,1)S(1)}, bf16[128,128]{1,0:T(8,128)(2,1)S(1)}, u32[]{:S(2)}, u32[]{:S(2)}) collective-permute-start(bf16[128,128]{1,0:T(8,128)(2,1)S(1)} %get-tuple-element.74), channel_id=1, source_target_pairs={{0,8},{4,12},{8,0},{12,4},{1,9},{5,13},{9,1},{13,5},{2,10},{6,14},... | collective-permute-start | bytes 98312 | tf_op jit(solution)/shard_map/ppermute | solution.py:15
  47.5 0.9 %shard_map.121.own_ref = f32[4,128,128]{2,1,0:T(8,128)S(1)} custom-call(s32[27]{0:T(128)S(1)} %concatenate.3.s_ref, bf16[512,128]{1,0:T(8,128)(2,1)S(1)} %copy-done.3, bf16[4,128,128]{2,1,0:T(8,128)(2,1)S(1)} %get-tuple-element.75.d_node, bf16[4,128,128]{2,1,0:T(8,128)(2,1)S(1)} %get-tuple-element.76.d_recv, ...), custom_call_target="tpu_custom_call" | custom-call | bytes 1048576 | tf_op jit(solution)/shard_map/pallas_call | solution.py:32
  48.5 2.1 %collective-permute-done.13.r1 = bf16[128,128]{1,0:T(8,128)(2,1)S(1)} collective-permute-done((bf16[128,128]{1,0:T(8,128)(2,1)S(1)}, bf16[128,128]{1,0:T(8,128)(2,1)S(1)}, u32[]{:S(2)}, u32[]{:S(2)}) %collective-permute-start.13) | collective-permute-done | bytes 32800 | tf_op jit(solution)/shard_map/ppermute | solution.py:15
  50.6 0.7 shard_map.122
  51.2 0.1 collective-permute-start.14
  51.3 0.9 %collective-permute-start.15 = (bf16[128,128]{1,0:T(8,128)(2,1)S(1)}, bf16[128,128]{1,0:T(8,128)(2,1)S(1)}, u32[]{:S(2)}, u32[]{:S(2)}) collective-permute-start(bf16[128,128]{1,0:T(8,128)(2,1)S(1)} %get-tuple-element.80), channel_id=1, source_target_pairs={{0,2},{1,3},{2,0},{3,1},{4,6},{5,7},{6,4},{7,5},{8,10},{9,11},{10,... | collective-permute-start | bytes 98312 | tf_op jit(solution)/shard_map/ppermute | solution.py:15
  52.1 1.0 %collective-permute-start.16 = (bf16[128,128]{1,0:T(8,128)(2,1)S(1)}, bf16[128,128]{1,0:T(8,128)(2,1)S(1)}, u32[]{:S(2)}, u32[]{:S(2)}) collective-permute-start(bf16[128,128]{1,0:T(8,128)(2,1)S(1)} %get-tuple-element.81), channel_id=1, source_target_pairs={{0,3},{1,2},{2,1},{3,0},{4,7},{5,6},{6,5},{7,4},{8,11},{9,10},{10,... | collective-permute-start | bytes 98312 | tf_op jit(solution)/shard_map/ppermute | solution.py:15
  53.2 2.2 %collective-permute-done.15.refs_2_ = bf16[128,128]{1,0:T(8,128)(2,1)S(1)} collective-permute-done((bf16[128,128]{1,0:T(8,128)(2,1)S(1)}, bf16[128,128]{1,0:T(8,128)(2,1)S(1)}, u32[]{:S(2)}, u32[]{:S(2)}) %collective-permute-start.15) | collective-permute-done | bytes 32800 | tf_op jit(solution)/shard_map/ppermute | solution.py:15
  55.4 0.4 collective-permute-done.16.refs_3_
  55.8 1.4 %shard_map.123 = (f32[128,128]{1,0:T(8,128)S(1)}, bf16[128,128]{1,0:T(8,128)(2,1)S(1)}, bf16[128,128]{1,0:T(8,128)(2,1)S(1)}) custom-call(s32[27]{0:T(128)S(1)} %concatenate.3.s_ref, bf16[128,128]{1,0:T(8,128)(2,1)S(1)} %get-tuple-element.78.refs_0_, bf16[128,128]{1,0:T(8,128)(2,1)S(1)} %collective-permute-done.14.refs_1_, ...), custom_call_target="tpu_custom_call" | custom-call | bytes 1048576 | tf_op jit(solution)/shard_map/pallas_call | solution.py:32
  57.1 0.3 collective-permute-start.17
  57.4 1.8 %collective-permute-start.18 = (bf16[128,128]{1,0:T(8,128)(2,1)S(1)}, bf16[128,128]{1,0:T(8,128)(2,1)S(1)}, u32[]{:S(2)}, u32[]{:S(2)}) collective-permute-start(bf16[128,128]{1,0:T(8,128)(2,1)S(1)} %get-tuple-element.87), channel_id=1, source_target_pairs={{0,8},{4,12},{8,0},{12,4},{1,9},{5,13},{9,1},{13,5},{2,10},{6,14},... | collective-permute-start | bytes 98312 | tf_op jit(solution)/shard_map/ppermute | solution.py:15
  59.2 2.2 %collective-permute-done.17.r0 = bf16[128,128]{1,0:T(8,128)(2,1)S(1)} collective-permute-done((bf16[128,128]{1,0:T(8,128)(2,1)S(1)}, bf16[128,128]{1,0:T(8,128)(2,1)S(1)}, u32[]{:S(2)}, u32[]{:S(2)}) %collective-permute-start.17) | collective-permute-done | bytes 32800 | tf_op jit(solution)/shard_map/ppermute | solution.py:15
  61.5 1.1 %collective-permute-done.18.r1 = bf16[128,128]{1,0:T(8,128)(2,1)S(1)} collective-permute-done((bf16[128,128]{1,0:T(8,128)(2,1)S(1)}, bf16[128,128]{1,0:T(8,128)(2,1)S(1)}, u32[]{:S(2)}, u32[]{:S(2)}) %collective-permute-start.18) | collective-permute-done | bytes 32800 | tf_op jit(solution)/shard_map/ppermute | solution.py:15
  62.5 0.6 shard_map.124.refs_0_
  63.1 0.1 collective-permute-start.21
  63.2 1.0 %collective-permute-start.20 = (bf16[128,128]{1,0:T(8,128)(2,1)S(1)}, bf16[128,128]{1,0:T(8,128)(2,1)S(1)}, u32[]{:S(2)}, u32[]{:S(2)}) collective-permute-start(bf16[128,128]{1,0:T(8,128)(2,1)S(1)} %shard_map.124.refs_0_), channel_id=1, source_target_pairs={{0,2},{1,3},{2,0},{3,1},{4,6},{5,7},{6,4},{7,5},{8,10},{9,11},{10,... | collective-permute-start | bytes 98312 | tf_op jit(solution)/shard_map/ppermute | solution.py:15
  64.1 0.9 %collective-permute-start.19 = (bf16[128,128]{1,0:T(8,128)(2,1)S(1)}, bf16[128,128]{1,0:T(8,128)(2,1)S(1)}, u32[]{:S(2)}, u32[]{:S(2)}) collective-permute-start(bf16[128,128]{1,0:T(8,128)(2,1)S(1)} %shard_map.124.refs_0_), channel_id=1, source_target_pairs={{0,1},{1,0},{2,3},{3,2},{4,5},{5,4},{6,7},{7,6},{8,9},{9,8},{10,11... | collective-permute-start | bytes 98312 | tf_op jit(solution)/shard_map/ppermute | solution.py:15
  65.0 1.5 %collective-permute-done.21.refs_3_ = bf16[128,128]{1,0:T(8,128)(2,1)S(1)} collective-permute-done((bf16[128,128]{1,0:T(8,128)(2,1)S(1)}, bf16[128,128]{1,0:T(8,128)(2,1)S(1)}, u32[]{:S(2)}, u32[]{:S(2)}) %collective-permute-start.21) | collective-permute-done | bytes 32800 | tf_op jit(solution)/shard_map/ppermute | solution.py:15
  66.5 1.0 %collective-permute-done.20.refs_2_ = bf16[128,128]{1,0:T(8,128)(2,1)S(1)} collective-permute-done((bf16[128,128]{1,0:T(8,128)(2,1)S(1)}, bf16[128,128]{1,0:T(8,128)(2,1)S(1)}, u32[]{:S(2)}, u32[]{:S(2)}) %collective-permute-start.20) | collective-permute-done | bytes 32800 | tf_op jit(solution)/shard_map/ppermute | solution.py:15
  67.5 2.5 %shard_map.125 = (f32[4,128,128]{2,1,0:T(8,128)S(1)}, bf16[128,128]{1,0:T(8,128)(2,1)S(1)}, bf16[128,128]{1,0:T(8,128)(2,1)S(1)}, bf16[4,128,128]{2,1,0:T(8,128)...) custom-call(s32[27]{0:T(128)S(1)} %concatenate.3.s_ref, ...), custom_call_target="tpu_custom_call" | custom-call | bytes 1048576 | tf_op jit(solution)/shard_map/pallas_call | solution.py:32
  70.0 1.6 %collective-permute-start.22 = (bf16[128,128]{1,0:T(8,128)(2,1)S(1)}, bf16[128,128]{1,0:T(8,128)(2,1)S(1)}, u32[]{:S(2)}, u32[]{:S(2)}) collective-permute-start(bf16[128,128]{1,0:T(8,128)(2,1)S(1)} %get-tuple-element.92), channel_id=1, source_target_pairs={{0,4},{4,0},{8,12},{12,8},{1,5},{5,1},{9,13},{13,9},{2,6},{6,2},{1... | collective-permute-start | bytes 98312 | tf_op jit(solution)/shard_map/ppermute | solution.py:15
  71.6 1.8 %collective-permute-start.23 = (bf16[128,128]{1,0:T(8,128)(2,1)S(1)}, bf16[128,128]{1,0:T(8,128)(2,1)S(1)}, u32[]{:S(2)}, u32[]{:S(2)}) collective-permute-start(bf16[128,128]{1,0:T(8,128)(2,1)S(1)} %get-tuple-element.93), channel_id=1, source_target_pairs={{0,8},{4,12},{8,0},{12,4},{1,9},{5,13},{9,1},{13,5},{2,10},{6,14},... | collective-permute-start | bytes 98312 | tf_op jit(solution)/shard_map/ppermute | solution.py:15
  73.4 0.9 %shard_map.126.own_ref = f32[4,128,128]{2,1,0:T(8,128)S(1)} custom-call(s32[27]{0:T(128)S(1)} %concatenate.3.s_ref, f32[4,128,128]{2,1,0:T(8,128)S(1)} %get-tuple-element.94.first_ref, bf16[4,128,128]{2,1,0:T(8,128)(2,1)S(1)} %get-tuple-element.95.d_node, bf16[4,128,128]{2,1,0:T(8,128)(2,1)S(1)} %get-tuple-element.96.d_recv, ...), custom_call_target="tpu_custom_call" | custom-call | bytes 1048576 | tf_op jit(solution)/shard_map/pallas_call | solution.py:32
  74.3 2.4 %collective-permute-done.23.r1 = bf16[128,128]{1,0:T(8,128)(2,1)S(1)} collective-permute-done((bf16[128,128]{1,0:T(8,128)(2,1)S(1)}, bf16[128,128]{1,0:T(8,128)(2,1)S(1)}, u32[]{:S(2)}, u32[]{:S(2)}) %collective-permute-start.23) | collective-permute-done | bytes 32800 | tf_op jit(solution)/shard_map/ppermute | solution.py:15
  76.7 1.3 %shard_map.127 = f32[4,128,128]{2,1,0:T(8,128)} custom-call(s32[27]{0:T(128)S(1)} %concatenate.3.s_ref, bf16[128,128]{1,0:T(8,128)(2,1)S(1)} %collective-permute-done.22.r0, bf16[128,128]{1,0:T(8,128)(2,1)S(1)} %collective-permute-done.23.r1, f32[4,128,128]{2,1,0:T(8,128)S(1)} %shard_map.126.own_ref), custom_call_target="tpu_custom_call" | custom-call | bytes 1048576 | tf_op jit(solution)/shard_map/pallas_call | solution.py:32
  (25 shorter events, 0.1 us)
Async XLA Ops:
  0.6 10.6 %copy-start.2 = (bf16[512,128]{1,0:T(8,128)(2,1)S(1)}, bf16[512,128]{1,0:T(8,128)(2,1)}, u32[]{:S(2)}) copy-start(bf16[512,128]{1,0:T(8,128)(2,1)} %h_ref.3) | copy-start | bytes 393220
  4.1 10.0 %collective-permute-start.1 = (bf16[128,128]{1,0:T(8,128)(2,1)S(1)}, bf16[128,128]{1,0:T(8,128)(2,1)S(1)}, u32[]{:S(2)}, u32[]{:S(2)}) collective-permute-start(bf16[128,128]{1,0:T(8,128)(2,1)S(1)} %get-tuple-element.98), channel_id=1, source_target_pairs={{0,8},{4,12},{8,0},{12,4},{1,9},{5,13},{9,1},{13,5},{2,10},{6,14},... | collective-permute-start | bytes 98312 | tf_op jit(solution)/shard_map/ppermute | solution.py:15
  8.1 6.0 %collective-permute-start = (bf16[128,128]{1,0:T(8,128)(2,1)S(1)}, bf16[128,128]{1,0:T(8,128)(2,1)S(1)}, u32[]{:S(2)}, u32[]{:S(2)}) collective-permute-start(bf16[128,128]{1,0:T(8,128)(2,1)S(1)} %get-tuple-element.99), channel_id=1, source_target_pairs={{0,4},{4,0},{8,12},{12,8},{1,5},{5,1},{9,13},{13,9},{2,6},{6,2},{1... | collective-permute-start | bytes 98312 | tf_op jit(solution)/shard_map/ppermute | solution.py:15
  9.7 0.7 copy-start.8
  10.3 0.7 copy-start.10
  10.4 0.8 copy-start.5
  10.4 0.7 copy-start.7
  10.4 0.7 copy-start.9
  11.1 0.7 copy-start.4
  11.2 0.7 copy-start.6
  11.9 1.1 %copy-start = (bf16[3,6,128,128]{3,2,1,0:T(8,128)(2,1)S(1)}, bf16[3,6,128,128]{3,2,1,0:T(8,128)(2,1)}, u32[]{:S(2)}) copy-start(bf16[3,6,128,128]{3,2,1,0:T(8,128)(2,1)} %w_ref.15) | copy-start | bytes 1769476
  13.0 1.2 %copy-start.1 = (bf16[3,6,128,128]{3,2,1,0:T(8,128)(2,1)S(1)}, bf16[3,6,128,128]{3,2,1,0:T(8,128)(2,1)}, u32[]{:S(2)}) copy-start(bf16[3,6,128,128]{3,2,1,0:T(8,128)(2,1)} %w_ref.15) | copy-start | bytes 1769476
  16.8 1.9 %collective-permute-start.2 = (bf16[144,128]{1,0:T(8,128)(2,1)S(1)}, bf16[144,128]{1,0:T(8,128)(2,1)S(1)}, u32[]{:S(2)}, u32[]{:S(2)}) collective-permute-start(bf16[144,128]{1,0:T(8,128)(2,1)S(1)} %get-tuple-element.55), channel_id=1, source_target_pairs={{0,1},{1,0},{2,3},{3,2},{4,5},{5,4},{6,7},{7,6},{8,9},{9,8},{10,11... | collective-permute-start | bytes 110600 | tf_op jit(solution)/shard_map/ppermute | solution.py:15
  16.9 4.0 %collective-permute-start.3 = (bf16[144,128]{1,0:T(8,128)(2,1)S(1)}, bf16[144,128]{1,0:T(8,128)(2,1)S(1)}, u32[]{:S(2)}, u32[]{:S(2)}) collective-permute-start(bf16[144,128]{1,0:T(8,128)(2,1)S(1)} %get-tuple-element.56), channel_id=1, source_target_pairs={{0,2},{1,3},{2,0},{3,1},{4,6},{5,7},{6,4},{7,5},{8,10},{9,11},{10,... | collective-permute-start | bytes 110600 | tf_op jit(solution)/shard_map/ppermute | solution.py:15
  18.4 3.4 %collective-permute-start.4 = (bf16[144,128]{1,0:T(8,128)(2,1)S(1)}, bf16[144,128]{1,0:T(8,128)(2,1)S(1)}, u32[]{:S(2)}, u32[]{:S(2)}) collective-permute-start(bf16[144,128]{1,0:T(8,128)(2,1)S(1)} %get-tuple-element.57), channel_id=1, source_target_pairs={{0,3},{1,2},{2,1},{3,0},{4,7},{5,6},{6,5},{7,4},{8,11},{9,10},{10,... | collective-permute-start | bytes 110600 | tf_op jit(solution)/shard_map/ppermute | solution.py:15
  22.4 5.1 %collective-permute-start.6 = (bf16[128,128]{1,0:T(8,128)(2,1)S(1)}, bf16[128,128]{1,0:T(8,128)(2,1)S(1)}, u32[]{:S(2)}, u32[]{:S(2)}) collective-permute-start(bf16[128,128]{1,0:T(8,128)(2,1)S(1)} %get-tuple-element.58.h_ref), channel_id=1, source_target_pairs={{0,8},{4,12},{8,0},{12,4},{1,9},{5,13},{9,1},{13,5},{2,10},{6,14},... | collective-permute-start | bytes 98312 | tf_op jit(solution)/shard_map/ppermute | solution.py:15
  22.9 4.7 %collective-permute-start.5 = (bf16[128,128]{1,0:T(8,128)(2,1)S(1)}, bf16[128,128]{1,0:T(8,128)(2,1)S(1)}, u32[]{:S(2)}, u32[]{:S(2)}) collective-permute-start(bf16[128,128]{1,0:T(8,128)(2,1)S(1)} %get-tuple-element.58.h_ref), channel_id=1, source_target_pairs={{0,4},{4,0},{8,12},{12,8},{1,5},{5,1},{9,13},{13,9},{2,6},{6,2},{1... | collective-permute-start | bytes 98312 | tf_op jit(solution)/shard_map/ppermute | solution.py:15
  28.9 3.4 %collective-permute-start.9 = (bf16[128,128]{1,0:T(8,128)(2,1)S(1)}, bf16[128,128]{1,0:T(8,128)(2,1)S(1)}, u32[]{:S(2)}, u32[]{:S(2)}) collective-permute-start(bf16[128,128]{1,0:T(8,128)(2,1)S(1)} %get-tuple-element.63.refs_0_), channel_id=1, source_target_pairs={{0,3},{1,2},{2,1},{3,0},{4,7},{5,6},{6,5},{7,4},{8,11},{9,10},{10,... | collective-permute-start | bytes 98312 | tf_op jit(solution)/shard_map/ppermute | solution.py:15
  29.0 4.3 %collective-permute-start.8 = (bf16[128,128]{1,0:T(8,128)(2,1)S(1)}, bf16[128,128]{1,0:T(8,128)(2,1)S(1)}, u32[]{:S(2)}, u32[]{:S(2)}) collective-permute-start(bf16[128,128]{1,0:T(8,128)(2,1)S(1)} %get-tuple-element.63.refs_0_), channel_id=1, source_target_pairs={{0,2},{1,3},{2,0},{3,1},{4,6},{5,7},{6,4},{7,5},{8,10},{9,11},{10,... | collective-permute-start | bytes 98312 | tf_op jit(solution)/shard_map/ppermute | solution.py:15
  30.0 3.3 %collective-permute-start.7 = (bf16[128,128]{1,0:T(8,128)(2,1)S(1)}, bf16[128,128]{1,0:T(8,128)(2,1)S(1)}, u32[]{:S(2)}, u32[]{:S(2)}) collective-permute-start(bf16[128,128]{1,0:T(8,128)(2,1)S(1)} %get-tuple-element.63.refs_0_), channel_id=1, source_target_pairs={{0,1},{1,0},{2,3},{3,2},{4,5},{5,4},{6,7},{7,6},{8,9},{9,8},{10,11... | collective-permute-start | bytes 98312 | tf_op jit(solution)/shard_map/ppermute | solution.py:15
  33.9 4.3 %collective-permute-start.10 = (bf16[128,128]{1,0:T(8,128)(2,1)S(1)}, bf16[128,128]{1,0:T(8,128)(2,1)S(1)}, u32[]{:S(2)}, u32[]{:S(2)}) collective-permute-start(bf16[128,128]{1,0:T(8,128)(2,1)S(1)} %get-tuple-element.65), channel_id=1, source_target_pairs={{0,4},{4,0},{8,12},{12,8},{1,5},{5,1},{9,13},{13,9},{2,6},{6,2},{1... | collective-permute-start | bytes 98312 | tf_op jit(solution)/shard_map/ppermute | solution.py:15
  34.2 5.0 %collective-permute-start.11 = (bf16[128,128]{1,0:T(8,128)(2,1)S(1)}, bf16[128,128]{1,0:T(8,128)(2,1)S(1)}, u32[]{:S(2)}, u32[]{:S(2)}) collective-permute-start(bf16[128,128]{1,0:T(8,128)(2,1)S(1)} %get-tuple-element.66), channel_id=1, source_target_pairs={{0,8},{4,12},{8,0},{12,4},{1,9},{5,13},{9,1},{13,5},{2,10},{6,14},... | collective-permute-start | bytes 98312 | tf_op jit(solution)/shard_map/ppermute | solution.py:15
  36.2 3.0 %copy-start.3 = (bf16[512,128]{1,0:T(8,128)(2,1)S(1)}, bf16[512,128]{1,0:T(8,128)(2,1)}, u32[]{:S(2)}) copy-start(bf16[512,128]{1,0:T(8,128)(2,1)} %cot_ref.3) | copy-start | bytes 393220
  43.9 4.5 %collective-permute-start.12 = (bf16[128,128]{1,0:T(8,128)(2,1)S(1)}, bf16[128,128]{1,0:T(8,128)(2,1)S(1)}, u32[]{:S(2)}, u32[]{:S(2)}) collective-permute-start(bf16[128,128]{1,0:T(8,128)(2,1)S(1)} %get-tuple-element.73), channel_id=1, source_target_pairs={{0,4},{4,0},{8,12},{12,8},{1,5},{5,1},{9,13},{13,9},{2,6},{6,2},{1... | collective-permute-start | bytes 98312 | tf_op jit(solution)/shard_map/ppermute | solution.py:15
  45.5 5.0 %collective-permute-start.13 = (bf16[128,128]{1,0:T(8,128)(2,1)S(1)}, bf16[128,128]{1,0:T(8,128)(2,1)S(1)}, u32[]{:S(2)}, u32[]{:S(2)}) collective-permute-start(bf16[128,128]{1,0:T(8,128)(2,1)S(1)} %get-tuple-element.74), channel_id=1, source_target_pairs={{0,8},{4,12},{8,0},{12,4},{1,9},{5,13},{9,1},{13,5},{2,10},{6,14},... | collective-permute-start | bytes 98312 | tf_op jit(solution)/shard_map/ppermute | solution.py:15
  51.2 1.9 %collective-permute-start.14 = (bf16[128,128]{1,0:T(8,128)(2,1)S(1)}, bf16[128,128]{1,0:T(8,128)(2,1)S(1)}, u32[]{:S(2)}, u32[]{:S(2)}) collective-permute-start(bf16[128,128]{1,0:T(8,128)(2,1)S(1)} %get-tuple-element.79), channel_id=1, source_target_pairs={{0,1},{1,0},{2,3},{3,2},{4,5},{5,4},{6,7},{7,6},{8,9},{9,8},{10,11... | collective-permute-start | bytes 98312 | tf_op jit(solution)/shard_map/ppermute | solution.py:15
  51.3 4.1 %collective-permute-start.15 = (bf16[128,128]{1,0:T(8,128)(2,1)S(1)}, bf16[128,128]{1,0:T(8,128)(2,1)S(1)}, u32[]{:S(2)}, u32[]{:S(2)}) collective-permute-start(bf16[128,128]{1,0:T(8,128)(2,1)S(1)} %get-tuple-element.80), channel_id=1, source_target_pairs={{0,2},{1,3},{2,0},{3,1},{4,6},{5,7},{6,4},{7,5},{8,10},{9,11},{10,... | collective-permute-start | bytes 98312 | tf_op jit(solution)/shard_map/ppermute | solution.py:15
  52.1 3.6 %collective-permute-start.16 = (bf16[128,128]{1,0:T(8,128)(2,1)S(1)}, bf16[128,128]{1,0:T(8,128)(2,1)S(1)}, u32[]{:S(2)}, u32[]{:S(2)}) collective-permute-start(bf16[128,128]{1,0:T(8,128)(2,1)S(1)} %get-tuple-element.81), channel_id=1, source_target_pairs={{0,3},{1,2},{2,1},{3,0},{4,7},{5,6},{6,5},{7,4},{8,11},{9,10},{10,... | collective-permute-start | bytes 98312 | tf_op jit(solution)/shard_map/ppermute | solution.py:15
  57.1 4.3 %collective-permute-start.17 = (bf16[128,128]{1,0:T(8,128)(2,1)S(1)}, bf16[128,128]{1,0:T(8,128)(2,1)S(1)}, u32[]{:S(2)}, u32[]{:S(2)}) collective-permute-start(bf16[128,128]{1,0:T(8,128)(2,1)S(1)} %get-tuple-element.86), channel_id=1, source_target_pairs={{0,4},{4,0},{8,12},{12,8},{1,5},{5,1},{9,13},{13,9},{2,6},{6,2},{1... | collective-permute-start | bytes 98312 | tf_op jit(solution)/shard_map/ppermute | solution.py:15
  57.4 5.1 %collective-permute-start.18 = (bf16[128,128]{1,0:T(8,128)(2,1)S(1)}, bf16[128,128]{1,0:T(8,128)(2,1)S(1)}, u32[]{:S(2)}, u32[]{:S(2)}) collective-permute-start(bf16[128,128]{1,0:T(8,128)(2,1)S(1)} %get-tuple-element.87), channel_id=1, source_target_pairs={{0,8},{4,12},{8,0},{12,4},{1,9},{5,13},{9,1},{13,5},{2,10},{6,14},... | collective-permute-start | bytes 98312 | tf_op jit(solution)/shard_map/ppermute | solution.py:15
  63.1 3.4 %collective-permute-start.21 = (bf16[128,128]{1,0:T(8,128)(2,1)S(1)}, bf16[128,128]{1,0:T(8,128)(2,1)S(1)}, u32[]{:S(2)}, u32[]{:S(2)}) collective-permute-start(bf16[128,128]{1,0:T(8,128)(2,1)S(1)} %shard_map.124.refs_0_), channel_id=1, source_target_pairs={{0,3},{1,2},{2,1},{3,0},{4,7},{5,6},{6,5},{7,4},{8,11},{9,10},{10,... | collective-permute-start | bytes 98312 | tf_op jit(solution)/shard_map/ppermute | solution.py:15
  63.2 4.3 %collective-permute-start.20 = (bf16[128,128]{1,0:T(8,128)(2,1)S(1)}, bf16[128,128]{1,0:T(8,128)(2,1)S(1)}, u32[]{:S(2)}, u32[]{:S(2)}) collective-permute-start(bf16[128,128]{1,0:T(8,128)(2,1)S(1)} %shard_map.124.refs_0_), channel_id=1, source_target_pairs={{0,2},{1,3},{2,0},{3,1},{4,6},{5,7},{6,4},{7,5},{8,10},{9,11},{10,... | collective-permute-start | bytes 98312 | tf_op jit(solution)/shard_map/ppermute | solution.py:15
  64.1 3.3 %collective-permute-start.19 = (bf16[128,128]{1,0:T(8,128)(2,1)S(1)}, bf16[128,128]{1,0:T(8,128)(2,1)S(1)}, u32[]{:S(2)}, u32[]{:S(2)}) collective-permute-start(bf16[128,128]{1,0:T(8,128)(2,1)S(1)} %shard_map.124.refs_0_), channel_id=1, source_target_pairs={{0,1},{1,0},{2,3},{3,2},{4,5},{5,4},{6,7},{7,6},{8,9},{9,8},{10,11... | collective-permute-start | bytes 98312 | tf_op jit(solution)/shard_map/ppermute | solution.py:15
  70.0 4.3 %collective-permute-start.22 = (bf16[128,128]{1,0:T(8,128)(2,1)S(1)}, bf16[128,128]{1,0:T(8,128)(2,1)S(1)}, u32[]{:S(2)}, u32[]{:S(2)}) collective-permute-start(bf16[128,128]{1,0:T(8,128)(2,1)S(1)} %get-tuple-element.92), channel_id=1, source_target_pairs={{0,4},{4,0},{8,12},{12,8},{1,5},{5,1},{9,13},{13,9},{2,6},{6,2},{1... | collective-permute-start | bytes 98312 | tf_op jit(solution)/shard_map/ppermute | solution.py:15
  71.6 5.1 %collective-permute-start.23 = (bf16[128,128]{1,0:T(8,128)(2,1)S(1)}, bf16[128,128]{1,0:T(8,128)(2,1)S(1)}, u32[]{:S(2)}, u32[]{:S(2)}) collective-permute-start(bf16[128,128]{1,0:T(8,128)(2,1)S(1)} %get-tuple-element.93), channel_id=1, source_target_pairs={{0,8},{4,12},{8,0},{12,4},{1,9},{5,13},{9,1},{13,5},{2,10},{6,14},... | collective-permute-start | bytes 98312 | tf_op jit(solution)/shard_map/ppermute | solution.py:15

commit v2 on v1

v2 whole, which is shorter than its diff:
```python
import jax
import jax.numpy as jnp
from jax import lax
from jax.experimental import pallas as pl
from jax.experimental.pallas import tpu as pltpu
from jax.sharding import PartitionSpec as P

F32 = jnp.float32
BF16 = jnp.bfloat16
I32 = jnp.int32
COUNT_ROWS = 16
GROUP_AXES = ("pair", "sub")


def swapped(value, axis, mask):
    size = lax.axis_size(axis)
    return lax.ppermute(value, axis, [(source, source ^ mask) for source in range(size)])


def mm(a, b):
    return jnp.dot(a, b, preferred_element_type=F32)


def mm_t(a, b):
    return lax.dot_general(a, b, (((1,), (1,)), ((), ())), preferred_element_type=F32)


def sigmoid(x):
    return 0.5 * jnp.tanh(0.5 * x) + 0.5


def scalar(table, index):
    return table[index : index + 1, :][0, 0]


def run(kernel, outs, *arrays, scratch=(), flops=0, space=pltpu.VMEM):
    return pl.pallas_call(
        kernel,
        out_shape=[jax.ShapeDtypeStruct(shape, dtype) for shape, dtype in outs],
        in_specs=[pl.BlockSpec(memory_space=space)] * len(arrays),
        out_specs=[pl.BlockSpec(memory_space=pltpu.VMEM)] * len(outs),
        scratch_shapes=list(scratch),
        compiler_params=pltpu.CompilerParams(vmem_limit_bytes=12 * 2**20),
        cost_estimate=pl.CostEstimate(flops=flops, bytes_accessed=2**20, transcendentals=0),
    )(*arrays)


def per_device(
    nodes,
    cotangent,
    send_blocks,
    neighbour_blocks,
    neighbour_nodes,
    pool_map,
    coarse_blocks,
    coarse_nodes,
    weights,
    biases,
):
    size, features = neighbour_nodes.shape[2], nodes.shape[1]
    blocks, degree = neighbour_blocks.shape
    xor_bits = (1, lax.axis_size("dom") // 2)
    rounds = len(xor_bits)
    slots = lax.axis_size(GROUP_AXES)
    pair_size, sub_size = lax.axis_size("pair"), lax.axis_size("sub")
    edges = blocks * degree
    everyone = blocks + rounds
    tile = (size, features)
    fine = (blocks * size, features)
    tiles = (blocks,) + tile

    at_near = rounds
    at_pool = at_near + edges
    at_coarse = at_pool + blocks
    at_me = at_coarse + degree
    table_rows = -(-(at_me + 1) // 8) * 8

    def exchange(pieces):
        return [swapped(piece, "dom", bit) for piece, bit in zip(pieces, xor_bits)]

    def spread(pieces):
        return [swapped(pieces[mask], GROUP_AXES, mask) for mask in range(1, slots)]

    def rows_of(b):
        return pl.ds(b * size, size)

    def choose(send_ref, nodes_hbm, h_ref, out0, out1, send_smem, sems):
        copies = [
            pltpu.make_async_copy(send_ref, send_smem, sems.at[0]),
            pltpu.make_async_copy(nodes_hbm, h_ref, sems.at[1]),
        ]
        for copy in copies:
            copy.start()
        for copy in copies:
            copy.wait()
        for r, out in enumerate((out0, out1)):
            at = pl.multiple_of(send_smem[0, r, 0] * size, size)
            out[...] = h_ref[pl.ds(at, size), :]

    h0, *first_sends = run(
        choose,
        [(fine, BF16)] + [(tile, BF16)] * rounds,
        send_blocks,
        nodes,
        space=pltpu.HBM,
        scratch=[pltpu.SMEM(send_blocks.shape, I32), pltpu.SemaphoreType.DMA((2,))],
    )
    halo = exchange(first_sends)

    def tables_into(ends, count, pick_ref, put_ref):
        rows = lax.broadcasted_iota(I32, (size, size), 0)
        columns = lax.broadcasted_iota(I32, (size, size), 1)
        upright = jnp.transpose(ends)
        for edge in range(count):
            put_ref[edge] = (rows == ends[edge : edge + 1, :]).astype(BF16)
            pick_ref[edge] = (columns == upright[:, edge : edge + 1]).astype(BF16)

    def own_into(state, layer, w_ref, b_ref, recv_ref, node_ref, sender_ref):
        recv_ref[...] = mm(state, w_ref[layer, 0]) + b_ref[layer, 0:1, :]
        node_ref[...] = mm(state, w_ref[layer, 3]) + b_ref[layer, 1:2, :]
        sender_ref[...] = mm(state, w_ref[layer, 1]).astype(BF16)

    def layer_forward(count, near_at, layer, s_ref, w_ref, recv, node, send_scr, pick_ref, slope_ref, node_slope_ref, sum_scr):
        for b in range(count):
            receiver = recv[rows_of(b), :]
            total = None
            for e in range(degree):
                edge = b * degree + e
                pre = receiver + mm(pick_ref[edge], send_scr[scalar(s_ref, near_at + edge)])
                gate = sigmoid(pre)
                active = pre * gate
                slope_ref[edge] = (gate + active * (1.0 - gate)).astype(BF16)
                total = active if total is None else total + active
            sum_scr[rows_of(b), :] = total.astype(BF16)
        average = (mm(sum_scr[...], w_ref[layer, 2]) * (1.0 / degree)).astype(BF16)
        hidden_pre = node[...] + mm(average, w_ref[layer, 4])
        gate = sigmoid(hidden_pre)
        hidden = hidden_pre * gate
        node_slope_ref[...] = (gate + hidden * (1.0 - gate)).astype(BF16)
        return mm(hidden.astype(BF16), w_ref[layer, 5])

    def senders_into(own, halos, layer, w_ref, send_scr):
        count = send_scr.shape[0] - rounds
        for r, g in enumerate(halos):
            send_scr[count + r] = mm(g[...], w_ref[layer, 1]).astype(BF16)
        for b in range(count):
            send_scr[b] = own[rows_of(b), :]

    def layer_backward(grad, count, near_at, layer, s_ref, w_ref, put_ref, slope_ref, node_slope_ref, d_node, d_recv, act_scr, acc_scr):
        d_hidden = (mm_t(grad, w_ref[layer, 5]) * node_slope_ref[...].astype(F32)).astype(BF16)
        d_node[...] = d_hidden
        d_average = (mm_t(d_hidden, w_ref[layer, 4]) * (1.0 / degree)).astype(BF16)
        act_scr[...] = mm_t(d_average, w_ref[layer, 2])
        acc_scr[...] = jnp.zeros_like(acc_scr)
        for b in range(count):
            d_active = act_scr[rows_of(b), :]
            total = None
            for e in range(degree):
                edge = b * degree + e
                d_pre = d_active * slope_ref[edge].astype(F32)
                total = d_pre if total is None else total + d_pre
                near = scalar(s_ref, near_at + edge)
                acc_scr[near] = acc_scr[near] + mm(put_ref[edge], d_pre.astype(BF16))
            d_recv[rows_of(b), :] = total.astype(BF16)

    def halo_grads_into(outs, layer, w_ref, acc_scr):
        count = acc_scr.shape[0] - rounds
        for r, out in enumerate(outs):
            out[...] = mm_t(acc_scr[count + r].astype(BF16), w_ref[layer, 1]).astype(BF16)

    def own_back(grad, layer, w_ref, d_node, d_recv, d_send):
        return grad + mm_t(d_recv, w_ref[layer, 0]) + mm_t(d_node, w_ref[layer, 3]) + mm_t(d_send, w_ref[layer, 1])

    def pooled_into(read, s_ref, out_refs, with_count):
        me = scalar(s_ref, at_me)
        for mask in range(slots):
            slot = me ^ mask
            total, count = None, None
            for b in range(blocks):
                hit = (scalar(s_ref, at_pool + b) == slot).astype(F32)
                part = read(b) * hit
                total = part if total is None else total + part
                count = hit if count is None else count + hit
            out_refs[mask][0:size, :] = total.astype(BF16)
            if with_count:
                out_refs[mask][size:, :] = jnp.full((COUNT_ROWS, features), count, F32).astype(BF16)

    inputs = (
        send_blocks,
        neighbour_blocks,
        pool_map,
        coarse_blocks,
        neighbour_nodes.reshape(edges, size),
        coarse_nodes.reshape(degree, size),
        weights,
        biases,
        cotangent,
    )
    own_out = [(fine, F32), (fine, F32), (fine, BF16)]

    def prepare(send_in, near_in, pool_in, coarse_in, ends_in, cends_in, w_in, b_in, c_in, h_ref,
                s_ref, w_ref, b_ref, c_ref, pick, put, cpick, cput, recv, node, sender,
                send_s, near_s, pool_s, coarse_s, ends, cends, sems):
        pairs = (
            (send_in, send_s), (near_in, near_s), (pool_in, pool_s), (coarse_in, coarse_s),
            (ends_in, ends), (cends_in, cends), (w_in, w_ref), (b_in, b_ref), (c_in, c_ref),
        )
        copies = [pltpu.make_async_copy(source, target, sems.at[i]) for i, (source, target) in enumerate(pairs)]
        for copy in copies:
            copy.start()
        for copy in copies:
            copy.wait()

        def put_row(index, value):
            s_ref[index : index + 1, :] = jnp.full((1, features), value, I32)

        for r in range(rounds):
            put_row(r, send_s[0, r, 0])
        for b in range(blocks):
            for e in range(degree):
                put_row(at_near + b * degree + e, near_s[b, e])
            put_row(at_pool + b, pool_s[b])
        for e in range(degree):
            put_row(at_coarse + e, coarse_s[0, e])
        put_row(at_me, lax.axis_index("pair") * sub_size + lax.axis_index("sub"))
        own_into(h_ref[...], 0, w_ref, b_ref, recv, node, sender)
        tables_into(ends[...], edges, pick, put)
        tables_into(cends[...], degree, cpick, cput)

    hbm, vmem = pl.BlockSpec(memory_space=pltpu.HBM), pl.BlockSpec(memory_space=pltpu.VMEM)
    prepared = [
        ((table_rows, features), I32), (weights.shape, BF16), (biases.shape, F32), (fine, BF16),
        ((edges, size, size), BF16), ((edges, size, size), BF16),
        ((degree, size, size), BF16), ((degree, size, size), BF16),
    ] + own_out
    table, w, bias, cot, pick, put, coarse_pick, coarse_put, recv0, node0, sender0 = pl.pallas_call(
        prepare,
        out_shape=[jax.ShapeDtypeStruct(shape, dtype) for shape, dtype in prepared],
        in_specs=[hbm] * len(inputs) + [vmem],
        out_specs=[vmem] * len(prepared),
        scratch_shapes=[pltpu.SMEM(a.shape, I32) for a in inputs[:4]]
        + [pltpu.VMEM(a.shape, I32) for a in inputs[4:6]]
        + [pltpu.SemaphoreType.DMA((len(inputs),))],
        compiler_params=pltpu.CompilerParams(vmem_limit_bytes=12 * 2**20),
        cost_estimate=pl.CostEstimate(flops=0, bytes_accessed=2**22, transcendentals=0),
    )(*inputs, h0)

    slopes = [((edges,) + tile, BF16), (fine, BF16)]
    pool_out = [((size + COUNT_ROWS, features), BF16)] * slots
    layer_scratch = [pltpu.VMEM((everyone,) + tile, BF16), pltpu.VMEM(fine, BF16)]
    coarse_scratch = [pltpu.VMEM((1 + rounds,) + tile, BF16), pltpu.VMEM(tile, BF16)]

    def first_layer(s_ref, g0, g1, h_ref, recv, node, sender, pick, w_ref, *rest):
        first_ref, slope_ref, node_slope_ref = rest[:3]
        sends, (send_scr, sum_scr) = rest[3:-2], rest[-2:]
        senders_into(sender, (g0, g1), 0, w_ref, send_scr)
        change = layer_forward(
            blocks, at_near, 0, s_ref, w_ref, recv, node, send_scr, pick, slope_ref, node_slope_ref, sum_scr
        )
        first_ref[...] = (h_ref[...].astype(F32) + change).astype(BF16)
        pooled_into(lambda b: first_ref[rows_of(b), :].astype(F32), s_ref, sends, True)

    first, slope0, node_slope0, *pool_sends = run(
        first_layer,
        [(fine, BF16)] + slopes + pool_out,
        table, halo[0], halo[1], h0, recv0, node0, sender0, pick, w,
        scratch=layer_scratch,
    )

    pool_in = spread(pool_sends)

    def coarse_begin(*refs):
        parts, (start_ref, divisor_ref) = refs[:slots], refs[slots:]
        total = parts[0][...].astype(F32)
        for part in parts[1:]:
            total = total + part[...].astype(F32)
        divisor = jnp.maximum(total[size : size + 8, :], 1.0)
        divisor_ref[...] = divisor
        start_ref[...] = (total[:size, :] / divisor[0:1, :]).astype(BF16)

    coarse_start, divisor = run(coarse_begin, [(tile, BF16), ((8, features), F32)], pool_sends[0], *pool_in)
    coarse_halo = exchange([coarse_start] * rounds)

    def coarse_prepare(h_ref, w_ref, b_ref, recv, node, sender):
        own_into(h_ref[...], 1, w_ref, b_ref, recv, node, sender)

    recv1, node1, sender1 = run(coarse_prepare, [(tile, F32), (tile, F32), (tile, BF16)], coarse_start, w, bias)

    def coarse_layer(s_ref, g0, g1, h_ref, recv, node, sender, pick, w_ref, end_ref, slope_ref, node_slope_ref, send_scr, sum_scr):
        senders_into(sender, (g0, g1), 1, w_ref, send_scr)
        change = layer_forward(
            1, at_coarse, 1, s_ref, w_ref, recv, node, send_scr, pick, slope_ref, node_slope_ref, sum_scr
        )
        end_ref[...] = (h_ref[...].astype(F32) + change).astype(BF16)

    coarse_end, slope1, node_slope1 = run(
        coarse_layer,
        [(tile, BF16), ((degree,) + tile, BF16), (tile, BF16)],
        table, coarse_halo[0], coarse_halo[1], coarse_start, recv1, node1, sender1, coarse_pick, w,
        scratch=coarse_scratch,
    )
    ends_in = spread([coarse_end] * slots)

    def lift(s_ref, *refs):
        parts, first_ref = refs[:slots], refs[slots]
        middle_ref, out0, out1, lift_scr = refs[slots + 1 :]
        me = scalar(s_ref, at_me)
        for mask in range(slots):
            lift_scr[me ^ mask] = parts[mask][...]
        for b in range(blocks):
            lifted = lift_scr[scalar(s_ref, at_pool + b)].astype(F32)
            middle_ref[b] = (first_ref[rows_of(b), :].astype(F32) + lifted).astype(BF16)
        for r, out in enumerate((out0, out1)):
            out[...] = middle_ref[scalar(s_ref, r)]

    middle, *middle_sends = run(
        lift,
        [(tiles, BF16)] + [(tile, BF16)] * rounds,
        table, coarse_end, *ends_in, first,
        scratch=[pltpu.VMEM((slots,) + tile, BF16)],
    )
    middle = middle.reshape(fine)
    halo = exchange(middle_sends)

    def last_prepare(h_ref, w_ref, b_ref, recv, node, sender):
        own_into(h_ref[...], 2, w_ref, b_ref, recv, node, sender)

    recv2, node2, sender2 = run(last_prepare, own_out, middle, w, bias)

    back_out = [(tile, BF16)] * rounds + [(fine, BF16), (fine, BF16), (tiles, BF16)]
    back_scratch = [pltpu.VMEM(fine, F32), pltpu.VMEM((everyone,) + tile, F32)]

    def last_layer(s_ref, g0, g1, h_ref, recv, node, sender, pick, put, w_ref, cot_ref,
                   out_ref, r0, r1, d_node, d_recv, d_send,
                   send_scr, sum_scr, slope_scr, node_slope_scr, act_scr, acc_scr):
        senders_into(sender, (g0, g1), 2, w_ref, send_scr)
        change = layer_forward(
            blocks, at_near, 2, s_ref, w_ref, recv, node, send_scr, pick, slope_scr, node_slope_scr, sum_scr
        )
        out_ref[...] = (h_ref[...].astype(F32) + change).astype(BF16)
        layer_backward(
            cot_ref[...], blocks, at_near, 2, s_ref, w_ref, put, slope_scr, node_slope_scr, d_node, d_recv, act_scr, acc_scr
        )
        halo_grads_into((r0, r1), 2, w_ref, acc_scr)
        d_send[...] = acc_scr[0:blocks].astype(BF16)

    out_nodes, *rest = run(
        last_layer,
        [(fine, BF16)] + back_out,
        table, halo[0], halo[1], middle, recv2, node2, sender2, pick, put, w, cot,
        scratch=layer_scratch + [pltpu.VMEM((edges,) + tile, BF16), pltpu.VMEM(fine, BF16)] + back_scratch,
    )
    halo_grads, (d_node, d_recv, d_send) = rest[:rounds], rest[rounds:]
    returned = exchange(halo_grads)

    def last_own(cot_ref, d_node, d_recv, d_send, w_ref, grad_ref):
        grad_ref[...] = own_back(cot_ref[...].astype(F32), 2, w_ref, d_node[...], d_recv[...], d_send[...])

    (grad_own,) = run(last_own, [(fine, F32)], cot, d_node, d_recv, d_send.reshape(fine), w)

    def pool_grads(s_ref, r0, r1, own_ref, grad_ref, *sends):
        grad_ref[...] = own_ref[...]
        for r, arrived in enumerate((r0, r1)):
            at = scalar(s_ref, r)
            grad_ref[at] = grad_ref[at] + arrived[...].astype(F32)
        pooled_into(lambda b: grad_ref[b], s_ref, sends, False)

    grad_middle, *grad_sends = run(
        pool_grads,
        [(tiles, F32)] + [(tile, BF16)] * slots,
        table, returned[0], returned[1], grad_own.reshape(tiles),
    )
    grads_in = spread(grad_sends)

    def coarse_back(s_ref, *refs):
        parts = refs[:slots]
        put, slope_ref, node_slope_ref, w_ref, own_ref, r0, r1, d_node, d_recv, act_scr, acc_scr = refs[slots:]
        grad = parts[0][...].astype(F32)
        for part in parts[1:]:
            grad = grad + part[...].astype(F32)
        layer_backward(
            grad.astype(BF16), 1, at_coarse, 1, s_ref, w_ref, put, slope_ref, node_slope_ref, d_node, d_recv, act_scr, acc_scr
        )
        halo_grads_into((r0, r1), 1, w_ref, acc_scr)
        own_ref[...] = own_back(grad, 1, w_ref, d_node[...], d_recv[...], acc_scr[0].astype(BF16))

    coarse_grad, *coarse_sends = run(
        coarse_back,
        [(tile, F32)] + [(tile, BF16)] * rounds,
        table, grad_sends[0], *grads_in, coarse_put, slope1, node_slope1, w,
        scratch=[
            pltpu.VMEM(tile, BF16), pltpu.VMEM(tile, BF16), pltpu.VMEM(tile, F32), pltpu.VMEM((1 + rounds,) + tile, F32),
        ],
    )
    coarse_returned = exchange(coarse_sends)

    def scale(own_ref, r0, r1, divisor_ref, out_ref):
        total = own_ref[...] + r0[...].astype(F32) + r1[...].astype(F32)
        out_ref[...] = (total / divisor_ref[0:1, :]).astype(BF16)

    (scaled,) = run(scale, [(tile, BF16)], coarse_grad, *coarse_returned, divisor)
    scaled_in = spread([scaled] * slots)

    def first_back(s_ref, *refs):
        parts = refs[:slots]
        middle_ref, put, slope_ref, node_slope_ref, w_ref = refs[slots : slots + 5]
        grad_ref, r0, r1, d_node, d_recv, d_send, lift_scr, act_scr, acc_scr = refs[slots + 5 :]
        me = scalar(s_ref, at_me)
        for mask in range(slots):
            lift_scr[me ^ mask] = parts[mask][...]
        for b in range(blocks):
            lifted = lift_scr[scalar(s_ref, at_pool + b)].astype(F32)
            grad_ref[rows_of(b), :] = middle_ref[b] + lifted
        layer_backward(
            grad_ref[...].astype(BF16), blocks, at_near, 0, s_ref, w_ref, put, slope_ref, node_slope_ref, d_node, d_recv, act_scr, acc_scr
        )
        halo_grads_into((r0, r1), 0, w_ref, acc_scr)
        d_send[...] = acc_scr[0:blocks].astype(BF16)

    grad_first, *rest = run(
        first_back,
        [(fine, F32)] + back_out,
        table, scaled, *scaled_in, grad_middle, put, slope0, node_slope0, w,
        scratch=[pltpu.VMEM((slots,) + tile, BF16)] + back_scratch,
    )
    halo_grads, (d_node, d_recv, d_send) = rest[:rounds], rest[rounds:]
    returned = exchange(halo_grads)

    def first_own(first_ref, d_node, d_recv, d_send, w_ref, grad_ref):
        grad_ref[...] = own_back(first_ref[...], 0, w_ref, d_node[...], d_recv[...], d_send[...])

    (grad_own,) = run(first_own, [(fine, F32)], grad_first, d_node, d_recv, d_send.reshape(fine), w)

    def finish(s_ref, r0, r1, own_ref, out_ref):
        out_ref[...] = own_ref[...]
        for r, arrived in enumerate((r0, r1)):
            at = scalar(s_ref, r)
            out_ref[at] = out_ref[at] + arrived[...].astype(F32)

    (grad_nodes,) = run(finish, [(tiles, F32)], table, returned[0], returned[1], grad_own.reshape(tiles))
    return (out_nodes, grad_nodes.reshape(fine))


def solution(mesh):
    split = ("groups", "dom", "pair", "sub")
    placed = (
        P(split, None),
        P(split, None),
        P(split, None, None),
        P(split, None),
        P(split, None, None),
        P(split),
        P(split, None),
        P(split, None, None),
        P(),
        P(),
    )
    return jax.shard_map(
        per_device,
        mesh=mesh,
        in_specs=placed,
        out_specs=(P(split, None), P(split, None)),
        check_vma=False,
    )
```

time: 78.3 us -> 66.9 us (0.85)
  Pallas kernels: 20.7 us -> 9.56 us
  waiting for transfers between devices: 24.2 us -> 26.1 us
  local copies, waits for them, and re-layouts: 5.45 us -> 4.1 us
  between operations: 2.1 us -> 0.83 us
    pallas_call x15, Pallas kernels: 20.7 us -> 8.31 us  [run(): pl.pallas_call(kernel, out_shape=[jax.ShapeDtypeStruct(shape, dtype) for...]
    ppermute x24, waiting for transfers between devices: 24.2 us -> 26.1 us  [swapped(): lax.ppermute(value, axis, [(source, source ^ mask) for source in range(si...]
    slice x1 -> x0, local copies, waits for them, and re-layouts: 1.31 us -> none  [per_device(): halo = exchange([send_rows(send_blocks[0, r, 0]) for r in range(rounds)])]
    pallas_call x0 -> x1, Pallas kernels: none -> 1.25 us  [per_device(): pl.pallas_call(prepare, out_shape=[jax.ShapeDtypeStruct(shape, dtype) for...]
    unnamed x22 -> x19, local copies, waits for them, and re-layouts: 3.12 us -> 4.1 us
    dynamic_slice x1 -> x0, local copies, waits for them, and re-layouts: 0.84 us -> none  [send_rows(): return lax.dynamic_slice_in_dim(nodes, b * size, size, axis=0)]
  transfers between devices with their start and end apart: 24 -> 24, of which waited for: 15 -> 18; matrix products, arithmetic and copies ran while one was open for 0% -> 0% of each run, Pallas kernels for 6% -> 3%
where the time goes in v2:
time: 66.9 us; the launch traced here: 66.6 us
  starting transfers between devices  26.1 us (39%)
  waiting for transfers between devices  26.1 us (39%)
  Pallas kernels  9.56 us (14%)
  local copies, waits for them, and re-layouts  4.1 us (6%)
  between operations  0.83 us (1%)
    ppermute x24, waiting for transfers between devices, swapped(): lax.ppermute(value, axis, [(source, source ^ mask) for source in range(si...  26.1 us
    ppermute x24, starting transfers between devices, swapped(): lax.ppermute(value, axis, [(source, source ^ mask) for source in range(si...  26.1 us
    pallas_call x15, Pallas kernels, run(): pl.pallas_call(kernel, out_shape=[jax.ShapeDtypeStruct(shape, dtype) for...  8.31 us
    unnamed x19, local copies, waits for them, and re-layouts  4.1 us
  transfers between devices with their start and end apart: 24, of which 18 were waited for; matrix products, arithmetic and copies ran while one was open for 0% of the time, Pallas kernels for 3%

profile of v2, /device:TPU:0, one launch (start us, length us, event | category | flops | bytes accessed | tf_op | source)
XLA Modules:
  0.0 66.6 jit_solution(1273672345587933103)
XLA Ops:
  0.7 0.8 %copy.13.send_ref.send_in = s32[1,2,1]{2,1,0:T(2,128)S(1)} copy(s32[1,2,1]{1,2,0:T(1,128)} %param.12) | data formatting | bytes 16 | tf_op args[2]
  1.4 0.9 %copy-done.1 = bf16[512,128]{1,0:T(8,128)(2,1)S(1)} copy-done((bf16[512,128]{1,0:T(8,128)(2,1)S(1)}, bf16[512,128]{1,0:T(8,128)(2,1)}, u32[]{:S(2)}) %copy-start.1) | copy-done | bytes 131096
  2.3 0.6 shard_map.113
  2.9 0.0 copy-start.3
  2.9 3.1 %collective-permute-start = (bf16[128,128]{1,0:T(8,128)(2,1)S(1)}, bf16[128,128]{1,0:T(8,128)(2,1)S(1)}, u32[]{:S(2)}, u32[]{:S(2)}) collective-permute-start(bf16[128,128]{1,0:T(8,128)(2,1)S(1)} %get-tuple-element.59), channel_id=1, source_target_pairs={{0,4},{4,0},{8,12},{12,8},{1,5},{5,1},{9,13},{13,9},{2,6},{6,2},{1... | collective-permute-start | bytes 98312 | tf_op jit(solution)/shard_map/ppermute | solution.py:17
  6.0 2.6 %collective-permute-start.1 = (bf16[128,128]{1,0:T(8,128)(2,1)S(1)}, bf16[128,128]{1,0:T(8,128)(2,1)S(1)}, u32[]{:S(2)}, u32[]{:S(2)}) collective-permute-start(bf16[128,128]{1,0:T(8,128)(2,1)S(1)} %get-tuple-element.60), channel_id=1, source_target_pairs={{0,8},{4,12},{8,0},{12,4},{1,9},{5,13},{9,1},{13,5},{2,10},{6,14},... | collective-permute-start | bytes 98312 | tf_op jit(solution)/shard_map/ppermute | solution.py:17
  8.6 0.0 copy-start
  8.6 1.1 %copy-done = bf16[3,6,128,128]{3,2,1,0:T(8,128)(2,1)S(1)} copy-done((bf16[3,6,128,128]{3,2,1,0:T(8,128)(2,1)S(1)}, bf16[3,6,128,128]{3,2,1,0:T(8,128)(2,1)}, u32[]{:S(2)}) %copy-start) | copy-done | bytes 589848
  9.7 0.7 %copy-done.4 = f32[3,2,128]{2,1,0:T(2,128)S(1)} copy-done((f32[3,2,128]{2,1,0:T(2,128)S(1)}, f32[3,2,128]{2,1,0:T(2,128)}, u32[]{:S(2)}) %copy-start.4) | copy-done | bytes 3096
  10.4 0.7 %copy-done.6 = s32[1,4,128]{2,1,0:T(4,128)S(1)} copy-done((s32[1,4,128]{2,1,0:T(4,128)S(1)}, s32[1,4,128]{2,1,0:T(4,128)}, u32[]{:S(2)}) %copy-start.6) | copy-done | bytes 2072
  11.0 1.3 %shard_map.114 = (s32[32,128]{1,0:T(8,128)S(1)}, bf16[3,6,128,128]{3,2,1,0:T(8,128)(2,1)S(1)}, f32[3,2,128]{2,1,0:T(2,128)S(1)}, bf16[512,128]{1,0:T(8,128)(2,1)...) custom-call(s32[1,2,1]{2,1,0:T(2,128)S(1)} %copy.13.send_ref.send_in, ...), custom_call_target="tpu_custom_call" | custom-call | bytes 4194304 | tf_op jit(solution)/shard_map/pallas_call | solution.py:236
  12.3 1.1 %shard_map.115 = (bf16[512,128]{1,0:T(8,128)(2,1)S(1)}, bf16[16,128,128]{2,1,0:T(8,128)(2,1)S(1)}, bf16[512,128]{1,0:T(8,128)(2,1)S(1)}, bf16[144,128]{1,0:T(8,1...) custom-call(s32[32,128]{1,0:T(8,128)S(1)} %get-tuple-element.58.s_ref, ...), custom_call_target="tpu_custom_call" | custom-call | bytes 1048576 | tf_op jit(solution)/shard_map/pallas_call | solution.py:37
  13.4 0.1 collective-permute-start.2
  13.5 1.6 %collective-permute-start.3 = (bf16[144,128]{1,0:T(8,128)(2,1)S(1)}, bf16[144,128]{1,0:T(8,128)(2,1)S(1)}, u32[]{:S(2)}, u32[]{:S(2)}) collective-permute-start(bf16[144,128]{1,0:T(8,128)(2,1)S(1)} %get-tuple-element.68), channel_id=1, source_target_pairs={{0,2},{1,3},{2,0},{3,1},{4,6},{5,7},{6,4},{7,5},{8,10},{9,11},{10,... | collective-permute-start | bytes 110600 | tf_op jit(solution)/shard_map/ppermute | solution.py:17
  15.1 0.3 collective-permute-start.4
  15.4 0.0 collective-permute-done.2.refs_1_
  15.4 2.2 %collective-permute-done.3.refs_2_ = bf16[144,128]{1,0:T(8,128)(2,1)S(1)} collective-permute-done((bf16[144,128]{1,0:T(8,128)(2,1)S(1)}, bf16[144,128]{1,0:T(8,128)(2,1)S(1)}, u32[]{:S(2)}, u32[]{:S(2)}) %collective-permute-start.3) | collective-permute-done | bytes 36896 | tf_op jit(solution)/shard_map/ppermute | solution.py:17
  17.5 1.0 %collective-permute-done.4.refs_3_ = bf16[144,128]{1,0:T(8,128)(2,1)S(1)} collective-permute-done((bf16[144,128]{1,0:T(8,128)(2,1)S(1)}, bf16[144,128]{1,0:T(8,128)(2,1)S(1)}, u32[]{:S(2)}, u32[]{:S(2)}) %collective-permute-start.4) | collective-permute-done | bytes 36896 | tf_op jit(solution)/shard_map/ppermute | solution.py:17
  18.5 1.1 %collective-permute-start.6 = (bf16[128,128]{1,0:T(8,128)(2,1)S(1)}, bf16[128,128]{1,0:T(8,128)(2,1)S(1)}, u32[]{:S(2)}, u32[]{:S(2)}) collective-permute-start(bf16[128,128]{1,0:T(8,128)(2,1)S(1)} %get-tuple-element.70.h_ref), channel_id=1, source_target_pairs={{0,8},{4,12},{8,0},{12,4},{1,9},{5,13},{9,1},{13,5},{2,10},{6,14},... | collective-permute-start | bytes 98312 | tf_op jit(solution)/shard_map/ppermute | solution.py:17
  19.7 0.4 collective-permute-start.5
  20.1 0.2 shard_map.117
  20.3 3.4 %collective-permute-done.6.g1 = bf16[128,128]{1,0:T(8,128)(2,1)S(1)} collective-permute-done((bf16[128,128]{1,0:T(8,128)(2,1)S(1)}, bf16[128,128]{1,0:T(8,128)(2,1)S(1)}, u32[]{:S(2)}, u32[]{:S(2)}) %collective-permute-start.6) | collective-permute-done | bytes 32800 | tf_op jit(solution)/shard_map/ppermute | solution.py:17
  23.7 0.3 collective-permute-done.5.g0
  23.9 0.8 %shard_map.118 = (bf16[128,128]{1,0:T(8,128)(2,1)S(1)}, bf16[4,128,128]{2,1,0:T(8,128)(2,1)S(1)}, bf16[128,128]{1,0:T(8,128)(2,1)S(1)}) custom-call(s32[32,128]{1,0:T(8,128)S(1)} %get-tuple-element.58.s_ref, bf16[128,128]{1,0:T(8,128)(2,1)S(1)} %collective-permute-done.5.g0, bf16[128,128]{1,0:T(8,128)(2,1)S(1)} %collective-permute-done.6.g1, ...), custom_call_target="tpu_custom_call" | custom-call | bytes 1048576 | tf_op jit(solution)/shard_map/pallas_call | solution.py:37
  24.7 0.1 collective-permute-start.9
  24.8 0.9 %collective-permute-start.8 = (bf16[128,128]{1,0:T(8,128)(2,1)S(1)}, bf16[128,128]{1,0:T(8,128)(2,1)S(1)}, u32[]{:S(2)}, u32[]{:S(2)}) collective-permute-start(bf16[128,128]{1,0:T(8,128)(2,1)S(1)} %get-tuple-element.76.refs_0_), channel_id=1, source_target_pairs={{0,2},{1,3},{2,0},{3,1},{4,6},{5,7},{6,4},{7,5},{8,10},{9,11},{10,... | collective-permute-start | bytes 98312 | tf_op jit(solution)/shard_map/ppermute | solution.py:17
  25.7 0.9 %collective-permute-start.7 = (bf16[128,128]{1,0:T(8,128)(2,1)S(1)}, bf16[128,128]{1,0:T(8,128)(2,1)S(1)}, u32[]{:S(2)}, u32[]{:S(2)}) collective-permute-start(bf16[128,128]{1,0:T(8,128)(2,1)S(1)} %get-tuple-element.76.refs_0_), channel_id=1, source_target_pairs={{0,1},{1,0},{2,3},{3,2},{4,5},{5,4},{6,7},{7,6},{8,9},{9,8},{10,11... | collective-permute-start | bytes 98312 | tf_op jit(solution)/shard_map/ppermute | solution.py:17
  26.6 1.5 %collective-permute-done.9.refs_3_ = bf16[128,128]{1,0:T(8,128)(2,1)S(1)} collective-permute-done((bf16[128,128]{1,0:T(8,128)(2,1)S(1)}, bf16[128,128]{1,0:T(8,128)(2,1)S(1)}, u32[]{:S(2)}, u32[]{:S(2)}) %collective-permute-start.9) | collective-permute-done | bytes 32800 | tf_op jit(solution)/shard_map/ppermute | solution.py:17
  28.1 0.9 %collective-permute-done.8.refs_2_ = bf16[128,128]{1,0:T(8,128)(2,1)S(1)} collective-permute-done((bf16[128,128]{1,0:T(8,128)(2,1)S(1)}, bf16[128,128]{1,0:T(8,128)(2,1)S(1)}, u32[]{:S(2)}, u32[]{:S(2)}) %collective-permute-start.8) | collective-permute-done | bytes 32800 | tf_op jit(solution)/shard_map/ppermute | solution.py:17
  29.1 0.1 shard_map.119
  29.1 0.2 collective-permute-start.10
  29.3 1.9 %collective-permute-start.11 = (bf16[128,128]{1,0:T(8,128)(2,1)S(1)}, bf16[128,128]{1,0:T(8,128)(2,1)S(1)}, u32[]{:S(2)}, u32[]{:S(2)}) collective-permute-start(bf16[128,128]{1,0:T(8,128)(2,1)S(1)} %get-tuple-element.79), channel_id=1, source_target_pairs={{0,8},{4,12},{8,0},{12,4},{1,9},{5,13},{9,1},{13,5},{2,10},{6,14},... | collective-permute-start | bytes 98312 | tf_op jit(solution)/shard_map/ppermute | solution.py:17
  31.2 0.3 shard_map.120
  31.4 2.0 %collective-permute-done.10.g0 = bf16[128,128]{1,0:T(8,128)(2,1)S(1)} collective-permute-done((bf16[128,128]{1,0:T(8,128)(2,1)S(1)}, bf16[128,128]{1,0:T(8,128)(2,1)S(1)}, u32[]{:S(2)}, u32[]{:S(2)}) %collective-permute-start.10) | collective-permute-done | bytes 32800 | tf_op jit(solution)/shard_map/ppermute | solution.py:17
  33.5 0.8 %collective-permute-done.11.g1 = bf16[128,128]{1,0:T(8,128)(2,1)S(1)} collective-permute-done((bf16[128,128]{1,0:T(8,128)(2,1)S(1)}, bf16[128,128]{1,0:T(8,128)(2,1)S(1)}, u32[]{:S(2)}, u32[]{:S(2)}) %collective-permute-start.11) | collective-permute-done | bytes 32800 | tf_op jit(solution)/shard_map/ppermute | solution.py:17
  34.3 2.2 %shard_map.121 = (bf16[512,128]{1,0:T(8,128)(2,1)}, bf16[128,128]{1,0:T(8,128)(2,1)S(1)}, bf16[128,128]{1,0:T(8,128)(2,1)S(1)}, bf16[512,128]{1,0:T(8,128)(2,1)S...) custom-call(s32[32,128]{1,0:T(8,128)S(1)} %get-tuple-element.58.s_ref, ...), custom_call_target="tpu_custom_call" | custom-call | bytes 1048576 | tf_op jit(solution)/shard_map/pallas_call | solution.py:37
  36.4 1.8 %collective-permute-start.12 = (bf16[128,128]{1,0:T(8,128)(2,1)S(1)}, bf16[128,128]{1,0:T(8,128)(2,1)S(1)}, u32[]{:S(2)}, u32[]{:S(2)}) collective-permute-start(bf16[128,128]{1,0:T(8,128)(2,1)S(1)} %get-tuple-element.87), channel_id=1, source_target_pairs={{0,4},{4,0},{8,12},{12,8},{1,5},{5,1},{9,13},{13,9},{2,6},{6,2},{1... | collective-permute-start | bytes 98312 | tf_op jit(solution)/shard_map/ppermute | solution.py:17
  38.2 1.7 %collective-permute-start.13 = (bf16[128,128]{1,0:T(8,128)(2,1)S(1)}, bf16[128,128]{1,0:T(8,128)(2,1)S(1)}, u32[]{:S(2)}, u32[]{:S(2)}) collective-permute-start(bf16[128,128]{1,0:T(8,128)(2,1)S(1)} %get-tuple-element.88), channel_id=1, source_target_pairs={{0,8},{4,12},{8,0},{12,4},{1,9},{5,13},{9,1},{13,5},{2,10},{6,14},... | collective-permute-start | bytes 98312 | tf_op jit(solution)/shard_map/ppermute | solution.py:17
  40.0 0.3 shard_map.122
  40.2 0.1 collective-permute-done.12.r0
  40.4 2.7 %collective-permute-done.13.r1 = bf16[128,128]{1,0:T(8,128)(2,1)S(1)} collective-permute-done((bf16[128,128]{1,0:T(8,128)(2,1)S(1)}, bf16[128,128]{1,0:T(8,128)(2,1)S(1)}, u32[]{:S(2)}, u32[]{:S(2)}) %collective-permute-start.13) | collective-permute-done | bytes 32800 | tf_op jit(solution)/shard_map/ppermute | solution.py:17
  43.1 0.1 shard_map.123
  43.2 0.1 collective-permute-start.14
  43.3 0.7 %collective-permute-start.15 = (bf16[128,128]{1,0:T(8,128)(2,1)S(1)}, bf16[128,128]{1,0:T(8,128)(2,1)S(1)}, u32[]{:S(2)}, u32[]{:S(2)}) collective-permute-start(bf16[128,128]{1,0:T(8,128)(2,1)S(1)} %get-tuple-element.94), channel_id=1, source_target_pairs={{0,2},{1,3},{2,0},{3,1},{4,6},{5,7},{6,4},{7,5},{8,10},{9,11},{10,... | collective-permute-start | bytes 98312 | tf_op jit(solution)/shard_map/ppermute | solution.py:17
  44.0 1.1 %collective-permute-start.16 = (bf16[128,128]{1,0:T(8,128)(2,1)S(1)}, bf16[128,128]{1,0:T(8,128)(2,1)S(1)}, u32[]{:S(2)}, u32[]{:S(2)}) collective-permute-start(bf16[128,128]{1,0:T(8,128)(2,1)S(1)} %get-tuple-element.95), channel_id=1, source_target_pairs={{0,3},{1,2},{2,1},{3,0},{4,7},{5,6},{6,5},{7,4},{8,11},{9,10},{10,... | collective-permute-start | bytes 98312 | tf_op jit(solution)/shard_map/ppermute | solution.py:17
  45.1 2.4 %collective-permute-done.15.refs_2_ = bf16[128,128]{1,0:T(8,128)(2,1)S(1)} collective-permute-done((bf16[128,128]{1,0:T(8,128)(2,1)S(1)}, bf16[128,128]{1,0:T(8,128)(2,1)S(1)}, u32[]{:S(2)}, u32[]{:S(2)}) %collective-permute-start.15) | collective-permute-done | bytes 32800 | tf_op jit(solution)/shard_map/ppermute | solution.py:17
  47.5 0.2 collective-permute-done.16.refs_3_
  47.7 0.8 %shard_map.124 = (f32[128,128]{1,0:T(8,128)S(1)}, bf16[128,128]{1,0:T(8,128)(2,1)S(1)}, bf16[128,128]{1,0:T(8,128)(2,1)S(1)}) custom-call(s32[32,128]{1,0:T(8,128)S(1)} %get-tuple-element.58.s_ref, bf16[128,128]{1,0:T(8,128)(2,1)S(1)} %get-tuple-element.92.refs_0_, bf16[128,128]{1,0:T(8,128)(2,1)S(1)} %collective-permute-done.14.refs_1_, ...), custom_call_target="tpu_custom_call" | custom-call | bytes 1048576 | tf_op jit(solution)/shard_map/pallas_call | solution.py:37
  48.6 0.3 collective-permute-start.17
  48.8 1.8 %collective-permute-start.18 = (bf16[128,128]{1,0:T(8,128)(2,1)S(1)}, bf16[128,128]{1,0:T(8,128)(2,1)S(1)}, u32[]{:S(2)}, u32[]{:S(2)}) collective-permute-start(bf16[128,128]{1,0:T(8,128)(2,1)S(1)} %get-tuple-element.101), channel_id=1, source_target_pairs={{0,8},{4,12},{8,0},{12,4},{1,9},{5,13},{9,1},{13,5},{2,10},{6,14},... | collective-permute-start | bytes 98312 | tf_op jit(solution)/shard_map/ppermute | solution.py:17
  50.6 2.3 %collective-permute-done.17.r0 = bf16[128,128]{1,0:T(8,128)(2,1)S(1)} collective-permute-done((bf16[128,128]{1,0:T(8,128)(2,1)S(1)}, bf16[128,128]{1,0:T(8,128)(2,1)S(1)}, u32[]{:S(2)}, u32[]{:S(2)}) %collective-permute-start.17) | collective-permute-done | bytes 32800 | tf_op jit(solution)/shard_map/ppermute | solution.py:17
  52.9 1.0 %collective-permute-done.18.r1 = bf16[128,128]{1,0:T(8,128)(2,1)S(1)} collective-permute-done((bf16[128,128]{1,0:T(8,128)(2,1)S(1)}, bf16[128,128]{1,0:T(8,128)(2,1)S(1)}, u32[]{:S(2)}, u32[]{:S(2)}) %collective-permute-start.18) | collective-permute-done | bytes 32800 | tf_op jit(solution)/shard_map/ppermute | solution.py:17
  53.9 0.1 collective-permute-start.21
  54.0 1.0 %collective-permute-start.20 = (bf16[128,128]{1,0:T(8,128)(2,1)S(1)}, bf16[128,128]{1,0:T(8,128)(2,1)S(1)}, u32[]{:S(2)}, u32[]{:S(2)}) collective-permute-start(bf16[128,128]{1,0:T(8,128)(2,1)S(1)} %shard_map.125.refs_0_), channel_id=1, source_target_pairs={{0,2},{1,3},{2,0},{3,1},{4,6},{5,7},{6,4},{7,5},{8,10},{9,11},{10,... | collective-permute-start | bytes 98312 | tf_op jit(solution)/shard_map/ppermute | solution.py:17
  55.0 0.8 %collective-permute-start.19 = (bf16[128,128]{1,0:T(8,128)(2,1)S(1)}, bf16[128,128]{1,0:T(8,128)(2,1)S(1)}, u32[]{:S(2)}, u32[]{:S(2)}) collective-permute-start(bf16[128,128]{1,0:T(8,128)(2,1)S(1)} %shard_map.125.refs_0_), channel_id=1, source_target_pairs={{0,1},{1,0},{2,3},{3,2},{4,5},{5,4},{6,7},{7,6},{8,9},{9,8},{10,11... | collective-permute-start | bytes 98312 | tf_op jit(solution)/shard_map/ppermute | solution.py:17
  55.8 1.5 %collective-permute-done.21.refs_3_ = bf16[128,128]{1,0:T(8,128)(2,1)S(1)} collective-permute-done((bf16[128,128]{1,0:T(8,128)(2,1)S(1)}, bf16[128,128]{1,0:T(8,128)(2,1)S(1)}, u32[]{:S(2)}, u32[]{:S(2)}) %collective-permute-start.21) | collective-permute-done | bytes 32800 | tf_op jit(solution)/shard_map/ppermute | solution.py:17
  57.3 1.0 %collective-permute-done.20.refs_2_ = bf16[128,128]{1,0:T(8,128)(2,1)S(1)} collective-permute-done((bf16[128,128]{1,0:T(8,128)(2,1)S(1)}, bf16[128,128]{1,0:T(8,128)(2,1)S(1)}, u32[]{:S(2)}, u32[]{:S(2)}) %collective-permute-start.20) | collective-permute-done | bytes 32800 | tf_op jit(solution)/shard_map/ppermute | solution.py:17
  58.3 0.9 %shard_map.126 = (f32[512,128]{1,0:T(8,128)S(1)}, bf16[128,128]{1,0:T(8,128)(2,1)S(1)}, bf16[128,128]{1,0:T(8,128)(2,1)S(1)}, bf16[512,128]{1,0:T(8,128)(2,1)S(1...) custom-call(s32[32,128]{1,0:T(8,128)S(1)} %get-tuple-element.58.s_ref, ...), custom_call_target="tpu_custom_call" | custom-call | bytes 1048576 | tf_op jit(solution)/shard_map/pallas_call | solution.py:37
  59.2 1.6 %collective-permute-start.22 = (bf16[128,128]{1,0:T(8,128)(2,1)S(1)}, bf16[128,128]{1,0:T(8,128)(2,1)S(1)}, u32[]{:S(2)}, u32[]{:S(2)}) collective-permute-start(bf16[128,128]{1,0:T(8,128)(2,1)S(1)} %get-tuple-element.106), channel_id=1, source_target_pairs={{0,4},{4,0},{8,12},{12,8},{1,5},{5,1},{9,13},{13,9},{2,6},{6,2},{1... | collective-permute-start | bytes 98312 | tf_op jit(solution)/shard_map/ppermute | solution.py:17
  60.8 1.9 %collective-permute-start.23 = (bf16[128,128]{1,0:T(8,128)(2,1)S(1)}, bf16[128,128]{1,0:T(8,128)(2,1)S(1)}, u32[]{:S(2)}, u32[]{:S(2)}) collective-permute-start(bf16[128,128]{1,0:T(8,128)(2,1)S(1)} %get-tuple-element.107), channel_id=1, source_target_pairs={{0,8},{4,12},{8,0},{12,4},{1,9},{5,13},{9,1},{13,5},{2,10},{6,14},... | collective-permute-start | bytes 98312 | tf_op jit(solution)/shard_map/ppermute | solution.py:17
  62.7 0.3 shard_map.127
  62.9 0.2 collective-permute-done.22.r0
  63.2 2.7 %collective-permute-done.23.r1 = bf16[128,128]{1,0:T(8,128)(2,1)S(1)} collective-permute-done((bf16[128,128]{1,0:T(8,128)(2,1)S(1)}, bf16[128,128]{1,0:T(8,128)(2,1)S(1)}, u32[]{:S(2)}, u32[]{:S(2)}) %collective-permute-start.23) | collective-permute-done | bytes 32800 | tf_op jit(solution)/shard_map/ppermute | solution.py:17
  65.9 0.7 %shard_map.128 = f32[4,128,128]{2,1,0:T(8,128)} custom-call(s32[32,128]{1,0:T(8,128)S(1)} %get-tuple-element.58.s_ref, bf16[128,128]{1,0:T(8,128)(2,1)S(1)} %collective-permute-done.22.r0, bf16[128,128]{1,0:T(8,128)(2,1)S(1)} %collective-permute-done.23.r1, f32[4,128,128]{2,1,0:T(8,128)S(1)} %bitcast.8), custom_call_target="tpu_custom_call" | custom-call | bytes 1048576 | tf_op jit(solution)/shard_map/pallas_call | solution.py:37
  (19 shorter events, 0.1 us)
Async XLA Ops:
  0.6 8.0 %copy-start.7 = (s32[4]{0:T(128)S(1)}, s32[4]{0:T(128)}, u32[]{:S(2)}) copy-start(s32[4]{0:T(128)} %pool_in.1) | copy-start | bytes 52
  0.6 8.0 %copy-start.8 = (s32[1,4]{1,0:T(1,128)S(1)}, s32[1,4]{1,0:T(1,128)}, u32[]{:S(2)}) copy-start(s32[1,4]{1,0:T(1,128)} %coarse_in.1) | copy-start | bytes 52
  1.4 0.9 %copy-start.1 = (bf16[512,128]{1,0:T(8,128)(2,1)S(1)}, bf16[512,128]{1,0:T(8,128)(2,1)}, u32[]{:S(2)}) copy-start(bf16[512,128]{1,0:T(8,128)(2,1)} %nodes_hbm.1) | copy-start | bytes 393220
  2.3 6.3 %copy-start.2 = (bf16[512,128]{1,0:T(8,128)(2,1)S(1)}, bf16[512,128]{1,0:T(8,128)(2,1)}, u32[]{:S(2)}) copy-start(bf16[512,128]{1,0:T(8,128)(2,1)} %c_in.1) | copy-start | bytes 393220
  2.3 6.3 %copy-start.5 = (s32[4,4]{1,0:T(4,128)S(1)}, s32[4,4]{1,0:T(4,128)}, u32[]{:S(2)}) copy-start(s32[4,4]{1,0:T(4,128)} %near_in.1) | copy-start | bytes 196
  2.9 5.7 %copy-start.3 = (s32[4,4,128]{2,1,0:T(4,128)S(1)}, s32[4,4,128]{2,1,0:T(4,128)}, u32[]{:S(2)}) copy-start(s32[4,4,128]{2,1,0:T(4,128)} %param.14) | copy-start | bytes 24580
  2.9 9.4 %collective-permute-start = (bf16[128,128]{1,0:T(8,128)(2,1)S(1)}, bf16[128,128]{1,0:T(8,128)(2,1)S(1)}, u32[]{:S(2)}, u32[]{:S(2)}) collective-permute-start(bf16[128,128]{1,0:T(8,128)(2,1)S(1)} %get-tuple-element.59), channel_id=1, source_target_pairs={{0,4},{4,0},{8,12},{12,8},{1,5},{5,1},{9,13},{13,9},{2,6},{6,2},{1... | collective-permute-start | bytes 98312 | tf_op jit(solution)/shard_map/ppermute | solution.py:17
  6.0 6.3 %collective-permute-start.1 = (bf16[128,128]{1,0:T(8,128)(2,1)S(1)}, bf16[128,128]{1,0:T(8,128)(2,1)S(1)}, u32[]{:S(2)}, u32[]{:S(2)}) collective-permute-start(bf16[128,128]{1,0:T(8,128)(2,1)S(1)} %get-tuple-element.60), channel_id=1, source_target_pairs={{0,8},{4,12},{8,0},{12,4},{1,9},{5,13},{9,1},{13,5},{2,10},{6,14},... | collective-permute-start | bytes 98312 | tf_op jit(solution)/shard_map/ppermute | solution.py:17
  8.6 1.1 %copy-start = (bf16[3,6,128,128]{3,2,1,0:T(8,128)(2,1)S(1)}, bf16[3,6,128,128]{3,2,1,0:T(8,128)(2,1)}, u32[]{:S(2)}) copy-start(bf16[3,6,128,128]{3,2,1,0:T(8,128)(2,1)} %w_in.1) | copy-start | bytes 1769476
  9.7 0.7 %copy-start.4 = (f32[3,2,128]{2,1,0:T(2,128)S(1)}, f32[3,2,128]{2,1,0:T(2,128)}, u32[]{:S(2)}) copy-start(f32[3,2,128]{2,1,0:T(2,128)} %b_in.1) | copy-start | bytes 9220
  10.4 0.7 %copy-start.6 = (s32[1,4,128]{2,1,0:T(4,128)S(1)}, s32[1,4,128]{2,1,0:T(4,128)}, u32[]{:S(2)}) copy-start(s32[1,4,128]{2,1,0:T(4,128)} %param.17) | copy-start | bytes 6148
  13.4 1.9 %collective-permute-start.2 = (bf16[144,128]{1,0:T(8,128)(2,1)S(1)}, bf16[144,128]{1,0:T(8,128)(2,1)S(1)}, u32[]{:S(2)}, u32[]{:S(2)}) collective-permute-start(bf16[144,128]{1,0:T(8,128)(2,1)S(1)} %get-tuple-element.67), channel_id=1, source_target_pairs={{0,1},{1,0},{2,3},{3,2},{4,5},{5,4},{6,7},{7,6},{8,9},{9,8},{10,11... | collective-permute-start | bytes 110600 | tf_op jit(solution)/shard_map/ppermute | solution.py:17
  13.5 4.0 %collective-permute-start.3 = (bf16[144,128]{1,0:T(8,128)(2,1)S(1)}, bf16[144,128]{1,0:T(8,128)(2,1)S(1)}, u32[]{:S(2)}, u32[]{:S(2)}) collective-permute-start(bf16[144,128]{1,0:T(8,128)(2,1)S(1)} %get-tuple-element.68), channel_id=1, source_target_pairs={{0,2},{1,3},{2,0},{3,1},{4,6},{5,7},{6,4},{7,5},{8,10},{9,11},{10,... | collective-permute-start | bytes 110600 | tf_op jit(solution)/shard_map/ppermute | solution.py:17
  15.1 3.4 %collective-permute-start.4 = (bf16[144,128]{1,0:T(8,128)(2,1)S(1)}, bf16[144,128]{1,0:T(8,128)(2,1)S(1)}, u32[]{:S(2)}, u32[]{:S(2)}) collective-permute-start(bf16[144,128]{1,0:T(8,128)(2,1)S(1)} %get-tuple-element.69), channel_id=1, source_target_pairs={{0,3},{1,2},{2,1},{3,0},{4,7},{5,6},{6,5},{7,4},{8,11},{9,10},{10,... | collective-permute-start | bytes 110600 | tf_op jit(solution)/shard_map/ppermute | solution.py:17
  18.5 5.2 %collective-permute-start.6 = (bf16[128,128]{1,0:T(8,128)(2,1)S(1)}, bf16[128,128]{1,0:T(8,128)(2,1)S(1)}, u32[]{:S(2)}, u32[]{:S(2)}) collective-permute-start(bf16[128,128]{1,0:T(8,128)(2,1)S(1)} %get-tuple-element.70.h_ref), channel_id=1, source_target_pairs={{0,8},{4,12},{8,0},{12,4},{1,9},{5,13},{9,1},{13,5},{2,10},{6,14},... | collective-permute-start | bytes 98312 | tf_op jit(solution)/shard_map/ppermute | solution.py:17
  19.7 4.3 %collective-permute-start.5 = (bf16[128,128]{1,0:T(8,128)(2,1)S(1)}, bf16[128,128]{1,0:T(8,128)(2,1)S(1)}, u32[]{:S(2)}, u32[]{:S(2)}) collective-permute-start(bf16[128,128]{1,0:T(8,128)(2,1)S(1)} %get-tuple-element.70.h_ref), channel_id=1, source_target_pairs={{0,4},{4,0},{8,12},{12,8},{1,5},{5,1},{9,13},{13,9},{2,6},{6,2},{1... | collective-permute-start | bytes 98312 | tf_op jit(solution)/shard_map/ppermute | solution.py:17
  24.7 3.4 %collective-permute-start.9 = (bf16[128,128]{1,0:T(8,128)(2,1)S(1)}, bf16[128,128]{1,0:T(8,128)(2,1)S(1)}, u32[]{:S(2)}, u32[]{:S(2)}) collective-permute-start(bf16[128,128]{1,0:T(8,128)(2,1)S(1)} %get-tuple-element.76.refs_0_), channel_id=1, source_target_pairs={{0,3},{1,2},{2,1},{3,0},{4,7},{5,6},{6,5},{7,4},{8,11},{9,10},{10,... | collective-permute-start | bytes 98312 | tf_op jit(solution)/shard_map/ppermute | solution.py:17
  24.8 4.3 %collective-permute-start.8 = (bf16[128,128]{1,0:T(8,128)(2,1)S(1)}, bf16[128,128]{1,0:T(8,128)(2,1)S(1)}, u32[]{:S(2)}, u32[]{:S(2)}) collective-permute-start(bf16[128,128]{1,0:T(8,128)(2,1)S(1)} %get-tuple-element.76.refs_0_), channel_id=1, source_target_pairs={{0,2},{1,3},{2,0},{3,1},{4,6},{5,7},{6,4},{7,5},{8,10},{9,11},{10,... | collective-permute-start | bytes 98312 | tf_op jit(solution)/shard_map/ppermute | solution.py:17
  25.7 3.3 %collective-permute-start.7 = (bf16[128,128]{1,0:T(8,128)(2,1)S(1)}, bf16[128,128]{1,0:T(8,128)(2,1)S(1)}, u32[]{:S(2)}, u32[]{:S(2)}) collective-permute-start(bf16[128,128]{1,0:T(8,128)(2,1)S(1)} %get-tuple-element.76.refs_0_), channel_id=1, source_target_pairs={{0,1},{1,0},{2,3},{3,2},{4,5},{5,4},{6,7},{7,6},{8,9},{9,8},{10,11... | collective-permute-start | bytes 98312 | tf_op jit(solution)/shard_map/ppermute | solution.py:17
  29.1 4.3 %collective-permute-start.10 = (bf16[128,128]{1,0:T(8,128)(2,1)S(1)}, bf16[128,128]{1,0:T(8,128)(2,1)S(1)}, u32[]{:S(2)}, u32[]{:S(2)}) collective-permute-start(bf16[128,128]{1,0:T(8,128)(2,1)S(1)} %get-tuple-element.78), channel_id=1, source_target_pairs={{0,4},{4,0},{8,12},{12,8},{1,5},{5,1},{9,13},{13,9},{2,6},{6,2},{1... | collective-permute-start | bytes 98312 | tf_op jit(solution)/shard_map/ppermute | solution.py:17
  29.3 5.0 %collective-permute-start.11 = (bf16[128,128]{1,0:T(8,128)(2,1)S(1)}, bf16[128,128]{1,0:T(8,128)(2,1)S(1)}, u32[]{:S(2)}, u32[]{:S(2)}) collective-permute-start(bf16[128,128]{1,0:T(8,128)(2,1)S(1)} %get-tuple-element.79), channel_id=1, source_target_pairs={{0,8},{4,12},{8,0},{12,4},{1,9},{5,13},{9,1},{13,5},{2,10},{6,14},... | collective-permute-start | bytes 98312 | tf_op jit(solution)/shard_map/ppermute | solution.py:17
  36.4 3.9 %collective-permute-start.12 = (bf16[128,128]{1,0:T(8,128)(2,1)S(1)}, bf16[128,128]{1,0:T(8,128)(2,1)S(1)}, u32[]{:S(2)}, u32[]{:S(2)}) collective-permute-start(bf16[128,128]{1,0:T(8,128)(2,1)S(1)} %get-tuple-element.87), channel_id=1, source_target_pairs={{0,4},{4,0},{8,12},{12,8},{1,5},{5,1},{9,13},{13,9},{2,6},{6,2},{1... | collective-permute-start | bytes 98312 | tf_op jit(solution)/shard_map/ppermute | solution.py:17
  38.2 4.9 %collective-permute-start.13 = (bf16[128,128]{1,0:T(8,128)(2,1)S(1)}, bf16[128,128]{1,0:T(8,128)(2,1)S(1)}, u32[]{:S(2)}, u32[]{:S(2)}) collective-permute-start(bf16[128,128]{1,0:T(8,128)(2,1)S(1)} %get-tuple-element.88), channel_id=1, source_target_pairs={{0,8},{4,12},{8,0},{12,4},{1,9},{5,13},{9,1},{13,5},{2,10},{6,14},... | collective-permute-start | bytes 98312 | tf_op jit(solution)/shard_map/ppermute | solution.py:17
  43.2 1.9 %collective-permute-start.14 = (bf16[128,128]{1,0:T(8,128)(2,1)S(1)}, bf16[128,128]{1,0:T(8,128)(2,1)S(1)}, u32[]{:S(2)}, u32[]{:S(2)}) collective-permute-start(bf16[128,128]{1,0:T(8,128)(2,1)S(1)} %get-tuple-element.93), channel_id=1, source_target_pairs={{0,1},{1,0},{2,3},{3,2},{4,5},{5,4},{6,7},{7,6},{8,9},{9,8},{10,11... | collective-permute-start | bytes 98312 | tf_op jit(solution)/shard_map/ppermute | solution.py:17
  43.3 4.2 %collective-permute-start.15 = (bf16[128,128]{1,0:T(8,128)(2,1)S(1)}, bf16[128,128]{1,0:T(8,128)(2,1)S(1)}, u32[]{:S(2)}, u32[]{:S(2)}) collective-permute-start(bf16[128,128]{1,0:T(8,128)(2,1)S(1)} %get-tuple-element.94), channel_id=1, source_target_pairs={{0,2},{1,3},{2,0},{3,1},{4,6},{5,7},{6,4},{7,5},{8,10},{9,11},{10,... | collective-permute-start | bytes 98312 | tf_op jit(solution)/shard_map/ppermute | solution.py:17
  44.0 3.7 %collective-permute-start.16 = (bf16[128,128]{1,0:T(8,128)(2,1)S(1)}, bf16[128,128]{1,0:T(8,128)(2,1)S(1)}, u32[]{:S(2)}, u32[]{:S(2)}) collective-permute-start(bf16[128,128]{1,0:T(8,128)(2,1)S(1)} %get-tuple-element.95), channel_id=1, source_target_pairs={{0,3},{1,2},{2,1},{3,0},{4,7},{5,6},{6,5},{7,4},{8,11},{9,10},{10,... | collective-permute-start | bytes 98312 | tf_op jit(solution)/shard_map/ppermute | solution.py:17
  48.6 4.3 %collective-permute-start.17 = (bf16[128,128]{1,0:T(8,128)(2,1)S(1)}, bf16[128,128]{1,0:T(8,128)(2,1)S(1)}, u32[]{:S(2)}, u32[]{:S(2)}) collective-permute-start(bf16[128,128]{1,0:T(8,128)(2,1)S(1)} %get-tuple-element.100), channel_id=1, source_target_pairs={{0,4},{4,0},{8,12},{12,8},{1,5},{5,1},{9,13},{13,9},{2,6},{6,2},{1... | collective-permute-start | bytes 98312 | tf_op jit(solution)/shard_map/ppermute | solution.py:17
  48.8 5.0 %collective-permute-start.18 = (bf16[128,128]{1,0:T(8,128)(2,1)S(1)}, bf16[128,128]{1,0:T(8,128)(2,1)S(1)}, u32[]{:S(2)}, u32[]{:S(2)}) collective-permute-start(bf16[128,128]{1,0:T(8,128)(2,1)S(1)} %get-tuple-element.101), channel_id=1, source_target_pairs={{0,8},{4,12},{8,0},{12,4},{1,9},{5,13},{9,1},{13,5},{2,10},{6,14},... | collective-permute-start | bytes 98312 | tf_op jit(solution)/shard_map/ppermute | solution.py:17
  53.9 3.4 %collective-permute-start.21 = (bf16[128,128]{1,0:T(8,128)(2,1)S(1)}, bf16[128,128]{1,0:T(8,128)(2,1)S(1)}, u32[]{:S(2)}, u32[]{:S(2)}) collective-permute-start(bf16[128,128]{1,0:T(8,128)(2,1)S(1)} %shard_map.125.refs_0_), channel_id=1, source_target_pairs={{0,3},{1,2},{2,1},{3,0},{4,7},{5,6},{6,5},{7,4},{8,11},{9,10},{10,... | collective-permute-start | bytes 98312 | tf_op jit(solution)/shard_map/ppermute | solution.py:17
  54.0 4.3 %collective-permute-start.20 = (bf16[128,128]{1,0:T(8,128)(2,1)S(1)}, bf16[128,128]{1,0:T(8,128)(2,1)S(1)}, u32[]{:S(2)}, u32[]{:S(2)}) collective-permute-start(bf16[128,128]{1,0:T(8,128)(2,1)S(1)} %shard_map.125.refs_0_), channel_id=1, source_target_pairs={{0,2},{1,3},{2,0},{3,1},{4,6},{5,7},{6,4},{7,5},{8,10},{9,11},{10,... | collective-permute-start | bytes 98312 | tf_op jit(solution)/shard_map/ppermute | solution.py:17
  55.0 3.3 %collective-permute-start.19 = (bf16[128,128]{1,0:T(8,128)(2,1)S(1)}, bf16[128,128]{1,0:T(8,128)(2,1)S(1)}, u32[]{:S(2)}, u32[]{:S(2)}) collective-permute-start(bf16[128,128]{1,0:T(8,128)(2,1)S(1)} %shard_map.125.refs_0_), channel_id=1, source_target_pairs={{0,1},{1,0},{2,3},{3,2},{4,5},{5,4},{6,7},{7,6},{8,9},{9,8},{10,11... | collective-permute-start | bytes 98312 | tf_op jit(solution)/shard_map/ppermute | solution.py:17
  59.2 4.0 %collective-permute-start.22 = (bf16[128,128]{1,0:T(8,128)(2,1)S(1)}, bf16[128,128]{1,0:T(8,128)(2,1)S(1)}, u32[]{:S(2)}, u32[]{:S(2)}) collective-permute-start(bf16[128,128]{1,0:T(8,128)(2,1)S(1)} %get-tuple-element.106), channel_id=1, source_target_pairs={{0,4},{4,0},{8,12},{12,8},{1,5},{5,1},{9,13},{13,9},{2,6},{6,2},{1... | collective-permute-start | bytes 98312 | tf_op jit(solution)/shard_map/ppermute | solution.py:17
  60.8 5.1 %collective-permute-start.23 = (bf16[128,128]{1,0:T(8,128)(2,1)S(1)}, bf16[128,128]{1,0:T(8,128)(2,1)S(1)}, u32[]{:S(2)}, u32[]{:S(2)}) collective-permute-start(bf16[128,128]{1,0:T(8,128)(2,1)S(1)} %get-tuple-element.107), channel_id=1, source_target_pairs={{0,8},{4,12},{8,0},{12,4},{1,9},{5,13},{9,1},{13,5},{2,10},{6,14},... | collective-permute-start | bytes 98312 | tf_op jit(solution)/shard_map/ppermute | solution.py:17

commit v3 on v2

--- a/solution.py
+++ b/solution.py
@@ -10,6 +10,7 @@
 I32 = jnp.int32
 COUNT_ROWS = 16
 GROUP_AXES = ("pair", "sub")
+ORDER = (1, 0)
 
 
 def swapped(value, axis, mask):
@@ -33,16 +34,28 @@
     return table[index : index + 1, :][0, 0]
 
 
-def run(kernel, outs, *arrays, scratch=(), flops=0, space=pltpu.VMEM):
+def run(kernel, outs, *arrays, scratch=(), flops=0):
     return pl.pallas_call(
         kernel,
         out_shape=[jax.ShapeDtypeStruct(shape, dtype) for shape, dtype in outs],
-        in_specs=[pl.BlockSpec(memory_space=space)] * len(arrays),
+        in_specs=[pl.BlockSpec(memory_space=pltpu.VMEM)] * len(arrays),
         out_specs=[pl.BlockSpec(memory_space=pltpu.VMEM)] * len(outs),
         scratch_shapes=list(scratch),
         compiler_params=pltpu.CompilerParams(vmem_limit_bytes=12 * 2**20),
         cost_estimate=pl.CostEstimate(flops=flops, bytes_accessed=2**20, transcendentals=0),
     )(*arrays)
+
+
+def run_hbm(kernel, outs, far, *near, scratch=()):
+    return pl.pallas_call(
+        kernel,
+        out_shape=[pltpu.VMEM(shape, dtype) for shape, dtype in outs],
+        in_specs=[pl.BlockSpec(memory_space=pltpu.HBM)] * len(far) + [pl.BlockSpec(memory_space=pltpu.VMEM)] * len(near),
+        out_specs=[pl.BlockSpec(memory_space=pltpu.VMEM)] * len(outs),
+        scratch_shapes=list(scratch),
+        compiler_params=pltpu.CompilerParams(vmem_limit_bytes=12 * 2**20),
+        cost_estimate=pl.CostEstimate(flops=0, bytes_accessed=2**20, transcendentals=0),
+    )(*[pltpu.with_memory_space_constraint(array, pltpu.HBM) for array in far], *near)
 
 
 def per_device(
@@ -75,35 +88,43 @@
     at_me = at_coarse + degree
     table_rows = -(-(at_me + 1) // 8) * 8
 
+    masks = (0,) + tuple(range(slots - 1, 0, -1))
+    same_masks = tuple(range(slots))
+
     def exchange(pieces):
-        return [swapped(piece, "dom", bit) for piece, bit in zip(pieces, xor_bits)]
+        return [swapped(piece, "dom", xor_bits[r]) for r, piece in zip(ORDER, pieces)]
+
+    def exchange_same(piece):
+        return [swapped(piece, "dom", bit) for bit in xor_bits]
 
     def spread(pieces):
-        return [swapped(pieces[mask], GROUP_AXES, mask) for mask in range(1, slots)]
+        return [swapped(piece, GROUP_AXES, mask) for mask, piece in zip(masks[1:], pieces[1:])]
+
+    def spread_same(piece):
+        return [swapped(piece, GROUP_AXES, mask) for mask in same_masks[1:]]
 
     def rows_of(b):
         return pl.ds(b * size, size)
 
-    def choose(send_ref, nodes_hbm, h_ref, out0, out1, send_smem, sems):
-        copies = [
-            pltpu.make_async_copy(send_ref, send_smem, sems.at[0]),
-            pltpu.make_async_copy(nodes_hbm, h_ref, sems.at[1]),
-        ]
+    def fetch(pairs, sems):
+        copies = [pltpu.make_async_copy(source, target, sems.at[i]) for i, (source, target) in enumerate(pairs)]
         for copy in copies:
             copy.start()
         for copy in copies:
             copy.wait()
-        for r, out in enumerate((out0, out1)):
-            at = pl.multiple_of(send_smem[0, r, 0] * size, size)
+
+    def choose(send_in, nodes_in, h_ref, out0, out1, send_scr, sems):
+        fetch([(send_in, send_scr), (nodes_in, h_ref)], sems)
+        for r, out in zip(ORDER, (out0, out1)):
+            at = pl.multiple_of(send_scr[0:1, r : r + 1][0, 0] * size, size)
             out[...] = h_ref[pl.ds(at, size), :]
 
-    h0, *first_sends = run(
+    sent = send_blocks.reshape(1, rounds)
+    h0, *first_sends = run_hbm(
         choose,
         [(fine, BF16)] + [(tile, BF16)] * rounds,
-        send_blocks,
-        nodes,
-        space=pltpu.HBM,
-        scratch=[pltpu.SMEM(send_blocks.shape, I32), pltpu.SemaphoreType.DMA((2,))],
+        [sent, nodes],
+        scratch=[pltpu.VMEM((1, rounds), I32), pltpu.SemaphoreType.DMA((2,))],
     )
     halo = exchange(first_sends)
 
@@ -139,9 +160,9 @@
         node_slope_ref[...] = (gate + hidden * (1.0 - gate)).astype(BF16)
         return mm(hidden.astype(BF16), w_ref[layer, 5])
 
-    def senders_into(own, halos, layer, w_ref, send_scr):
+    def senders_into(own, halos, layer, w_ref, send_scr, order=ORDER):
         count = send_scr.shape[0] - rounds
-        for r, g in enumerate(halos):
+        for r, g in zip(order, halos):
             send_scr[count + r] = mm(g[...], w_ref[layer, 1]).astype(BF16)
         for b in range(count):
             send_scr[b] = own[rows_of(b), :]
@@ -165,7 +186,7 @@
 
     def halo_grads_into(outs, layer, w_ref, acc_scr):
         count = acc_scr.shape[0] - rounds
-        for r, out in enumerate(outs):
+        for r, out in zip(ORDER, outs):
             out[...] = mm_t(acc_scr[count + r].astype(BF16), w_ref[layer, 1]).astype(BF16)
 
     def own_back(grad, layer, w_ref, d_node, d_recv, d_send):
@@ -173,7 +194,7 @@
 
     def pooled_into(read, s_ref, out_refs, with_count):
         me = scalar(s_ref, at_me)
-        for mask in range(slots):
+        for mask, out in zip(masks, out_refs):
             slot = me ^ mask
             total, count = None, None
             for b in range(blocks):
@@ -181,69 +202,58 @@
                 part = read(b) * hit
                 total = part if total is None else total + part
                 count = hit if count is None else count + hit
-            out_refs[mask][0:size, :] = total.astype(BF16)
+            out[0:size, :] = total.astype(BF16)
             if with_count:
-                out_refs[mask][size:, :] = jnp.full((COUNT_ROWS, features), count, F32).astype(BF16)
-
-    inputs = (
-        send_blocks,
+                out[size:, :] = jnp.full((COUNT_ROWS, features), count, F32).astype(BF16)
+
+    inputs = [
+        sent,
         neighbour_blocks,
-        pool_map,
+        pool_map.reshape(1, blocks),
         coarse_blocks,
         neighbour_nodes.reshape(edges, size),
         coarse_nodes.reshape(degree, size),
         weights,
         biases,
         cotangent,
-    )
+    ]
     own_out = [(fine, F32), (fine, F32), (fine, BF16)]
 
-    def prepare(send_in, near_in, pool_in, coarse_in, ends_in, cends_in, w_in, b_in, c_in, h_ref,
-                s_ref, w_ref, b_ref, c_ref, pick, put, cpick, cput, recv, node, sender,
-                send_s, near_s, pool_s, coarse_s, ends, cends, sems):
-        pairs = (
-            (send_in, send_s), (near_in, near_s), (pool_in, pool_s), (coarse_in, coarse_s),
-            (ends_in, ends), (cends_in, cends), (w_in, w_ref), (b_in, b_ref), (c_in, c_ref),
-        )
-        copies = [pltpu.make_async_copy(source, target, sems.at[i]) for i, (source, target) in enumerate(pairs)]
-        for copy in copies:
-            copy.start()
-        for copy in copies:
-            copy.wait()
-
-        def put_row(index, value):
-            s_ref[index : index + 1, :] = jnp.full((1, features), value, I32)
+    def prepare(*refs):
+        sources, h_ref = refs[: len(inputs)], refs[len(inputs)]
+        w_ref, b_ref, c_ref, s_ref, pick, put, cpick, cput, recv, node, sender, *kept, sems = refs[len(inputs) + 1 :]
+        send_scr, near_scr, pool_scr, coarse_scr, ends, cends = kept
+        fetch(list(zip(sources, kept + [w_ref, b_ref, c_ref])), sems)
+
+        def put_row(index, ref, i, j):
+            s_ref[index : index + 1, :] = jnp.broadcast_to(ref[i : i + 1, j : j + 1], (1, features))
 
         for r in range(rounds):
-            put_row(r, send_s[0, r, 0])
+            put_row(r, send_scr, 0, r)
         for b in range(blocks):
             for e in range(degree):
-                put_row(at_near + b * degree + e, near_s[b, e])
-            put_row(at_pool + b, pool_s[b])
+                put_row(at_near + b * degree + e, near_scr, b, e)
+            put_row(at_pool + b, pool_scr, 0, b)
         for e in range(degree):
-            put_row(at_coarse + e, coarse_s[0, e])
-        put_row(at_me, lax.axis_index("pair") * sub_size + lax.axis_index("sub"))
+            put_row(at_coarse + e, coarse_scr, 0, e)
+        own = lax.axis_index("pair") * sub_size + lax.axis_index("sub")
+        s_ref[at_me : at_me + 1, :] = jnp.full((1, features), own, I32)
         own_into(h_ref[...], 0, w_ref, b_ref, recv, node, sender)
         tables_into(ends[...], edges, pick, put)
         tables_into(cends[...], degree, cpick, cput)
 
-    hbm, vmem = pl.BlockSpec(memory_space=pltpu.HBM), pl.BlockSpec(memory_space=pltpu.VMEM)
-    prepared = [
-        ((table_rows, features), I32), (weights.shape, BF16), (biases.shape, F32), (fine, BF16),
-        ((edges, size, size), BF16), ((edges, size, size), BF16),
-        ((degree, size, size), BF16), ((degree, size, size), BF16),
-    ] + own_out
-    table, w, bias, cot, pick, put, coarse_pick, coarse_put, recv0, node0, sender0 = pl.pallas_call(
+    w, bias, cot, table, pick, put, coarse_pick, coarse_put, recv0, node0, sender0 = run_hbm(
         prepare,
-        out_shape=[jax.ShapeDtypeStruct(shape, dtype) for shape, dtype in prepared],
-        in_specs=[hbm] * len(inputs) + [vmem],
-        out_specs=[vmem] * len(prepared),
-        scratch_shapes=[pltpu.SMEM(a.shape, I32) for a in inputs[:4]]
-        + [pltpu.VMEM(a.shape, I32) for a in inputs[4:6]]
-        + [pltpu.SemaphoreType.DMA((len(inputs),))],
-        compiler_params=pltpu.CompilerParams(vmem_limit_bytes=12 * 2**20),
-        cost_estimate=pl.CostEstimate(flops=0, bytes_accessed=2**22, transcendentals=0),
-    )(*inputs, h0)
+        [
+            (weights.shape, BF16), (biases.shape, F32), (fine, BF16),
+            ((table_rows, features), I32),
+            ((edges, size, size), BF16), ((edges, size, size), BF16),
+            ((degree, size, size), BF16), ((degree, size, size), BF16),
+        ] + own_out,
+        inputs,
+        h0,
+        scratch=[pltpu.VMEM(a.shape, I32) for a in inputs[:6]] + [pltpu.SemaphoreType.DMA((len(inputs),))],
+    )
 
     slopes = [((edges,) + tile, BF16), (fine, BF16)]
     pool_out = [((size + COUNT_ROWS, features), BF16)] * slots
@@ -279,7 +289,7 @@
         start_ref[...] = (total[:size, :] / divisor[0:1, :]).astype(BF16)
 
     coarse_start, divisor = run(coarse_begin, [(tile, BF16), ((8, features), F32)], pool_sends[0], *pool_in)
-    coarse_halo = exchange([coarse_start] * rounds)
+    coarse_halo = exchange_same(coarse_start)
 
     def coarse_prepare(h_ref, w_ref, b_ref, recv, node, sender):
         own_into(h_ref[...], 1, w_ref, b_ref, recv, node, sender)
@@ -287,7 +297,7 @@
     recv1, node1, sender1 = run(coarse_prepare, [(tile, F32), (tile, F32), (tile, BF16)], coarse_start, w, bias)
 
     def coarse_layer(s_ref, g0, g1, h_ref, recv, node, sender, pick, w_ref, end_ref, slope_ref, node_slope_ref, send_scr, sum_scr):
-        senders_into(sender, (g0, g1), 1, w_ref, send_scr)
+        senders_into(sender, (g0, g1), 1, w_ref, send_scr, range(rounds))
         change = layer_forward(
             1, at_coarse, 1, s_ref, w_ref, recv, node, send_scr, pick, slope_ref, node_slope_ref, sum_scr
         )
@@ -299,18 +309,18 @@
         table, coarse_halo[0], coarse_halo[1], coarse_start, recv1, node1, sender1, coarse_pick, w,
         scratch=coarse_scratch,
     )
-    ends_in = spread([coarse_end] * slots)
+    ends_in = spread_same(coarse_end)
 
     def lift(s_ref, *refs):
         parts, first_ref = refs[:slots], refs[slots]
         middle_ref, out0, out1, lift_scr = refs[slots + 1 :]
         me = scalar(s_ref, at_me)
-        for mask in range(slots):
-            lift_scr[me ^ mask] = parts[mask][...]
+        for mask, part in zip(same_masks, parts):
+            lift_scr[me ^ mask] = part[...]
         for b in range(blocks):
             lifted = lift_scr[scalar(s_ref, at_pool + b)].astype(F32)
             middle_ref[b] = (first_ref[rows_of(b), :].astype(F32) + lifted).astype(BF16)
-        for r, out in enumerate((out0, out1)):
+        for r, out in zip(ORDER, (out0, out1)):
             out[...] = middle_ref[scalar(s_ref, r)]
 
     middle, *middle_sends = run(
@@ -360,7 +370,7 @@
 
     def pool_grads(s_ref, r0, r1, own_ref, grad_ref, *sends):
         grad_ref[...] = own_ref[...]
-        for r, arrived in enumerate((r0, r1)):
+        for r, arrived in zip(ORDER, (r0, r1)):
             at = scalar(s_ref, r)
             grad_ref[at] = grad_ref[at] + arrived[...].astype(F32)
         pooled_into(lambda b: grad_ref[b], s_ref, sends, False)
@@ -399,15 +409,15 @@
         out_ref[...] = (total / divisor_ref[0:1, :]).astype(BF16)
 
     (scaled,) = run(scale, [(tile, BF16)], coarse_grad, *coarse_returned, divisor)
-    scaled_in = spread([scaled] * slots)
+    scaled_in = spread_same(scaled)
 
     def first_back(s_ref, *refs):
         parts = refs[:slots]
         middle_ref, put, slope_ref, node_slope_ref, w_ref = refs[slots : slots + 5]
         grad_ref, r0, r1, d_node, d_recv, d_send, lift_scr, act_scr, acc_scr = refs[slots + 5 :]
         me = scalar(s_ref, at_me)
-        for mask in range(slots):
-            lift_scr[me ^ mask] = parts[mask][...]
+        for mask, part in zip(same_masks, parts):
+            lift_scr[me ^ mask] = part[...]
         for b in range(blocks):
             lifted = lift_scr[scalar(s_ref, at_pool + b)].astype(F32)
             grad_ref[rows_of(b), :] = middle_ref[b] + lifted
@@ -433,7 +443,7 @@
 
     def finish(s_ref, r0, r1, own_ref, out_ref):
         out_ref[...] = own_ref[...]
-        for r, arrived in enumerate((r0, r1)):
+        for r, arrived in zip(ORDER, (r0, r1)):
             at = scalar(s_ref, r)
             out_ref[at] = out_ref[at] + arrived[...].astype(F32)
 

time: 66.9 us -> 60.3 us (0.901)
  waiting for transfers between devices: 26.1 us -> 19.7 us
  local copies, waits for them, and re-layouts: 4.1 us -> 0 us
  starting transfers between devices: 26.1 us -> 29.1 us
  Pallas kernels: 9.56 us -> 10.6 us
    ppermute x24, waiting for transfers between devices: 26.1 us -> 19.7 us  [swapped(): lax.ppermute(value, axis, [(source, source ^ mask) for source in range(si...]
    unnamed x19 -> x0, local copies, waits for them, and re-layouts: 4.1 us -> none
    ppermute x24, starting transfers between devices: 26.1 us -> 29.1 us  [swapped(): lax.ppermute(value, axis, [(source, source ^ mask) for source in range(si...]
    pallas_call x1 -> x2, Pallas kernels: 1.25 us -> 2.92 us  [run_hbm(): pl.pallas_call(kernel, out_shape=[pltpu.VMEM(shape, dtype) for shape, dty...]
    pallas_call x15 -> x14, Pallas kernels: 8.31 us -> 7.7 us  [run(): pl.pallas_call(kernel, out_shape=[jax.ShapeDtypeStruct(shape, dtype) for...]
  transfers between devices with their start and end apart: 24 -> 24, of which waited for: 18 -> 19; matrix products, arithmetic and copies ran while one was open for 0% -> 0% of each run, Pallas kernels for 3% -> 5%
where the time goes in v3:
time: 60.3 us; the launch traced here: 60.2 us
  starting transfers between devices  29.1 us (48%)
  waiting for transfers between devices  19.7 us (33%)
  Pallas kernels  10.6 us (18%)
  between operations  0.77 us (1%)
    ppermute x24, starting transfers between devices, swapped(): lax.ppermute(value, axis, [(source, source ^ mask) for source in range(si...  29.1 us
    ppermute x24, waiting for transfers between devices, swapped(): lax.ppermute(value, axis, [(source, source ^ mask) for source in range(si...  19.7 us
    pallas_call x14, Pallas kernels, run(): pl.pallas_call(kernel, out_shape=[jax.ShapeDtypeStruct(shape, dtype) for...  7.7 us
    pallas_call x2, Pallas kernels, run_hbm(): pl.pallas_call(kernel, out_shape=[pltpu.VMEM(shape, dtype) for shape, dty...  2.92 us
  transfers between devices with their start and end apart: 24, of which 19 were waited for; matrix products, arithmetic and copies ran while one was open for 0% of the time, Pallas kernels for 5%

profile of v3, /device:TPU:0, one launch (start us, length us, event | category | flops | bytes accessed | tf_op | source)
XLA Modules:
  0.0 60.2 jit_solution(12431597691193179375)
XLA Ops:
  0.6 1.0 %shard_map.113 = (bf16[512,128]{1,0:T(8,128)(2,1)S(1)}, bf16[128,128]{1,0:T(8,128)(2,1)S(1)}, bf16[128,128]{1,0:T(8,128)(2,1)S(1)}) custom-call(s32[1,2]{1,0:T(1,128)} %bitcast.19, bf16[512,128]{1,0:T(8,128)(2,1)} %nodes_in.1), custom_call_target="tpu_custom_call" | custom-call | bytes 1048576 | tf_op jit(solution)/shard_map/pallas_call | solution.py:50
  1.7 4.1 %collective-permute-start = (bf16[128,128]{1,0:T(8,128)(2,1)S(1)}, bf16[128,128]{1,0:T(8,128)(2,1)S(1)}, u32[]{:S(2)}, u32[]{:S(2)}) collective-permute-start(bf16[128,128]{1,0:T(8,128)(2,1)S(1)} %get-tuple-element.59), channel_id=1, source_target_pairs={{0,8},{4,12},{8,0},{12,4},{1,9},{5,13},{9,1},{13,5},{2,10},{6,14},... | collective-permute-start | bytes 98312 | tf_op jit(solution)/shard_map/ppermute | solution.py:18
  5.8 1.6 %collective-permute-start.1 = (bf16[128,128]{1,0:T(8,128)(2,1)S(1)}, bf16[128,128]{1,0:T(8,128)(2,1)S(1)}, u32[]{:S(2)}, u32[]{:S(2)}) collective-permute-start(bf16[128,128]{1,0:T(8,128)(2,1)S(1)} %get-tuple-element.60), channel_id=1, source_target_pairs={{0,4},{4,0},{8,12},{12,8},{1,5},{5,1},{9,13},{13,9},{2,6},{6,2},{1... | collective-permute-start | bytes 98312 | tf_op jit(solution)/shard_map/ppermute | solution.py:18
  7.4 1.9 %shard_map.114 = (bf16[3,6,128,128]{3,2,1,0:T(8,128)(2,1)S(1)}, f32[3,2,128]{2,1,0:T(2,128)S(1)}, bf16[512,128]{1,0:T(8,128)(2,1)S(1)}, s32[32,128]{1,0:T(8,128)...) custom-call(s32[1,2]{1,0:T(1,128)} %bitcast.20, ...), custom_call_target="tpu_custom_call" | custom-call | bytes 1048576 | tf_op jit(solution)/shard_map/pallas_call | solution.py:50
  9.2 0.0 collective-permute-done.g0
  9.2 0.5 collective-permute-done.1.g1
  9.7 1.1 %shard_map.115 = (bf16[512,128]{1,0:T(8,128)(2,1)S(1)}, bf16[16,128,128]{2,1,0:T(8,128)(2,1)S(1)}, bf16[512,128]{1,0:T(8,128)(2,1)S(1)}, bf16[144,128]{1,0:T(8,1...) custom-call(s32[32,128]{1,0:T(8,128)S(1)} %get-tuple-element.58.s_ref, ...), custom_call_target="tpu_custom_call" | custom-call | bytes 1048576 | tf_op jit(solution)/shard_map/pallas_call | solution.py:38
  10.8 0.1 collective-permute-start.2
  10.9 1.6 %collective-permute-start.3 = (bf16[144,128]{1,0:T(8,128)(2,1)S(1)}, bf16[144,128]{1,0:T(8,128)(2,1)S(1)}, u32[]{:S(2)}, u32[]{:S(2)}) collective-permute-start(bf16[144,128]{1,0:T(8,128)(2,1)S(1)} %get-tuple-element.68), channel_id=1, source_target_pairs={{0,2},{1,3},{2,0},{3,1},{4,6},{5,7},{6,4},{7,5},{8,10},{9,11},{10,... | collective-permute-start | bytes 110600 | tf_op jit(solution)/shard_map/ppermute | solution.py:18
  12.5 0.3 collective-permute-start.4
  12.7 1.9 %collective-permute-done.2.refs_1_ = bf16[144,128]{1,0:T(8,128)(2,1)S(1)} collective-permute-done((bf16[144,128]{1,0:T(8,128)(2,1)S(1)}, bf16[144,128]{1,0:T(8,128)(2,1)S(1)}, u32[]{:S(2)}, u32[]{:S(2)}) %collective-permute-start.2) | collective-permute-done | bytes 36896 | tf_op jit(solution)/shard_map/ppermute | solution.py:18
  14.6 0.4 collective-permute-done.3.refs_2_
  15.1 0.0 collective-permute-done.4.refs_3_
  15.1 1.1 %collective-permute-start.6 = (bf16[128,128]{1,0:T(8,128)(2,1)S(1)}, bf16[128,128]{1,0:T(8,128)(2,1)S(1)}, u32[]{:S(2)}, u32[]{:S(2)}) collective-permute-start(bf16[128,128]{1,0:T(8,128)(2,1)S(1)} %get-tuple-element.70.h_ref), channel_id=1, source_target_pairs={{0,8},{4,12},{8,0},{12,4},{1,9},{5,13},{9,1},{13,5},{2,10},{6,14},... | collective-permute-start | bytes 98312 | tf_op jit(solution)/shard_map/ppermute | solution.py:18
  16.2 1.6 %collective-permute-start.5 = (bf16[128,128]{1,0:T(8,128)(2,1)S(1)}, bf16[128,128]{1,0:T(8,128)(2,1)S(1)}, u32[]{:S(2)}, u32[]{:S(2)}) collective-permute-start(bf16[128,128]{1,0:T(8,128)(2,1)S(1)} %get-tuple-element.70.h_ref), channel_id=1, source_target_pairs={{0,4},{4,0},{8,12},{12,8},{1,5},{5,1},{9,13},{13,9},{2,6},{6,2},{1... | collective-permute-start | bytes 98312 | tf_op jit(solution)/shard_map/ppermute | solution.py:18
  17.9 0.2 shard_map.117
  18.0 2.0 %collective-permute-done.6.g1 = bf16[128,128]{1,0:T(8,128)(2,1)S(1)} collective-permute-done((bf16[128,128]{1,0:T(8,128)(2,1)S(1)}, bf16[128,128]{1,0:T(8,128)(2,1)S(1)}, u32[]{:S(2)}, u32[]{:S(2)}) %collective-permute-start.6) | collective-permute-done | bytes 32800 | tf_op jit(solution)/shard_map/ppermute | solution.py:18
  20.0 0.3 collective-permute-done.5.g0
  20.3 0.8 %shard_map.118 = (bf16[128,128]{1,0:T(8,128)(2,1)S(1)}, bf16[4,128,128]{2,1,0:T(8,128)(2,1)S(1)}, bf16[128,128]{1,0:T(8,128)(2,1)S(1)}) custom-call(s32[32,128]{1,0:T(8,128)S(1)} %get-tuple-element.58.s_ref, bf16[128,128]{1,0:T(8,128)(2,1)S(1)} %collective-permute-done.5.g0, bf16[128,128]{1,0:T(8,128)(2,1)S(1)} %collective-permute-done.6.g1, ...), custom_call_target="tpu_custom_call" | custom-call | bytes 1048576 | tf_op jit(solution)/shard_map/pallas_call | solution.py:38
  21.1 0.1 collective-permute-start.9
  21.2 1.7 %collective-permute-start.8 = (bf16[128,128]{1,0:T(8,128)(2,1)S(1)}, bf16[128,128]{1,0:T(8,128)(2,1)S(1)}, u32[]{:S(2)}, u32[]{:S(2)}) collective-permute-start(bf16[128,128]{1,0:T(8,128)(2,1)S(1)} %get-tuple-element.76.refs_0_), channel_id=1, source_target_pairs={{0,2},{1,3},{2,0},{3,1},{4,6},{5,7},{6,4},{7,5},{8,10},{9,11},{10,... | collective-permute-start | bytes 98312 | tf_op jit(solution)/shard_map/ppermute | solution.py:18
  22.9 0.1 collective-permute-start.7
  23.0 1.6 %collective-permute-done.9.refs_3_ = bf16[128,128]{1,0:T(8,128)(2,1)S(1)} collective-permute-done((bf16[128,128]{1,0:T(8,128)(2,1)S(1)}, bf16[128,128]{1,0:T(8,128)(2,1)S(1)}, u32[]{:S(2)}, u32[]{:S(2)}) %collective-permute-start.9) | collective-permute-done | bytes 32800 | tf_op jit(solution)/shard_map/ppermute | solution.py:18
  24.6 0.6 collective-permute-done.8.refs_2_
  25.2 0.0 collective-permute-done.7.refs_1_
  25.2 0.1 shard_map.119
  25.3 1.7 %collective-permute-start.10 = (bf16[128,128]{1,0:T(8,128)(2,1)S(1)}, bf16[128,128]{1,0:T(8,128)(2,1)S(1)}, u32[]{:S(2)}, u32[]{:S(2)}) collective-permute-start(bf16[128,128]{1,0:T(8,128)(2,1)S(1)} %get-tuple-element.78), channel_id=1, source_target_pairs={{0,8},{4,12},{8,0},{12,4},{1,9},{5,13},{9,1},{13,5},{2,10},{6,14},... | collective-permute-start | bytes 98312 | tf_op jit(solution)/shard_map/ppermute | solution.py:18
  27.0 1.6 %collective-permute-start.11 = (bf16[128,128]{1,0:T(8,128)(2,1)S(1)}, bf16[128,128]{1,0:T(8,128)(2,1)S(1)}, u32[]{:S(2)}, u32[]{:S(2)}) collective-permute-start(bf16[128,128]{1,0:T(8,128)(2,1)S(1)} %get-tuple-element.79), channel_id=1, source_target_pairs={{0,4},{4,0},{8,12},{12,8},{1,5},{5,1},{9,13},{13,9},{2,6},{6,2},{1... | collective-permute-start | bytes 98312 | tf_op jit(solution)/shard_map/ppermute | solution.py:18
  28.6 0.2 shard_map.120
  28.8 1.4 %collective-permute-done.10.g0 = bf16[128,128]{1,0:T(8,128)(2,1)S(1)} collective-permute-done((bf16[128,128]{1,0:T(8,128)(2,1)S(1)}, bf16[128,128]{1,0:T(8,128)(2,1)S(1)}, u32[]{:S(2)}, u32[]{:S(2)}) %collective-permute-start.10) | collective-permute-done | bytes 32800 | tf_op jit(solution)/shard_map/ppermute | solution.py:18
  30.2 0.7 %collective-permute-done.11.g1 = bf16[128,128]{1,0:T(8,128)(2,1)S(1)} collective-permute-done((bf16[128,128]{1,0:T(8,128)(2,1)S(1)}, bf16[128,128]{1,0:T(8,128)(2,1)S(1)}, u32[]{:S(2)}, u32[]{:S(2)}) %collective-permute-start.11) | collective-permute-done | bytes 32800 | tf_op jit(solution)/shard_map/ppermute | solution.py:18
  30.9 2.2 %shard_map.121 = (bf16[512,128]{1,0:T(8,128)(2,1)}, bf16[128,128]{1,0:T(8,128)(2,1)S(1)}, bf16[128,128]{1,0:T(8,128)(2,1)S(1)}, bf16[512,128]{1,0:T(8,128)(2,1)S...) custom-call(s32[32,128]{1,0:T(8,128)S(1)} %get-tuple-element.58.s_ref, ...), custom_call_target="tpu_custom_call" | custom-call | bytes 1048576 | tf_op jit(solution)/shard_map/pallas_call | solution.py:38
  33.1 1.2 %collective-permute-start.12 = (bf16[128,128]{1,0:T(8,128)(2,1)S(1)}, bf16[128,128]{1,0:T(8,128)(2,1)S(1)}, u32[]{:S(2)}, u32[]{:S(2)}) collective-permute-start(bf16[128,128]{1,0:T(8,128)(2,1)S(1)} %get-tuple-element.87), channel_id=1, source_target_pairs={{0,8},{4,12},{8,0},{12,4},{1,9},{5,13},{9,1},{13,5},{2,10},{6,14},... | collective-permute-start | bytes 98312 | tf_op jit(solution)/shard_map/ppermute | solution.py:18
  34.3 1.9 %collective-permute-start.13 = (bf16[128,128]{1,0:T(8,128)(2,1)S(1)}, bf16[128,128]{1,0:T(8,128)(2,1)S(1)}, u32[]{:S(2)}, u32[]{:S(2)}) collective-permute-start(bf16[128,128]{1,0:T(8,128)(2,1)S(1)} %get-tuple-element.88), channel_id=1, source_target_pairs={{0,4},{4,0},{8,12},{12,8},{1,5},{5,1},{9,13},{13,9},{2,6},{6,2},{1... | collective-permute-start | bytes 98312 | tf_op jit(solution)/shard_map/ppermute | solution.py:18
  36.2 0.3 shard_map.122
  36.5 1.4 %collective-permute-done.12.r0 = bf16[128,128]{1,0:T(8,128)(2,1)S(1)} collective-permute-done((bf16[128,128]{1,0:T(8,128)(2,1)S(1)}, bf16[128,128]{1,0:T(8,128)(2,1)S(1)}, u32[]{:S(2)}, u32[]{:S(2)}) %collective-permute-start.12) | collective-permute-done | bytes 32800 | tf_op jit(solution)/shard_map/ppermute | solution.py:18
  37.9 0.4 collective-permute-done.13.r1
  38.3 0.1 shard_map.123
  38.4 0.1 collective-permute-start.14
  38.5 1.8 %collective-permute-start.15 = (bf16[128,128]{1,0:T(8,128)(2,1)S(1)}, bf16[128,128]{1,0:T(8,128)(2,1)S(1)}, u32[]{:S(2)}, u32[]{:S(2)}) collective-permute-start(bf16[128,128]{1,0:T(8,128)(2,1)S(1)} %get-tuple-element.94), channel_id=1, source_target_pairs={{0,2},{1,3},{2,0},{3,1},{4,6},{5,7},{6,4},{7,5},{8,10},{9,11},{10,... | collective-permute-start | bytes 98312 | tf_op jit(solution)/shard_map/ppermute | solution.py:18
  40.2 0.1 collective-permute-start.16
  40.3 1.6 %collective-permute-done.14.refs_1_ = bf16[128,128]{1,0:T(8,128)(2,1)S(1)} collective-permute-done((bf16[128,128]{1,0:T(8,128)(2,1)S(1)}, bf16[128,128]{1,0:T(8,128)(2,1)S(1)}, u32[]{:S(2)}, u32[]{:S(2)}) %collective-permute-start.14) | collective-permute-done | bytes 32800 | tf_op jit(solution)/shard_map/ppermute | solution.py:18
  41.9 0.6 collective-permute-done.15.refs_2_
  42.5 0.0 collective-permute-done.16.refs_3_
  42.5 0.8 %shard_map.124 = (f32[128,128]{1,0:T(8,128)S(1)}, bf16[128,128]{1,0:T(8,128)(2,1)S(1)}, bf16[128,128]{1,0:T(8,128)(2,1)S(1)}) custom-call(s32[32,128]{1,0:T(8,128)S(1)} %get-tuple-element.58.s_ref, bf16[128,128]{1,0:T(8,128)(2,1)S(1)} %get-tuple-element.92.refs_0_, bf16[128,128]{1,0:T(8,128)(2,1)S(1)} %collective-permute-done.14.refs_1_, ...), custom_call_target="tpu_custom_call" | custom-call | bytes 1048576 | tf_op jit(solution)/shard_map/pallas_call | solution.py:38
  43.4 1.7 %collective-permute-start.17 = (bf16[128,128]{1,0:T(8,128)(2,1)S(1)}, bf16[128,128]{1,0:T(8,128)(2,1)S(1)}, u32[]{:S(2)}, u32[]{:S(2)}) collective-permute-start(bf16[128,128]{1,0:T(8,128)(2,1)S(1)} %get-tuple-element.100), channel_id=1, source_target_pairs={{0,8},{4,12},{8,0},{12,4},{1,9},{5,13},{9,1},{13,5},{2,10},{6,14},... | collective-permute-start | bytes 98312 | tf_op jit(solution)/shard_map/ppermute | solution.py:18
  45.1 1.6 %collective-permute-start.18 = (bf16[128,128]{1,0:T(8,128)(2,1)S(1)}, bf16[128,128]{1,0:T(8,128)(2,1)S(1)}, u32[]{:S(2)}, u32[]{:S(2)}) collective-permute-start(bf16[128,128]{1,0:T(8,128)(2,1)S(1)} %get-tuple-element.101), channel_id=1, source_target_pairs={{0,4},{4,0},{8,12},{12,8},{1,5},{5,1},{9,13},{13,9},{2,6},{6,2},{1... | collective-permute-start | bytes 98312 | tf_op jit(solution)/shard_map/ppermute | solution.py:18
  46.7 1.6 %collective-permute-done.17.r0 = bf16[128,128]{1,0:T(8,128)(2,1)S(1)} collective-permute-done((bf16[128,128]{1,0:T(8,128)(2,1)S(1)}, bf16[128,128]{1,0:T(8,128)(2,1)S(1)}, u32[]{:S(2)}, u32[]{:S(2)}) %collective-permute-start.17) | collective-permute-done | bytes 32800 | tf_op jit(solution)/shard_map/ppermute | solution.py:18
  48.3 0.7 %collective-permute-done.18.r1 = bf16[128,128]{1,0:T(8,128)(2,1)S(1)} collective-permute-done((bf16[128,128]{1,0:T(8,128)(2,1)S(1)}, bf16[128,128]{1,0:T(8,128)(2,1)S(1)}, u32[]{:S(2)}, u32[]{:S(2)}) %collective-permute-start.18) | collective-permute-done | bytes 32800 | tf_op jit(solution)/shard_map/ppermute | solution.py:18
  49.0 0.1 collective-permute-start.21
  49.1 1.6 %collective-permute-start.20 = (bf16[128,128]{1,0:T(8,128)(2,1)S(1)}, bf16[128,128]{1,0:T(8,128)(2,1)S(1)}, u32[]{:S(2)}, u32[]{:S(2)}) collective-permute-start(bf16[128,128]{1,0:T(8,128)(2,1)S(1)} %shard_map.125.refs_0_), channel_id=1, source_target_pairs={{0,2},{1,3},{2,0},{3,1},{4,6},{5,7},{6,4},{7,5},{8,10},{9,11},{10,... | collective-permute-start | bytes 98312 | tf_op jit(solution)/shard_map/ppermute | solution.py:18
  50.7 0.3 collective-permute-start.19
  51.0 1.8 %collective-permute-done.21.refs_3_ = bf16[128,128]{1,0:T(8,128)(2,1)S(1)} collective-permute-done((bf16[128,128]{1,0:T(8,128)(2,1)S(1)}, bf16[128,128]{1,0:T(8,128)(2,1)S(1)}, u32[]{:S(2)}, u32[]{:S(2)}) %collective-permute-start.21) | collective-permute-done | bytes 32800 | tf_op jit(solution)/shard_map/ppermute | solution.py:18
  52.7 0.4 collective-permute-done.20.refs_2_
  53.1 0.0 collective-permute-done.19.refs_1_
  53.1 0.9 %shard_map.126 = (f32[512,128]{1,0:T(8,128)S(1)}, bf16[128,128]{1,0:T(8,128)(2,1)S(1)}, bf16[128,128]{1,0:T(8,128)(2,1)S(1)}, bf16[512,128]{1,0:T(8,128)(2,1)S(1...) custom-call(s32[32,128]{1,0:T(8,128)S(1)} %get-tuple-element.58.s_ref, ...), custom_call_target="tpu_custom_call" | custom-call | bytes 1048576 | tf_op jit(solution)/shard_map/pallas_call | solution.py:38
  54.0 1.5 %collective-permute-start.22 = (bf16[128,128]{1,0:T(8,128)(2,1)S(1)}, bf16[128,128]{1,0:T(8,128)(2,1)S(1)}, u32[]{:S(2)}, u32[]{:S(2)}) collective-permute-start(bf16[128,128]{1,0:T(8,128)(2,1)S(1)} %get-tuple-element.106), channel_id=1, source_target_pairs={{0,8},{4,12},{8,0},{12,4},{1,9},{5,13},{9,1},{13,5},{2,10},{6,14},... | collective-permute-start | bytes 98312 | tf_op jit(solution)/shard_map/ppermute | solution.py:18
  55.5 1.7 %collective-permute-start.23 = (bf16[128,128]{1,0:T(8,128)(2,1)S(1)}, bf16[128,128]{1,0:T(8,128)(2,1)S(1)}, u32[]{:S(2)}, u32[]{:S(2)}) collective-permute-start(bf16[128,128]{1,0:T(8,128)(2,1)S(1)} %get-tuple-element.107), channel_id=1, source_target_pairs={{0,4},{4,0},{8,12},{12,8},{1,5},{5,1},{9,13},{13,9},{2,6},{6,2},{1... | collective-permute-start | bytes 98312 | tf_op jit(solution)/shard_map/ppermute | solution.py:18
  57.2 0.3 shard_map.127
  57.5 1.5 %collective-permute-done.22.r0 = bf16[128,128]{1,0:T(8,128)(2,1)S(1)} collective-permute-done((bf16[128,128]{1,0:T(8,128)(2,1)S(1)}, bf16[128,128]{1,0:T(8,128)(2,1)S(1)}, u32[]{:S(2)}, u32[]{:S(2)}) %collective-permute-start.22) | collective-permute-done | bytes 32800 | tf_op jit(solution)/shard_map/ppermute | solution.py:18
  59.0 0.5 collective-permute-done.23.r1
  59.4 0.7 %shard_map.128 = f32[4,128,128]{2,1,0:T(8,128)} custom-call(s32[32,128]{1,0:T(8,128)S(1)} %get-tuple-element.58.s_ref, bf16[128,128]{1,0:T(8,128)(2,1)S(1)} %collective-permute-done.22.r0, bf16[128,128]{1,0:T(8,128)(2,1)S(1)} %collective-permute-done.23.r1, f32[4,128,128]{2,1,0:T(8,128)S(1)} %bitcast.10), custom_call_target="tpu_custom_call" | custom-call | bytes 1048576 | tf_op jit(solution)/shard_map/pallas_call | solution.py:38
  (2 shorter events, 0.0 us)
Async XLA Ops:
  1.7 7.6 %collective-permute-start = (bf16[128,128]{1,0:T(8,128)(2,1)S(1)}, bf16[128,128]{1,0:T(8,128)(2,1)S(1)}, u32[]{:S(2)}, u32[]{:S(2)}) collective-permute-start(bf16[128,128]{1,0:T(8,128)(2,1)S(1)} %get-tuple-element.59), channel_id=1, source_target_pairs={{0,8},{4,12},{8,0},{12,4},{1,9},{5,13},{9,1},{13,5},{2,10},{6,14},... | collective-permute-start | bytes 98312 | tf_op jit(solution)/shard_map/ppermute | solution.py:18
  5.8 3.9 %collective-permute-start.1 = (bf16[128,128]{1,0:T(8,128)(2,1)S(1)}, bf16[128,128]{1,0:T(8,128)(2,1)S(1)}, u32[]{:S(2)}, u32[]{:S(2)}) collective-permute-start(bf16[128,128]{1,0:T(8,128)(2,1)S(1)} %get-tuple-element.60), channel_id=1, source_target_pairs={{0,4},{4,0},{8,12},{12,8},{1,5},{5,1},{9,13},{13,9},{2,6},{6,2},{1... | collective-permute-start | bytes 98312 | tf_op jit(solution)/shard_map/ppermute | solution.py:18
  10.8 3.8 %collective-permute-start.2 = (bf16[144,128]{1,0:T(8,128)(2,1)S(1)}, bf16[144,128]{1,0:T(8,128)(2,1)S(1)}, u32[]{:S(2)}, u32[]{:S(2)}) collective-permute-start(bf16[144,128]{1,0:T(8,128)(2,1)S(1)} %get-tuple-element.67), channel_id=1, source_target_pairs={{0,3},{1,2},{2,1},{3,0},{4,7},{5,6},{6,5},{7,4},{8,11},{9,10},{10,... | collective-permute-start | bytes 110600 | tf_op jit(solution)/shard_map/ppermute | solution.py:18
  10.9 4.2 %collective-permute-start.3 = (bf16[144,128]{1,0:T(8,128)(2,1)S(1)}, bf16[144,128]{1,0:T(8,128)(2,1)S(1)}, u32[]{:S(2)}, u32[]{:S(2)}) collective-permute-start(bf16[144,128]{1,0:T(8,128)(2,1)S(1)} %get-tuple-element.68), channel_id=1, source_target_pairs={{0,2},{1,3},{2,0},{3,1},{4,6},{5,7},{6,4},{7,5},{8,10},{9,11},{10,... | collective-permute-start | bytes 110600 | tf_op jit(solution)/shard_map/ppermute | solution.py:18
  12.5 2.6 %collective-permute-start.4 = (bf16[144,128]{1,0:T(8,128)(2,1)S(1)}, bf16[144,128]{1,0:T(8,128)(2,1)S(1)}, u32[]{:S(2)}, u32[]{:S(2)}) collective-permute-start(bf16[144,128]{1,0:T(8,128)(2,1)S(1)} %get-tuple-element.69), channel_id=1, source_target_pairs={{0,1},{1,0},{2,3},{3,2},{4,5},{5,4},{6,7},{7,6},{8,9},{9,8},{10,11... | collective-permute-start | bytes 110600 | tf_op jit(solution)/shard_map/ppermute | solution.py:18
  15.1 4.9 %collective-permute-start.6 = (bf16[128,128]{1,0:T(8,128)(2,1)S(1)}, bf16[128,128]{1,0:T(8,128)(2,1)S(1)}, u32[]{:S(2)}, u32[]{:S(2)}) collective-permute-start(bf16[128,128]{1,0:T(8,128)(2,1)S(1)} %get-tuple-element.70.h_ref), channel_id=1, source_target_pairs={{0,8},{4,12},{8,0},{12,4},{1,9},{5,13},{9,1},{13,5},{2,10},{6,14},... | collective-permute-start | bytes 98312 | tf_op jit(solution)/shard_map/ppermute | solution.py:18
  16.2 4.1 %collective-permute-start.5 = (bf16[128,128]{1,0:T(8,128)(2,1)S(1)}, bf16[128,128]{1,0:T(8,128)(2,1)S(1)}, u32[]{:S(2)}, u32[]{:S(2)}) collective-permute-start(bf16[128,128]{1,0:T(8,128)(2,1)S(1)} %get-tuple-element.70.h_ref), channel_id=1, source_target_pairs={{0,4},{4,0},{8,12},{12,8},{1,5},{5,1},{9,13},{13,9},{2,6},{6,2},{1... | collective-permute-start | bytes 98312 | tf_op jit(solution)/shard_map/ppermute | solution.py:18
  21.1 3.5 %collective-permute-start.9 = (bf16[128,128]{1,0:T(8,128)(2,1)S(1)}, bf16[128,128]{1,0:T(8,128)(2,1)S(1)}, u32[]{:S(2)}, u32[]{:S(2)}) collective-permute-start(bf16[128,128]{1,0:T(8,128)(2,1)S(1)} %get-tuple-element.76.refs_0_), channel_id=1, source_target_pairs={{0,3},{1,2},{2,1},{3,0},{4,7},{5,6},{6,5},{7,4},{8,11},{9,10},{10,... | collective-permute-start | bytes 98312 | tf_op jit(solution)/shard_map/ppermute | solution.py:18
  21.2 4.0 %collective-permute-start.8 = (bf16[128,128]{1,0:T(8,128)(2,1)S(1)}, bf16[128,128]{1,0:T(8,128)(2,1)S(1)}, u32[]{:S(2)}, u32[]{:S(2)}) collective-permute-start(bf16[128,128]{1,0:T(8,128)(2,1)S(1)} %get-tuple-element.76.refs_0_), channel_id=1, source_target_pairs={{0,2},{1,3},{2,0},{3,1},{4,6},{5,7},{6,4},{7,5},{8,10},{9,11},{10,... | collective-permute-start | bytes 98312 | tf_op jit(solution)/shard_map/ppermute | solution.py:18
  22.9 2.3 %collective-permute-start.7 = (bf16[128,128]{1,0:T(8,128)(2,1)S(1)}, bf16[128,128]{1,0:T(8,128)(2,1)S(1)}, u32[]{:S(2)}, u32[]{:S(2)}) collective-permute-start(bf16[128,128]{1,0:T(8,128)(2,1)S(1)} %get-tuple-element.76.refs_0_), channel_id=1, source_target_pairs={{0,1},{1,0},{2,3},{3,2},{4,5},{5,4},{6,7},{7,6},{8,9},{9,8},{10,11... | collective-permute-start | bytes 98312 | tf_op jit(solution)/shard_map/ppermute | solution.py:18
  25.3 4.9 %collective-permute-start.10 = (bf16[128,128]{1,0:T(8,128)(2,1)S(1)}, bf16[128,128]{1,0:T(8,128)(2,1)S(1)}, u32[]{:S(2)}, u32[]{:S(2)}) collective-permute-start(bf16[128,128]{1,0:T(8,128)(2,1)S(1)} %get-tuple-element.78), channel_id=1, source_target_pairs={{0,8},{4,12},{8,0},{12,4},{1,9},{5,13},{9,1},{13,5},{2,10},{6,14},... | collective-permute-start | bytes 98312 | tf_op jit(solution)/shard_map/ppermute | solution.py:18
  27.0 3.9 %collective-permute-start.11 = (bf16[128,128]{1,0:T(8,128)(2,1)S(1)}, bf16[128,128]{1,0:T(8,128)(2,1)S(1)}, u32[]{:S(2)}, u32[]{:S(2)}) collective-permute-start(bf16[128,128]{1,0:T(8,128)(2,1)S(1)} %get-tuple-element.79), channel_id=1, source_target_pairs={{0,4},{4,0},{8,12},{12,8},{1,5},{5,1},{9,13},{13,9},{2,6},{6,2},{1... | collective-permute-start | bytes 98312 | tf_op jit(solution)/shard_map/ppermute | solution.py:18
  33.1 4.8 %collective-permute-start.12 = (bf16[128,128]{1,0:T(8,128)(2,1)S(1)}, bf16[128,128]{1,0:T(8,128)(2,1)S(1)}, u32[]{:S(2)}, u32[]{:S(2)}) collective-permute-start(bf16[128,128]{1,0:T(8,128)(2,1)S(1)} %get-tuple-element.87), channel_id=1, source_target_pairs={{0,8},{4,12},{8,0},{12,4},{1,9},{5,13},{9,1},{13,5},{2,10},{6,14},... | collective-permute-start | bytes 98312 | tf_op jit(solution)/shard_map/ppermute | solution.py:18
  34.3 3.9 %collective-permute-start.13 = (bf16[128,128]{1,0:T(8,128)(2,1)S(1)}, bf16[128,128]{1,0:T(8,128)(2,1)S(1)}, u32[]{:S(2)}, u32[]{:S(2)}) collective-permute-start(bf16[128,128]{1,0:T(8,128)(2,1)S(1)} %get-tuple-element.88), channel_id=1, source_target_pairs={{0,4},{4,0},{8,12},{12,8},{1,5},{5,1},{9,13},{13,9},{2,6},{6,2},{1... | collective-permute-start | bytes 98312 | tf_op jit(solution)/shard_map/ppermute | solution.py:18
  38.4 3.5 %collective-permute-start.14 = (bf16[128,128]{1,0:T(8,128)(2,1)S(1)}, bf16[128,128]{1,0:T(8,128)(2,1)S(1)}, u32[]{:S(2)}, u32[]{:S(2)}) collective-permute-start(bf16[128,128]{1,0:T(8,128)(2,1)S(1)} %get-tuple-element.93), channel_id=1, source_target_pairs={{0,3},{1,2},{2,1},{3,0},{4,7},{5,6},{6,5},{7,4},{8,11},{9,10},{10,... | collective-permute-start | bytes 98312 | tf_op jit(solution)/shard_map/ppermute | solution.py:18
  38.5 4.0 %collective-permute-start.15 = (bf16[128,128]{1,0:T(8,128)(2,1)S(1)}, bf16[128,128]{1,0:T(8,128)(2,1)S(1)}, u32[]{:S(2)}, u32[]{:S(2)}) collective-permute-start(bf16[128,128]{1,0:T(8,128)(2,1)S(1)} %get-tuple-element.94), channel_id=1, source_target_pairs={{0,2},{1,3},{2,0},{3,1},{4,6},{5,7},{6,4},{7,5},{8,10},{9,11},{10,... | collective-permute-start | bytes 98312 | tf_op jit(solution)/shard_map/ppermute | solution.py:18
  40.2 2.3 %collective-permute-start.16 = (bf16[128,128]{1,0:T(8,128)(2,1)S(1)}, bf16[128,128]{1,0:T(8,128)(2,1)S(1)}, u32[]{:S(2)}, u32[]{:S(2)}) collective-permute-start(bf16[128,128]{1,0:T(8,128)(2,1)S(1)} %get-tuple-element.95), channel_id=1, source_target_pairs={{0,1},{1,0},{2,3},{3,2},{4,5},{5,4},{6,7},{7,6},{8,9},{9,8},{10,11... | collective-permute-start | bytes 98312 | tf_op jit(solution)/shard_map/ppermute | solution.py:18
  43.4 4.9 %collective-permute-start.17 = (bf16[128,128]{1,0:T(8,128)(2,1)S(1)}, bf16[128,128]{1,0:T(8,128)(2,1)S(1)}, u32[]{:S(2)}, u32[]{:S(2)}) collective-permute-start(bf16[128,128]{1,0:T(8,128)(2,1)S(1)} %get-tuple-element.100), channel_id=1, source_target_pairs={{0,8},{4,12},{8,0},{12,4},{1,9},{5,13},{9,1},{13,5},{2,10},{6,14},... | collective-permute-start | bytes 98312 | tf_op jit(solution)/shard_map/ppermute | solution.py:18
  45.1 3.9 %collective-permute-start.18 = (bf16[128,128]{1,0:T(8,128)(2,1)S(1)}, bf16[128,128]{1,0:T(8,128)(2,1)S(1)}, u32[]{:S(2)}, u32[]{:S(2)}) collective-permute-start(bf16[128,128]{1,0:T(8,128)(2,1)S(1)} %get-tuple-element.101), channel_id=1, source_target_pairs={{0,4},{4,0},{8,12},{12,8},{1,5},{5,1},{9,13},{13,9},{2,6},{6,2},{1... | collective-permute-start | bytes 98312 | tf_op jit(solution)/shard_map/ppermute | solution.py:18
  49.0 3.7 %collective-permute-start.21 = (bf16[128,128]{1,0:T(8,128)(2,1)S(1)}, bf16[128,128]{1,0:T(8,128)(2,1)S(1)}, u32[]{:S(2)}, u32[]{:S(2)}) collective-permute-start(bf16[128,128]{1,0:T(8,128)(2,1)S(1)} %shard_map.125.refs_0_), channel_id=1, source_target_pairs={{0,3},{1,2},{2,1},{3,0},{4,7},{5,6},{6,5},{7,4},{8,11},{9,10},{10,... | collective-permute-start | bytes 98312 | tf_op jit(solution)/shard_map/ppermute | solution.py:18
  49.1 4.0 %collective-permute-start.20 = (bf16[128,128]{1,0:T(8,128)(2,1)S(1)}, bf16[128,128]{1,0:T(8,128)(2,1)S(1)}, u32[]{:S(2)}, u32[]{:S(2)}) collective-permute-start(bf16[128,128]{1,0:T(8,128)(2,1)S(1)} %shard_map.125.refs_0_), channel_id=1, source_target_pairs={{0,2},{1,3},{2,0},{3,1},{4,6},{5,7},{6,4},{7,5},{8,10},{9,11},{10,... | collective-permute-start | bytes 98312 | tf_op jit(solution)/shard_map/ppermute | solution.py:18
  50.7 2.5 %collective-permute-start.19 = (bf16[128,128]{1,0:T(8,128)(2,1)S(1)}, bf16[128,128]{1,0:T(8,128)(2,1)S(1)}, u32[]{:S(2)}, u32[]{:S(2)}) collective-permute-start(bf16[128,128]{1,0:T(8,128)(2,1)S(1)} %shard_map.125.refs_0_), channel_id=1, source_target_pairs={{0,1},{1,0},{2,3},{3,2},{4,5},{5,4},{6,7},{7,6},{8,9},{9,8},{10,11... | collective-permute-start | bytes 98312 | tf_op jit(solution)/shard_map/ppermute | solution.py:18
  54.0 4.9 %collective-permute-start.22 = (bf16[128,128]{1,0:T(8,128)(2,1)S(1)}, bf16[128,128]{1,0:T(8,128)(2,1)S(1)}, u32[]{:S(2)}, u32[]{:S(2)}) collective-permute-start(bf16[128,128]{1,0:T(8,128)(2,1)S(1)} %get-tuple-element.106), channel_id=1, source_target_pairs={{0,8},{4,12},{8,0},{12,4},{1,9},{5,13},{9,1},{13,5},{2,10},{6,14},... | collective-permute-start | bytes 98312 | tf_op jit(solution)/shard_map/ppermute | solution.py:18
  55.5 3.9 %collective-permute-start.23 = (bf16[128,128]{1,0:T(8,128)(2,1)S(1)}, bf16[128,128]{1,0:T(8,128)(2,1)S(1)}, u32[]{:S(2)}, u32[]{:S(2)}) collective-permute-start(bf16[128,128]{1,0:T(8,128)(2,1)S(1)} %get-tuple-element.107), channel_id=1, source_target_pairs={{0,4},{4,0},{8,12},{12,8},{1,5},{5,1},{9,13},{13,9},{2,6},{6,2},{1... | collective-permute-start | bytes 98312 | tf_op jit(solution)/shard_map/ppermute | solution.py:18

commit v4 on v3

v4 whole, which is shorter than its diff:
```python
import jax
import jax.numpy as jnp
from jax import lax
from jax.experimental import pallas as pl
from jax.experimental.pallas import tpu as pltpu
from jax.sharding import PartitionSpec as P

F32 = jnp.float32
BF16 = jnp.bfloat16
I32 = jnp.int32
TAIL = 16
GROUP_AXES = ("pair", "sub")
ORDER = (1, 0)


def swapped(value, axis, mask):
    size = lax.axis_size(axis)
    return lax.ppermute(value, axis, [(source, source ^ mask) for source in range(size)])


def mm(a, b):
    return jnp.dot(a, b, preferred_element_type=F32)


def mm_t(a, b):
    return lax.dot_general(a, b, (((1,), (1,)), ((), ())), preferred_element_type=F32)


def sigmoid(x):
    return 0.5 * jnp.tanh(0.5 * x) + 0.5


def scalar(table, index):
    return table[index : index + 1, :][0, 0]


def run(kernel, outs, *arrays, scratch=(), flops=0):
    return pl.pallas_call(
        kernel,
        out_shape=[jax.ShapeDtypeStruct(shape, dtype) for shape, dtype in outs],
        in_specs=[pl.BlockSpec(memory_space=pltpu.VMEM)] * len(arrays),
        out_specs=[pl.BlockSpec(memory_space=pltpu.VMEM)] * len(outs),
        scratch_shapes=list(scratch),
        compiler_params=pltpu.CompilerParams(vmem_limit_bytes=12 * 2**20),
        cost_estimate=pl.CostEstimate(flops=flops, bytes_accessed=2**20, transcendentals=0),
    )(*arrays)


def run_hbm(kernel, outs, far, *near, scratch=()):
    return pl.pallas_call(
        kernel,
        out_shape=[pltpu.VMEM(shape, dtype) for shape, dtype in outs],
        in_specs=[pl.BlockSpec(memory_space=pltpu.HBM)] * len(far) + [pl.BlockSpec(memory_space=pltpu.VMEM)] * len(near),
        out_specs=[pl.BlockSpec(memory_space=pltpu.VMEM)] * len(outs),
        scratch_shapes=list(scratch),
        compiler_params=pltpu.CompilerParams(vmem_limit_bytes=12 * 2**20),
        cost_estimate=pl.CostEstimate(flops=0, bytes_accessed=2**20, transcendentals=0),
    )(*[pltpu.with_memory_space_constraint(array, pltpu.HBM) for array in far], *near)


def per_device(
    nodes,
    cotangent,
    send_blocks,
    neighbour_blocks,
    neighbour_nodes,
    pool_map,
    coarse_blocks,
    coarse_nodes,
    weights,
    biases,
):
    size, features = neighbour_nodes.shape[2], nodes.shape[1]
    blocks, degree = neighbour_blocks.shape
    xor_bits = (1, lax.axis_size("dom") // 2)
    rounds = len(xor_bits)
    slots = lax.axis_size(GROUP_AXES)
    pair_size, sub_size = lax.axis_size("pair"), lax.axis_size("sub")
    edges = blocks * degree
    far_size = rounds * size
    everyone = blocks + rounds
    tile = (size, features)
    fine = (blocks * size, features)
    tiles = (blocks,) + tile

    held = pair_size
    wide = (held * size, features)
    at_ends = TAIL // 2
    at_blocks = at_ends + degree
    at_near = rounds
    at_pool = at_near + edges
    at_pair = at_pool + blocks
    at_sub = at_pair + 1
    table_rows = -(-(at_sub + 1) // 8) * 8

    def exchange(pieces):
        return [swapped(piece, "dom", xor_bits[r]) for r, piece in zip(ORDER, pieces)]

    def exchange_same(piece):
        return [swapped(piece, "dom", bit) for bit in xor_bits]

    def reduced(pieces):
        arrived = [swapped(piece, "sub", mask) for mask, piece in enumerate(pieces) if mask > 0]
        (chip,) = run(add_parts, [(pieces[0].shape, BF16)], pieces[0], *arrived)
        return [chip] + [swapped(chip, "pair", mask) for mask in range(1, pair_size)]

    def add_parts(*refs):
        total = refs[0][...].astype(F32)
        for part in refs[1:-1]:
            total = total + part[...].astype(F32)
        refs[-1][...] = total.astype(BF16)

    def share(piece):
        return [piece] + [swapped(piece, "sub", mask) for mask in range(1, sub_size)]

    def rows_of(b):
        return pl.ds(b * size, size)

    def fetch(pairs, sems):
        copies = [pltpu.make_async_copy(source, target, sems.at[i]) for i, (source, target) in enumerate(pairs)]
        for copy in copies:
            copy.start()
        for copy in copies:
            copy.wait()

    def choose(send_in, nodes_in, h_ref, out0, out1, send_scr, sems):
        parts = [(nodes_in.at[rows_of(b)], h_ref.at[rows_of(b)]) for b in range(blocks)]
        fetch([(send_in, send_scr)] + parts, sems)
        for r, out in zip(ORDER, (out0, out1)):
            at = pl.multiple_of(send_scr[0:1, r : r + 1][0, 0] * size, size)
            out[...] = h_ref[pl.ds(at, size), :]

    sent = send_blocks.reshape(1, rounds)
    h0, *first_sends = run_hbm(
        choose,
        [(fine, BF16)] + [(tile, BF16)] * rounds,
        [sent, nodes],
        scratch=[pltpu.VMEM((1, rounds), I32), pltpu.SemaphoreType.DMA((1 + blocks,))],
    )
    halo = exchange(first_sends)

    def grids():
        return lax.broadcasted_iota(I32, (size, size), 0), lax.broadcasted_iota(I32, (size, size), 1)

    def own_into(state, layer, w_ref, b_ref, recv_ref, node_ref, sender_ref):
        recv_ref[...] = mm(state, w_ref[layer, 0]) + b_ref[layer, 0:1, :]
        node_ref[...] = mm(state, w_ref[layer, 3]) + b_ref[layer, 1:2, :]
        sender_ref[...] = mm(state, w_ref[layer, 1]).astype(BF16)

    def layer_forward(count, fold, pre_of, node, slope_ref, node_slope_ref, sum_scr):
        for b in range(count):
            total = None
            for e in range(degree):
                edge = b * degree + e
                pre = pre_of(b, e)
                gate = sigmoid(pre)
                active = pre * gate
                slope_ref[edge] = (gate + active * (1.0 - gate)).astype(BF16)
                total = active if total is None else total + active
            sum_scr[rows_of(b), :] = total.astype(BF16)
        hidden_pre = node[...] + mm(sum_scr[...], fold)
        gate = sigmoid(hidden_pre)
        hidden = hidden_pre * gate
        node_slope_ref[...] = (gate + hidden * (1.0 - gate)).astype(BF16)
        return hidden.astype(BF16)

    def senders_into(own, halos, layer, w_ref, send_scr):
        for r, g in zip(ORDER, halos):
            send_scr[blocks + r] = mm(g[...], w_ref[layer, 1]).astype(BF16)
        for b in range(blocks):
            send_scr[b] = own[rows_of(b), :]

    def fine_pre(s_ref, recv, pick, send_scr):
        def pre_of(b, e):
            edge = b * degree + e
            return recv[rows_of(b), :] + mm(pick[edge], send_scr[scalar(s_ref, at_near + edge)])

        return pre_of

    def node_backward(d_out, fold, node_slope_ref, d_node, act_scr):
        d_hidden = (d_out * node_slope_ref[...].astype(F32)).astype(BF16)
        d_node[...] = d_hidden
        act_scr[...] = mm_t(d_hidden, fold)

    def fine_backward(d_out, s_ref, fold, put_ref, slope_ref, node_slope_ref, d_node, d_recv, act_scr, acc_scr):
        node_backward(d_out, fold, node_slope_ref, d_node, act_scr)
        acc_scr[...] = jnp.zeros_like(acc_scr)
        for b in range(blocks):
            d_active = act_scr[rows_of(b), :]
            total = None
            for e in range(degree):
                edge = b * degree + e
                d_pre = d_active * slope_ref[edge].astype(F32)
                total = d_pre if total is None else total + d_pre
                near = scalar(s_ref, at_near + edge)
                acc_scr[near] = acc_scr[near] + mm(put_ref[edge], d_pre.astype(BF16))
            d_recv[rows_of(b), :] = total.astype(BF16)

    def halo_grads_into(outs, grads, layer, w_ref):
        for r, out in zip(ORDER, outs):
            own = jnp.concatenate([g[r * size : (r + 1) * size, :] for g in grads], axis=0)
            out[...] = mm_t(own.astype(BF16), w_ref[layer, 1]).astype(BF16)

    def own_back(grad, layer, w_ref, d_node, d_recv, d_send):
        return (
            grad
            + mm_t(d_recv, w_ref[layer, 0])
            + mm_t(d_node, w_ref[layer, 3])
            + mm_t(d_send.astype(BF16), w_ref[layer, 1])
        )

    def pooled_into(read, s_ref, out_refs, tail_ref):
        sub = scalar(s_ref, at_sub)
        rows = lax.broadcasted_iota(I32, (TAIL, features), 0)
        for sub_mask, out in enumerate(out_refs):
            tail = None if tail_ref is None else tail_ref[...]
            for q in range(held):
                slot = q * sub_size + (sub ^ sub_mask)
                total, count = None, None
                for b in range(blocks):
                    hit = (scalar(s_ref, at_pool + b) == slot).astype(F32)
                    part = read(b) * hit
                    total = part if total is None else total + part
                    count = hit if count is None else count + hit
                out[rows_of(q), :] = total.astype(BF16)
                if tail is not None:
                    tail = tail + jnp.where(rows == q, count, 0.0)
            if tail is not None:
                if sub_mask > 0:
                    tail = jnp.where(rows < at_ends, tail, 0.0)
                out[held * size :, :] = tail.astype(BF16)

    def lift_into(parts, s_ref, lift_scr):
        sub = scalar(s_ref, at_sub)
        for mask, part in enumerate(parts):
            for q in range(held):
                lift_scr[q * sub_size + (sub ^ mask)] = part[rows_of(q), :]

    inputs = [
        sent,
        neighbour_blocks,
        pool_map.reshape(1, blocks),
        coarse_blocks,
        neighbour_nodes.reshape(edges, size),
        coarse_nodes.reshape(degree, size),
        weights,
        biases,
        cotangent,
    ]
    own_out = [(fine, F32), (fine, F32), (fine, BF16)]

    def prepare(*refs):
        sources, h_ref = refs[: len(inputs)], refs[len(inputs)]
        ends, w_ref, b_ref, c_ref, s_ref, fold_ref, tail_ref, pick, recv, node, sender, *kept, sems = refs[len(inputs) + 1 :]
        send_scr, near_scr, pool_scr, coarse_scr, cends = kept
        fetch(list(zip(sources, kept[:4] + [ends, cends, w_ref, b_ref, c_ref])), sems)

        def put_row(index, ref, i, j):
            s_ref[index : index + 1, :] = jnp.broadcast_to(ref[i : i + 1, j : j + 1], (1, features))

        for r in range(rounds):
            put_row(r, send_scr, 0, r)
        for b in range(blocks):
            for e in range(degree):
                put_row(at_near + b * degree + e, near_scr, b, e)
            put_row(at_pool + b, pool_scr, 0, b)
        s_ref[at_pair : at_pair + 1, :] = jnp.full((1, features), lax.axis_index("pair"), I32)
        s_ref[at_sub : at_sub + 1, :] = jnp.full((1, features), lax.axis_index("sub"), I32)
        lanes = lax.broadcasted_iota(I32, (1, features), 1)
        listed = jnp.zeros((1, features), I32)
        for e in range(degree):
            listed = jnp.where(lanes == e, jnp.broadcast_to(coarse_scr[0:1, e : e + 1], (1, features)), listed)
        tail_ref[...] = jnp.zeros_like(tail_ref)
        tail_ref[at_ends : at_ends + degree, :] = cends[...].astype(F32)
        tail_ref[at_blocks : at_blocks + 1, :] = listed.astype(F32)
        own_into(h_ref[...], 0, w_ref, b_ref, recv, node, sender)
        columns = grids()[1]
        upright = jnp.transpose(ends[...])
        for edge in range(edges):
            pick[edge] = (columns == upright[:, edge : edge + 1]).astype(BF16)
        fold_ref[...] = (mm(w_ref[0, 2], w_ref[0, 4]) * (1.0 / degree)).astype(BF16)

    ends, w, bias, cot, table, fold0, tail, pick, recv0, node0, sender0 = run_hbm(
        prepare,
        [
            ((edges, size), I32), (weights.shape, BF16), (biases.shape, F32), (fine, BF16),
            ((table_rows, features), I32), (tile, BF16), ((TAIL, features), F32),
            ((edges, size, size), BF16),
        ] + own_out,
        inputs,
        h0,
        scratch=[pltpu.VMEM(a.shape, I32) for a in inputs[:4] + inputs[5:6]]
        + [pltpu.SemaphoreType.DMA((len(inputs),))],
    )

    slopes = [((edges,) + tile, BF16), (fine, BF16)]

    layer_scratch = [pltpu.VMEM((everyone,) + tile, BF16), pltpu.VMEM(fine, BF16)]

    def first_layer(s_ref, g0, g1, h_ref, recv, node, sender, pick, w_ref, fold_ref, tail_ref, *rest):
        first_ref, slope_ref, node_slope_ref, *sends, send_scr, sum_scr = rest
        senders_into(sender, (g0, g1), 0, w_ref, send_scr)
        pre_of = fine_pre(s_ref, recv, pick, send_scr)
        hidden = layer_forward(blocks, fold_ref[...], pre_of, node, slope_ref, node_slope_ref, sum_scr)
        first_ref[...] = (h_ref[...].astype(F32) + mm(hidden, w_ref[0, 5])).astype(BF16)
        pooled_into(lambda b: first_ref[rows_of(b), :].astype(F32), s_ref, sends, tail_ref)

    first, slope0, node_slope0, *pool_sends = run(
        first_layer,
        [(fine, BF16)] + slopes + [((held * size + TAIL, features), BF16)] * sub_size,
        table, halo[0], halo[1], h0, recv0, node0, sender0, pick, w, fold0, tail,
        scratch=layer_scratch,
    )

    pool_in = reduced(pool_sends)

    def coarse_begin(s_ref, *refs):
        parts, (start_ref, divisor_ref, tails_ref) = refs[:pair_size], refs[pair_size:]
        total = parts[0][...].astype(F32)
        for part in parts[1:]:
            total = total + part[...].astype(F32)
        divisor = jnp.maximum(total[held * size : held * size + at_ends, :], 1.0)
        divisor_ref[...] = divisor
        for q in range(held):
            start_ref[rows_of(q), :] = (total[q * size : (q + 1) * size, :] / divisor[q : q + 1, :]).astype(BF16)
        pair = scalar(s_ref, at_pair)
        for mask, part in enumerate(parts):
            tails_ref[pair ^ mask] = part[held * size :, :].astype(F32)

    coarse_start, divisor, tails = run(
        coarse_begin,
        [(wide, BF16), ((at_ends, features), F32), ((held, TAIL, features), F32)],
        table, *pool_in,
    )
    coarse_halo = exchange_same(coarse_start)

    def coarse_prepare(h_ref, w_ref, b_ref, tails_ref, ends, pre, node, fold_ref, far_pick, cput, put, recv, sender):
        own_into(h_ref[...], 1, w_ref, b_ref, recv, node, sender)
        for i, layer in enumerate((1, 2)):
            fold_ref[i] = (mm(w_ref[layer, 2], w_ref[layer, 4]) * (1.0 / degree)).astype(BF16)
        rows, columns = grids()
        for q in range(held):
            around = tails_ref[q].astype(I32)
            upright = jnp.transpose(tails_ref[q]).astype(I32)
            own = sender[rows_of(q), :]
            for e in range(degree):
                edge = q * degree + e
                at = at_ends + e
                near = jnp.broadcast_to(around[at_blocks : at_blocks + 1, e : e + 1], (1, size))
                to = rows == around[at : at + 1, :]
                hit = columns == upright[:, at : at + 1]
                picked = mm((hit & (near == 0)).astype(BF16), own)
                pre[edge] = recv[rows_of(q), :] + picked
                for r in range(rounds):
                    far_pick[rows_of(edge), r * size : (r + 1) * size] = (hit & (near == 1 + r)).astype(BF16)
                for r in range(1 + rounds):
                    cput[q, r * size : (r + 1) * size, e * size : (e + 1) * size] = (to & (near == r)).astype(BF16)
        for edge in range(edges):
            put[edge] = (rows == ends[edge : edge + 1, :]).astype(BF16)

    pre1, node1, fold, coarse_far, coarse_put, put = run(
        coarse_prepare,
        [
            ((held * degree,) + tile, F32), (wide, F32), ((2,) + tile, BF16),
            ((held * degree * size, far_size), BF16), ((held, size + far_size, degree * size), BF16),
            ((edges, size, size), BF16),
        ],
        coarse_start, w, bias, tails, ends,
        scratch=[pltpu.VMEM(wide, F32), pltpu.VMEM(wide, BF16)],
    )

    def coarse_layer(g0, g1, h_ref, pre, node, far_pick, w_ref, fold_ref, end_ref, slope_ref, node_slope_ref, sum_scr):
        arrived = [mm(g[...], w_ref[1, 1]).astype(BF16) for g in (g0, g1)]
        picked = []
        for q in range(held):
            senders = jnp.concatenate([a[q * size : (q + 1) * size, :] for a in arrived], axis=0)
            width = degree * size
            picked.append(mm(far_pick[q * width : (q + 1) * width, :], senders))

        def pre_of(q, e):
            return pre[q * degree + e] + picked[q][e * size : (e + 1) * size, :]

        hidden = layer_forward(held, fold_ref[0], pre_of, node, slope_ref, node_slope_ref, sum_scr)
        end_ref[...] = (h_ref[...].astype(F32) + mm(hidden, w_ref[1, 5])).astype(BF16)

    coarse_end, slope1, node_slope1 = run(
        coarse_layer,
        [(wide, BF16), ((held * degree,) + tile, BF16), (wide, BF16)],
        coarse_halo[0], coarse_halo[1], coarse_start, pre1, node1, coarse_far, w, fold,
        scratch=[pltpu.VMEM(wide, BF16)],
    )
    coarse_ends = share(coarse_end)

    def lift(s_ref, *refs):
        parts, first_ref = refs[:sub_size], refs[sub_size]
        middle_ref, out0, out1, lift_scr = refs[sub_size + 1 :]
        lift_into(parts, s_ref, lift_scr)
        for b in range(blocks):
            lifted = lift_scr[scalar(s_ref, at_pool + b)].astype(F32)
            middle_ref[b] = (first_ref[rows_of(b), :].astype(F32) + lifted).astype(BF16)
        for r, out in zip(ORDER, (out0, out1)):
            out[...] = middle_ref[scalar(s_ref, r)]

    middle, *middle_sends = run(
        lift,
        [(tiles, BF16)] + [(tile, BF16)] * rounds,
        table, *coarse_ends, first,
        scratch=[pltpu.VMEM((slots,) + tile, BF16)],
    )
    middle = middle.reshape(fine)
    halo = exchange(middle_sends)

    def last_prepare(h_ref, w_ref, b_ref, cot_ref, recv, node, sender, d_out):
        own_into(h_ref[...], 2, w_ref, b_ref, recv, node, sender)
        d_out[...] = mm_t(cot_ref[...], w_ref[2, 5])

    recv2, node2, sender2, d_out2 = run(last_prepare, own_out + [(fine, F32)], middle, w, bias, cot)

    back_out = [(tile, BF16)] * rounds + [(fine, BF16), (fine, BF16), (tiles, BF16)]
    back_scratch = [pltpu.VMEM(fine, F32), pltpu.VMEM((everyone,) + tile, F32)]

    def last_layer(s_ref, g0, g1, recv, node, sender, pick, put, w_ref, fold_ref, d_out,
                   r0, r1, d_node, d_recv, d_send, hidden_ref,
                   send_scr, sum_scr, slope_scr, node_slope_scr, act_scr, acc_scr):
        senders_into(sender, (g0, g1), 2, w_ref, send_scr)
        fold = fold_ref[1]
        pre_of = fine_pre(s_ref, recv, pick, send_scr)
        hidden_ref[...] = layer_forward(blocks, fold, pre_of, node, slope_scr, node_slope_scr, sum_scr)
        fine_backward(d_out[...], s_ref, fold, put, slope_scr, node_slope_scr, d_node, d_recv, act_scr, acc_scr)
        halo_grads_into((r0, r1), [acc_scr[blocks:].reshape(far_size, features)], 2, w_ref)
        d_send[...] = acc_scr[0:blocks].astype(BF16)

    *halo_grads, d_node, d_recv, d_send, hidden2 = run(
        last_layer,
        back_out + [(fine, BF16)],
        table, halo[0], halo[1], recv2, node2, sender2, pick, put, w, fold, d_out2,
        scratch=layer_scratch + [pltpu.VMEM((edges,) + tile, BF16), pltpu.VMEM(fine, BF16)] + back_scratch,
    )
    returned = exchange(halo_grads)

    def last_own(cot_ref, d_node, d_recv, d_send, h_ref, hidden_ref, w_ref, grad_ref, out_ref):
        grad_ref[...] = own_back(cot_ref[...].astype(F32), 2, w_ref, d_node[...], d_recv[...], d_send[...])
        out_ref[...] = (h_ref[...].astype(F32) + mm(hidden_ref[...], w_ref[2, 5])).astype(BF16)

    grad_own, out_nodes = run(
        last_own, [(fine, F32), (fine, BF16)], cot, d_node, d_recv, d_send.reshape(fine), middle, hidden2, w
    )

    def pool_grads(s_ref, r0, r1, own_ref, grad_ref, *sends):
        grad_ref[...] = own_ref[...]
        for r, arrived in zip(ORDER, (r0, r1)):
            at = scalar(s_ref, r)
            grad_ref[at] = grad_ref[at] + arrived[...].astype(F32)
        pooled_into(lambda b: grad_ref[b], s_ref, sends, None)

    grad_middle, *grad_sends = run(
        pool_grads,
        [(tiles, F32)] + [(wide, BF16)] * sub_size,
        table, returned[0], returned[1], grad_own.reshape(tiles),
    )
    grads_in = reduced(grad_sends)

    def coarse_back(*refs):
        parts = refs[:pair_size]
        put, slope_ref, node_slope_ref, w_ref, fold_ref, r0, r1, grad_ref, d_node, d_pre, act_scr = refs[pair_size:]
        grad = parts[0][...].astype(F32)
        for part in parts[1:]:
            grad = grad + part[...].astype(F32)
        grad_ref[...] = grad
        d_out = mm_t(grad.astype(BF16), w_ref[1, 5])
        node_backward(d_out, fold_ref[0], node_slope_ref, d_node, act_scr)
        for q in range(held):
            for e in range(degree):
                edge = q * degree + e
                d_pre[rows_of(edge), :] = (act_scr[rows_of(q), :] * slope_ref[edge].astype(F32)).astype(BF16)
        width = degree * size
        grads = [mm(put[q, size:, :], d_pre[q * width : (q + 1) * width, :]) for q in range(held)]
        halo_grads_into((r0, r1), grads, 1, w_ref)

    *coarse_sends, coarse_grad, d_node, d_pre = run(
        coarse_back,
        [(wide, BF16)] * rounds + [(wide, F32), (wide, BF16), ((held * degree * size, features), BF16)],
        *grads_in, coarse_put, slope1, node_slope1, w, fold,
        scratch=[pltpu.VMEM(wide, F32)],
    )
    coarse_returned = exchange(coarse_sends)

    def coarse_own(grad_ref, put, d_node, d_pre, w_ref, own_ref):
        width = degree * size
        d_send = [mm(put[q, 0:size, :], d_pre[q * width : (q + 1) * width, :]) for q in range(held)]
        d_recv = []
        for q in range(held):
            total = None
            for e in range(degree):
                part = d_pre[rows_of(q * degree + e), :].astype(F32)
                total = part if total is None else total + part
            d_recv.append(total.astype(BF16))
        own_ref[...] = own_back(
            grad_ref[...], 1, w_ref, d_node[...], jnp.concatenate(d_recv, axis=0), jnp.concatenate(d_send, axis=0)
        )

    (coarse_grad,) = run(coarse_own, [(wide, F32)], coarse_grad, coarse_put, d_node, d_pre, w)

    def scale(own_ref, r0, r1, divisor_ref, out_ref):
        for q in range(held):
            rows = rows_of(q)
            total = own_ref[rows, :] + r0[rows, :].astype(F32) + r1[rows, :].astype(F32)
            out_ref[rows, :] = (total / divisor_ref[q : q + 1, :]).astype(BF16)

    (scaled,) = run(scale, [(wide, BF16)], coarse_grad, *coarse_returned, divisor)
    scaled_parts = share(scaled)

    def first_back(s_ref, *refs):
        parts = refs[:sub_size]
        middle_ref, put, slope_ref, node_slope_ref, w_ref, fold_ref = refs[sub_size : sub_size + 6]
        r0, r1, d_node, d_recv, d_send, grad_ref, lift_scr, act_scr, acc_scr = refs[sub_size + 6 :]
        lift_into(parts, s_ref, lift_scr)
        for b in range(blocks):
            lifted = lift_scr[scalar(s_ref, at_pool + b)].astype(F32)
            grad_ref[rows_of(b), :] = middle_ref[b] + lifted
        d_out = mm_t(grad_ref[...].astype(BF16), w_ref[0, 5])
        fine_backward(d_out, s_ref, fold_ref[...], put, slope_ref, node_slope_ref, d_node, d_recv, act_scr, acc_scr)
        halo_grads_into((r0, r1), [acc_scr[blocks:].reshape(far_size, features)], 0, w_ref)
        d_send[...] = acc_scr[0:blocks].astype(BF16)

    *halo_grads, d_node, d_recv, d_send, grad_first = run(
        first_back,
        back_out + [(fine, F32)],
        table, *scaled_parts, grad_middle, put, slope0, node_slope0, w, fold0,
        scratch=[pltpu.VMEM((slots,) + tile, BF16)] + back_scratch,
    )
    returned = exchange(halo_grads)

    def first_own(first_ref, d_node, d_recv, d_send, w_ref, grad_ref):
        grad_ref[...] = own_back(first_ref[...], 0, w_ref, d_node[...], d_recv[...], d_send[...])

    (grad_own,) = run(first_own, [(fine, F32)], grad_first, d_node, d_recv, d_send.reshape(fine), w)

    def finish(s_ref, r0, r1, own_ref, out_ref):
        out_ref[...] = own_ref[...]
        for r, arrived in zip(ORDER, (r0, r1)):
            at = scalar(s_ref, r)
            out_ref[at] = out_ref[at] + arrived[...].astype(F32)

    (grad_nodes,) = run(finish, [(tiles, F32)], table, returned[0], returned[1], grad_own.reshape(tiles))
    return (out_nodes, grad_nodes.reshape(fine))


def solution(mesh):
    split = ("groups", "dom", "pair", "sub")
    placed = (
        P(split, None),
        P(split, None),
        P(split, None, None),
        P(split, None),
        P(split, None, None),
        P(split),
        P(split, None),
        P(split, None, None),
        P(),
        P(),
    )
    return jax.shard_map(
        per_device,
        mesh=mesh,
        in_specs=placed,
        out_specs=(P(split, None), P(split, None)),
        check_vma=False,
    )
```

time: 60.3 us -> 57.7 us (0.957)
  starting transfers between devices: 29.1 us -> 24.9 us
  waiting for transfers between devices: 19.7 us -> 20.9 us
    ppermute x24 -> x18, starting transfers between devices: 29.1 us -> 24.9 us  [swapped(): lax.ppermute(value, axis, [(source, source ^ mask) for source in range(si...]
    ppermute x24 -> x18, waiting for transfers between devices: 19.7 us -> 20.9 us  [swapped(): lax.ppermute(value, axis, [(source, source ^ mask) for source in range(si...]
    pallas_call x14 -> x17, Pallas kernels: 7.7 us -> 8.21 us  [run(): pl.pallas_call(kernel, out_shape=[jax.ShapeDtypeStruct(shape, dtype) for...]
  transfers between devices with their start and end apart: 24 -> 18, of which waited for: 19 -> 17; matrix products, arithmetic and copies ran while one was open for 0% -> 0% of each run, Pallas kernels for 5% -> 7%
where the time goes in v4:
time: 57.7 us; the launch traced here: 57.5 us
  starting transfers between devices  24.9 us (43%)
  waiting for transfers between devices  20.9 us (36%)
  Pallas kernels  10.9 us (19%)
  between operations  0.78 us (1%)
    ppermute x18, starting transfers between devices, swapped(): lax.ppermute(value, axis, [(source, source ^ mask) for source in range(si...  24.9 us
    ppermute x18, waiting for transfers between devices, swapped(): lax.ppermute(value, axis, [(source, source ^ mask) for source in range(si...  20.9 us
    pallas_call x17, Pallas kernels, run(): pl.pallas_call(kernel, out_shape=[jax.ShapeDtypeStruct(shape, dtype) for...  8.21 us
    pallas_call x2, Pallas kernels, run_hbm(): pl.pallas_call(kernel, out_shape=[pltpu.VMEM(shape, dtype) for shape, dty...  2.69 us
  transfers between devices with their start and end apart: 18, of which 17 were waited for; matrix products, arithmetic and copies ran while one was open for 0% of the time, Pallas kernels for 7%

profile of v4, /device:TPU:0, one launch (start us, length us, event | category | flops | bytes accessed | tf_op | source)
XLA Modules:
  0.0 57.5 jit_solution(17991229396079268085)
XLA Ops:
  0.6 1.0 %shard_map.113 = (bf16[512,128]{1,0:T(8,128)(2,1)S(1)}, bf16[128,128]{1,0:T(8,128)(2,1)S(1)}, bf16[128,128]{1,0:T(8,128)(2,1)S(1)}) custom-call(s32[1,2]{1,0:T(1,128)} %bitcast.19, bf16[512,128]{1,0:T(8,128)(2,1)} %nodes_in.1), custom_call_target="tpu_custom_call" | custom-call | bytes 1048576 | tf_op jit(solution)/shard_map/pallas_call | solution.py:50
  1.6 4.1 %collective-permute-start = (bf16[128,128]{1,0:T(8,128)(2,1)S(1)}, bf16[128,128]{1,0:T(8,128)(2,1)S(1)}, u32[]{:S(2)}, u32[]{:S(2)}) collective-permute-start(bf16[128,128]{1,0:T(8,128)(2,1)S(1)} %get-tuple-element.65), channel_id=1, source_target_pairs={{0,8},{4,12},{8,0},{12,4},{1,9},{5,13},{9,1},{13,5},{2,10},{6,14},... | collective-permute-start | bytes 98312 | tf_op jit(solution)/shard_map/ppermute | solution.py:18
  5.7 1.6 %collective-permute-start.1 = (bf16[128,128]{1,0:T(8,128)(2,1)S(1)}, bf16[128,128]{1,0:T(8,128)(2,1)S(1)}, u32[]{:S(2)}, u32[]{:S(2)}) collective-permute-start(bf16[128,128]{1,0:T(8,128)(2,1)S(1)} %get-tuple-element.66), channel_id=1, source_target_pairs={{0,4},{4,0},{8,12},{12,8},{1,5},{5,1},{9,13},{13,9},{2,6},{6,2},{1... | collective-permute-start | bytes 98312 | tf_op jit(solution)/shard_map/ppermute | solution.py:18
  7.3 1.7 %shard_map.114 = (s32[16,128]{1,0:T(8,128)S(1)}, bf16[3,6,128,128]{3,2,1,0:T(8,128)(2,1)S(1)}, f32[3,2,128]{2,1,0:T(2,128)S(1)}, bf16[512,128]{1,0:T(8,128)(2,1)...) custom-call(s32[1,2]{1,0:T(1,128)} %bitcast.20, ...), custom_call_target="tpu_custom_call" | custom-call | bytes 1048576 | tf_op jit(solution)/shard_map/pallas_call | solution.py:50
  9.0 0.0 collective-permute-done.g0
  9.0 0.6 %collective-permute-done.1.g1 = bf16[128,128]{1,0:T(8,128)(2,1)S(1)} collective-permute-done((bf16[128,128]{1,0:T(8,128)(2,1)S(1)}, bf16[128,128]{1,0:T(8,128)(2,1)S(1)}, u32[]{:S(2)}, u32[]{:S(2)}) %collective-permute-start.1) | collective-permute-done | bytes 32800 | tf_op jit(solution)/shard_map/ppermute | solution.py:18
  9.6 1.0 %shard_map.115 = (bf16[512,128]{1,0:T(8,128)(2,1)S(1)}, bf16[16,128,128]{2,1,0:T(8,128)(2,1)S(1)}, bf16[512,128]{1,0:T(8,128)(2,1)S(1)}, bf16[272,128]{1,0:T(8,128)(2,1)S(1)}, bf16[272,128]{1,0:T(8,128)(2,1)S(1)}) custom-call(s32[24,128]{1,0:T(8,128)S(1)} %get-tuple-element.64.s_ref, bf16[128,128]{1,0:T(8,128)(2,1)S(1)} %collective-permute-done.g0, ...), custom_call_target="tpu_custom_call" | custom-call | bytes 1048576 | tf_op jit(solution)/shard_map/pallas_call | solution.py:38
  10.6 0.1 collective-permute-start.2
  10.7 1.2 %collective-permute-done.2.refs_1_ = bf16[272,128]{1,0:T(8,128)(2,1)S(1)} collective-permute-done((bf16[272,128]{1,0:T(8,128)(2,1)S(1)}, bf16[272,128]{1,0:T(8,128)(2,1)S(1)}, u32[]{:S(2)}, u32[]{:S(2)}) %collective-permute-start.2) | collective-permute-done | bytes 69664 | tf_op jit(solution)/shard_map/ppermute | solution.py:18
  12.0 1.6 %collective-permute-start.3 = (bf16[272,128]{1,0:T(8,128)(2,1)S(1)}, bf16[272,128]{1,0:T(8,128)(2,1)S(1)}, u32[]{:S(2)}, u32[]{:S(2)}) collective-permute-start(bf16[272,128]{1,0:T(8,128)(2,1)S(1)} %shard_map.116.refs_0_), channel_id=1, source_target_pairs={{0,2},{2,0},{1,3},{3,1},{4,6},{6,4},{5,7},{7,5},{8,10},{10,8},{9,1... | collective-permute-start | bytes 208904 | tf_op jit(solution)/shard_map/ppermute | solution.py:18
  13.5 2.8 %collective-permute-done.3.refs_1_ = bf16[272,128]{1,0:T(8,128)(2,1)S(1)} collective-permute-done((bf16[272,128]{1,0:T(8,128)(2,1)S(1)}, bf16[272,128]{1,0:T(8,128)(2,1)S(1)}, u32[]{:S(2)}, u32[]{:S(2)}) %collective-permute-start.3) | collective-permute-done | bytes 69664 | tf_op jit(solution)/shard_map/ppermute | solution.py:18
  16.4 1.2 %collective-permute-start.5 = (bf16[256,128]{1,0:T(8,128)(2,1)S(1)}, bf16[256,128]{1,0:T(8,128)(2,1)S(1)}, u32[]{:S(2)}, u32[]{:S(2)}) collective-permute-start(bf16[256,128]{1,0:T(8,128)(2,1)S(1)} %get-tuple-element.76.h_ref), channel_id=1, source_target_pairs={{0,8},{4,12},{8,0},{12,4},{1,9},{5,13},{9,1},{13,5},{2,10},{6,14},... | collective-permute-start | bytes 196616 | tf_op jit(solution)/shard_map/ppermute | solution.py:18
  17.5 1.6 %collective-permute-start.4 = (bf16[256,128]{1,0:T(8,128)(2,1)S(1)}, bf16[256,128]{1,0:T(8,128)(2,1)S(1)}, u32[]{:S(2)}, u32[]{:S(2)}) collective-permute-start(bf16[256,128]{1,0:T(8,128)(2,1)S(1)} %get-tuple-element.76.h_ref), channel_id=1, source_target_pairs={{0,4},{4,0},{8,12},{12,8},{1,5},{5,1},{9,13},{13,9},{2,6},{6,2},{1... | collective-permute-start | bytes 196616 | tf_op jit(solution)/shard_map/ppermute | solution.py:18
  19.2 0.7 %shard_map.118 = (f32[8,128,128]{2,1,0:T(8,128)S(1)}, f32[256,128]{1,0:T(8,128)S(1)}, bf16[2,128,128]{2,1,0:T(8,128)(2,1)S(1)}, bf16[1024,256]{1,0:T(8,128)(2,1)...) custom-call(bf16[256,128]{1,0:T(8,128)(2,1)S(1)} %get-tuple-element.76.h_ref, ...), custom_call_target="tpu_custom_call" | custom-call | bytes 1048576 | tf_op jit(solution)/shard_map/pallas_call | solution.py:38
  19.9 1.8 %collective-permute-done.5.g1 = bf16[256,128]{1,0:T(8,128)(2,1)S(1)} collective-permute-done((bf16[256,128]{1,0:T(8,128)(2,1)S(1)}, bf16[256,128]{1,0:T(8,128)(2,1)S(1)}, u32[]{:S(2)}, u32[]{:S(2)}) %collective-permute-start.5) | collective-permute-done | bytes 65568 | tf_op jit(solution)/shard_map/ppermute | solution.py:18
  21.7 0.6 %collective-permute-done.4.g0 = bf16[256,128]{1,0:T(8,128)(2,1)S(1)} collective-permute-done((bf16[256,128]{1,0:T(8,128)(2,1)S(1)}, bf16[256,128]{1,0:T(8,128)(2,1)S(1)}, u32[]{:S(2)}, u32[]{:S(2)}) %collective-permute-start.4) | collective-permute-done | bytes 65568 | tf_op jit(solution)/shard_map/ppermute | solution.py:18
  22.3 0.8 %shard_map.119 = (bf16[256,128]{1,0:T(8,128)(2,1)S(1)}, bf16[8,128,128]{2,1,0:T(8,128)(2,1)S(1)}, bf16[256,128]{1,0:T(8,128)(2,1)S(1)}) custom-call(bf16[256,128]{1,0:T(8,128)(2,1)S(1)} %collective-permute-done.4.g0, bf16[256,128]{1,0:T(8,128)(2,1)S(1)} %collective-permute-done.5.g1, bf16[256,128]{1,0:T(8,128)(2,1)S(1)} %get-tuple-element.76.h_ref, ...), custom_call_target="tpu_custom_call" | custom-call | bytes 1048576 | tf_op jit(solution)/shard_map/pallas_call | solution.py:38
  23.1 0.1 collective-permute-start.6
  23.2 1.2 %collective-permute-done.6.refs_1_ = bf16[256,128]{1,0:T(8,128)(2,1)S(1)} collective-permute-done((bf16[256,128]{1,0:T(8,128)(2,1)S(1)}, bf16[256,128]{1,0:T(8,128)(2,1)S(1)}, u32[]{:S(2)}, u32[]{:S(2)}) %collective-permute-start.6) | collective-permute-done | bytes 65568 | tf_op jit(solution)/shard_map/ppermute | solution.py:18
  24.4 0.1 shard_map.120
  24.5 1.6 %collective-permute-start.7 = (bf16[128,128]{1,0:T(8,128)(2,1)S(1)}, bf16[128,128]{1,0:T(8,128)(2,1)S(1)}, u32[]{:S(2)}, u32[]{:S(2)}) collective-permute-start(bf16[128,128]{1,0:T(8,128)(2,1)S(1)} %get-tuple-element.86), channel_id=1, source_target_pairs={{0,8},{4,12},{8,0},{12,4},{1,9},{5,13},{9,1},{13,5},{2,10},{6,14},... | collective-permute-start | bytes 98312 | tf_op jit(solution)/shard_map/ppermute | solution.py:18
  26.1 1.7 %collective-permute-start.8 = (bf16[128,128]{1,0:T(8,128)(2,1)S(1)}, bf16[128,128]{1,0:T(8,128)(2,1)S(1)}, u32[]{:S(2)}, u32[]{:S(2)}) collective-permute-start(bf16[128,128]{1,0:T(8,128)(2,1)S(1)} %get-tuple-element.87), channel_id=1, source_target_pairs={{0,4},{4,0},{8,12},{12,8},{1,5},{5,1},{9,13},{13,9},{2,6},{6,2},{1... | collective-permute-start | bytes 98312 | tf_op jit(solution)/shard_map/ppermute | solution.py:18
  27.9 0.3 shard_map.121
  28.2 1.3 %collective-permute-done.7.g0 = bf16[128,128]{1,0:T(8,128)(2,1)S(1)} collective-permute-done((bf16[128,128]{1,0:T(8,128)(2,1)S(1)}, bf16[128,128]{1,0:T(8,128)(2,1)S(1)}, u32[]{:S(2)}, u32[]{:S(2)}) %collective-permute-start.7) | collective-permute-done | bytes 32800 | tf_op jit(solution)/shard_map/ppermute | solution.py:18
  29.5 0.6 %collective-permute-done.8.g1 = bf16[128,128]{1,0:T(8,128)(2,1)S(1)} collective-permute-done((bf16[128,128]{1,0:T(8,128)(2,1)S(1)}, bf16[128,128]{1,0:T(8,128)(2,1)S(1)}, u32[]{:S(2)}, u32[]{:S(2)}) %collective-permute-start.8) | collective-permute-done | bytes 32800 | tf_op jit(solution)/shard_map/ppermute | solution.py:18
  30.1 1.3 %shard_map.122 = (bf16[128,128]{1,0:T(8,128)(2,1)S(1)}, bf16[128,128]{1,0:T(8,128)(2,1)S(1)}, bf16[512,128]{1,0:T(8,128)(2,1)S(1)}, bf16[512,128]{1,0:T(8,128)(2...) custom-call(s32[24,128]{1,0:T(8,128)S(1)} %get-tuple-element.64.s_ref, ...), custom_call_target="tpu_custom_call" | custom-call | bytes 1048576 | tf_op jit(solution)/shard_map/pallas_call | solution.py:38
  31.4 1.4 %collective-permute-start.9 = (bf16[128,128]{1,0:T(8,128)(2,1)S(1)}, bf16[128,128]{1,0:T(8,128)(2,1)S(1)}, u32[]{:S(2)}, u32[]{:S(2)}) collective-permute-start(bf16[128,128]{1,0:T(8,128)(2,1)S(1)} %get-tuple-element.99), channel_id=1, source_target_pairs={{0,8},{4,12},{8,0},{12,4},{1,9},{5,13},{9,1},{13,5},{2,10},{6,14},... | collective-permute-start | bytes 98312 | tf_op jit(solution)/shard_map/ppermute | solution.py:18
  32.8 1.5 %collective-permute-start.10 = (bf16[128,128]{1,0:T(8,128)(2,1)S(1)}, bf16[128,128]{1,0:T(8,128)(2,1)S(1)}, u32[]{:S(2)}, u32[]{:S(2)}) collective-permute-start(bf16[128,128]{1,0:T(8,128)(2,1)S(1)} %get-tuple-element.100), channel_id=1, source_target_pairs={{0,4},{4,0},{8,12},{12,8},{1,5},{5,1},{9,13},{13,9},{2,6},{6,2},{1... | collective-permute-start | bytes 98312 | tf_op jit(solution)/shard_map/ppermute | solution.py:18
  34.3 1.0 %shard_map.123 = (f32[512,128]{1,0:T(8,128)S(1)}, bf16[512,128]{1,0:T(8,128)(2,1)}) custom-call(bf16[512,128]{1,0:T(8,128)(2,1)S(1)} %get-tuple-element.63.cot_ref, bf16[512,128]{1,0:T(8,128)(2,1)S(1)} %get-tuple-element.94.d_node, bf16[512,128]{1,0:T(8,128)(2,1)S(1)} %get-tuple-element.95.d_recv, bf16[512,128]{1,0:T(8,128)(2,1)S(1)} %bitcast.15, ...), custom_call_target="tpu_custom_call" | custom-call | bytes 1048576 | tf_op jit(solution)/shard_map/pallas_call | solution.py:38
  35.2 1.0 %collective-permute-done.9.r0 = bf16[128,128]{1,0:T(8,128)(2,1)S(1)} collective-permute-done((bf16[128,128]{1,0:T(8,128)(2,1)S(1)}, bf16[128,128]{1,0:T(8,128)(2,1)S(1)}, u32[]{:S(2)}, u32[]{:S(2)}) %collective-permute-start.9) | collective-permute-done | bytes 32800 | tf_op jit(solution)/shard_map/ppermute | solution.py:18
  36.3 0.5 collective-permute-done.10.r1
  36.7 0.1 shard_map.124
  36.9 0.1 collective-permute-start.11
  36.9 1.2 %collective-permute-done.11.refs_1_ = bf16[256,128]{1,0:T(8,128)(2,1)S(1)} collective-permute-done((bf16[256,128]{1,0:T(8,128)(2,1)S(1)}, bf16[256,128]{1,0:T(8,128)(2,1)S(1)}, u32[]{:S(2)}, u32[]{:S(2)}) %collective-permute-start.11) | collective-permute-done | bytes 65568 | tf_op jit(solution)/shard_map/ppermute | solution.py:18
  38.2 1.6 %collective-permute-start.12 = (bf16[256,128]{1,0:T(8,128)(2,1)S(1)}, bf16[256,128]{1,0:T(8,128)(2,1)S(1)}, u32[]{:S(2)}, u32[]{:S(2)}) collective-permute-start(bf16[256,128]{1,0:T(8,128)(2,1)S(1)} %shard_map.125.refs_0_), channel_id=1, source_target_pairs={{0,2},{2,0},{1,3},{3,1},{4,6},{6,4},{5,7},{7,5},{8,10},{10,8},{9,1... | collective-permute-start | bytes 196616 | tf_op jit(solution)/shard_map/ppermute | solution.py:18
  39.8 2.8 %collective-permute-done.12.refs_1_ = bf16[256,128]{1,0:T(8,128)(2,1)S(1)} collective-permute-done((bf16[256,128]{1,0:T(8,128)(2,1)S(1)}, bf16[256,128]{1,0:T(8,128)(2,1)S(1)}, u32[]{:S(2)}, u32[]{:S(2)}) %collective-permute-start.12) | collective-permute-done | bytes 65568 | tf_op jit(solution)/shard_map/ppermute | solution.py:18
  42.5 0.7 %shard_map.126 = (bf16[256,128]{1,0:T(8,128)(2,1)S(1)}, bf16[256,128]{1,0:T(8,128)(2,1)S(1)}, f32[256,128]{1,0:T(8,128)S(1)}, bf16[256,128]{1,0:T(8,128)(2,1)S(1)}, bf16[1024,128]{1,0:T(8,128)(2,1)S(1)}) custom-call(bf16[256,128]{1,0:T(8,128)(2,1)S(1)} %shard_map.125.refs_0_, bf16[256,128]{1,0:T(8,128)(2,1)S(1)} %collective-permute-done.12.refs_1_, ...), custom_call_target="tpu_custom_call" | custom-call | bytes 1048576 | tf_op jit(solution)/shard_map/pallas_call | solution.py:38
  43.2 1.7 %collective-permute-start.13 = (bf16[256,128]{1,0:T(8,128)(2,1)S(1)}, bf16[256,128]{1,0:T(8,128)(2,1)S(1)}, u32[]{:S(2)}, u32[]{:S(2)}) collective-permute-start(bf16[256,128]{1,0:T(8,128)(2,1)S(1)} %get-tuple-element.110), channel_id=1, source_target_pairs={{0,8},{4,12},{8,0},{12,4},{1,9},{5,13},{9,1},{13,5},{2,10},{6,14},... | collective-permute-start | bytes 196616 | tf_op jit(solution)/shard_map/ppermute | solution.py:18
  44.9 1.7 %collective-permute-start.14 = (bf16[256,128]{1,0:T(8,128)(2,1)S(1)}, bf16[256,128]{1,0:T(8,128)(2,1)S(1)}, u32[]{:S(2)}, u32[]{:S(2)}) collective-permute-start(bf16[256,128]{1,0:T(8,128)(2,1)S(1)} %get-tuple-element.111), channel_id=1, source_target_pairs={{0,4},{4,0},{8,12},{12,8},{1,5},{5,1},{9,13},{13,9},{2,6},{6,2},{1... | collective-permute-start | bytes 196616 | tf_op jit(solution)/shard_map/ppermute | solution.py:18
  46.6 0.4 shard_map.127.own_ref
  47.0 1.5 %collective-permute-done.13.r0 = bf16[256,128]{1,0:T(8,128)(2,1)S(1)} collective-permute-done((bf16[256,128]{1,0:T(8,128)(2,1)S(1)}, bf16[256,128]{1,0:T(8,128)(2,1)S(1)}, u32[]{:S(2)}, u32[]{:S(2)}) %collective-permute-start.13) | collective-permute-done | bytes 65568 | tf_op jit(solution)/shard_map/ppermute | solution.py:18
  48.5 0.7 %collective-permute-done.14.r1 = bf16[256,128]{1,0:T(8,128)(2,1)S(1)} collective-permute-done((bf16[256,128]{1,0:T(8,128)(2,1)S(1)}, bf16[256,128]{1,0:T(8,128)(2,1)S(1)}, u32[]{:S(2)}, u32[]{:S(2)}) %collective-permute-start.14) | collective-permute-done | bytes 65568 | tf_op jit(solution)/shard_map/ppermute | solution.py:18
  49.2 0.1 collective-permute-start.15
  49.3 1.2 %collective-permute-done.15.refs_1_ = bf16[256,128]{1,0:T(8,128)(2,1)S(1)} collective-permute-done((bf16[256,128]{1,0:T(8,128)(2,1)S(1)}, bf16[256,128]{1,0:T(8,128)(2,1)S(1)}, u32[]{:S(2)}, u32[]{:S(2)}) %collective-permute-start.15) | collective-permute-done | bytes 65568 | tf_op jit(solution)/shard_map/ppermute | solution.py:18
  50.5 0.8 %shard_map.129 = (bf16[128,128]{1,0:T(8,128)(2,1)S(1)}, bf16[128,128]{1,0:T(8,128)(2,1)S(1)}, bf16[512,128]{1,0:T(8,128)(2,1)S(1)}, bf16[512,128]{1,0:T(8,128)(2...) custom-call(s32[24,128]{1,0:T(8,128)S(1)} %get-tuple-element.64.s_ref, ...), custom_call_target="tpu_custom_call" | custom-call | bytes 1048576 | tf_op jit(solution)/shard_map/pallas_call | solution.py:38
  51.3 1.5 %collective-permute-start.16 = (bf16[128,128]{1,0:T(8,128)(2,1)S(1)}, bf16[128,128]{1,0:T(8,128)(2,1)S(1)}, u32[]{:S(2)}, u32[]{:S(2)}) collective-permute-start(bf16[128,128]{1,0:T(8,128)(2,1)S(1)} %get-tuple-element.116), channel_id=1, source_target_pairs={{0,8},{4,12},{8,0},{12,4},{1,9},{5,13},{9,1},{13,5},{2,10},{6,14},... | collective-permute-start | bytes 98312 | tf_op jit(solution)/shard_map/ppermute | solution.py:18
  52.9 1.9 %collective-permute-start.17 = (bf16[128,128]{1,0:T(8,128)(2,1)S(1)}, bf16[128,128]{1,0:T(8,128)(2,1)S(1)}, u32[]{:S(2)}, u32[]{:S(2)}) collective-permute-start(bf16[128,128]{1,0:T(8,128)(2,1)S(1)} %get-tuple-element.117), channel_id=1, source_target_pairs={{0,4},{4,0},{8,12},{12,8},{1,5},{5,1},{9,13},{13,9},{2,6},{6,2},{1... | collective-permute-start | bytes 98312 | tf_op jit(solution)/shard_map/ppermute | solution.py:18
  54.8 0.3 shard_map.130
  55.0 1.2 %collective-permute-done.16.r0 = bf16[128,128]{1,0:T(8,128)(2,1)S(1)} collective-permute-done((bf16[128,128]{1,0:T(8,128)(2,1)S(1)}, bf16[128,128]{1,0:T(8,128)(2,1)S(1)}, u32[]{:S(2)}, u32[]{:S(2)}) %collective-permute-start.16) | collective-permute-done | bytes 32800 | tf_op jit(solution)/shard_map/ppermute | solution.py:18
  56.2 0.5 collective-permute-done.17.r1
  56.8 0.7 %shard_map.131 = f32[4,128,128]{2,1,0:T(8,128)} custom-call(s32[24,128]{1,0:T(8,128)S(1)} %get-tuple-element.64.s_ref, bf16[128,128]{1,0:T(8,128)(2,1)S(1)} %collective-permute-done.16.r0, bf16[128,128]{1,0:T(8,128)(2,1)S(1)} %collective-permute-done.17.r1, f32[4,128,128]{2,1,0:T(8,128)S(1)} %bitcast.10), custom_call_target="tpu_custom_call" | custom-call | bytes 1048576 | tf_op jit(solution)/shard_map/pallas_call | solution.py:38
  (4 shorter events, 0.1 us)
Async XLA Ops:
  1.6 7.4 %collective-permute-start = (bf16[128,128]{1,0:T(8,128)(2,1)S(1)}, bf16[128,128]{1,0:T(8,128)(2,1)S(1)}, u32[]{:S(2)}, u32[]{:S(2)}) collective-permute-start(bf16[128,128]{1,0:T(8,128)(2,1)S(1)} %get-tuple-element.65), channel_id=1, source_target_pairs={{0,8},{4,12},{8,0},{12,4},{1,9},{5,13},{9,1},{13,5},{2,10},{6,14},... | collective-permute-start | bytes 98312 | tf_op jit(solution)/shard_map/ppermute | solution.py:18
  5.7 3.9 %collective-permute-start.1 = (bf16[128,128]{1,0:T(8,128)(2,1)S(1)}, bf16[128,128]{1,0:T(8,128)(2,1)S(1)}, u32[]{:S(2)}, u32[]{:S(2)}) collective-permute-start(bf16[128,128]{1,0:T(8,128)(2,1)S(1)} %get-tuple-element.66), channel_id=1, source_target_pairs={{0,4},{4,0},{8,12},{12,8},{1,5},{5,1},{9,13},{13,9},{2,6},{6,2},{1... | collective-permute-start | bytes 98312 | tf_op jit(solution)/shard_map/ppermute | solution.py:18
  10.6 1.3 %collective-permute-start.2 = (bf16[272,128]{1,0:T(8,128)(2,1)S(1)}, bf16[272,128]{1,0:T(8,128)(2,1)S(1)}, u32[]{:S(2)}, u32[]{:S(2)}) collective-permute-start(bf16[272,128]{1,0:T(8,128)(2,1)S(1)} %get-tuple-element.75), channel_id=1, source_target_pairs={{0,1},{1,0},{2,3},{3,2},{4,5},{5,4},{6,7},{7,6},{8,9},{9,8},{10,11... | collective-permute-start | bytes 208904 | tf_op jit(solution)/shard_map/ppermute | solution.py:18
  12.0 4.4 %collective-permute-start.3 = (bf16[272,128]{1,0:T(8,128)(2,1)S(1)}, bf16[272,128]{1,0:T(8,128)(2,1)S(1)}, u32[]{:S(2)}, u32[]{:S(2)}) collective-permute-start(bf16[272,128]{1,0:T(8,128)(2,1)S(1)} %shard_map.116.refs_0_), channel_id=1, source_target_pairs={{0,2},{2,0},{1,3},{3,1},{4,6},{6,4},{5,7},{7,5},{8,10},{10,8},{9,1... | collective-permute-start | bytes 208904 | tf_op jit(solution)/shard_map/ppermute | solution.py:18
  16.4 5.3 %collective-permute-start.5 = (bf16[256,128]{1,0:T(8,128)(2,1)S(1)}, bf16[256,128]{1,0:T(8,128)(2,1)S(1)}, u32[]{:S(2)}, u32[]{:S(2)}) collective-permute-start(bf16[256,128]{1,0:T(8,128)(2,1)S(1)} %get-tuple-element.76.h_ref), channel_id=1, source_target_pairs={{0,8},{4,12},{8,0},{12,4},{1,9},{5,13},{9,1},{13,5},{2,10},{6,14},... | collective-permute-start | bytes 196616 | tf_op jit(solution)/shard_map/ppermute | solution.py:18
  17.5 4.8 %collective-permute-start.4 = (bf16[256,128]{1,0:T(8,128)(2,1)S(1)}, bf16[256,128]{1,0:T(8,128)(2,1)S(1)}, u32[]{:S(2)}, u32[]{:S(2)}) collective-permute-start(bf16[256,128]{1,0:T(8,128)(2,1)S(1)} %get-tuple-element.76.h_ref), channel_id=1, source_target_pairs={{0,4},{4,0},{8,12},{12,8},{1,5},{5,1},{9,13},{13,9},{2,6},{6,2},{1... | collective-permute-start | bytes 196616 | tf_op jit(solution)/shard_map/ppermute | solution.py:18
  23.1 1.3 %collective-permute-start.6 = (bf16[256,128]{1,0:T(8,128)(2,1)S(1)}, bf16[256,128]{1,0:T(8,128)(2,1)S(1)}, u32[]{:S(2)}, u32[]{:S(2)}) collective-permute-start(bf16[256,128]{1,0:T(8,128)(2,1)S(1)} %get-tuple-element.84.refs_0_), channel_id=1, source_target_pairs={{0,1},{1,0},{2,3},{3,2},{4,5},{5,4},{6,7},{7,6},{8,9},{9,8},{10,11... | collective-permute-start | bytes 196616 | tf_op jit(solution)/shard_map/ppermute | solution.py:18
  24.5 5.0 %collective-permute-start.7 = (bf16[128,128]{1,0:T(8,128)(2,1)S(1)}, bf16[128,128]{1,0:T(8,128)(2,1)S(1)}, u32[]{:S(2)}, u32[]{:S(2)}) collective-permute-start(bf16[128,128]{1,0:T(8,128)(2,1)S(1)} %get-tuple-element.86), channel_id=1, source_target_pairs={{0,8},{4,12},{8,0},{12,4},{1,9},{5,13},{9,1},{13,5},{2,10},{6,14},... | collective-permute-start | bytes 98312 | tf_op jit(solution)/shard_map/ppermute | solution.py:18
  26.1 3.9 %collective-permute-start.8 = (bf16[128,128]{1,0:T(8,128)(2,1)S(1)}, bf16[128,128]{1,0:T(8,128)(2,1)S(1)}, u32[]{:S(2)}, u32[]{:S(2)}) collective-permute-start(bf16[128,128]{1,0:T(8,128)(2,1)S(1)} %get-tuple-element.87), channel_id=1, source_target_pairs={{0,4},{4,0},{8,12},{12,8},{1,5},{5,1},{9,13},{13,9},{2,6},{6,2},{1... | collective-permute-start | bytes 98312 | tf_op jit(solution)/shard_map/ppermute | solution.py:18
  31.4 4.9 %collective-permute-start.9 = (bf16[128,128]{1,0:T(8,128)(2,1)S(1)}, bf16[128,128]{1,0:T(8,128)(2,1)S(1)}, u32[]{:S(2)}, u32[]{:S(2)}) collective-permute-start(bf16[128,128]{1,0:T(8,128)(2,1)S(1)} %get-tuple-element.99), channel_id=1, source_target_pairs={{0,8},{4,12},{8,0},{12,4},{1,9},{5,13},{9,1},{13,5},{2,10},{6,14},... | collective-permute-start | bytes 98312 | tf_op jit(solution)/shard_map/ppermute | solution.py:18
  32.8 3.9 %collective-permute-start.10 = (bf16[128,128]{1,0:T(8,128)(2,1)S(1)}, bf16[128,128]{1,0:T(8,128)(2,1)S(1)}, u32[]{:S(2)}, u32[]{:S(2)}) collective-permute-start(bf16[128,128]{1,0:T(8,128)(2,1)S(1)} %get-tuple-element.100), channel_id=1, source_target_pairs={{0,4},{4,0},{8,12},{12,8},{1,5},{5,1},{9,13},{13,9},{2,6},{6,2},{1... | collective-permute-start | bytes 98312 | tf_op jit(solution)/shard_map/ppermute | solution.py:18
  36.9 1.3 %collective-permute-start.11 = (bf16[256,128]{1,0:T(8,128)(2,1)S(1)}, bf16[256,128]{1,0:T(8,128)(2,1)S(1)}, u32[]{:S(2)}, u32[]{:S(2)}) collective-permute-start(bf16[256,128]{1,0:T(8,128)(2,1)S(1)} %get-tuple-element.103), channel_id=1, source_target_pairs={{0,1},{1,0},{2,3},{3,2},{4,5},{5,4},{6,7},{7,6},{8,9},{9,8},{10,11... | collective-permute-start | bytes 196616 | tf_op jit(solution)/shard_map/ppermute | solution.py:18
  38.2 4.3 %collective-permute-start.12 = (bf16[256,128]{1,0:T(8,128)(2,1)S(1)}, bf16[256,128]{1,0:T(8,128)(2,1)S(1)}, u32[]{:S(2)}, u32[]{:S(2)}) collective-permute-start(bf16[256,128]{1,0:T(8,128)(2,1)S(1)} %shard_map.125.refs_0_), channel_id=1, source_target_pairs={{0,2},{2,0},{1,3},{3,1},{4,6},{6,4},{5,7},{7,5},{8,10},{10,8},{9,1... | collective-permute-start | bytes 196616 | tf_op jit(solution)/shard_map/ppermute | solution.py:18
  43.2 5.2 %collective-permute-start.13 = (bf16[256,128]{1,0:T(8,128)(2,1)S(1)}, bf16[256,128]{1,0:T(8,128)(2,1)S(1)}, u32[]{:S(2)}, u32[]{:S(2)}) collective-permute-start(bf16[256,128]{1,0:T(8,128)(2,1)S(1)} %get-tuple-element.110), channel_id=1, source_target_pairs={{0,8},{4,12},{8,0},{12,4},{1,9},{5,13},{9,1},{13,5},{2,10},{6,14},... | collective-permute-start | bytes 196616 | tf_op jit(solution)/shard_map/ppermute | solution.py:18
  44.9 4.3 %collective-permute-start.14 = (bf16[256,128]{1,0:T(8,128)(2,1)S(1)}, bf16[256,128]{1,0:T(8,128)(2,1)S(1)}, u32[]{:S(2)}, u32[]{:S(2)}) collective-permute-start(bf16[256,128]{1,0:T(8,128)(2,1)S(1)} %get-tuple-element.111), channel_id=1, source_target_pairs={{0,4},{4,0},{8,12},{12,8},{1,5},{5,1},{9,13},{13,9},{2,6},{6,2},{1... | collective-permute-start | bytes 196616 | tf_op jit(solution)/shard_map/ppermute | solution.py:18
  49.2 1.3 %collective-permute-start.15 = (bf16[256,128]{1,0:T(8,128)(2,1)S(1)}, bf16[256,128]{1,0:T(8,128)(2,1)S(1)}, u32[]{:S(2)}, u32[]{:S(2)}) collective-permute-start(bf16[256,128]{1,0:T(8,128)(2,1)S(1)} %shard_map.128.refs_0_), channel_id=1, source_target_pairs={{0,1},{1,0},{2,3},{3,2},{4,5},{5,4},{6,7},{7,6},{8,9},{9,8},{10,11... | collective-permute-start | bytes 196616 | tf_op jit(solution)/shard_map/ppermute | solution.py:18
  51.3 4.9 %collective-permute-start.16 = (bf16[128,128]{1,0:T(8,128)(2,1)S(1)}, bf16[128,128]{1,0:T(8,128)(2,1)S(1)}, u32[]{:S(2)}, u32[]{:S(2)}) collective-permute-start(bf16[128,128]{1,0:T(8,128)(2,1)S(1)} %get-tuple-element.116), channel_id=1, source_target_pairs={{0,8},{4,12},{8,0},{12,4},{1,9},{5,13},{9,1},{13,5},{2,10},{6,14},... | collective-permute-start | bytes 98312 | tf_op jit(solution)/shard_map/ppermute | solution.py:18
  52.9 3.9 %collective-permute-start.17 = (bf16[128,128]{1,0:T(8,128)(2,1)S(1)}, bf16[128,128]{1,0:T(8,128)(2,1)S(1)}, u32[]{:S(2)}, u32[]{:S(2)}) collective-permute-start(bf16[128,128]{1,0:T(8,128)(2,1)S(1)} %get-tuple-element.117), channel_id=1, source_target_pairs={{0,4},{4,0},{8,12},{12,8},{1,5},{5,1},{9,13},{13,9},{2,6},{6,2},{1... | collective-permute-start | bytes 98312 | tf_op jit(solution)/shard_map/ppermute | solution.py:18

commit v5 on v4

--- a/solution.py
+++ b/solution.py
@@ -24,10 +24,6 @@
 
 def mm_t(a, b):
     return lax.dot_general(a, b, (((1,), (1,)), ((), ())), preferred_element_type=F32)
-
-
-def sigmoid(x):
-    return 0.5 * jnp.tanh(0.5 * x) + 0.5
 
 
 def scalar(table, index):
@@ -85,19 +81,21 @@
 
     held = pair_size
     wide = (held * size, features)
-    at_ends = TAIL // 2
-    at_blocks = at_ends + degree
+    at_listed = degree
+    doms = 1 + rounds
+    at_info = held * size + TAIL
+    pool_rows = at_info + doms * TAIL
+    at_first = held * size
+    halo_rows = at_first + size + TAIL
     at_near = rounds
     at_pool = at_near + edges
     at_pair = at_pool + blocks
     at_sub = at_pair + 1
-    table_rows = -(-(at_sub + 1) // 8) * 8
+    at_sent = at_sub + 1
+    table_rows = -(-(at_sent + rounds) // 8) * 8
 
     def exchange(pieces):
         return [swapped(piece, "dom", xor_bits[r]) for r, piece in zip(ORDER, pieces)]
-
-    def exchange_same(piece):
-        return [swapped(piece, "dom", bit) for bit in xor_bits]
 
     def reduced(pieces):
         arrived = [swapped(piece, "sub", mask) for mask, piece in enumerate(pieces) if mask > 0]
@@ -105,10 +103,14 @@
         return [chip] + [swapped(chip, "pair", mask) for mask in range(1, pair_size)]
 
     def add_parts(*refs):
-        total = refs[0][...].astype(F32)
+        own, out = refs[0], refs[-1]
+        shared = refs[1].shape[0] if len(refs) > 2 else own.shape[0]
+        total = own[0:shared, :].astype(F32)
         for part in refs[1:-1]:
             total = total + part[...].astype(F32)
-        refs[-1][...] = total.astype(BF16)
+        out[0:shared, :] = total.astype(BF16)
+        if shared < own.shape[0]:
+            out[shared:, :] = own[shared:, :]
 
     def share(piece):
         return [piece] + [swapped(piece, "sub", mask) for mask in range(1, sub_size)]
@@ -123,19 +125,29 @@
         for copy in copies:
             copy.wait()
 
-    def choose(send_in, nodes_in, h_ref, out0, out1, send_scr, sems):
+    def choose(send_in, ends_in, listed_in, nodes_in, h_ref, info_ref, out0, out1, send_scr, ends_scr, listed_scr, sems):
         parts = [(nodes_in.at[rows_of(b)], h_ref.at[rows_of(b)]) for b in range(blocks)]
-        fetch([(send_in, send_scr)] + parts, sems)
+        fetch([(send_in, send_scr), (ends_in, ends_scr), (listed_in, listed_scr)] + parts, sems)
+        lanes = lax.broadcasted_iota(I32, (1, features), 1)
+        listed = jnp.zeros((1, features), I32)
+        for e in range(degree):
+            listed = jnp.where(lanes == e, jnp.broadcast_to(listed_scr[0:1, e : e + 1], (1, features)), listed)
+        rest = jnp.zeros((TAIL - degree - 1, features), F32)
+        info = jnp.concatenate([ends_scr[...].astype(F32), listed.astype(F32), rest], axis=0).astype(BF16)
+        info_ref[...] = info
         for r, out in zip(ORDER, (out0, out1)):
             at = pl.multiple_of(send_scr[0:1, r : r + 1][0, 0] * size, size)
-            out[...] = h_ref[pl.ds(at, size), :]
+            out[0:size, :] = h_ref[pl.ds(at, size), :]
+            out[size:, :] = info
 
     sent = send_blocks.reshape(1, rounds)
-    h0, *first_sends = run_hbm(
+    coarse_ends = coarse_nodes.reshape(degree, size)
+    h0, info, *first_sends = run_hbm(
         choose,
-        [(fine, BF16)] + [(tile, BF16)] * rounds,
-        [sent, nodes],
-        scratch=[pltpu.VMEM((1, rounds), I32), pltpu.SemaphoreType.DMA((1 + blocks,))],
+        [(fine, BF16), ((TAIL, features), BF16)] + [((size + TAIL, features), BF16)] * rounds,
+        [sent, coarse_ends, coarse_blocks, nodes],
+        scratch=[pltpu.VMEM(a.shape, I32) for a in (sent, coarse_ends, coarse_blocks)]
+        + [pltpu.SemaphoreType.DMA((3 + blocks,))],
     )
     halo = exchange(first_sends)
 
@@ -143,30 +155,32 @@
         return lax.broadcasted_iota(I32, (size, size), 0), lax.broadcasted_iota(I32, (size, size), 1)
 
     def own_into(state, layer, w_ref, b_ref, recv_ref, node_ref, sender_ref):
-        recv_ref[...] = mm(state, w_ref[layer, 0]) + b_ref[layer, 0:1, :]
-        node_ref[...] = mm(state, w_ref[layer, 3]) + b_ref[layer, 1:2, :]
-        sender_ref[...] = mm(state, w_ref[layer, 1]).astype(BF16)
+        recv_ref[...] = 0.5 * (mm(state, w_ref[layer, 0]) + b_ref[layer, 0:1, :])
+        node_ref[...] = 0.5 * (mm(state, w_ref[layer, 3]) + b_ref[layer, 1:2, :])
+        sender_ref[...] = (0.5 * mm(state, w_ref[layer, 1])).astype(BF16)
 
     def layer_forward(count, fold, pre_of, node, slope_ref, node_slope_ref, sum_scr):
         for b in range(count):
             total = None
             for e in range(degree):
                 edge = b * degree + e
-                pre = pre_of(b, e)
-                gate = sigmoid(pre)
-                active = pre * gate
-                slope_ref[edge] = (gate + active * (1.0 - gate)).astype(BF16)
+                half = pre_of(b, e)
+                up = 1.0 + jnp.tanh(half)
+                active = half * up
+                if edge < slope_ref.shape[0]:
+                    slope_ref[edge] = (up + active * (2.0 - up)).astype(BF16)
                 total = active if total is None else total + active
             sum_scr[rows_of(b), :] = total.astype(BF16)
-        hidden_pre = node[...] + mm(sum_scr[...], fold)
-        gate = sigmoid(hidden_pre)
-        hidden = hidden_pre * gate
-        node_slope_ref[...] = (gate + hidden * (1.0 - gate)).astype(BF16)
+        half = node + mm(sum_scr[...], fold)
+        up = 1.0 + jnp.tanh(half)
+        hidden = half * up
+        kept = node_slope_ref.shape[0]
+        node_slope_ref[...] = (0.5 * (up + hidden * (2.0 - up))).astype(BF16)[0:kept, :]
         return hidden.astype(BF16)
 
     def senders_into(own, halos, layer, w_ref, send_scr):
         for r, g in zip(ORDER, halos):
-            send_scr[blocks + r] = mm(g[...], w_ref[layer, 1]).astype(BF16)
+            send_scr[blocks + r] = (0.5 * mm(g, w_ref[layer, 1])).astype(BF16)
         for b in range(blocks):
             send_scr[b] = own[rows_of(b), :]
 
@@ -209,11 +223,11 @@
             + mm_t(d_send.astype(BF16), w_ref[layer, 1])
         )
 
-    def pooled_into(read, s_ref, out_refs, tail_ref):
+    def pooled_into(read, s_ref, out_refs, with_count):
         sub = scalar(s_ref, at_sub)
         rows = lax.broadcasted_iota(I32, (TAIL, features), 0)
         for sub_mask, out in enumerate(out_refs):
-            tail = None if tail_ref is None else tail_ref[...]
+            counts = jnp.zeros((TAIL, features), F32)
             for q in range(held):
                 slot = q * sub_size + (sub ^ sub_mask)
                 total, count = None, None
@@ -223,26 +237,22 @@
                     total = part if total is None else total + part
                     count = hit if count is None else count + hit
                 out[rows_of(q), :] = total.astype(BF16)
-                if tail is not None:
-                    tail = tail + jnp.where(rows == q, count, 0.0)
-            if tail is not None:
-                if sub_mask > 0:
-                    tail = jnp.where(rows < at_ends, tail, 0.0)
-                out[held * size :, :] = tail.astype(BF16)
+                counts = counts + jnp.where(rows == q, count, 0.0)
+            if with_count:
+                out[held * size : at_info, :] = counts.astype(BF16)
 
     def lift_into(parts, s_ref, lift_scr):
         sub = scalar(s_ref, at_sub)
         for mask, part in enumerate(parts):
             for q in range(held):
-                lift_scr[q * sub_size + (sub ^ mask)] = part[rows_of(q), :]
+                for v in range(part.shape[0] // (held * size)):
+                    lift_scr[v * slots + q * sub_size + (sub ^ mask)] = part[rows_of(v * held + q), :]
 
     inputs = [
         sent,
         neighbour_blocks,
         pool_map.reshape(1, blocks),
-        coarse_blocks,
         neighbour_nodes.reshape(edges, size),
-        coarse_nodes.reshape(degree, size),
         weights,
         biases,
         cotangent,
@@ -251,9 +261,9 @@
 
     def prepare(*refs):
         sources, h_ref = refs[: len(inputs)], refs[len(inputs)]
-        ends, w_ref, b_ref, c_ref, s_ref, fold_ref, tail_ref, pick, recv, node, sender, *kept, sems = refs[len(inputs) + 1 :]
-        send_scr, near_scr, pool_scr, coarse_scr, cends = kept
-        fetch(list(zip(sources, kept[:4] + [ends, cends, w_ref, b_ref, c_ref])), sems)
+        ends, w_ref, b_ref, c_ref, s_ref, fold_ref, pick, recv, node, sender, *kept, sems = refs[len(inputs) + 1 :]
+        send_scr, near_scr, pool_scr = kept
+        fetch(list(zip(sources, kept + [ends, w_ref, b_ref, c_ref])), sems)
 
         def put_row(index, ref, i, j):
             s_ref[index : index + 1, :] = jnp.broadcast_to(ref[i : i + 1, j : j + 1], (1, features))
@@ -266,30 +276,28 @@
             put_row(at_pool + b, pool_scr, 0, b)
         s_ref[at_pair : at_pair + 1, :] = jnp.full((1, features), lax.axis_index("pair"), I32)
         s_ref[at_sub : at_sub + 1, :] = jnp.full((1, features), lax.axis_index("sub"), I32)
-        lanes = lax.broadcasted_iota(I32, (1, features), 1)
-        listed = jnp.zeros((1, features), I32)
-        for e in range(degree):
-            listed = jnp.where(lanes == e, jnp.broadcast_to(coarse_scr[0:1, e : e + 1], (1, features)), listed)
-        tail_ref[...] = jnp.zeros_like(tail_ref)
-        tail_ref[at_ends : at_ends + degree, :] = cends[...].astype(F32)
-        tail_ref[at_blocks : at_blocks + 1, :] = listed.astype(F32)
+        for r in range(rounds):
+            slot = jnp.zeros((1, features), I32)
+            for b in range(blocks):
+                slot = jnp.where(s_ref[r : r + 1, :] == b, s_ref[at_pool + b : at_pool + b + 1, :], slot)
+            s_ref[at_sent + r : at_sent + r + 1, :] = slot
         own_into(h_ref[...], 0, w_ref, b_ref, recv, node, sender)
         columns = grids()[1]
         upright = jnp.transpose(ends[...])
         for edge in range(edges):
             pick[edge] = (columns == upright[:, edge : edge + 1]).astype(BF16)
-        fold_ref[...] = (mm(w_ref[0, 2], w_ref[0, 4]) * (1.0 / degree)).astype(BF16)
-
-    ends, w, bias, cot, table, fold0, tail, pick, recv0, node0, sender0 = run_hbm(
+        fold_ref[...] = (mm(w_ref[0, 2], w_ref[0, 4]) * (0.5 / degree)).astype(BF16)
+
+    ends, w, bias, cot, table, fold0, pick, recv0, node0, sender0 = run_hbm(
         prepare,
         [
             ((edges, size), I32), (weights.shape, BF16), (biases.shape, F32), (fine, BF16),
-            ((table_rows, features), I32), (tile, BF16), ((TAIL, features), F32),
+            ((table_rows, features), I32), (tile, BF16),
             ((edges, size, size), BF16),
         ] + own_out,
         inputs,
         h0,
-        scratch=[pltpu.VMEM(a.shape, I32) for a in inputs[:4] + inputs[5:6]]
+        scratch=[pltpu.VMEM(a.shape, I32) for a in inputs[:3]]
         + [pltpu.SemaphoreType.DMA((len(inputs),))],
     )
 
@@ -297,144 +305,165 @@
 
     layer_scratch = [pltpu.VMEM((everyone,) + tile, BF16), pltpu.VMEM(fine, BF16)]
 
-    def first_layer(s_ref, g0, g1, h_ref, recv, node, sender, pick, w_ref, fold_ref, tail_ref, *rest):
+    def first_layer(s_ref, g0, g1, h_ref, recv, node, sender, pick, w_ref, fold_ref, info_ref, *rest):
         first_ref, slope_ref, node_slope_ref, *sends, send_scr, sum_scr = rest
-        senders_into(sender, (g0, g1), 0, w_ref, send_scr)
+        senders_into(sender, (g0[0:size, :], g1[0:size, :]), 0, w_ref, send_scr)
         pre_of = fine_pre(s_ref, recv, pick, send_scr)
-        hidden = layer_forward(blocks, fold_ref[...], pre_of, node, slope_ref, node_slope_ref, sum_scr)
+        hidden = layer_forward(blocks, fold_ref[...], pre_of, node[...], slope_ref, node_slope_ref, sum_scr)
         first_ref[...] = (h_ref[...].astype(F32) + mm(hidden, w_ref[0, 5])).astype(BF16)
-        pooled_into(lambda b: first_ref[rows_of(b), :].astype(F32), s_ref, sends, tail_ref)
+        pooled_into(lambda b: first_ref[rows_of(b), :].astype(F32), s_ref, sends, True)
+        sends[0][at_info : at_info + TAIL, :] = info_ref[...]
+        for r, g in zip(ORDER, (g0, g1)):
+            sends[0][at_info + (1 + r) * TAIL : at_info + (2 + r) * TAIL, :] = g[size:, :]
 
     first, slope0, node_slope0, *pool_sends = run(
         first_layer,
-        [(fine, BF16)] + slopes + [((held * size + TAIL, features), BF16)] * sub_size,
-        table, halo[0], halo[1], h0, recv0, node0, sender0, pick, w, fold0, tail,
+        [(fine, BF16)] + slopes + [((pool_rows, features), BF16)] + [((at_info, features), BF16)] * (sub_size - 1),
+        table, halo[0], halo[1], h0, recv0, node0, sender0, pick, w, fold0, info,
         scratch=layer_scratch,
     )
 
     pool_in = reduced(pool_sends)
 
-    def coarse_begin(s_ref, *refs):
-        parts, (start_ref, divisor_ref, tails_ref) = refs[:pair_size], refs[pair_size:]
-        total = parts[0][...].astype(F32)
+    def coarse_begin(s_ref, first_ref, *refs):
+        parts, (start_ref, divisor_ref, infos_ref, other, out0, out1) = refs[:pair_size], refs[pair_size:]
+        total = parts[0][0:at_info, :].astype(F32)
         for part in parts[1:]:
-            total = total + part[...].astype(F32)
-        divisor = jnp.maximum(total[held * size : held * size + at_ends, :], 1.0)
+            total = total + part[0:at_info, :].astype(F32)
+        divisor = jnp.maximum(total[held * size : held * size + 8, :], 1.0)
         divisor_ref[...] = divisor
         for q in range(held):
-            start_ref[rows_of(q), :] = (total[q * size : (q + 1) * size, :] / divisor[q : q + 1, :]).astype(BF16)
+            start = (total[q * size : (q + 1) * size, :] / divisor[q : q + 1, :]).astype(BF16)
+            for out in (start_ref, other, out0, out1):
+                out[rows_of(q), :] = start
+        for r, out in zip(ORDER, (out0, out1)):
+            at = pl.multiple_of(scalar(s_ref, r) * size, size)
+            out[at_first : at_first + size, :] = first_ref[pl.ds(at, size), :]
+            slot = s_ref[at_sent + r : at_sent + r + 1, :].astype(F32)
+            out[at_first + size :, :] = jnp.broadcast_to(slot, (TAIL, features)).astype(BF16)
         pair = scalar(s_ref, at_pair)
         for mask, part in enumerate(parts):
-            tails_ref[pair ^ mask] = part[held * size :, :].astype(F32)
-
-    coarse_start, divisor, tails = run(
+            for v in range(doms):
+                at = at_info + v * TAIL
+                infos_ref[v * held + (pair ^ mask)] = part[at : at + TAIL, :].astype(F32)
+
+    coarse_start, divisor, infos, other_send, *halo_sends = run(
         coarse_begin,
-        [(wide, BF16), ((at_ends, features), F32), ((held, TAIL, features), F32)],
-        table, *pool_in,
-    )
-    coarse_halo = exchange_same(coarse_start)
-
-    def coarse_prepare(h_ref, w_ref, b_ref, tails_ref, ends, pre, node, fold_ref, far_pick, cput, put, recv, sender):
+        [(wide, BF16), ((8, features), F32), ((doms * held, TAIL, features), F32), (wide, BF16)]
+        + [((halo_rows, features), BF16)] * rounds,
+        table, first, *pool_in,
+    )
+    other = swapped(other_send, "dom", xor_bits[0] ^ xor_bits[1])
+    coarse_halo = exchange(halo_sends)
+
+    def coarse_prepare(h_ref, w_ref, b_ref, cot_ref, infos_ref, ends, pre, node, fold_ref, far_pick, cput, put, d_out, recv, sender):
         own_into(h_ref[...], 1, w_ref, b_ref, recv, node, sender)
         for i, layer in enumerate((1, 2)):
-            fold_ref[i] = (mm(w_ref[layer, 2], w_ref[layer, 4]) * (1.0 / degree)).astype(BF16)
+            fold_ref[i] = (mm(w_ref[layer, 2], w_ref[layer, 4]) * (0.5 / degree)).astype(BF16)
+        d_out[...] = mm_t(cot_ref[...], w_ref[2, 5])
         rows, columns = grids()
-        for q in range(held):
-            around = tails_ref[q].astype(I32)
-            upright = jnp.transpose(tails_ref[q]).astype(I32)
-            own = sender[rows_of(q), :]
-            for e in range(degree):
-                edge = q * degree + e
-                at = at_ends + e
-                near = jnp.broadcast_to(around[at_blocks : at_blocks + 1, e : e + 1], (1, size))
-                to = rows == around[at : at + 1, :]
-                hit = columns == upright[:, at : at + 1]
-                picked = mm((hit & (near == 0)).astype(BF16), own)
-                pre[edge] = recv[rows_of(q), :] + picked
-                for r in range(rounds):
-                    far_pick[rows_of(edge), r * size : (r + 1) * size] = (hit & (near == 1 + r)).astype(BF16)
-                for r in range(1 + rounds):
-                    cput[q, r * size : (r + 1) * size, e * size : (e + 1) * size] = (to & (near == r)).astype(BF16)
+        for v in range(doms):
+            for q in range(held):
+                tile_at = v * held + q
+                around = infos_ref[tile_at].astype(I32)
+                upright = jnp.transpose(infos_ref[tile_at]).astype(I32)
+                own = sender[rows_of(q), :]
+                for e in range(degree):
+                    edge = tile_at * degree + e
+                    near = jnp.broadcast_to(around[at_listed : at_listed + 1, e : e + 1], (1, size))
+                    hit = columns == upright[:, e : e + 1]
+                    picked = mm((hit & (near == v)).astype(BF16), own)
+                    pre[edge] = picked + recv[rows_of(q), :] if v == 0 else picked
+                    for i, source in enumerate([n for n in range(doms) if n != v]):
+                        far_pick[rows_of(edge), i * size : (i + 1) * size] = (hit & (near == source)).astype(BF16)
+                    if v == 0:
+                        to = rows == around[e : e + 1, :]
+                        for r in range(doms):
+                            cput[q, r * size : (r + 1) * size, e * size : (e + 1) * size] = (to & (near == r)).astype(BF16)
         for edge in range(edges):
             put[edge] = (rows == ends[edge : edge + 1, :]).astype(BF16)
 
-    pre1, node1, fold, coarse_far, coarse_put, put = run(
+    coarse_edges = doms * held * degree
+    pre1, node1, fold, coarse_far, coarse_put, put, d_out2 = run(
         coarse_prepare,
         [
-            ((held * degree,) + tile, F32), (wide, F32), ((2,) + tile, BF16),
-            ((held * degree * size, far_size), BF16), ((held, size + far_size, degree * size), BF16),
-            ((edges, size, size), BF16),
+            ((coarse_edges,) + tile, F32), (wide, F32), ((2,) + tile, BF16),
+            ((coarse_edges * size, far_size), BF16), ((held, size + far_size, degree * size), BF16),
+            ((edges, size, size), BF16), (fine, F32),
         ],
-        coarse_start, w, bias, tails, ends,
+        coarse_start, w, bias, cot, infos, ends,
         scratch=[pltpu.VMEM(wide, F32), pltpu.VMEM(wide, BF16)],
     )
 
-    def coarse_layer(g0, g1, h_ref, pre, node, far_pick, w_ref, fold_ref, end_ref, slope_ref, node_slope_ref, sum_scr):
-        arrived = [mm(g[...], w_ref[1, 1]).astype(BF16) for g in (g0, g1)]
+    def coarse_layer(other_ref, g0, g1, h_ref, pre, node, far_pick, w_ref, b_ref, fold_ref, end_ref, slope_ref, node_slope_ref, slots_ref, sum_scr):
+        halos = [g[0:at_first, :] for _, g in sorted(zip(ORDER, (g0, g1)))]
+        states = [h_ref[...]] + halos
+        third = (0.5 * mm(other_ref[...], w_ref[1, 1])).astype(BF16)
+        arrived = [(0.5 * mm(g, w_ref[1, 1])).astype(BF16) for g in halos]
+        recvs = [None] + [0.5 * (mm(g, w_ref[1, 0]) + b_ref[1, 0:1, :]) for g in halos]
+        nodes_all = [node[...]] + [0.5 * (mm(g, w_ref[1, 3]) + b_ref[1, 1:2, :]) for g in halos]
+        sources = [arrived, [arrived[0], third], [arrived[1], third]]
+        width = degree * size
         picked = []
-        for q in range(held):
-            senders = jnp.concatenate([a[q * size : (q + 1) * size, :] for a in arrived], axis=0)
-            width = degree * size
-            picked.append(mm(far_pick[q * width : (q + 1) * width, :], senders))
-
-        def pre_of(q, e):
-            return pre[q * degree + e] + picked[q][e * size : (e + 1) * size, :]
-
-        hidden = layer_forward(held, fold_ref[0], pre_of, node, slope_ref, node_slope_ref, sum_scr)
-        end_ref[...] = (h_ref[...].astype(F32) + mm(hidden, w_ref[1, 5])).astype(BF16)
-
-    coarse_end, slope1, node_slope1 = run(
+        for v in range(doms):
+            for q in range(held):
+                at = (v * held + q) * width
+                senders = jnp.concatenate([a[q * size : (q + 1) * size, :] for a in sources[v]], axis=0)
+                picked.append(mm(far_pick[at : at + width, :], senders))
+
+        def pre_of(b, e):
+            v, q = divmod(b, held)
+            value = pre[b * degree + e] + picked[b][e * size : (e + 1) * size, :]
+            return value if v == 0 else value + recvs[v][q * size : (q + 1) * size, :]
+
+        hidden = layer_forward(
+            doms * held, fold_ref[0], pre_of, jnp.concatenate(nodes_all, axis=0), slope_ref, node_slope_ref, sum_scr
+        )
+        state = jnp.concatenate(states, axis=0).astype(F32)
+        end_ref[...] = (state + mm(hidden, w_ref[1, 5])).astype(BF16)
+        for r, g in zip(ORDER, (g0, g1)):
+            slots_ref[r * 8 : (r + 1) * 8, :] = g[at_first + size :, :].astype(F32).astype(I32)[0:8, :]
+
+    coarse_end, slope1, node_slope1, halo_slots = run(
         coarse_layer,
-        [(wide, BF16), ((held * degree,) + tile, BF16), (wide, BF16)],
-        coarse_halo[0], coarse_halo[1], coarse_start, pre1, node1, coarse_far, w, fold,
-        scratch=[pltpu.VMEM(wide, BF16)],
+        [((doms * held * size, features), BF16), ((held * degree,) + tile, BF16), (wide, BF16), ((rounds * 8, features), I32)],
+        other, coarse_halo[0], coarse_halo[1], coarse_start, pre1, node1, coarse_far, w, bias, fold,
+        scratch=[pltpu.VMEM((doms * held * size, features), BF16)],
     )
     coarse_ends = share(coarse_end)
 
-    def lift(s_ref, *refs):
-        parts, first_ref = refs[:sub_size], refs[sub_size]
-        middle_ref, out0, out1, lift_scr = refs[sub_size + 1 :]
+    back_out = [(tile, BF16)] * rounds + [(fine, BF16), (fine, BF16), (tiles, BF16)]
+    back_scratch = [pltpu.VMEM(fine, F32), pltpu.VMEM((everyone,) + tile, F32)]
+
+    def last_layer(s_ref, slots_ref, g0, g1, *refs):
+        parts = refs[:sub_size]
+        first_ref, pick, put, w_ref, b_ref, fold_ref, d_out = refs[sub_size : sub_size + 7]
+        (r0, r1, d_node, d_recv, d_send, hidden_ref, middle_ref,
+         lift_scr, recv, node, sender, send_scr, sum_scr, slope_scr, node_slope_scr, act_scr, acc_scr) = refs[sub_size + 7 :]
         lift_into(parts, s_ref, lift_scr)
         for b in range(blocks):
             lifted = lift_scr[scalar(s_ref, at_pool + b)].astype(F32)
-            middle_ref[b] = (first_ref[rows_of(b), :].astype(F32) + lifted).astype(BF16)
-        for r, out in zip(ORDER, (out0, out1)):
-            out[...] = middle_ref[scalar(s_ref, r)]
-
-    middle, *middle_sends = run(
-        lift,
-        [(tiles, BF16)] + [(tile, BF16)] * rounds,
-        table, *coarse_ends, first,
-        scratch=[pltpu.VMEM((slots,) + tile, BF16)],
-    )
-    middle = middle.reshape(fine)
-    halo = exchange(middle_sends)
-
-    def last_prepare(h_ref, w_ref, b_ref, cot_ref, recv, node, sender, d_out):
-        own_into(h_ref[...], 2, w_ref, b_ref, recv, node, sender)
-        d_out[...] = mm_t(cot_ref[...], w_ref[2, 5])
-
-    recv2, node2, sender2, d_out2 = run(last_prepare, own_out + [(fine, F32)], middle, w, bias, cot)
-
-    back_out = [(tile, BF16)] * rounds + [(fine, BF16), (fine, BF16), (tiles, BF16)]
-    back_scratch = [pltpu.VMEM(fine, F32), pltpu.VMEM((everyone,) + tile, F32)]
-
-    def last_layer(s_ref, g0, g1, recv, node, sender, pick, put, w_ref, fold_ref, d_out,
-                   r0, r1, d_node, d_recv, d_send, hidden_ref,
-                   send_scr, sum_scr, slope_scr, node_slope_scr, act_scr, acc_scr):
-        senders_into(sender, (g0, g1), 2, w_ref, send_scr)
+            middle_ref[rows_of(b), :] = (first_ref[rows_of(b), :].astype(F32) + lifted).astype(BF16)
+        halos = []
+        for r, g in zip(ORDER, (g0, g1)):
+            lifted = lift_scr[(1 + r) * slots + scalar(slots_ref, r * 8)].astype(F32)
+            halos.append((g[at_first : at_first + size, :].astype(F32) + lifted).astype(BF16))
+        own_into(middle_ref[...], 2, w_ref, b_ref, recv, node, sender)
+        senders_into(sender, halos, 2, w_ref, send_scr)
         fold = fold_ref[1]
         pre_of = fine_pre(s_ref, recv, pick, send_scr)
-        hidden_ref[...] = layer_forward(blocks, fold, pre_of, node, slope_scr, node_slope_scr, sum_scr)
+        hidden_ref[...] = layer_forward(blocks, fold, pre_of, node[...], slope_scr, node_slope_scr, sum_scr)
         fine_backward(d_out[...], s_ref, fold, put, slope_scr, node_slope_scr, d_node, d_recv, act_scr, acc_scr)
         halo_grads_into((r0, r1), [acc_scr[blocks:].reshape(far_size, features)], 2, w_ref)
         d_send[...] = acc_scr[0:blocks].astype(BF16)
 
-    *halo_grads, d_node, d_recv, d_send, hidden2 = run(
+    *halo_grads, d_node, d_recv, d_send, hidden2, middle = run(
         last_layer,
-        back_out + [(fine, BF16)],
-        table, halo[0], halo[1], recv2, node2, sender2, pick, put, w, fold, d_out2,
-        scratch=layer_scratch + [pltpu.VMEM((edges,) + tile, BF16), pltpu.VMEM(fine, BF16)] + back_scratch,
+        back_out + [(fine, BF16), (fine, BF16)],
+        table, halo_slots, *coarse_halo, *coarse_ends, first, pick, put, w, bias, fold, d_out2,
+        scratch=[pltpu.VMEM((doms * slots,) + tile, BF16)]
+        + [pltpu.VMEM(fine, F32), pltpu.VMEM(fine, F32), pltpu.VMEM(fine, BF16)]
+        + layer_scratch + [pltpu.VMEM((edges,) + tile, BF16), pltpu.VMEM(fine, BF16)] + back_scratch,
     )
     returned = exchange(halo_grads)
 
@@ -451,7 +480,7 @@
         for r, arrived in zip(ORDER, (r0, r1)):
             at = scalar(s_ref, r)
             grad_ref[at] = grad_ref[at] + arrived[...].astype(F32)
-        pooled_into(lambda b: grad_ref[b], s_ref, sends, None)
+        pooled_into(lambda b: grad_ref[b], s_ref, sends, False)
 
     grad_middle, *grad_sends = run(
         pool_grads,

time: 57.7 us -> 57.3 us (level)
  starting transfers between devices: 24.9 us -> 20 us
  waiting for transfers between devices: 20.9 us -> 24.7 us
  Pallas kernels: 10.9 us -> 11.6 us
    ppermute x18 -> x17, starting transfers between devices: 24.9 us -> 20 us  [swapped(): lax.ppermute(value, axis, [(source, source ^ mask) for source in range(si...]
    ppermute x18 -> x17, waiting for transfers between devices: 20.9 us -> 24.7 us  [swapped(): lax.ppermute(value, axis, [(source, source ^ mask) for source in range(si...]
    pallas_call x17 -> x15, Pallas kernels: 8.21 us -> 8.85 us  [run(): pl.pallas_call(kernel, out_shape=[jax.ShapeDtypeStruct(shape, dtype) for...]
  transfers between devices with their start and end apart: 18 -> 17, of which waited for: 17 -> 14; matrix products, arithmetic and copies ran while one was open for 0% -> 0% of each run, Pallas kernels for 7% -> 8%
where the time goes in v5:
time: 57.3 us; the launch traced here: 57.1 us
  waiting for transfers between devices  24.7 us (43%)
  starting transfers between devices  20 us (35%)
  Pallas kernels  11.6 us (20%)
  between operations  0.75 us (1%)
    ppermute x17, waiting for transfers between devices, swapped(): lax.ppermute(value, axis, [(source, source ^ mask) for source in range(si...  24.7 us
    ppermute x17, starting transfers between devices, swapped(): lax.ppermute(value, axis, [(source, source ^ mask) for source in range(si...  20 us
    pallas_call x15, Pallas kernels, run(): pl.pallas_call(kernel, out_shape=[jax.ShapeDtypeStruct(shape, dtype) for...  8.85 us
    pallas_call x2, Pallas kernels, run_hbm(): pl.pallas_call(kernel, out_shape=[pltpu.VMEM(shape, dtype) for shape, dty...  2.72 us
  transfers between devices with their start and end apart: 17, of which 14 were waited for; matrix products, arithmetic and copies ran while one was open for 0% of the time, Pallas kernels for 8%

profile of v5, /device:TPU:0, one launch (start us, length us, event | category | flops | bytes accessed | tf_op | source)
XLA Modules:
  0.0 57.1 jit_solution(10434689020163872985)
XLA Ops:
  0.6 1.0 %shard_map.113 = (bf16[512,128]{1,0:T(8,128)(2,1)S(1)}, bf16[16,128]{1,0:T(8,128)(2,1)S(1)}, bf16[144,128]{1,0:T(8,128)(2,1)S(1)}, bf16[144,128]{1,0:T(8,128)(2,1)S(1)}) custom-call(s32[1,2]{1,0:T(1,128)} %bitcast.16, s32[4,128]{1,0:T(4,128)} %bitcast.15, s32[1,4]{1,0:T(1,128)} %listed_in.1, bf16[512,128]{1,0:T(8,128)(2,1)} %nodes_in.1), custom_call_target="tpu_custom_call" | custom-call | bytes 1048576 | tf_op jit(solution)/shard_map/pallas_call | solution.py:46
  1.7 4.1 %collective-permute-start = (bf16[144,128]{1,0:T(8,128)(2,1)S(1)}, bf16[144,128]{1,0:T(8,128)(2,1)S(1)}, u32[]{:S(2)}, u32[]{:S(2)}) collective-permute-start(bf16[144,128]{1,0:T(8,128)(2,1)S(1)} %get-tuple-element.64), channel_id=1, source_target_pairs={{0,8},{4,12},{8,0},{12,4},{1,9},{5,13},{9,1},{13,5},{2,10},{6,14},... | collective-permute-start | bytes 110600 | tf_op jit(solution)/shard_map/ppermute | solution.py:18
  5.8 1.6 %collective-permute-start.1 = (bf16[144,128]{1,0:T(8,128)(2,1)S(1)}, bf16[144,128]{1,0:T(8,128)(2,1)S(1)}, u32[]{:S(2)}, u32[]{:S(2)}) collective-permute-start(bf16[144,128]{1,0:T(8,128)(2,1)S(1)} %get-tuple-element.65), channel_id=1, source_target_pairs={{0,4},{4,0},{8,12},{12,8},{1,5},{5,1},{9,13},{13,9},{2,6},{6,2},{1... | collective-permute-start | bytes 110600 | tf_op jit(solution)/shard_map/ppermute | solution.py:18
  7.3 1.7 %shard_map.114 = (s32[16,128]{1,0:T(8,128)S(1)}, bf16[3,6,128,128]{3,2,1,0:T(8,128)(2,1)S(1)}, f32[3,2,128]{2,1,0:T(2,128)S(1)}, bf16[512,128]{1,0:T(8,128)(2,1)...) custom-call(s32[1,2]{1,0:T(1,128)} %bitcast.17, ...), custom_call_target="tpu_custom_call" | custom-call | bytes 1048576 | tf_op jit(solution)/shard_map/pallas_call | solution.py:46
  9.0 0.0 collective-permute-done.g0
  9.1 0.7 %collective-permute-done.1.g1 = bf16[144,128]{1,0:T(8,128)(2,1)S(1)} collective-permute-done((bf16[144,128]{1,0:T(8,128)(2,1)S(1)}, bf16[144,128]{1,0:T(8,128)(2,1)S(1)}, u32[]{:S(2)}, u32[]{:S(2)}) %collective-permute-start.1) | collective-permute-done | bytes 36896 | tf_op jit(solution)/shard_map/ppermute | solution.py:18
  9.7 0.9 %shard_map.115 = (bf16[512,128]{1,0:T(8,128)(2,1)S(1)}, bf16[16,128,128]{2,1,0:T(8,128)(2,1)S(1)}, bf16[512,128]{1,0:T(8,128)(2,1)S(1)}, bf16[320,128]{1,0:T(8,128)(2,1)S(1)}, bf16[272,128]{1,0:T(8,128)(2,1)S(1)}) custom-call(s32[32,128]{1,0:T(8,128)S(1)} %get-tuple-element.63.s_ref, bf16[144,128]{1,0:T(8,128)(2,1)S(1)} %collective-permute-done.g0, ...), custom_call_target="tpu_custom_call" | custom-call | bytes 1048576 | tf_op jit(solution)/shard_map/pallas_call | solution.py:34
  10.7 0.1 collective-permute-start.2
  10.7 1.2 %collective-permute-done.2.refs_1_ = bf16[272,128]{1,0:T(8,128)(2,1)S(1)} collective-permute-done((bf16[272,128]{1,0:T(8,128)(2,1)S(1)}, bf16[272,128]{1,0:T(8,128)(2,1)S(1)}, u32[]{:S(2)}, u32[]{:S(2)}) %collective-permute-start.2) | collective-permute-done | bytes 69664 | tf_op jit(solution)/shard_map/ppermute | solution.py:18
  12.0 1.6 %collective-permute-start.3 = (bf16[320,128]{1,0:T(8,128)(2,1)S(1)}, bf16[320,128]{1,0:T(8,128)(2,1)S(1)}, u32[]{:S(2)}, u32[]{:S(2)}) collective-permute-start(bf16[320,128]{1,0:T(8,128)(2,1)S(1)} %shard_map.116.refs_0_), channel_id=1, source_target_pairs={{0,2},{2,0},{1,3},{3,1},{4,6},{6,4},{5,7},{7,5},{8,10},{10,8},{9,1... | collective-permute-start | bytes 245768 | tf_op jit(solution)/shard_map/ppermute | solution.py:18
  13.6 3.0 %collective-permute-done.3.refs_1_ = bf16[320,128]{1,0:T(8,128)(2,1)S(1)} collective-permute-done((bf16[320,128]{1,0:T(8,128)(2,1)S(1)}, bf16[320,128]{1,0:T(8,128)(2,1)S(1)}, u32[]{:S(2)}, u32[]{:S(2)}) %collective-permute-start.3) | collective-permute-done | bytes 81952 | tf_op jit(solution)/shard_map/ppermute | solution.py:18
  16.6 0.1 shard_map.117
  16.6 1.2 %collective-permute-start.5 = (bf16[400,128]{1,0:T(8,128)(2,1)S(1)}, bf16[400,128]{1,0:T(8,128)(2,1)S(1)}, u32[]{:S(2)}, u32[]{:S(2)}) collective-permute-start(bf16[400,128]{1,0:T(8,128)(2,1)S(1)} %get-tuple-element.77), channel_id=1, source_target_pairs={{0,8},{4,12},{8,0},{12,4},{1,9},{5,13},{9,1},{13,5},{2,10},{6,14},... | collective-permute-start | bytes 307208 | tf_op jit(solution)/shard_map/ppermute | solution.py:18
  17.8 1.6 %collective-permute-start.6 = (bf16[400,128]{1,0:T(8,128)(2,1)S(1)}, bf16[400,128]{1,0:T(8,128)(2,1)S(1)}, u32[]{:S(2)}, u32[]{:S(2)}) collective-permute-start(bf16[400,128]{1,0:T(8,128)(2,1)S(1)} %get-tuple-element.78), channel_id=1, source_target_pairs={{0,4},{4,0},{8,12},{12,8},{1,5},{5,1},{9,13},{13,9},{2,6},{6,2},{1... | collective-permute-start | bytes 307208 | tf_op jit(solution)/shard_map/ppermute | solution.py:18
  19.5 1.6 %collective-permute-start.4 = (bf16[256,128]{1,0:T(8,128)(2,1)S(1)}, bf16[256,128]{1,0:T(8,128)(2,1)S(1)}, u32[]{:S(2)}, u32[]{:S(2)}) collective-permute-start(bf16[256,128]{1,0:T(8,128)(2,1)S(1)} %get-tuple-element.76), channel_id=1, source_target_pairs={{0,12},{4,8},{8,4},{12,0},{1,13},{5,9},{9,5},{13,1},{2,14},{6,10},... | collective-permute-start | bytes 196616 | tf_op jit(solution)/shard_map/ppermute | solution.py:18
  21.1 1.2 %shard_map.118 = (f32[24,128,128]{2,1,0:T(8,128)S(1)}, f32[256,128]{1,0:T(8,128)S(1)}, bf16[2,128,128]{2,1,0:T(8,128)(2,1)S(1)}, bf16[3072,256]{1,0:T(8,128)(2,1...) custom-call(bf16[256,128]{1,0:T(8,128)(2,1)S(1)} %get-tuple-element.79.h_ref, ...), custom_call_target="tpu_custom_call" | custom-call | bytes 1048576 | tf_op jit(solution)/shard_map/pallas_call | solution.py:34
  22.3 4.2 %collective-permute-done.4.other_ref = bf16[256,128]{1,0:T(8,128)(2,1)S(1)} collective-permute-done((bf16[256,128]{1,0:T(8,128)(2,1)S(1)}, bf16[256,128]{1,0:T(8,128)(2,1)S(1)}, u32[]{:S(2)}, u32[]{:S(2)}) %collective-permute-start.4) | collective-permute-done | bytes 65568 | tf_op jit(solution)/shard_map/ppermute | solution.py:18
  26.5 0.0 collective-permute-done.5.g0
  26.5 0.0 collective-permute-done.6.g1
  26.5 1.1 %shard_map.119 = (bf16[768,128]{1,0:T(8,128)(2,1)S(1)}, bf16[8,128,128]{2,1,0:T(8,128)(2,1)S(1)}, bf16[256,128]{1,0:T(8,128)(2,1)S(1)}, s32[16,128]{1,0:T(8,128)S(1)}) custom-call(bf16[256,128]{1,0:T(8,128)(2,1)S(1)} %collective-permute-done.4.other_ref, bf16[400,128]{1,0:T(8,128)(2,1)S(1)} %collective-permute-done.5.g0, ...), custom_call_target="tpu_custom_call" | custom-call | bytes 1048576 | tf_op jit(solution)/shard_map/pallas_call | solution.py:34
  27.6 0.1 collective-permute-start.7
  27.7 1.4 %collective-permute-done.7.refs_1_ = bf16[768,128]{1,0:T(8,128)(2,1)S(1)} collective-permute-done((bf16[768,128]{1,0:T(8,128)(2,1)S(1)}, bf16[768,128]{1,0:T(8,128)(2,1)S(1)}, u32[]{:S(2)}, u32[]{:S(2)}) %collective-permute-start.7) | collective-permute-done | bytes 196640 | tf_op jit(solution)/shard_map/ppermute | solution.py:18
  29.1 1.5 %shard_map.120 = (bf16[128,128]{1,0:T(8,128)(2,1)S(1)}, bf16[128,128]{1,0:T(8,128)(2,1)S(1)}, bf16[512,128]{1,0:T(8,128)(2,1)S(1)}, bf16[512,128]{1,0:T(8,128)(2...) custom-call(s32[32,128]{1,0:T(8,128)S(1)} %get-tuple-element.63.s_ref, ...), custom_call_target="tpu_custom_call" | custom-call | bytes 1048576 | tf_op jit(solution)/shard_map/pallas_call | solution.py:34
  30.7 1.4 %collective-permute-start.8 = (bf16[128,128]{1,0:T(8,128)(2,1)S(1)}, bf16[128,128]{1,0:T(8,128)(2,1)S(1)}, u32[]{:S(2)}, u32[]{:S(2)}) collective-permute-start(bf16[128,128]{1,0:T(8,128)(2,1)S(1)} %get-tuple-element.97), channel_id=1, source_target_pairs={{0,8},{4,12},{8,0},{12,4},{1,9},{5,13},{9,1},{13,5},{2,10},{6,14},... | collective-permute-start | bytes 98312 | tf_op jit(solution)/shard_map/ppermute | solution.py:18
  32.1 0.7 %collective-permute-start.9 = (bf16[128,128]{1,0:T(8,128)(2,1)S(1)}, bf16[128,128]{1,0:T(8,128)(2,1)S(1)}, u32[]{:S(2)}, u32[]{:S(2)}) collective-permute-start(bf16[128,128]{1,0:T(8,128)(2,1)S(1)} %get-tuple-element.98), channel_id=1, source_target_pairs={{0,4},{4,0},{8,12},{12,8},{1,5},{5,1},{9,13},{13,9},{2,6},{6,2},{1... | collective-permute-start | bytes 98312 | tf_op jit(solution)/shard_map/ppermute | solution.py:18
  32.8 1.0 %shard_map.121 = (f32[512,128]{1,0:T(8,128)S(1)}, bf16[512,128]{1,0:T(8,128)(2,1)}) custom-call(bf16[512,128]{1,0:T(8,128)(2,1)S(1)} %get-tuple-element.62.cot_ref, bf16[512,128]{1,0:T(8,128)(2,1)S(1)} %get-tuple-element.91.d_node, bf16[512,128]{1,0:T(8,128)(2,1)S(1)} %get-tuple-element.92.d_recv, bf16[512,128]{1,0:T(8,128)(2,1)S(1)} %bitcast.12, ...), custom_call_target="tpu_custom_call" | custom-call | bytes 1048576 | tf_op jit(solution)/shard_map/pallas_call | solution.py:34
  33.8 2.0 %collective-permute-done.8.r0 = bf16[128,128]{1,0:T(8,128)(2,1)S(1)} collective-permute-done((bf16[128,128]{1,0:T(8,128)(2,1)S(1)}, bf16[128,128]{1,0:T(8,128)(2,1)S(1)}, u32[]{:S(2)}, u32[]{:S(2)}) %collective-permute-start.8) | collective-permute-done | bytes 32800 | tf_op jit(solution)/shard_map/ppermute | solution.py:18
  35.8 0.3 collective-permute-done.9.r1
  36.1 0.1 shard_map.122
  36.2 0.1 collective-permute-start.10
  36.3 1.2 %collective-permute-done.10.refs_1_ = bf16[256,128]{1,0:T(8,128)(2,1)S(1)} collective-permute-done((bf16[256,128]{1,0:T(8,128)(2,1)S(1)}, bf16[256,128]{1,0:T(8,128)(2,1)S(1)}, u32[]{:S(2)}, u32[]{:S(2)}) %collective-permute-start.10) | collective-permute-done | bytes 65568 | tf_op jit(solution)/shard_map/ppermute | solution.py:18
  37.5 1.5 %collective-permute-start.11 = (bf16[256,128]{1,0:T(8,128)(2,1)S(1)}, bf16[256,128]{1,0:T(8,128)(2,1)S(1)}, u32[]{:S(2)}, u32[]{:S(2)}) collective-permute-start(bf16[256,128]{1,0:T(8,128)(2,1)S(1)} %shard_map.123.refs_0_), channel_id=1, source_target_pairs={{0,2},{2,0},{1,3},{3,1},{4,6},{6,4},{5,7},{7,5},{8,10},{10,8},{9,1... | collective-permute-start | bytes 196616 | tf_op jit(solution)/shard_map/ppermute | solution.py:18
  39.1 2.8 %collective-permute-done.11.refs_1_ = bf16[256,128]{1,0:T(8,128)(2,1)S(1)} collective-permute-done((bf16[256,128]{1,0:T(8,128)(2,1)S(1)}, bf16[256,128]{1,0:T(8,128)(2,1)S(1)}, u32[]{:S(2)}, u32[]{:S(2)}) %collective-permute-start.11) | collective-permute-done | bytes 65568 | tf_op jit(solution)/shard_map/ppermute | solution.py:18
  41.9 0.7 %shard_map.124 = (bf16[256,128]{1,0:T(8,128)(2,1)S(1)}, bf16[256,128]{1,0:T(8,128)(2,1)S(1)}, f32[256,128]{1,0:T(8,128)S(1)}, bf16[256,128]{1,0:T(8,128)(2,1)S(1)}, bf16[1024,128]{1,0:T(8,128)(2,1)S(1)}) custom-call(bf16[256,128]{1,0:T(8,128)(2,1)S(1)} %shard_map.123.refs_0_, bf16[256,128]{1,0:T(8,128)(2,1)S(1)} %collective-permute-done.11.refs_1_, ...), custom_call_target="tpu_custom_call" | custom-call | bytes 1048576 | tf_op jit(solution)/shard_map/pallas_call | solution.py:34
  42.6 1.6 %collective-permute-start.12 = (bf16[256,128]{1,0:T(8,128)(2,1)S(1)}, bf16[256,128]{1,0:T(8,128)(2,1)S(1)}, u32[]{:S(2)}, u32[]{:S(2)}) collective-permute-start(bf16[256,128]{1,0:T(8,128)(2,1)S(1)} %get-tuple-element.108), channel_id=1, source_target_pairs={{0,8},{4,12},{8,0},{12,4},{1,9},{5,13},{9,1},{13,5},{2,10},{6,14},... | collective-permute-start | bytes 196616 | tf_op jit(solution)/shard_map/ppermute | solution.py:18
  44.2 0.8 %collective-permute-start.13 = (bf16[256,128]{1,0:T(8,128)(2,1)S(1)}, bf16[256,128]{1,0:T(8,128)(2,1)S(1)}, u32[]{:S(2)}, u32[]{:S(2)}) collective-permute-start(bf16[256,128]{1,0:T(8,128)(2,1)S(1)} %get-tuple-element.109), channel_id=1, source_target_pairs={{0,4},{4,0},{8,12},{12,8},{1,5},{5,1},{9,13},{13,9},{2,6},{6,2},{1... | collective-permute-start | bytes 196616 | tf_op jit(solution)/shard_map/ppermute | solution.py:18
  45.0 0.4 shard_map.125.own_ref
  45.3 3.3 %collective-permute-done.12.r0 = bf16[256,128]{1,0:T(8,128)(2,1)S(1)} collective-permute-done((bf16[256,128]{1,0:T(8,128)(2,1)S(1)}, bf16[256,128]{1,0:T(8,128)(2,1)S(1)}, u32[]{:S(2)}, u32[]{:S(2)}) %collective-permute-start.12) | collective-permute-done | bytes 65568 | tf_op jit(solution)/shard_map/ppermute | solution.py:18
  48.6 0.3 collective-permute-done.13.r1
  49.0 0.1 collective-permute-start.14
  49.0 1.2 %collective-permute-done.14.refs_1_ = bf16[256,128]{1,0:T(8,128)(2,1)S(1)} collective-permute-done((bf16[256,128]{1,0:T(8,128)(2,1)S(1)}, bf16[256,128]{1,0:T(8,128)(2,1)S(1)}, u32[]{:S(2)}, u32[]{:S(2)}) %collective-permute-start.14) | collective-permute-done | bytes 65568 | tf_op jit(solution)/shard_map/ppermute | solution.py:18
  50.3 0.8 %shard_map.127 = (bf16[128,128]{1,0:T(8,128)(2,1)S(1)}, bf16[128,128]{1,0:T(8,128)(2,1)S(1)}, bf16[512,128]{1,0:T(8,128)(2,1)S(1)}, bf16[512,128]{1,0:T(8,128)(2...) custom-call(s32[32,128]{1,0:T(8,128)S(1)} %get-tuple-element.63.s_ref, ...), custom_call_target="tpu_custom_call" | custom-call | bytes 1048576 | tf_op jit(solution)/shard_map/pallas_call | solution.py:34
  51.1 1.0 %collective-permute-start.15 = (bf16[128,128]{1,0:T(8,128)(2,1)S(1)}, bf16[128,128]{1,0:T(8,128)(2,1)S(1)}, u32[]{:S(2)}, u32[]{:S(2)}) collective-permute-start(bf16[128,128]{1,0:T(8,128)(2,1)S(1)} %get-tuple-element.114), channel_id=1, source_target_pairs={{0,8},{4,12},{8,0},{12,4},{1,9},{5,13},{9,1},{13,5},{2,10},{6,14},... | collective-permute-start | bytes 98312 | tf_op jit(solution)/shard_map/ppermute | solution.py:18
  52.0 1.0 %collective-permute-start.16 = (bf16[128,128]{1,0:T(8,128)(2,1)S(1)}, bf16[128,128]{1,0:T(8,128)(2,1)S(1)}, u32[]{:S(2)}, u32[]{:S(2)}) collective-permute-start(bf16[128,128]{1,0:T(8,128)(2,1)S(1)} %get-tuple-element.115), channel_id=1, source_target_pairs={{0,4},{4,0},{8,12},{12,8},{1,5},{5,1},{9,13},{13,9},{2,6},{6,2},{1... | collective-permute-start | bytes 98312 | tf_op jit(solution)/shard_map/ppermute | solution.py:18
  53.0 0.3 shard_map.128
  53.3 2.8 %collective-permute-done.15.r0 = bf16[128,128]{1,0:T(8,128)(2,1)S(1)} collective-permute-done((bf16[128,128]{1,0:T(8,128)(2,1)S(1)}, bf16[128,128]{1,0:T(8,128)(2,1)S(1)}, u32[]{:S(2)}, u32[]{:S(2)}) %collective-permute-start.15) | collective-permute-done | bytes 32800 | tf_op jit(solution)/shard_map/ppermute | solution.py:18
  56.1 0.2 collective-permute-done.16.r1
  56.3 0.8 %shard_map.129 = f32[4,128,128]{2,1,0:T(8,128)} custom-call(s32[32,128]{1,0:T(8,128)S(1)} %get-tuple-element.63.s_ref, bf16[128,128]{1,0:T(8,128)(2,1)S(1)} %collective-permute-done.15.r0, bf16[128,128]{1,0:T(8,128)(2,1)S(1)} %collective-permute-done.16.r1, f32[4,128,128]{2,1,0:T(8,128)S(1)} %bitcast.9), custom_call_target="tpu_custom_call" | custom-call | bytes 1048576 | tf_op jit(solution)/shard_map/pallas_call | solution.py:34
  (3 shorter events, 0.1 us)
Async XLA Ops:
  1.7 7.4 %collective-permute-start = (bf16[144,128]{1,0:T(8,128)(2,1)S(1)}, bf16[144,128]{1,0:T(8,128)(2,1)S(1)}, u32[]{:S(2)}, u32[]{:S(2)}) collective-permute-start(bf16[144,128]{1,0:T(8,128)(2,1)S(1)} %get-tuple-element.64), channel_id=1, source_target_pairs={{0,8},{4,12},{8,0},{12,4},{1,9},{5,13},{9,1},{13,5},{2,10},{6,14},... | collective-permute-start | bytes 110600 | tf_op jit(solution)/shard_map/ppermute | solution.py:18
  5.8 4.0 %collective-permute-start.1 = (bf16[144,128]{1,0:T(8,128)(2,1)S(1)}, bf16[144,128]{1,0:T(8,128)(2,1)S(1)}, u32[]{:S(2)}, u32[]{:S(2)}) collective-permute-start(bf16[144,128]{1,0:T(8,128)(2,1)S(1)} %get-tuple-element.65), channel_id=1, source_target_pairs={{0,4},{4,0},{8,12},{12,8},{1,5},{5,1},{9,13},{13,9},{2,6},{6,2},{1... | collective-permute-start | bytes 110600 | tf_op jit(solution)/shard_map/ppermute | solution.py:18
  10.7 1.3 %collective-permute-start.2 = (bf16[272,128]{1,0:T(8,128)(2,1)S(1)}, bf16[272,128]{1,0:T(8,128)(2,1)S(1)}, u32[]{:S(2)}, u32[]{:S(2)}) collective-permute-start(bf16[272,128]{1,0:T(8,128)(2,1)S(1)} %get-tuple-element.75), channel_id=1, source_target_pairs={{0,1},{1,0},{2,3},{3,2},{4,5},{5,4},{6,7},{7,6},{8,9},{9,8},{10,11... | collective-permute-start | bytes 208904 | tf_op jit(solution)/shard_map/ppermute | solution.py:18
  12.0 4.6 %collective-permute-start.3 = (bf16[320,128]{1,0:T(8,128)(2,1)S(1)}, bf16[320,128]{1,0:T(8,128)(2,1)S(1)}, u32[]{:S(2)}, u32[]{:S(2)}) collective-permute-start(bf16[320,128]{1,0:T(8,128)(2,1)S(1)} %shard_map.116.refs_0_), channel_id=1, source_target_pairs={{0,2},{2,0},{1,3},{3,1},{4,6},{6,4},{5,7},{7,5},{8,10},{10,8},{9,1... | collective-permute-start | bytes 245768 | tf_op jit(solution)/shard_map/ppermute | solution.py:18
  16.6 9.9 %collective-permute-start.5 = (bf16[400,128]{1,0:T(8,128)(2,1)S(1)}, bf16[400,128]{1,0:T(8,128)(2,1)S(1)}, u32[]{:S(2)}, u32[]{:S(2)}) collective-permute-start(bf16[400,128]{1,0:T(8,128)(2,1)S(1)} %get-tuple-element.77), channel_id=1, source_target_pairs={{0,8},{4,12},{8,0},{12,4},{1,9},{5,13},{9,1},{13,5},{2,10},{6,14},... | collective-permute-start | bytes 307208 | tf_op jit(solution)/shard_map/ppermute | solution.py:18
  17.8 8.7 %collective-permute-start.6 = (bf16[400,128]{1,0:T(8,128)(2,1)S(1)}, bf16[400,128]{1,0:T(8,128)(2,1)S(1)}, u32[]{:S(2)}, u32[]{:S(2)}) collective-permute-start(bf16[400,128]{1,0:T(8,128)(2,1)S(1)} %get-tuple-element.78), channel_id=1, source_target_pairs={{0,4},{4,0},{8,12},{12,8},{1,5},{5,1},{9,13},{13,9},{2,6},{6,2},{1... | collective-permute-start | bytes 307208 | tf_op jit(solution)/shard_map/ppermute | solution.py:18
  19.5 7.1 %collective-permute-start.4 = (bf16[256,128]{1,0:T(8,128)(2,1)S(1)}, bf16[256,128]{1,0:T(8,128)(2,1)S(1)}, u32[]{:S(2)}, u32[]{:S(2)}) collective-permute-start(bf16[256,128]{1,0:T(8,128)(2,1)S(1)} %get-tuple-element.76), channel_id=1, source_target_pairs={{0,12},{4,8},{8,4},{12,0},{1,13},{5,9},{9,5},{13,1},{2,14},{6,10},... | collective-permute-start | bytes 196616 | tf_op jit(solution)/shard_map/ppermute | solution.py:18
  27.6 1.5 %collective-permute-start.7 = (bf16[768,128]{1,0:T(8,128)(2,1)S(1)}, bf16[768,128]{1,0:T(8,128)(2,1)S(1)}, u32[]{:S(2)}, u32[]{:S(2)}) collective-permute-start(bf16[768,128]{1,0:T(8,128)(2,1)S(1)} %get-tuple-element.88.refs_0_), channel_id=1, source_target_pairs={{0,1},{1,0},{2,3},{3,2},{4,5},{5,4},{6,7},{7,6},{8,9},{9,8},{10,11... | collective-permute-start | bytes 589832 | tf_op jit(solution)/shard_map/ppermute | solution.py:18
  30.7 5.1 %collective-permute-start.8 = (bf16[128,128]{1,0:T(8,128)(2,1)S(1)}, bf16[128,128]{1,0:T(8,128)(2,1)S(1)}, u32[]{:S(2)}, u32[]{:S(2)}) collective-permute-start(bf16[128,128]{1,0:T(8,128)(2,1)S(1)} %get-tuple-element.97), channel_id=1, source_target_pairs={{0,8},{4,12},{8,0},{12,4},{1,9},{5,13},{9,1},{13,5},{2,10},{6,14},... | collective-permute-start | bytes 98312 | tf_op jit(solution)/shard_map/ppermute | solution.py:18
  32.1 4.0 %collective-permute-start.9 = (bf16[128,128]{1,0:T(8,128)(2,1)S(1)}, bf16[128,128]{1,0:T(8,128)(2,1)S(1)}, u32[]{:S(2)}, u32[]{:S(2)}) collective-permute-start(bf16[128,128]{1,0:T(8,128)(2,1)S(1)} %get-tuple-element.98), channel_id=1, source_target_pairs={{0,4},{4,0},{8,12},{12,8},{1,5},{5,1},{9,13},{13,9},{2,6},{6,2},{1... | collective-permute-start | bytes 98312 | tf_op jit(solution)/shard_map/ppermute | solution.py:18
  36.2 1.3 %collective-permute-start.10 = (bf16[256,128]{1,0:T(8,128)(2,1)S(1)}, bf16[256,128]{1,0:T(8,128)(2,1)S(1)}, u32[]{:S(2)}, u32[]{:S(2)}) collective-permute-start(bf16[256,128]{1,0:T(8,128)(2,1)S(1)} %get-tuple-element.101), channel_id=1, source_target_pairs={{0,1},{1,0},{2,3},{3,2},{4,5},{5,4},{6,7},{7,6},{8,9},{9,8},{10,11... | collective-permute-start | bytes 196616 | tf_op jit(solution)/shard_map/ppermute | solution.py:18
  37.5 4.3 %collective-permute-start.11 = (bf16[256,128]{1,0:T(8,128)(2,1)S(1)}, bf16[256,128]{1,0:T(8,128)(2,1)S(1)}, u32[]{:S(2)}, u32[]{:S(2)}) collective-permute-start(bf16[256,128]{1,0:T(8,128)(2,1)S(1)} %shard_map.123.refs_0_), channel_id=1, source_target_pairs={{0,2},{2,0},{1,3},{3,1},{4,6},{6,4},{5,7},{7,5},{8,10},{10,8},{9,1... | collective-permute-start | bytes 196616 | tf_op jit(solution)/shard_map/ppermute | solution.py:18
  42.6 6.0 %collective-permute-start.12 = (bf16[256,128]{1,0:T(8,128)(2,1)S(1)}, bf16[256,128]{1,0:T(8,128)(2,1)S(1)}, u32[]{:S(2)}, u32[]{:S(2)}) collective-permute-start(bf16[256,128]{1,0:T(8,128)(2,1)S(1)} %get-tuple-element.108), channel_id=1, source_target_pairs={{0,8},{4,12},{8,0},{12,4},{1,9},{5,13},{9,1},{13,5},{2,10},{6,14},... | collective-permute-start | bytes 196616 | tf_op jit(solution)/shard_map/ppermute | solution.py:18
  44.2 4.8 %collective-permute-start.13 = (bf16[256,128]{1,0:T(8,128)(2,1)S(1)}, bf16[256,128]{1,0:T(8,128)(2,1)S(1)}, u32[]{:S(2)}, u32[]{:S(2)}) collective-permute-start(bf16[256,128]{1,0:T(8,128)(2,1)S(1)} %get-tuple-element.109), channel_id=1, source_target_pairs={{0,4},{4,0},{8,12},{12,8},{1,5},{5,1},{9,13},{13,9},{2,6},{6,2},{1... | collective-permute-start | bytes 196616 | tf_op jit(solution)/shard_map/ppermute | solution.py:18
  49.0 1.3 %collective-permute-start.14 = (bf16[256,128]{1,0:T(8,128)(2,1)S(1)}, bf16[256,128]{1,0:T(8,128)(2,1)S(1)}, u32[]{:S(2)}, u32[]{:S(2)}) collective-permute-start(bf16[256,128]{1,0:T(8,128)(2,1)S(1)} %shard_map.126.refs_0_), channel_id=1, source_target_pairs={{0,1},{1,0},{2,3},{3,2},{4,5},{5,4},{6,7},{7,6},{8,9},{9,8},{10,11... | collective-permute-start | bytes 196616 | tf_op jit(solution)/shard_map/ppermute | solution.py:18
  51.1 5.1 %collective-permute-start.15 = (bf16[128,128]{1,0:T(8,128)(2,1)S(1)}, bf16[128,128]{1,0:T(8,128)(2,1)S(1)}, u32[]{:S(2)}, u32[]{:S(2)}) collective-permute-start(bf16[128,128]{1,0:T(8,128)(2,1)S(1)} %get-tuple-element.114), channel_id=1, source_target_pairs={{0,8},{4,12},{8,0},{12,4},{1,9},{5,13},{9,1},{13,5},{2,10},{6,14},... | collective-permute-start | bytes 98312 | tf_op jit(solution)/shard_map/ppermute | solution.py:18
  52.0 4.3 %collective-permute-start.16 = (bf16[128,128]{1,0:T(8,128)(2,1)S(1)}, bf16[128,128]{1,0:T(8,128)(2,1)S(1)}, u32[]{:S(2)}, u32[]{:S(2)}) collective-permute-start(bf16[128,128]{1,0:T(8,128)(2,1)S(1)} %get-tuple-element.115), channel_id=1, source_target_pairs={{0,4},{4,0},{8,12},{12,8},{1,5},{5,1},{9,13},{13,9},{2,6},{6,2},{1... | collective-permute-start | bytes 98312 | tf_op jit(solution)/shard_map/ppermute | solution.py:18

commit v6 on v5

--- a/solution.py
+++ b/solution.py
@@ -81,18 +81,18 @@
 
     held = pair_size
     wide = (held * size, features)
-    at_listed = degree
     doms = 1 + rounds
-    at_info = held * size + TAIL
-    pool_rows = at_info + doms * TAIL
-    at_first = held * size
-    halo_rows = at_first + size + TAIL
+    listed_rows = degree + 1
+    at_last = doms * listed_rows
+    at_tail = held * size
+    pool_rows = at_tail + TAIL
+    halo_rows = at_tail + size
+
     at_near = rounds
     at_pool = at_near + edges
     at_pair = at_pool + blocks
     at_sub = at_pair + 1
-    at_sent = at_sub + 1
-    table_rows = -(-(at_sent + rounds) // 8) * 8
+    table_rows = -(-(at_sub + 1) // 8) * 8
 
     def exchange(pieces):
         return [swapped(piece, "dom", xor_bits[r]) for r, piece in zip(ORDER, pieces)]
@@ -103,14 +103,10 @@
         return [chip] + [swapped(chip, "pair", mask) for mask in range(1, pair_size)]
 
     def add_parts(*refs):
-        own, out = refs[0], refs[-1]
-        shared = refs[1].shape[0] if len(refs) > 2 else own.shape[0]
-        total = own[0:shared, :].astype(F32)
+        total = refs[0][...].astype(F32)
         for part in refs[1:-1]:
             total = total + part[...].astype(F32)
-        out[0:shared, :] = total.astype(BF16)
-        if shared < own.shape[0]:
-            out[shared:, :] = own[shared:, :]
+        refs[-1][...] = total.astype(BF16)
 
     def share(piece):
         return [piece] + [swapped(piece, "sub", mask) for mask in range(1, sub_size)]
@@ -125,29 +121,41 @@
         for copy in copies:
             copy.wait()
 
-    def choose(send_in, ends_in, listed_in, nodes_in, h_ref, info_ref, out0, out1, send_scr, ends_scr, listed_scr, sems):
+    def choose(send_in, ends_in, listed_in, pool_in, nodes_in, h_ref, info_ref, out0, out1,
+               send_scr, ends_scr, listed_scr, pool_scr, sems):
         parts = [(nodes_in.at[rows_of(b)], h_ref.at[rows_of(b)]) for b in range(blocks)]
-        fetch([(send_in, send_scr), (ends_in, ends_scr), (listed_in, listed_scr)] + parts, sems)
+        fetch([(send_in, send_scr), (ends_in, ends_scr), (listed_in, listed_scr), (pool_in, pool_scr)] + parts, sems)
         lanes = lax.broadcasted_iota(I32, (1, features), 1)
         listed = jnp.zeros((1, features), I32)
         for e in range(degree):
             listed = jnp.where(lanes == e, jnp.broadcast_to(listed_scr[0:1, e : e + 1], (1, features)), listed)
-        rest = jnp.zeros((TAIL - degree - 1, features), F32)
-        info = jnp.concatenate([ends_scr[...].astype(F32), listed.astype(F32), rest], axis=0).astype(BF16)
-        info_ref[...] = info
+        listed = [ends_scr[...].astype(F32), listed.astype(F32)]
+
+        def tail_of(v, last):
+            before = [jnp.zeros((v * listed_rows, features), F32)] if v else []
+            left = TAIL - 1 - (v + 1) * listed_rows
+            after = [jnp.zeros((left, features), F32)] if left else []
+            return jnp.concatenate(before + listed + after + [last.astype(F32)], axis=0).astype(BF16)
+
+        info_ref[...] = tail_of(0, jnp.zeros((1, features), I32))
         for r, out in zip(ORDER, (out0, out1)):
-            at = pl.multiple_of(send_scr[0:1, r : r + 1][0, 0] * size, size)
+            chosen = send_scr[0:1, r : r + 1]
+            at = pl.multiple_of(chosen[0, 0] * size, size)
             out[0:size, :] = h_ref[pl.ds(at, size), :]
-            out[size:, :] = info
+            slot = jnp.zeros((1, 1), I32)
+            for b in range(blocks):
+                slot = jnp.where(chosen == b, pool_scr[0:1, b : b + 1], slot)
+            out[size:, :] = tail_of(1 + r, jnp.broadcast_to(slot, (1, features)))
 
     sent = send_blocks.reshape(1, rounds)
     coarse_ends = coarse_nodes.reshape(degree, size)
+    pools = pool_map.reshape(1, blocks)
     h0, info, *first_sends = run_hbm(
         choose,
         [(fine, BF16), ((TAIL, features), BF16)] + [((size + TAIL, features), BF16)] * rounds,
-        [sent, coarse_ends, coarse_blocks, nodes],
-        scratch=[pltpu.VMEM(a.shape, I32) for a in (sent, coarse_ends, coarse_blocks)]
-        + [pltpu.SemaphoreType.DMA((3 + blocks,))],
+        [sent, coarse_ends, coarse_blocks, pools, nodes],
+        scratch=[pltpu.VMEM(a.shape, I32) for a in (sent, coarse_ends, coarse_blocks, pools)]
+        + [pltpu.SemaphoreType.DMA((4 + blocks,))],
     )
     halo = exchange(first_sends)
 
@@ -223,11 +231,11 @@
             + mm_t(d_send.astype(BF16), w_ref[layer, 1])
         )
 
-    def pooled_into(read, s_ref, out_refs, with_count):
+    def pooled_into(read, s_ref, out_refs, tail=None):
         sub = scalar(s_ref, at_sub)
-        rows = lax.broadcasted_iota(I32, (TAIL, features), 0)
+        lanes = lax.broadcasted_iota(I32, (1, features), 1)
         for sub_mask, out in enumerate(out_refs):
-            counts = jnp.zeros((TAIL, features), F32)
+            counts = jnp.zeros((1, features), F32)
             for q in range(held):
                 slot = q * sub_size + (sub ^ sub_mask)
                 total, count = None, None
@@ -237,9 +245,11 @@
                     total = part if total is None else total + part
                     count = hit if count is None else count + hit
                 out[rows_of(q), :] = total.astype(BF16)
-                counts = counts + jnp.where(rows == q, count, 0.0)
-            if with_count:
-                out[held * size : at_info, :] = counts.astype(BF16)
+                counts = counts + jnp.where(lanes == q, count, 0.0)
+            if tail is not None:
+                last = lax.broadcasted_iota(I32, (TAIL, features), 0) == at_last
+                kept = tail if sub_mask == 0 else jnp.zeros_like(tail)
+                out[at_tail:, :] = jnp.where(last, jnp.broadcast_to(counts, tail.shape), kept).astype(BF16)
 
     def lift_into(parts, s_ref, lift_scr):
         sub = scalar(s_ref, at_sub)
@@ -251,7 +261,7 @@
     inputs = [
         sent,
         neighbour_blocks,
-        pool_map.reshape(1, blocks),
+        pools,
         neighbour_nodes.reshape(edges, size),
         weights,
         biases,
@@ -276,11 +286,6 @@
             put_row(at_pool + b, pool_scr, 0, b)
         s_ref[at_pair : at_pair + 1, :] = jnp.full((1, features), lax.axis_index("pair"), I32)
         s_ref[at_sub : at_sub + 1, :] = jnp.full((1, features), lax.axis_index("sub"), I32)
-        for r in range(rounds):
-            slot = jnp.zeros((1, features), I32)
-            for b in range(blocks):
-                slot = jnp.where(s_ref[r : r + 1, :] == b, s_ref[at_pool + b : at_pool + b + 1, :], slot)
-            s_ref[at_sent + r : at_sent + r + 1, :] = slot
         own_into(h_ref[...], 0, w_ref, b_ref, recv, node, sender)
         columns = grids()[1]
         upright = jnp.transpose(ends[...])
@@ -306,19 +311,20 @@
     layer_scratch = [pltpu.VMEM((everyone,) + tile, BF16), pltpu.VMEM(fine, BF16)]
 
     def first_layer(s_ref, g0, g1, h_ref, recv, node, sender, pick, w_ref, fold_ref, info_ref, *rest):
-        first_ref, slope_ref, node_slope_ref, *sends, send_scr, sum_scr = rest
+        first_ref, slope_ref, node_slope_ref, slots_ref, *sends, send_scr, sum_scr = rest
         senders_into(sender, (g0[0:size, :], g1[0:size, :]), 0, w_ref, send_scr)
         pre_of = fine_pre(s_ref, recv, pick, send_scr)
         hidden = layer_forward(blocks, fold_ref[...], pre_of, node[...], slope_ref, node_slope_ref, sum_scr)
         first_ref[...] = (h_ref[...].astype(F32) + mm(hidden, w_ref[0, 5])).astype(BF16)
-        pooled_into(lambda b: first_ref[rows_of(b), :].astype(F32), s_ref, sends, True)
-        sends[0][at_info : at_info + TAIL, :] = info_ref[...]
+        tail = info_ref[...].astype(F32) + g0[size:, :].astype(F32) + g1[size:, :].astype(F32)
+        pooled_into(lambda b: first_ref[rows_of(b), :].astype(F32), s_ref, sends, tail)
         for r, g in zip(ORDER, (g0, g1)):
-            sends[0][at_info + (1 + r) * TAIL : at_info + (2 + r) * TAIL, :] = g[size:, :]
-
-    first, slope0, node_slope0, *pool_sends = run(
+            last = g[size:, :].astype(F32).astype(I32)[at_last : at_last + 1, :]
+            slots_ref[r : r + 1, :] = last
+
+    first, slope0, node_slope0, halo_slots, *pool_sends = run(
         first_layer,
-        [(fine, BF16)] + slopes + [((pool_rows, features), BF16)] + [((at_info, features), BF16)] * (sub_size - 1),
+        [(fine, BF16)] + slopes + [((8, features), I32)] + [((pool_rows, features), BF16)] * sub_size,
         table, halo[0], halo[1], h0, recv0, node0, sender0, pick, w, fold0, info,
         scratch=layer_scratch,
     )
@@ -327,29 +333,28 @@
 
     def coarse_begin(s_ref, first_ref, *refs):
         parts, (start_ref, divisor_ref, infos_ref, other, out0, out1) = refs[:pair_size], refs[pair_size:]
-        total = parts[0][0:at_info, :].astype(F32)
-        for part in parts[1:]:
-            total = total + part[0:at_info, :].astype(F32)
-        divisor = jnp.maximum(total[held * size : held * size + 8, :], 1.0)
-        divisor_ref[...] = divisor
+        total = parts[0][0:at_tail, :].astype(F32)
+        tails = [part[at_tail:, :].astype(F32) for part in parts]
+        counts = tails[0][at_last : at_last + 1, :]
+        for part, tail in zip(parts[1:], tails[1:]):
+            total = total + part[0:at_tail, :].astype(F32)
+            counts = counts + tail[at_last : at_last + 1, :]
         for q in range(held):
-            start = (total[q * size : (q + 1) * size, :] / divisor[q : q + 1, :]).astype(BF16)
+            divisor_ref[q : q + 1, :] = jnp.broadcast_to(jnp.maximum(counts[:, q : q + 1], 1.0), (1, features))
+        for q in range(held):
+            start = (total[q * size : (q + 1) * size, :] / divisor_ref[q : q + 1, :]).astype(BF16)
             for out in (start_ref, other, out0, out1):
                 out[rows_of(q), :] = start
         for r, out in zip(ORDER, (out0, out1)):
             at = pl.multiple_of(scalar(s_ref, r) * size, size)
-            out[at_first : at_first + size, :] = first_ref[pl.ds(at, size), :]
-            slot = s_ref[at_sent + r : at_sent + r + 1, :].astype(F32)
-            out[at_first + size :, :] = jnp.broadcast_to(slot, (TAIL, features)).astype(BF16)
+            out[at_tail:, :] = first_ref[pl.ds(at, size), :]
         pair = scalar(s_ref, at_pair)
-        for mask, part in enumerate(parts):
-            for v in range(doms):
-                at = at_info + v * TAIL
-                infos_ref[v * held + (pair ^ mask)] = part[at : at + TAIL, :].astype(F32)
+        for mask, tail in enumerate(tails):
+            infos_ref[pair ^ mask] = tail
 
     coarse_start, divisor, infos, other_send, *halo_sends = run(
         coarse_begin,
-        [(wide, BF16), ((8, features), F32), ((doms * held, TAIL, features), F32), (wide, BF16)]
+        [(wide, BF16), ((8, features), F32), ((held, TAIL, features), F32), (wide, BF16)]
         + [((halo_rows, features), BF16)] * rounds,
         table, first, *pool_in,
     )
@@ -365,13 +370,15 @@
         for v in range(doms):
             for q in range(held):
                 tile_at = v * held + q
-                around = infos_ref[tile_at].astype(I32)
-                upright = jnp.transpose(infos_ref[tile_at]).astype(I32)
+                around = infos_ref[q].astype(I32)
+                upright = jnp.transpose(infos_ref[q]).astype(I32)
+                listed = (v + 1) * listed_rows - 1
                 own = sender[rows_of(q), :]
                 for e in range(degree):
                     edge = tile_at * degree + e
-                    near = jnp.broadcast_to(around[at_listed : at_listed + 1, e : e + 1], (1, size))
-                    hit = columns == upright[:, e : e + 1]
+                    near = jnp.broadcast_to(around[listed : listed + 1, e : e + 1], (1, size))
+                    at = v * listed_rows + e
+                    hit = columns == upright[:, at : at + 1]
                     picked = mm((hit & (near == v)).astype(BF16), own)
                     pre[edge] = picked + recv[rows_of(q), :] if v == 0 else picked
                     for i, source in enumerate([n for n in range(doms) if n != v]):
@@ -395,8 +402,8 @@
         scratch=[pltpu.VMEM(wide, F32), pltpu.VMEM(wide, BF16)],
     )
 
-    def coarse_layer(other_ref, g0, g1, h_ref, pre, node, far_pick, w_ref, b_ref, fold_ref, end_ref, slope_ref, node_slope_ref, slots_ref, sum_scr):
-        halos = [g[0:at_first, :] for _, g in sorted(zip(ORDER, (g0, g1)))]
+    def coarse_layer(other_ref, g0, g1, h_ref, pre, node, far_pick, w_ref, b_ref, fold_ref, end_ref, slope_ref, node_slope_ref, sum_scr):
+        halos = [g[0:at_tail, :] for _, g in sorted(zip(ORDER, (g0, g1)))]
         states = [h_ref[...]] + halos
         third = (0.5 * mm(other_ref[...], w_ref[1, 1])).astype(BF16)
         arrived = [(0.5 * mm(g, w_ref[1, 1])).astype(BF16) for g in halos]
@@ -421,12 +428,9 @@
         )
         state = jnp.concatenate(states, axis=0).astype(F32)
         end_ref[...] = (state + mm(hidden, w_ref[1, 5])).astype(BF16)
-        for r, g in zip(ORDER, (g0, g1)):
-            slots_ref[r * 8 : (r + 1) * 8, :] = g[at_first + size :, :].astype(F32).astype(I32)[0:8, :]
-
-    coarse_end, slope1, node_slope1, halo_slots = run(
+    coarse_end, slope1, node_slope1 = run(
         coarse_layer,
-        [((doms * held * size, features), BF16), ((held * degree,) + tile, BF16), (wide, BF16), ((rounds * 8, features), I32)],
+        [((doms * held * size, features), BF16), ((held * degree,) + tile, BF16), (wide, BF16)],
         other, coarse_halo[0], coarse_halo[1], coarse_start, pre1, node1, coarse_far, w, bias, fold,
         scratch=[pltpu.VMEM((doms * held * size, features), BF16)],
     )
@@ -446,8 +450,8 @@
             middle_ref[rows_of(b), :] = (first_ref[rows_of(b), :].astype(F32) + lifted).astype(BF16)
         halos = []
         for r, g in zip(ORDER, (g0, g1)):
-            lifted = lift_scr[(1 + r) * slots + scalar(slots_ref, r * 8)].astype(F32)
-            halos.append((g[at_first : at_first + size, :].astype(F32) + lifted).astype(BF16))
+            lifted = lift_scr[(1 + r) * slots + scalar(slots_ref, r)].astype(F32)
+            halos.append((g[at_tail:, :].astype(F32) + lifted).astype(BF16))
         own_into(middle_ref[...], 2, w_ref, b_ref, recv, node, sender)
         senders_into(sender, halos, 2, w_ref, send_scr)
         fold = fold_ref[1]
@@ -480,7 +484,7 @@
         for r, arrived in zip(ORDER, (r0, r1)):
             at = scalar(s_ref, r)
             grad_ref[at] = grad_ref[at] + arrived[...].astype(F32)
-        pooled_into(lambda b: grad_ref[b], s_ref, sends, False)
+        pooled_into(lambda b: grad_ref[b], s_ref, sends)
 
     grad_middle, *grad_sends = run(
         pool_grads,

time: 57.3 us -> 56.7 us (0.990)
  waiting for transfers between devices: 24.7 us -> 24 us
    ppermute x17, waiting for transfers between devices: 24.7 us -> 24 us  [swapped(): lax.ppermute(value, axis, [(source, source ^ mask) for source in range(si...]
where the time goes in v6:
time: 56.7 us; the launch traced here: 56.5 us
  waiting for transfers between devices  24 us (42%)
  starting transfers between devices  20.1 us (35%)
  Pallas kernels  11.6 us (20%)
  between operations  0.75 us (1%)
    ppermute x17, waiting for transfers between devices, swapped(): lax.ppermute(value, axis, [(source, source ^ mask) for source in range(si...  24 us
    ppermute x17, starting transfers between devices, swapped(): lax.ppermute(value, axis, [(source, source ^ mask) for source in range(si...  20.1 us
    pallas_call x15, Pallas kernels, run(): pl.pallas_call(kernel, out_shape=[jax.ShapeDtypeStruct(shape, dtype) for...  8.83 us
    pallas_call x2, Pallas kernels, run_hbm(): pl.pallas_call(kernel, out_shape=[pltpu.VMEM(shape, dtype) for shape, dty...  2.78 us
  transfers between devices with their start and end apart: 17, of which 14 were waited for; matrix products, arithmetic and copies ran while one was open for 0% of the time, Pallas kernels for 8%

profile of v6, /device:TPU:0, one launch (start us, length us, event | category | flops | bytes accessed | tf_op | source)
XLA Modules:
  0.0 56.5 jit_solution(9760982341553201501)
XLA Ops:
  0.6 1.1 %shard_map.113 = (bf16[512,128]{1,0:T(8,128)(2,1)S(1)}, bf16[16,128]{1,0:T(8,128)(2,1)S(1)}, bf16[144,128]{1,0:T(8,128)(2,1)S(1)}, bf16[144,128]{1,0:T(8,128)(2,1)S(1)}) custom-call(s32[1,2]{1,0:T(1,128)} %bitcast.16, s32[4,128]{1,0:T(4,128)} %bitcast.15, s32[1,4]{1,0:T(1,128)} %listed_in.1, s32[1,4]{1,0:T(1,128)} %bitcast.18, bf16[512,128]{1,0:T(8,128)(2,1)} %nodes_in.1), custom_call_target="tpu_custom_call" | custom-call | bytes 1048576 | tf_op jit(solution)/shard_map/pallas_call | solution.py:46
  1.7 4.1 %collective-permute-start = (bf16[144,128]{1,0:T(8,128)(2,1)S(1)}, bf16[144,128]{1,0:T(8,128)(2,1)S(1)}, u32[]{:S(2)}, u32[]{:S(2)}) collective-permute-start(bf16[144,128]{1,0:T(8,128)(2,1)S(1)} %get-tuple-element.64), channel_id=1, source_target_pairs={{0,8},{4,12},{8,0},{12,4},{1,9},{5,13},{9,1},{13,5},{2,10},{6,14},... | collective-permute-start | bytes 110600 | tf_op jit(solution)/shard_map/ppermute | solution.py:18
  5.8 1.6 %collective-permute-start.1 = (bf16[144,128]{1,0:T(8,128)(2,1)S(1)}, bf16[144,128]{1,0:T(8,128)(2,1)S(1)}, u32[]{:S(2)}, u32[]{:S(2)}) collective-permute-start(bf16[144,128]{1,0:T(8,128)(2,1)S(1)} %get-tuple-element.65), channel_id=1, source_target_pairs={{0,4},{4,0},{8,12},{12,8},{1,5},{5,1},{9,13},{13,9},{2,6},{6,2},{1... | collective-permute-start | bytes 110600 | tf_op jit(solution)/shard_map/ppermute | solution.py:18
  7.4 1.7 %shard_map.114 = (s32[16,128]{1,0:T(8,128)S(1)}, bf16[3,6,128,128]{3,2,1,0:T(8,128)(2,1)S(1)}, f32[3,2,128]{2,1,0:T(2,128)S(1)}, bf16[512,128]{1,0:T(8,128)(2,1)...) custom-call(s32[1,2]{1,0:T(1,128)} %bitcast.17, ...), custom_call_target="tpu_custom_call" | custom-call | bytes 1048576 | tf_op jit(solution)/shard_map/pallas_call | solution.py:46
  9.1 0.0 collective-permute-done.g0
  9.1 0.7 %collective-permute-done.1.g1 = bf16[144,128]{1,0:T(8,128)(2,1)S(1)} collective-permute-done((bf16[144,128]{1,0:T(8,128)(2,1)S(1)}, bf16[144,128]{1,0:T(8,128)(2,1)S(1)}, u32[]{:S(2)}, u32[]{:S(2)}) %collective-permute-start.1) | collective-permute-done | bytes 36896 | tf_op jit(solution)/shard_map/ppermute | solution.py:18
  9.8 0.9 %shard_map.115 = (bf16[512,128]{1,0:T(8,128)(2,1)S(1)}, bf16[16,128,128]{2,1,0:T(8,128)(2,1)S(1)}, bf16[512,128]{1,0:T(8,128)(2,1)S(1)}, s32[8,128]{1,0:T(8,128)...) custom-call(s32[24,128]{1,0:T(8,128)S(1)} %get-tuple-element.63.s_ref, ...), custom_call_target="tpu_custom_call" | custom-call | bytes 1048576 | tf_op jit(solution)/shard_map/pallas_call | solution.py:34
  10.7 0.1 collective-permute-start.2
  10.8 1.2 %collective-permute-done.2.refs_1_ = bf16[272,128]{1,0:T(8,128)(2,1)S(1)} collective-permute-done((bf16[272,128]{1,0:T(8,128)(2,1)S(1)}, bf16[272,128]{1,0:T(8,128)(2,1)S(1)}, u32[]{:S(2)}, u32[]{:S(2)}) %collective-permute-start.2) | collective-permute-done | bytes 69664 | tf_op jit(solution)/shard_map/ppermute | solution.py:18
  12.1 1.6 %collective-permute-start.3 = (bf16[272,128]{1,0:T(8,128)(2,1)S(1)}, bf16[272,128]{1,0:T(8,128)(2,1)S(1)}, u32[]{:S(2)}, u32[]{:S(2)}) collective-permute-start(bf16[272,128]{1,0:T(8,128)(2,1)S(1)} %shard_map.116.refs_0_), channel_id=1, source_target_pairs={{0,2},{2,0},{1,3},{3,1},{4,6},{6,4},{5,7},{7,5},{8,10},{10,8},{9,1... | collective-permute-start | bytes 208904 | tf_op jit(solution)/shard_map/ppermute | solution.py:18
  13.6 2.8 %collective-permute-done.3.refs_1_ = bf16[272,128]{1,0:T(8,128)(2,1)S(1)} collective-permute-done((bf16[272,128]{1,0:T(8,128)(2,1)S(1)}, bf16[272,128]{1,0:T(8,128)(2,1)S(1)}, u32[]{:S(2)}, u32[]{:S(2)}) %collective-permute-start.3) | collective-permute-done | bytes 69664 | tf_op jit(solution)/shard_map/ppermute | solution.py:18
  16.5 0.1 shard_map.117
  16.6 1.2 %collective-permute-start.4 = (bf16[384,128]{1,0:T(8,128)(2,1)S(1)}, bf16[384,128]{1,0:T(8,128)(2,1)S(1)}, u32[]{:S(2)}, u32[]{:S(2)}) collective-permute-start(bf16[384,128]{1,0:T(8,128)(2,1)S(1)} %get-tuple-element.77), channel_id=1, source_target_pairs={{0,8},{4,12},{8,0},{12,4},{1,9},{5,13},{9,1},{13,5},{2,10},{6,14},... | collective-permute-start | bytes 294920 | tf_op jit(solution)/shard_map/ppermute | solution.py:18
  17.8 1.6 %collective-permute-start.5 = (bf16[384,128]{1,0:T(8,128)(2,1)S(1)}, bf16[384,128]{1,0:T(8,128)(2,1)S(1)}, u32[]{:S(2)}, u32[]{:S(2)}) collective-permute-start(bf16[384,128]{1,0:T(8,128)(2,1)S(1)} %get-tuple-element.78), channel_id=1, source_target_pairs={{0,4},{4,0},{8,12},{12,8},{1,5},{5,1},{9,13},{13,9},{2,6},{6,2},{1... | collective-permute-start | bytes 294920 | tf_op jit(solution)/shard_map/ppermute | solution.py:18
  19.4 1.6 %collective-permute-start.6 = (bf16[256,128]{1,0:T(8,128)(2,1)S(1)}, bf16[256,128]{1,0:T(8,128)(2,1)S(1)}, u32[]{:S(2)}, u32[]{:S(2)}) collective-permute-start(bf16[256,128]{1,0:T(8,128)(2,1)S(1)} %get-tuple-element.79), channel_id=1, source_target_pairs={{0,12},{4,8},{8,4},{12,0},{1,13},{5,9},{9,5},{13,1},{2,14},{6,10},... | collective-permute-start | bytes 196616 | tf_op jit(solution)/shard_map/ppermute | solution.py:18
  21.0 1.1 %shard_map.118 = (f32[24,128,128]{2,1,0:T(8,128)S(1)}, f32[256,128]{1,0:T(8,128)S(1)}, bf16[2,128,128]{2,1,0:T(8,128)(2,1)S(1)}, bf16[3072,256]{1,0:T(8,128)(2,1...) custom-call(bf16[256,128]{1,0:T(8,128)(2,1)S(1)} %get-tuple-element.80.h_ref, ...), custom_call_target="tpu_custom_call" | custom-call | bytes 1048576 | tf_op jit(solution)/shard_map/pallas_call | solution.py:34
  22.1 3.8 %collective-permute-done.6.other_ref = bf16[256,128]{1,0:T(8,128)(2,1)S(1)} collective-permute-done((bf16[256,128]{1,0:T(8,128)(2,1)S(1)}, bf16[256,128]{1,0:T(8,128)(2,1)S(1)}, u32[]{:S(2)}, u32[]{:S(2)}) %collective-permute-start.6) | collective-permute-done | bytes 65568 | tf_op jit(solution)/shard_map/ppermute | solution.py:18
  25.9 0.0 collective-permute-done.4.g0
  25.9 0.0 collective-permute-done.5.g1
  25.9 1.1 %shard_map.119 = (bf16[768,128]{1,0:T(8,128)(2,1)S(1)}, bf16[8,128,128]{2,1,0:T(8,128)(2,1)S(1)}, bf16[256,128]{1,0:T(8,128)(2,1)S(1)}) custom-call(bf16[256,128]{1,0:T(8,128)(2,1)S(1)} %collective-permute-done.6.other_ref, bf16[384,128]{1,0:T(8,128)(2,1)S(1)} %collective-permute-done.4.g0, bf16[384,128]{1,0:T(8,128)(2,1)S(1)} %collective-permute-done.5.g1, ...), custom_call_target="tpu_custom_call" | custom-call | bytes 1048576 | tf_op jit(solution)/shard_map/pallas_call | solution.py:34
  27.0 0.1 collective-permute-start.7
  27.1 1.4 %collective-permute-done.7.refs_1_ = bf16[768,128]{1,0:T(8,128)(2,1)S(1)} collective-permute-done((bf16[768,128]{1,0:T(8,128)(2,1)S(1)}, bf16[768,128]{1,0:T(8,128)(2,1)S(1)}, u32[]{:S(2)}, u32[]{:S(2)}) %collective-permute-start.7) | collective-permute-done | bytes 196640 | tf_op jit(solution)/shard_map/ppermute | solution.py:18
  28.5 1.5 %shard_map.120 = (bf16[128,128]{1,0:T(8,128)(2,1)S(1)}, bf16[128,128]{1,0:T(8,128)(2,1)S(1)}, bf16[512,128]{1,0:T(8,128)(2,1)S(1)}, bf16[512,128]{1,0:T(8,128)(2...) custom-call(s32[24,128]{1,0:T(8,128)S(1)} %get-tuple-element.63.s_ref, ...), custom_call_target="tpu_custom_call" | custom-call | bytes 1048576 | tf_op jit(solution)/shard_map/pallas_call | solution.py:34
  30.1 1.4 %collective-permute-start.8 = (bf16[128,128]{1,0:T(8,128)(2,1)S(1)}, bf16[128,128]{1,0:T(8,128)(2,1)S(1)}, u32[]{:S(2)}, u32[]{:S(2)}) collective-permute-start(bf16[128,128]{1,0:T(8,128)(2,1)S(1)} %get-tuple-element.97), channel_id=1, source_target_pairs={{0,8},{4,12},{8,0},{12,4},{1,9},{5,13},{9,1},{13,5},{2,10},{6,14},... | collective-permute-start | bytes 98312 | tf_op jit(solution)/shard_map/ppermute | solution.py:18
  31.5 0.7 %collective-permute-start.9 = (bf16[128,128]{1,0:T(8,128)(2,1)S(1)}, bf16[128,128]{1,0:T(8,128)(2,1)S(1)}, u32[]{:S(2)}, u32[]{:S(2)}) collective-permute-start(bf16[128,128]{1,0:T(8,128)(2,1)S(1)} %get-tuple-element.98), channel_id=1, source_target_pairs={{0,4},{4,0},{8,12},{12,8},{1,5},{5,1},{9,13},{13,9},{2,6},{6,2},{1... | collective-permute-start | bytes 98312 | tf_op jit(solution)/shard_map/ppermute | solution.py:18
  32.3 1.0 %shard_map.121 = (f32[512,128]{1,0:T(8,128)S(1)}, bf16[512,128]{1,0:T(8,128)(2,1)}) custom-call(bf16[512,128]{1,0:T(8,128)(2,1)S(1)} %get-tuple-element.62.cot_ref, bf16[512,128]{1,0:T(8,128)(2,1)S(1)} %get-tuple-element.91.d_node, bf16[512,128]{1,0:T(8,128)(2,1)S(1)} %get-tuple-element.92.d_recv, bf16[512,128]{1,0:T(8,128)(2,1)S(1)} %bitcast.12, ...), custom_call_target="tpu_custom_call" | custom-call | bytes 1048576 | tf_op jit(solution)/shard_map/pallas_call | solution.py:34
  33.2 1.9 %collective-permute-done.8.r0 = bf16[128,128]{1,0:T(8,128)(2,1)S(1)} collective-permute-done((bf16[128,128]{1,0:T(8,128)(2,1)S(1)}, bf16[128,128]{1,0:T(8,128)(2,1)S(1)}, u32[]{:S(2)}, u32[]{:S(2)}) %collective-permute-start.8) | collective-permute-done | bytes 32800 | tf_op jit(solution)/shard_map/ppermute | solution.py:18
  35.2 0.3 collective-permute-done.9.r1
  35.5 0.1 shard_map.122
  35.6 0.1 collective-permute-start.10
  35.7 1.2 %collective-permute-done.10.refs_1_ = bf16[256,128]{1,0:T(8,128)(2,1)S(1)} collective-permute-done((bf16[256,128]{1,0:T(8,128)(2,1)S(1)}, bf16[256,128]{1,0:T(8,128)(2,1)S(1)}, u32[]{:S(2)}, u32[]{:S(2)}) %collective-permute-start.10) | collective-permute-done | bytes 65568 | tf_op jit(solution)/shard_map/ppermute | solution.py:18
  36.9 1.5 %collective-permute-start.11 = (bf16[256,128]{1,0:T(8,128)(2,1)S(1)}, bf16[256,128]{1,0:T(8,128)(2,1)S(1)}, u32[]{:S(2)}, u32[]{:S(2)}) collective-permute-start(bf16[256,128]{1,0:T(8,128)(2,1)S(1)} %shard_map.123.refs_0_), channel_id=1, source_target_pairs={{0,2},{2,0},{1,3},{3,1},{4,6},{6,4},{5,7},{7,5},{8,10},{10,8},{9,1... | collective-permute-start | bytes 196616 | tf_op jit(solution)/shard_map/ppermute | solution.py:18
  38.5 2.8 %collective-permute-done.11.refs_1_ = bf16[256,128]{1,0:T(8,128)(2,1)S(1)} collective-permute-done((bf16[256,128]{1,0:T(8,128)(2,1)S(1)}, bf16[256,128]{1,0:T(8,128)(2,1)S(1)}, u32[]{:S(2)}, u32[]{:S(2)}) %collective-permute-start.11) | collective-permute-done | bytes 65568 | tf_op jit(solution)/shard_map/ppermute | solution.py:18
  41.3 0.7 %shard_map.124 = (bf16[256,128]{1,0:T(8,128)(2,1)S(1)}, bf16[256,128]{1,0:T(8,128)(2,1)S(1)}, f32[256,128]{1,0:T(8,128)S(1)}, bf16[256,128]{1,0:T(8,128)(2,1)S(1)}, bf16[1024,128]{1,0:T(8,128)(2,1)S(1)}) custom-call(bf16[256,128]{1,0:T(8,128)(2,1)S(1)} %shard_map.123.refs_0_, bf16[256,128]{1,0:T(8,128)(2,1)S(1)} %collective-permute-done.11.refs_1_, ...), custom_call_target="tpu_custom_call" | custom-call | bytes 1048576 | tf_op jit(solution)/shard_map/pallas_call | solution.py:34
  42.0 1.6 %collective-permute-start.12 = (bf16[256,128]{1,0:T(8,128)(2,1)S(1)}, bf16[256,128]{1,0:T(8,128)(2,1)S(1)}, u32[]{:S(2)}, u32[]{:S(2)}) collective-permute-start(bf16[256,128]{1,0:T(8,128)(2,1)S(1)} %get-tuple-element.108), channel_id=1, source_target_pairs={{0,8},{4,12},{8,0},{12,4},{1,9},{5,13},{9,1},{13,5},{2,10},{6,14},... | collective-permute-start | bytes 196616 | tf_op jit(solution)/shard_map/ppermute | solution.py:18
  43.6 0.8 %collective-permute-start.13 = (bf16[256,128]{1,0:T(8,128)(2,1)S(1)}, bf16[256,128]{1,0:T(8,128)(2,1)S(1)}, u32[]{:S(2)}, u32[]{:S(2)}) collective-permute-start(bf16[256,128]{1,0:T(8,128)(2,1)S(1)} %get-tuple-element.109), channel_id=1, source_target_pairs={{0,4},{4,0},{8,12},{12,8},{1,5},{5,1},{9,13},{13,9},{2,6},{6,2},{1... | collective-permute-start | bytes 196616 | tf_op jit(solution)/shard_map/ppermute | solution.py:18
  44.4 0.4 shard_map.125.own_ref
  44.7 3.3 %collective-permute-done.12.r0 = bf16[256,128]{1,0:T(8,128)(2,1)S(1)} collective-permute-done((bf16[256,128]{1,0:T(8,128)(2,1)S(1)}, bf16[256,128]{1,0:T(8,128)(2,1)S(1)}, u32[]{:S(2)}, u32[]{:S(2)}) %collective-permute-start.12) | collective-permute-done | bytes 65568 | tf_op jit(solution)/shard_map/ppermute | solution.py:18
  48.0 0.3 collective-permute-done.13.r1
  48.3 0.1 collective-permute-start.14
  48.4 1.2 %collective-permute-done.14.refs_1_ = bf16[256,128]{1,0:T(8,128)(2,1)S(1)} collective-permute-done((bf16[256,128]{1,0:T(8,128)(2,1)S(1)}, bf16[256,128]{1,0:T(8,128)(2,1)S(1)}, u32[]{:S(2)}, u32[]{:S(2)}) %collective-permute-start.14) | collective-permute-done | bytes 65568 | tf_op jit(solution)/shard_map/ppermute | solution.py:18
  49.6 0.8 %shard_map.127 = (bf16[128,128]{1,0:T(8,128)(2,1)S(1)}, bf16[128,128]{1,0:T(8,128)(2,1)S(1)}, bf16[512,128]{1,0:T(8,128)(2,1)S(1)}, bf16[512,128]{1,0:T(8,128)(2...) custom-call(s32[24,128]{1,0:T(8,128)S(1)} %get-tuple-element.63.s_ref, ...), custom_call_target="tpu_custom_call" | custom-call | bytes 1048576 | tf_op jit(solution)/shard_map/pallas_call | solution.py:34
  50.4 1.0 %collective-permute-start.15 = (bf16[128,128]{1,0:T(8,128)(2,1)S(1)}, bf16[128,128]{1,0:T(8,128)(2,1)S(1)}, u32[]{:S(2)}, u32[]{:S(2)}) collective-permute-start(bf16[128,128]{1,0:T(8,128)(2,1)S(1)} %get-tuple-element.114), channel_id=1, source_target_pairs={{0,8},{4,12},{8,0},{12,4},{1,9},{5,13},{9,1},{13,5},{2,10},{6,14},... | collective-permute-start | bytes 98312 | tf_op jit(solution)/shard_map/ppermute | solution.py:18
  51.4 1.0 %collective-permute-start.16 = (bf16[128,128]{1,0:T(8,128)(2,1)S(1)}, bf16[128,128]{1,0:T(8,128)(2,1)S(1)}, u32[]{:S(2)}, u32[]{:S(2)}) collective-permute-start(bf16[128,128]{1,0:T(8,128)(2,1)S(1)} %get-tuple-element.115), channel_id=1, source_target_pairs={{0,4},{4,0},{8,12},{12,8},{1,5},{5,1},{9,13},{13,9},{2,6},{6,2},{1... | collective-permute-start | bytes 98312 | tf_op jit(solution)/shard_map/ppermute | solution.py:18
  52.5 0.3 shard_map.128
  52.7 2.8 %collective-permute-done.15.r0 = bf16[128,128]{1,0:T(8,128)(2,1)S(1)} collective-permute-done((bf16[128,128]{1,0:T(8,128)(2,1)S(1)}, bf16[128,128]{1,0:T(8,128)(2,1)S(1)}, u32[]{:S(2)}, u32[]{:S(2)}) %collective-permute-start.15) | collective-permute-done | bytes 32800 | tf_op jit(solution)/shard_map/ppermute | solution.py:18
  55.6 0.1 collective-permute-done.16.r1
  55.7 0.7 %shard_map.129 = f32[4,128,128]{2,1,0:T(8,128)} custom-call(s32[24,128]{1,0:T(8,128)S(1)} %get-tuple-element.63.s_ref, bf16[128,128]{1,0:T(8,128)(2,1)S(1)} %collective-permute-done.15.r0, bf16[128,128]{1,0:T(8,128)(2,1)S(1)} %collective-permute-done.16.r1, f32[4,128,128]{2,1,0:T(8,128)S(1)} %bitcast.9), custom_call_target="tpu_custom_call" | custom-call | bytes 1048576 | tf_op jit(solution)/shard_map/pallas_call | solution.py:34
  (3 shorter events, 0.1 us)
Async XLA Ops:
  1.7 7.4 %collective-permute-start = (bf16[144,128]{1,0:T(8,128)(2,1)S(1)}, bf16[144,128]{1,0:T(8,128)(2,1)S(1)}, u32[]{:S(2)}, u32[]{:S(2)}) collective-permute-start(bf16[144,128]{1,0:T(8,128)(2,1)S(1)} %get-tuple-element.64), channel_id=1, source_target_pairs={{0,8},{4,12},{8,0},{12,4},{1,9},{5,13},{9,1},{13,5},{2,10},{6,14},... | collective-permute-start | bytes 110600 | tf_op jit(solution)/shard_map/ppermute | solution.py:18
  5.8 4.0 %collective-permute-start.1 = (bf16[144,128]{1,0:T(8,128)(2,1)S(1)}, bf16[144,128]{1,0:T(8,128)(2,1)S(1)}, u32[]{:S(2)}, u32[]{:S(2)}) collective-permute-start(bf16[144,128]{1,0:T(8,128)(2,1)S(1)} %get-tuple-element.65), channel_id=1, source_target_pairs={{0,4},{4,0},{8,12},{12,8},{1,5},{5,1},{9,13},{13,9},{2,6},{6,2},{1... | collective-permute-start | bytes 110600 | tf_op jit(solution)/shard_map/ppermute | solution.py:18
  10.7 1.3 %collective-permute-start.2 = (bf16[272,128]{1,0:T(8,128)(2,1)S(1)}, bf16[272,128]{1,0:T(8,128)(2,1)S(1)}, u32[]{:S(2)}, u32[]{:S(2)}) collective-permute-start(bf16[272,128]{1,0:T(8,128)(2,1)S(1)} %get-tuple-element.76), channel_id=1, source_target_pairs={{0,1},{1,0},{2,3},{3,2},{4,5},{5,4},{6,7},{7,6},{8,9},{9,8},{10,11... | collective-permute-start | bytes 208904 | tf_op jit(solution)/shard_map/ppermute | solution.py:18
  12.1 4.4 %collective-permute-start.3 = (bf16[272,128]{1,0:T(8,128)(2,1)S(1)}, bf16[272,128]{1,0:T(8,128)(2,1)S(1)}, u32[]{:S(2)}, u32[]{:S(2)}) collective-permute-start(bf16[272,128]{1,0:T(8,128)(2,1)S(1)} %shard_map.116.refs_0_), channel_id=1, source_target_pairs={{0,2},{2,0},{1,3},{3,1},{4,6},{6,4},{5,7},{7,5},{8,10},{10,8},{9,1... | collective-permute-start | bytes 208904 | tf_op jit(solution)/shard_map/ppermute | solution.py:18
  16.6 9.4 %collective-permute-start.4 = (bf16[384,128]{1,0:T(8,128)(2,1)S(1)}, bf16[384,128]{1,0:T(8,128)(2,1)S(1)}, u32[]{:S(2)}, u32[]{:S(2)}) collective-permute-start(bf16[384,128]{1,0:T(8,128)(2,1)S(1)} %get-tuple-element.77), channel_id=1, source_target_pairs={{0,8},{4,12},{8,0},{12,4},{1,9},{5,13},{9,1},{13,5},{2,10},{6,14},... | collective-permute-start | bytes 294920 | tf_op jit(solution)/shard_map/ppermute | solution.py:18
  17.8 8.2 %collective-permute-start.5 = (bf16[384,128]{1,0:T(8,128)(2,1)S(1)}, bf16[384,128]{1,0:T(8,128)(2,1)S(1)}, u32[]{:S(2)}, u32[]{:S(2)}) collective-permute-start(bf16[384,128]{1,0:T(8,128)(2,1)S(1)} %get-tuple-element.78), channel_id=1, source_target_pairs={{0,4},{4,0},{8,12},{12,8},{1,5},{5,1},{9,13},{13,9},{2,6},{6,2},{1... | collective-permute-start | bytes 294920 | tf_op jit(solution)/shard_map/ppermute | solution.py:18
  19.4 6.6 %collective-permute-start.6 = (bf16[256,128]{1,0:T(8,128)(2,1)S(1)}, bf16[256,128]{1,0:T(8,128)(2,1)S(1)}, u32[]{:S(2)}, u32[]{:S(2)}) collective-permute-start(bf16[256,128]{1,0:T(8,128)(2,1)S(1)} %get-tuple-element.79), channel_id=1, source_target_pairs={{0,12},{4,8},{8,4},{12,0},{1,13},{5,9},{9,5},{13,1},{2,14},{6,10},... | collective-permute-start | bytes 196616 | tf_op jit(solution)/shard_map/ppermute | solution.py:18
  27.0 1.5 %collective-permute-start.7 = (bf16[768,128]{1,0:T(8,128)(2,1)S(1)}, bf16[768,128]{1,0:T(8,128)(2,1)S(1)}, u32[]{:S(2)}, u32[]{:S(2)}) collective-permute-start(bf16[768,128]{1,0:T(8,128)(2,1)S(1)} %get-tuple-element.88.refs_0_), channel_id=1, source_target_pairs={{0,1},{1,0},{2,3},{3,2},{4,5},{5,4},{6,7},{7,6},{8,9},{9,8},{10,11... | collective-permute-start | bytes 589832 | tf_op jit(solution)/shard_map/ppermute | solution.py:18
  30.1 5.1 %collective-permute-start.8 = (bf16[128,128]{1,0:T(8,128)(2,1)S(1)}, bf16[128,128]{1,0:T(8,128)(2,1)S(1)}, u32[]{:S(2)}, u32[]{:S(2)}) collective-permute-start(bf16[128,128]{1,0:T(8,128)(2,1)S(1)} %get-tuple-element.97), channel_id=1, source_target_pairs={{0,8},{4,12},{8,0},{12,4},{1,9},{5,13},{9,1},{13,5},{2,10},{6,14},... | collective-permute-start | bytes 98312 | tf_op jit(solution)/shard_map/ppermute | solution.py:18
  31.5 4.0 %collective-permute-start.9 = (bf16[128,128]{1,0:T(8,128)(2,1)S(1)}, bf16[128,128]{1,0:T(8,128)(2,1)S(1)}, u32[]{:S(2)}, u32[]{:S(2)}) collective-permute-start(bf16[128,128]{1,0:T(8,128)(2,1)S(1)} %get-tuple-element.98), channel_id=1, source_target_pairs={{0,4},{4,0},{8,12},{12,8},{1,5},{5,1},{9,13},{13,9},{2,6},{6,2},{1... | collective-permute-start | bytes 98312 | tf_op jit(solution)/shard_map/ppermute | solution.py:18
  35.6 1.3 %collective-permute-start.10 = (bf16[256,128]{1,0:T(8,128)(2,1)S(1)}, bf16[256,128]{1,0:T(8,128)(2,1)S(1)}, u32[]{:S(2)}, u32[]{:S(2)}) collective-permute-start(bf16[256,128]{1,0:T(8,128)(2,1)S(1)} %get-tuple-element.101), channel_id=1, source_target_pairs={{0,1},{1,0},{2,3},{3,2},{4,5},{5,4},{6,7},{7,6},{8,9},{9,8},{10,11... | collective-permute-start | bytes 196616 | tf_op jit(solution)/shard_map/ppermute | solution.py:18
  36.9 4.3 %collective-permute-start.11 = (bf16[256,128]{1,0:T(8,128)(2,1)S(1)}, bf16[256,128]{1,0:T(8,128)(2,1)S(1)}, u32[]{:S(2)}, u32[]{:S(2)}) collective-permute-start(bf16[256,128]{1,0:T(8,128)(2,1)S(1)} %shard_map.123.refs_0_), channel_id=1, source_target_pairs={{0,2},{2,0},{1,3},{3,1},{4,6},{6,4},{5,7},{7,5},{8,10},{10,8},{9,1... | collective-permute-start | bytes 196616 | tf_op jit(solution)/shard_map/ppermute | solution.py:18
  42.0 6.0 %collective-permute-start.12 = (bf16[256,128]{1,0:T(8,128)(2,1)S(1)}, bf16[256,128]{1,0:T(8,128)(2,1)S(1)}, u32[]{:S(2)}, u32[]{:S(2)}) collective-permute-start(bf16[256,128]{1,0:T(8,128)(2,1)S(1)} %get-tuple-element.108), channel_id=1, source_target_pairs={{0,8},{4,12},{8,0},{12,4},{1,9},{5,13},{9,1},{13,5},{2,10},{6,14},... | collective-permute-start | bytes 196616 | tf_op jit(solution)/shard_map/ppermute | solution.py:18
  43.6 4.7 %collective-permute-start.13 = (bf16[256,128]{1,0:T(8,128)(2,1)S(1)}, bf16[256,128]{1,0:T(8,128)(2,1)S(1)}, u32[]{:S(2)}, u32[]{:S(2)}) collective-permute-start(bf16[256,128]{1,0:T(8,128)(2,1)S(1)} %get-tuple-element.109), channel_id=1, source_target_pairs={{0,4},{4,0},{8,12},{12,8},{1,5},{5,1},{9,13},{13,9},{2,6},{6,2},{1... | collective-permute-start | bytes 196616 | tf_op jit(solution)/shard_map/ppermute | solution.py:18
  48.3 1.3 %collective-permute-start.14 = (bf16[256,128]{1,0:T(8,128)(2,1)S(1)}, bf16[256,128]{1,0:T(8,128)(2,1)S(1)}, u32[]{:S(2)}, u32[]{:S(2)}) collective-permute-start(bf16[256,128]{1,0:T(8,128)(2,1)S(1)} %shard_map.126.refs_0_), channel_id=1, source_target_pairs={{0,1},{1,0},{2,3},{3,2},{4,5},{5,4},{6,7},{7,6},{8,9},{9,8},{10,11... | collective-permute-start | bytes 196616 | tf_op jit(solution)/shard_map/ppermute | solution.py:18
  50.4 5.1 %collective-permute-start.15 = (bf16[128,128]{1,0:T(8,128)(2,1)S(1)}, bf16[128,128]{1,0:T(8,128)(2,1)S(1)}, u32[]{:S(2)}, u32[]{:S(2)}) collective-permute-start(bf16[128,128]{1,0:T(8,128)(2,1)S(1)} %get-tuple-element.114), channel_id=1, source_target_pairs={{0,8},{4,12},{8,0},{12,4},{1,9},{5,13},{9,1},{13,5},{2,10},{6,14},... | collective-permute-start | bytes 98312 | tf_op jit(solution)/shard_map/ppermute | solution.py:18
  51.4 4.3 %collective-permute-start.16 = (bf16[128,128]{1,0:T(8,128)(2,1)S(1)}, bf16[128,128]{1,0:T(8,128)(2,1)S(1)}, u32[]{:S(2)}, u32[]{:S(2)}) collective-permute-start(bf16[128,128]{1,0:T(8,128)(2,1)S(1)} %get-tuple-element.115), channel_id=1, source_target_pairs={{0,4},{4,0},{8,12},{12,8},{1,5},{5,1},{9,13},{13,9},{2,6},{6,2},{1... | collective-permute-start | bytes 98312 | tf_op jit(solution)/shard_map/ppermute | solution.py:18

commit v7 on v6

--- a/solution.py
+++ b/solution.py
@@ -114,17 +114,23 @@
     def rows_of(b):
         return pl.ds(b * size, size)
 
-    def fetch(pairs, sems):
+    def begun(pairs, sems):
         copies = [pltpu.make_async_copy(source, target, sems.at[i]) for i, (source, target) in enumerate(pairs)]
         for copy in copies:
             copy.start()
-        for copy in copies:
+        return copies
+
+    def fetch(pairs, sems):
+        for copy in begun(pairs, sems):
             copy.wait()
 
     def choose(send_in, ends_in, listed_in, pool_in, nodes_in, h_ref, info_ref, out0, out1,
                send_scr, ends_scr, listed_scr, pool_scr, sems):
         parts = [(nodes_in.at[rows_of(b)], h_ref.at[rows_of(b)]) for b in range(blocks)]
-        fetch([(send_in, send_scr), (ends_in, ends_scr), (listed_in, listed_scr), (pool_in, pool_scr)] + parts, sems)
+        lists = [(send_in, send_scr), (ends_in, ends_scr), (listed_in, listed_scr), (pool_in, pool_scr)]
+        copies = begun(lists + parts, sems)
+        for copy in copies[: len(lists)]:
+            copy.wait()
         lanes = lax.broadcasted_iota(I32, (1, features), 1)
         listed = jnp.zeros((1, features), I32)
         for e in range(degree):
@@ -140,12 +146,15 @@
         info_ref[...] = tail_of(0, jnp.zeros((1, features), I32))
         for r, out in zip(ORDER, (out0, out1)):
             chosen = send_scr[0:1, r : r + 1]
-            at = pl.multiple_of(chosen[0, 0] * size, size)
-            out[0:size, :] = h_ref[pl.ds(at, size), :]
             slot = jnp.zeros((1, 1), I32)
             for b in range(blocks):
                 slot = jnp.where(chosen == b, pool_scr[0:1, b : b + 1], slot)
             out[size:, :] = tail_of(1 + r, jnp.broadcast_to(slot, (1, features)))
+        starts = [pl.multiple_of(send_scr[0:1, r : r + 1][0, 0] * size, size) for r in ORDER]
+        for copy in copies[len(lists) :]:
+            copy.wait()
+        for at, out in zip(starts, (out0, out1)):
+            out[0:size, :] = h_ref[pl.ds(at, size), :]
 
     sent = send_blocks.reshape(1, rounds)
     coarse_ends = coarse_nodes.reshape(degree, size)
@@ -361,10 +370,15 @@
     other = swapped(other_send, "dom", xor_bits[0] ^ xor_bits[1])
     coarse_halo = exchange(halo_sends)
 
-    def coarse_prepare(h_ref, w_ref, b_ref, cot_ref, infos_ref, ends, pre, node, fold_ref, far_pick, cput, put, d_out, recv, sender):
+    def coarse_prepare(h_ref, w_ref, b_ref, cot_ref, infos_ref, ends, pre, node, fold_ref, join_ref, bias_ref,
+                       far_pick, cput, put, d_out, recv, sender):
         own_into(h_ref[...], 1, w_ref, b_ref, recv, node, sender)
         for i, layer in enumerate((1, 2)):
             fold_ref[i] = (mm(w_ref[layer, 2], w_ref[layer, 4]) * (0.5 / degree)).astype(BF16)
+            for j, part in enumerate((0, 3)):
+                columns_j = slice(j * features, (j + 1) * features)
+                join_ref[i, :, columns_j] = w_ref[layer, part] * 0.5
+                bias_ref[i : i + 1, columns_j] = b_ref[layer, j : j + 1, :] * 0.5
         d_out[...] = mm_t(cot_ref[...], w_ref[2, 5])
         rows, columns = grids()
         for v in range(doms):
@@ -391,10 +405,11 @@
             put[edge] = (rows == ends[edge : edge + 1, :]).astype(BF16)
 
     coarse_edges = doms * held * degree
-    pre1, node1, fold, coarse_far, coarse_put, put, d_out2 = run(
+    pre1, node1, fold, joined, joined_bias, coarse_far, coarse_put, put, d_out2 = run(
         coarse_prepare,
         [
             ((coarse_edges,) + tile, F32), (wide, F32), ((2,) + tile, BF16),
+            ((2, features, 2 * features), BF16), ((8, 2 * features), F32),
             ((coarse_edges * size, far_size), BF16), ((held, size + far_size, degree * size), BF16),
             ((edges, size, size), BF16), (fine, F32),
         ],
@@ -402,13 +417,16 @@
         scratch=[pltpu.VMEM(wide, F32), pltpu.VMEM(wide, BF16)],
     )
 
-    def coarse_layer(other_ref, g0, g1, h_ref, pre, node, far_pick, w_ref, b_ref, fold_ref, end_ref, slope_ref, node_slope_ref, sum_scr):
+    def coarse_layer(other_ref, g0, g1, h_ref, pre, node, far_pick, w_ref, join_ref, bias_ref, fold_ref, end_ref, slope_ref, node_slope_ref, sum_scr):
         halos = [g[0:at_tail, :] for _, g in sorted(zip(ORDER, (g0, g1)))]
         states = [h_ref[...]] + halos
-        third = (0.5 * mm(other_ref[...], w_ref[1, 1])).astype(BF16)
-        arrived = [(0.5 * mm(g, w_ref[1, 1])).astype(BF16) for g in halos]
-        recvs = [None] + [0.5 * (mm(g, w_ref[1, 0]) + b_ref[1, 0:1, :]) for g in halos]
-        nodes_all = [node[...]] + [0.5 * (mm(g, w_ref[1, 3]) + b_ref[1, 1:2, :]) for g in halos]
+        arrived = (0.5 * mm(jnp.concatenate(halos + [other_ref[...]], axis=0), w_ref[1, 1])).astype(BF16)
+        rows_all = held * size
+        third = arrived[rounds * rows_all :, :]
+        arrived = [arrived[r * rows_all : (r + 1) * rows_all, :] for r in range(rounds)]
+        own = mm(jnp.concatenate(halos, axis=0), join_ref[0]) + bias_ref[0:1, :]
+        recvs = [None] + [own[r * rows_all : (r + 1) * rows_all, 0:features] for r in range(rounds)]
+        nodes_all = [node[...], own[:, features:]]
         sources = [arrived, [arrived[0], third], [arrived[1], third]]
         width = degree * size
         picked = []
@@ -431,7 +449,7 @@
     coarse_end, slope1, node_slope1 = run(
         coarse_layer,
         [((doms * held * size, features), BF16), ((held * degree,) + tile, BF16), (wide, BF16)],
-        other, coarse_halo[0], coarse_halo[1], coarse_start, pre1, node1, coarse_far, w, bias, fold,
+        other, coarse_halo[0], coarse_halo[1], coarse_start, pre1, node1, coarse_far, w, joined, joined_bias, fold,
         scratch=[pltpu.VMEM((doms * held * size, features), BF16)],
     )
     coarse_ends = share(coarse_end)
@@ -441,19 +459,22 @@
 
     def last_layer(s_ref, slots_ref, g0, g1, *refs):
         parts = refs[:sub_size]
-        first_ref, pick, put, w_ref, b_ref, fold_ref, d_out = refs[sub_size : sub_size + 7]
+        first_ref, pick, put, w_ref, join_ref, bias_ref, fold_ref, d_out = refs[sub_size : sub_size + 8]
         (r0, r1, d_node, d_recv, d_send, hidden_ref, middle_ref,
-         lift_scr, recv, node, sender, send_scr, sum_scr, slope_scr, node_slope_scr, act_scr, acc_scr) = refs[sub_size + 7 :]
+         lift_scr, own_scr, state_scr, send_scr, sum_scr, slope_scr, node_slope_scr, act_scr, acc_scr) = refs[sub_size + 8 :]
         lift_into(parts, s_ref, lift_scr)
         for b in range(blocks):
             lifted = lift_scr[scalar(s_ref, at_pool + b)].astype(F32)
-            middle_ref[rows_of(b), :] = (first_ref[rows_of(b), :].astype(F32) + lifted).astype(BF16)
-        halos = []
+            state_scr[rows_of(b), :] = (first_ref[rows_of(b), :].astype(F32) + lifted).astype(BF16)
         for r, g in zip(ORDER, (g0, g1)):
             lifted = lift_scr[(1 + r) * slots + scalar(slots_ref, r)].astype(F32)
-            halos.append((g[at_tail:, :].astype(F32) + lifted).astype(BF16))
-        own_into(middle_ref[...], 2, w_ref, b_ref, recv, node, sender)
-        senders_into(sender, halos, 2, w_ref, send_scr)
+            state_scr[rows_of(blocks + r), :] = (g[at_tail:, :].astype(F32) + lifted).astype(BF16)
+        senders = (0.5 * mm(state_scr[...], w_ref[2, 1])).astype(BF16)
+        send_scr[...] = senders.reshape((everyone,) + tile)
+        middle = state_scr[0 : blocks * size, :]
+        middle_ref[...] = middle
+        own_scr[...] = mm(middle, join_ref[1]) + bias_ref[1:2, :]
+        recv, node = own_scr.at[:, 0:features], own_scr.at[:, features:]
         fold = fold_ref[1]
         pre_of = fine_pre(s_ref, recv, pick, send_scr)
         hidden_ref[...] = layer_forward(blocks, fold, pre_of, node[...], slope_scr, node_slope_scr, sum_scr)
@@ -464,9 +485,9 @@
     *halo_grads, d_node, d_recv, d_send, hidden2, middle = run(
         last_layer,
         back_out + [(fine, BF16), (fine, BF16)],
-        table, halo_slots, *coarse_halo, *coarse_ends, first, pick, put, w, bias, fold, d_out2,
+        table, halo_slots, *coarse_halo, *coarse_ends, first, pick, put, w, joined, joined_bias, fold, d_out2,
         scratch=[pltpu.VMEM((doms * slots,) + tile, BF16)]
-        + [pltpu.VMEM(fine, F32), pltpu.VMEM(fine, F32), pltpu.VMEM(fine, BF16)]
+        + [pltpu.VMEM((blocks * size, 2 * features), F32), pltpu.VMEM((everyone * size, features), BF16)]
         + layer_scratch + [pltpu.VMEM((edges,) + tile, BF16), pltpu.VMEM(fine, BF16)] + back_scratch,
     )
     returned = exchange(halo_grads)

time: 56.7 us -> 56.5 us (level)
  no operation moved by 1% of the time
where the time goes in v7:
time: 56.5 us; the launch traced here: 56.3 us
  waiting for transfers between devices  23.9 us (42%)
  starting transfers between devices  20.1 us (36%)
  Pallas kernels  11.4 us (20%)
  between operations  0.76 us (1%)
    ppermute x17, waiting for transfers between devices, swapped(): lax.ppermute(value, axis, [(source, source ^ mask) for source in range(si...  23.9 us
    ppermute x17, starting transfers between devices, swapped(): lax.ppermute(value, axis, [(source, source ^ mask) for source in range(si...  20.1 us
    pallas_call x15, Pallas kernels, run(): pl.pallas_call(kernel, out_shape=[jax.ShapeDtypeStruct(shape, dtype) for...  8.81 us
    pallas_call x2, Pallas kernels, run_hbm(): pl.pallas_call(kernel, out_shape=[pltpu.VMEM(shape, dtype) for shape, dty...  2.63 us
  transfers between devices with their start and end apart: 17, of which 14 were waited for; matrix products, arithmetic and copies ran while one was open for 0% of the time, Pallas kernels for 8%

profile of v7, /device:TPU:0, one launch (start us, length us, event | category | flops | bytes accessed | tf_op | source)
XLA Modules:
  0.0 56.3 jit_solution(6445768474797017301)
XLA Ops:
  0.6 0.9 %shard_map.113 = (bf16[512,128]{1,0:T(8,128)(2,1)S(1)}, bf16[16,128]{1,0:T(8,128)(2,1)S(1)}, bf16[144,128]{1,0:T(8,128)(2,1)S(1)}, bf16[144,128]{1,0:T(8,128)(2,1)S(1)}) custom-call(s32[1,2]{1,0:T(1,128)} %bitcast.16, s32[4,128]{1,0:T(4,128)} %bitcast.15, s32[1,4]{1,0:T(1,128)} %listed_in.1, s32[1,4]{1,0:T(1,128)} %bitcast.18, bf16[512,128]{1,0:T(8,128)(2,1)} %nodes_in.1), custom_call_target="tpu_custom_call" | custom-call | bytes 1048576 | tf_op jit(solution)/shard_map/pallas_call | solution.py:46
  1.6 4.1 %collective-permute-start = (bf16[144,128]{1,0:T(8,128)(2,1)S(1)}, bf16[144,128]{1,0:T(8,128)(2,1)S(1)}, u32[]{:S(2)}, u32[]{:S(2)}) collective-permute-start(bf16[144,128]{1,0:T(8,128)(2,1)S(1)} %get-tuple-element.66), channel_id=1, source_target_pairs={{0,8},{4,12},{8,0},{12,4},{1,9},{5,13},{9,1},{13,5},{2,10},{6,14},... | collective-permute-start | bytes 110600 | tf_op jit(solution)/shard_map/ppermute | solution.py:18
  5.7 1.6 %collective-permute-start.1 = (bf16[144,128]{1,0:T(8,128)(2,1)S(1)}, bf16[144,128]{1,0:T(8,128)(2,1)S(1)}, u32[]{:S(2)}, u32[]{:S(2)}) collective-permute-start(bf16[144,128]{1,0:T(8,128)(2,1)S(1)} %get-tuple-element.67), channel_id=1, source_target_pairs={{0,4},{4,0},{8,12},{12,8},{1,5},{5,1},{9,13},{13,9},{2,6},{6,2},{1... | collective-permute-start | bytes 110600 | tf_op jit(solution)/shard_map/ppermute | solution.py:18
  7.3 1.7 %shard_map.114 = (s32[16,128]{1,0:T(8,128)S(1)}, bf16[3,6,128,128]{3,2,1,0:T(8,128)(2,1)S(1)}, f32[3,2,128]{2,1,0:T(2,128)S(1)}, bf16[512,128]{1,0:T(8,128)(2,1)...) custom-call(s32[1,2]{1,0:T(1,128)} %bitcast.17, ...), custom_call_target="tpu_custom_call" | custom-call | bytes 1048576 | tf_op jit(solution)/shard_map/pallas_call | solution.py:46
  9.0 0.0 collective-permute-done.g0
  9.0 0.7 %collective-permute-done.1.g1 = bf16[144,128]{1,0:T(8,128)(2,1)S(1)} collective-permute-done((bf16[144,128]{1,0:T(8,128)(2,1)S(1)}, bf16[144,128]{1,0:T(8,128)(2,1)S(1)}, u32[]{:S(2)}, u32[]{:S(2)}) %collective-permute-start.1) | collective-permute-done | bytes 36896 | tf_op jit(solution)/shard_map/ppermute | solution.py:18
  9.6 0.9 %shard_map.115 = (bf16[512,128]{1,0:T(8,128)(2,1)S(1)}, bf16[16,128,128]{2,1,0:T(8,128)(2,1)S(1)}, bf16[512,128]{1,0:T(8,128)(2,1)S(1)}, s32[8,128]{1,0:T(8,128)...) custom-call(s32[24,128]{1,0:T(8,128)S(1)} %get-tuple-element.65.s_ref, ...), custom_call_target="tpu_custom_call" | custom-call | bytes 1048576 | tf_op jit(solution)/shard_map/pallas_call | solution.py:34
  10.6 0.1 collective-permute-start.2
  10.7 1.2 %collective-permute-done.2.refs_1_ = bf16[272,128]{1,0:T(8,128)(2,1)S(1)} collective-permute-done((bf16[272,128]{1,0:T(8,128)(2,1)S(1)}, bf16[272,128]{1,0:T(8,128)(2,1)S(1)}, u32[]{:S(2)}, u32[]{:S(2)}) %collective-permute-start.2) | collective-permute-done | bytes 69664 | tf_op jit(solution)/shard_map/ppermute | solution.py:18
  11.9 1.6 %collective-permute-start.3 = (bf16[272,128]{1,0:T(8,128)(2,1)S(1)}, bf16[272,128]{1,0:T(8,128)(2,1)S(1)}, u32[]{:S(2)}, u32[]{:S(2)}) collective-permute-start(bf16[272,128]{1,0:T(8,128)(2,1)S(1)} %shard_map.116.refs_0_), channel_id=1, source_target_pairs={{0,2},{2,0},{1,3},{3,1},{4,6},{6,4},{5,7},{7,5},{8,10},{10,8},{9,1... | collective-permute-start | bytes 208904 | tf_op jit(solution)/shard_map/ppermute | solution.py:18
  13.5 2.8 %collective-permute-done.3.refs_1_ = bf16[272,128]{1,0:T(8,128)(2,1)S(1)} collective-permute-done((bf16[272,128]{1,0:T(8,128)(2,1)S(1)}, bf16[272,128]{1,0:T(8,128)(2,1)S(1)}, u32[]{:S(2)}, u32[]{:S(2)}) %collective-permute-start.3) | collective-permute-done | bytes 69664 | tf_op jit(solution)/shard_map/ppermute | solution.py:18
  16.3 0.1 shard_map.117
  16.4 1.2 %collective-permute-start.4 = (bf16[384,128]{1,0:T(8,128)(2,1)S(1)}, bf16[384,128]{1,0:T(8,128)(2,1)S(1)}, u32[]{:S(2)}, u32[]{:S(2)}) collective-permute-start(bf16[384,128]{1,0:T(8,128)(2,1)S(1)} %get-tuple-element.79), channel_id=1, source_target_pairs={{0,8},{4,12},{8,0},{12,4},{1,9},{5,13},{9,1},{13,5},{2,10},{6,14},... | collective-permute-start | bytes 294920 | tf_op jit(solution)/shard_map/ppermute | solution.py:18
  17.6 1.6 %collective-permute-start.5 = (bf16[384,128]{1,0:T(8,128)(2,1)S(1)}, bf16[384,128]{1,0:T(8,128)(2,1)S(1)}, u32[]{:S(2)}, u32[]{:S(2)}) collective-permute-start(bf16[384,128]{1,0:T(8,128)(2,1)S(1)} %get-tuple-element.80), channel_id=1, source_target_pairs={{0,4},{4,0},{8,12},{12,8},{1,5},{5,1},{9,13},{13,9},{2,6},{6,2},{1... | collective-permute-start | bytes 294920 | tf_op jit(solution)/shard_map/ppermute | solution.py:18
  19.2 1.6 %collective-permute-start.6 = (bf16[256,128]{1,0:T(8,128)(2,1)S(1)}, bf16[256,128]{1,0:T(8,128)(2,1)S(1)}, u32[]{:S(2)}, u32[]{:S(2)}) collective-permute-start(bf16[256,128]{1,0:T(8,128)(2,1)S(1)} %get-tuple-element.81), channel_id=1, source_target_pairs={{0,12},{4,8},{8,4},{12,0},{1,13},{5,9},{9,5},{13,1},{2,14},{6,10},... | collective-permute-start | bytes 196616 | tf_op jit(solution)/shard_map/ppermute | solution.py:18
  20.9 1.2 %shard_map.118 = (f32[24,128,128]{2,1,0:T(8,128)S(1)}, f32[256,128]{1,0:T(8,128)S(1)}, bf16[2,128,128]{2,1,0:T(8,128)(2,1)S(1)}, bf16[2,128,256]{2,1,0:T(8,128)(...) custom-call(bf16[256,128]{1,0:T(8,128)(2,1)S(1)} %get-tuple-element., ...), custom_call_target="tpu_custom_call" | custom-call | bytes 1048576 | tf_op jit(solution)/shard_map/pallas_call | solution.py:34
  22.0 3.8 %collective-permute-done.6.other_ref = bf16[256,128]{1,0:T(8,128)(2,1)S(1)} collective-permute-done((bf16[256,128]{1,0:T(8,128)(2,1)S(1)}, bf16[256,128]{1,0:T(8,128)(2,1)S(1)}, u32[]{:S(2)}, u32[]{:S(2)}) %collective-permute-start.6) | collective-permute-done | bytes 65568 | tf_op jit(solution)/shard_map/ppermute | solution.py:18
  25.8 0.0 collective-permute-done.4.g0
  25.8 0.0 collective-permute-done.5.g1
  25.8 1.1 %shard_map.119 = (bf16[768,128]{1,0:T(8,128)(2,1)S(1)}, bf16[8,128,128]{2,1,0:T(8,128)(2,1)S(1)}, bf16[256,128]{1,0:T(8,128)(2,1)S(1)}) custom-call(bf16[256,128]{1,0:T(8,128)(2,1)S(1)} %collective-permute-done.6.other_ref, bf16[384,128]{1,0:T(8,128)(2,1)S(1)} %collective-permute-done.4.g0, bf16[384,128]{1,0:T(8,128)(2,1)S(1)} %collective-permute-done.5.g1, ...), custom_call_target="tpu_custom_call" | custom-call | bytes 1048576 | tf_op jit(solution)/shard_map/pallas_call | solution.py:34
  26.9 0.1 collective-permute-start.7
  27.0 1.4 %collective-permute-done.7.refs_1_ = bf16[768,128]{1,0:T(8,128)(2,1)S(1)} collective-permute-done((bf16[768,128]{1,0:T(8,128)(2,1)S(1)}, bf16[768,128]{1,0:T(8,128)(2,1)S(1)}, u32[]{:S(2)}, u32[]{:S(2)}) %collective-permute-start.7) | collective-permute-done | bytes 196640 | tf_op jit(solution)/shard_map/ppermute | solution.py:18
  28.4 1.5 %shard_map.120 = (bf16[128,128]{1,0:T(8,128)(2,1)S(1)}, bf16[128,128]{1,0:T(8,128)(2,1)S(1)}, bf16[512,128]{1,0:T(8,128)(2,1)S(1)}, bf16[512,128]{1,0:T(8,128)(2...) custom-call(s32[24,128]{1,0:T(8,128)S(1)} %get-tuple-element.65.s_ref, ...), custom_call_target="tpu_custom_call" | custom-call | bytes 1048576 | tf_op jit(solution)/shard_map/pallas_call | solution.py:34
  29.9 1.4 %collective-permute-start.8 = (bf16[128,128]{1,0:T(8,128)(2,1)S(1)}, bf16[128,128]{1,0:T(8,128)(2,1)S(1)}, u32[]{:S(2)}, u32[]{:S(2)}) collective-permute-start(bf16[128,128]{1,0:T(8,128)(2,1)S(1)} %get-tuple-element.101), channel_id=1, source_target_pairs={{0,8},{4,12},{8,0},{12,4},{1,9},{5,13},{9,1},{13,5},{2,10},{6,14},... | collective-permute-start | bytes 98312 | tf_op jit(solution)/shard_map/ppermute | solution.py:18
  31.3 0.8 %collective-permute-start.9 = (bf16[128,128]{1,0:T(8,128)(2,1)S(1)}, bf16[128,128]{1,0:T(8,128)(2,1)S(1)}, u32[]{:S(2)}, u32[]{:S(2)}) collective-permute-start(bf16[128,128]{1,0:T(8,128)(2,1)S(1)} %get-tuple-element.102), channel_id=1, source_target_pairs={{0,4},{4,0},{8,12},{12,8},{1,5},{5,1},{9,13},{13,9},{2,6},{6,2},{1... | collective-permute-start | bytes 98312 | tf_op jit(solution)/shard_map/ppermute | solution.py:18
  32.1 1.0 %shard_map.121 = (f32[512,128]{1,0:T(8,128)S(1)}, bf16[512,128]{1,0:T(8,128)(2,1)}) custom-call(bf16[512,128]{1,0:T(8,128)(2,1)S(1)} %get-tuple-element.64.cot_ref, bf16[512,128]{1,0:T(8,128)(2,1)S(1)} %get-tuple-element.95.d_node, bf16[512,128]{1,0:T(8,128)(2,1)S(1)} %get-tuple-element.96.d_recv, bf16[512,128]{1,0:T(8,128)(2,1)S(1)} %bitcast.12, ...), custom_call_target="tpu_custom_call" | custom-call | bytes 1048576 | tf_op jit(solution)/shard_map/pallas_call | solution.py:34
  33.0 1.9 %collective-permute-done.8.r0 = bf16[128,128]{1,0:T(8,128)(2,1)S(1)} collective-permute-done((bf16[128,128]{1,0:T(8,128)(2,1)S(1)}, bf16[128,128]{1,0:T(8,128)(2,1)S(1)}, u32[]{:S(2)}, u32[]{:S(2)}) %collective-permute-start.8) | collective-permute-done | bytes 32800 | tf_op jit(solution)/shard_map/ppermute | solution.py:18
  35.0 0.3 collective-permute-done.9.r1
  35.3 0.1 shard_map.122
  35.4 0.1 collective-permute-start.10
  35.5 1.2 %collective-permute-done.10.refs_1_ = bf16[256,128]{1,0:T(8,128)(2,1)S(1)} collective-permute-done((bf16[256,128]{1,0:T(8,128)(2,1)S(1)}, bf16[256,128]{1,0:T(8,128)(2,1)S(1)}, u32[]{:S(2)}, u32[]{:S(2)}) %collective-permute-start.10) | collective-permute-done | bytes 65568 | tf_op jit(solution)/shard_map/ppermute | solution.py:18
  36.8 1.6 %collective-permute-start.11 = (bf16[256,128]{1,0:T(8,128)(2,1)S(1)}, bf16[256,128]{1,0:T(8,128)(2,1)S(1)}, u32[]{:S(2)}, u32[]{:S(2)}) collective-permute-start(bf16[256,128]{1,0:T(8,128)(2,1)S(1)} %shard_map.123.refs_0_), channel_id=1, source_target_pairs={{0,2},{2,0},{1,3},{3,1},{4,6},{6,4},{5,7},{7,5},{8,10},{10,8},{9,1... | collective-permute-start | bytes 196616 | tf_op jit(solution)/shard_map/ppermute | solution.py:18
  38.3 2.8 %collective-permute-done.11.refs_1_ = bf16[256,128]{1,0:T(8,128)(2,1)S(1)} collective-permute-done((bf16[256,128]{1,0:T(8,128)(2,1)S(1)}, bf16[256,128]{1,0:T(8,128)(2,1)S(1)}, u32[]{:S(2)}, u32[]{:S(2)}) %collective-permute-start.11) | collective-permute-done | bytes 65568 | tf_op jit(solution)/shard_map/ppermute | solution.py:18
  41.1 0.7 %shard_map.124 = (bf16[256,128]{1,0:T(8,128)(2,1)S(1)}, bf16[256,128]{1,0:T(8,128)(2,1)S(1)}, f32[256,128]{1,0:T(8,128)S(1)}, bf16[256,128]{1,0:T(8,128)(2,1)S(1)}, bf16[1024,128]{1,0:T(8,128)(2,1)S(1)}) custom-call(bf16[256,128]{1,0:T(8,128)(2,1)S(1)} %shard_map.123.refs_0_, bf16[256,128]{1,0:T(8,128)(2,1)S(1)} %collective-permute-done.11.refs_1_, ...), custom_call_target="tpu_custom_call" | custom-call | bytes 1048576 | tf_op jit(solution)/shard_map/pallas_call | solution.py:34
  41.8 1.6 %collective-permute-start.12 = (bf16[256,128]{1,0:T(8,128)(2,1)S(1)}, bf16[256,128]{1,0:T(8,128)(2,1)S(1)}, u32[]{:S(2)}, u32[]{:S(2)}) collective-permute-start(bf16[256,128]{1,0:T(8,128)(2,1)S(1)} %get-tuple-element.112), channel_id=1, source_target_pairs={{0,8},{4,12},{8,0},{12,4},{1,9},{5,13},{9,1},{13,5},{2,10},{6,14},... | collective-permute-start | bytes 196616 | tf_op jit(solution)/shard_map/ppermute | solution.py:18
  43.4 0.8 %collective-permute-start.13 = (bf16[256,128]{1,0:T(8,128)(2,1)S(1)}, bf16[256,128]{1,0:T(8,128)(2,1)S(1)}, u32[]{:S(2)}, u32[]{:S(2)}) collective-permute-start(bf16[256,128]{1,0:T(8,128)(2,1)S(1)} %get-tuple-element.113), channel_id=1, source_target_pairs={{0,4},{4,0},{8,12},{12,8},{1,5},{5,1},{9,13},{13,9},{2,6},{6,2},{1... | collective-permute-start | bytes 196616 | tf_op jit(solution)/shard_map/ppermute | solution.py:18
  44.2 0.4 shard_map.125.own_ref
  44.6 3.2 %collective-permute-done.12.r0 = bf16[256,128]{1,0:T(8,128)(2,1)S(1)} collective-permute-done((bf16[256,128]{1,0:T(8,128)(2,1)S(1)}, bf16[256,128]{1,0:T(8,128)(2,1)S(1)}, u32[]{:S(2)}, u32[]{:S(2)}) %collective-permute-start.12) | collective-permute-done | bytes 65568 | tf_op jit(solution)/shard_map/ppermute | solution.py:18
  47.8 0.3 collective-permute-done.13.r1
  48.1 0.1 collective-permute-start.14
  48.2 1.2 %collective-permute-done.14.refs_1_ = bf16[256,128]{1,0:T(8,128)(2,1)S(1)} collective-permute-done((bf16[256,128]{1,0:T(8,128)(2,1)S(1)}, bf16[256,128]{1,0:T(8,128)(2,1)S(1)}, u32[]{:S(2)}, u32[]{:S(2)}) %collective-permute-start.14) | collective-permute-done | bytes 65568 | tf_op jit(solution)/shard_map/ppermute | solution.py:18
  49.5 0.8 %shard_map.127 = (bf16[128,128]{1,0:T(8,128)(2,1)S(1)}, bf16[128,128]{1,0:T(8,128)(2,1)S(1)}, bf16[512,128]{1,0:T(8,128)(2,1)S(1)}, bf16[512,128]{1,0:T(8,128)(2...) custom-call(s32[24,128]{1,0:T(8,128)S(1)} %get-tuple-element.65.s_ref, ...), custom_call_target="tpu_custom_call" | custom-call | bytes 1048576 | tf_op jit(solution)/shard_map/pallas_call | solution.py:34
  50.2 1.0 %collective-permute-start.15 = (bf16[128,128]{1,0:T(8,128)(2,1)S(1)}, bf16[128,128]{1,0:T(8,128)(2,1)S(1)}, u32[]{:S(2)}, u32[]{:S(2)}) collective-permute-start(bf16[128,128]{1,0:T(8,128)(2,1)S(1)} %get-tuple-element.118), channel_id=1, source_target_pairs={{0,8},{4,12},{8,0},{12,4},{1,9},{5,13},{9,1},{13,5},{2,10},{6,14},... | collective-permute-start | bytes 98312 | tf_op jit(solution)/shard_map/ppermute | solution.py:18
  51.3 1.0 %collective-permute-start.16 = (bf16[128,128]{1,0:T(8,128)(2,1)S(1)}, bf16[128,128]{1,0:T(8,128)(2,1)S(1)}, u32[]{:S(2)}, u32[]{:S(2)}) collective-permute-start(bf16[128,128]{1,0:T(8,128)(2,1)S(1)} %get-tuple-element.119), channel_id=1, source_target_pairs={{0,4},{4,0},{8,12},{12,8},{1,5},{5,1},{9,13},{13,9},{2,6},{6,2},{1... | collective-permute-start | bytes 98312 | tf_op jit(solution)/shard_map/ppermute | solution.py:18
  52.3 0.3 shard_map.128
  52.6 2.8 %collective-permute-done.15.r0 = bf16[128,128]{1,0:T(8,128)(2,1)S(1)} collective-permute-done((bf16[128,128]{1,0:T(8,128)(2,1)S(1)}, bf16[128,128]{1,0:T(8,128)(2,1)S(1)}, u32[]{:S(2)}, u32[]{:S(2)}) %collective-permute-start.15) | collective-permute-done | bytes 32800 | tf_op jit(solution)/shard_map/ppermute | solution.py:18
  55.4 0.1 collective-permute-done.16.r1
  55.5 0.8 %shard_map.129 = f32[4,128,128]{2,1,0:T(8,128)} custom-call(s32[24,128]{1,0:T(8,128)S(1)} %get-tuple-element.65.s_ref, bf16[128,128]{1,0:T(8,128)(2,1)S(1)} %collective-permute-done.15.r0, bf16[128,128]{1,0:T(8,128)(2,1)S(1)} %collective-permute-done.16.r1, f32[4,128,128]{2,1,0:T(8,128)S(1)} %bitcast.9), custom_call_target="tpu_custom_call" | custom-call | bytes 1048576 | tf_op jit(solution)/shard_map/pallas_call | solution.py:34
  (3 shorter events, 0.1 us)
Async XLA Ops:
  1.6 7.4 %collective-permute-start = (bf16[144,128]{1,0:T(8,128)(2,1)S(1)}, bf16[144,128]{1,0:T(8,128)(2,1)S(1)}, u32[]{:S(2)}, u32[]{:S(2)}) collective-permute-start(bf16[144,128]{1,0:T(8,128)(2,1)S(1)} %get-tuple-element.66), channel_id=1, source_target_pairs={{0,8},{4,12},{8,0},{12,4},{1,9},{5,13},{9,1},{13,5},{2,10},{6,14},... | collective-permute-start | bytes 110600 | tf_op jit(solution)/shard_map/ppermute | solution.py:18
  5.7 4.0 %collective-permute-start.1 = (bf16[144,128]{1,0:T(8,128)(2,1)S(1)}, bf16[144,128]{1,0:T(8,128)(2,1)S(1)}, u32[]{:S(2)}, u32[]{:S(2)}) collective-permute-start(bf16[144,128]{1,0:T(8,128)(2,1)S(1)} %get-tuple-element.67), channel_id=1, source_target_pairs={{0,4},{4,0},{8,12},{12,8},{1,5},{5,1},{9,13},{13,9},{2,6},{6,2},{1... | collective-permute-start | bytes 110600 | tf_op jit(solution)/shard_map/ppermute | solution.py:18
  10.6 1.3 %collective-permute-start.2 = (bf16[272,128]{1,0:T(8,128)(2,1)S(1)}, bf16[272,128]{1,0:T(8,128)(2,1)S(1)}, u32[]{:S(2)}, u32[]{:S(2)}) collective-permute-start(bf16[272,128]{1,0:T(8,128)(2,1)S(1)} %get-tuple-element.78), channel_id=1, source_target_pairs={{0,1},{1,0},{2,3},{3,2},{4,5},{5,4},{6,7},{7,6},{8,9},{9,8},{10,11... | collective-permute-start | bytes 208904 | tf_op jit(solution)/shard_map/ppermute | solution.py:18
  11.9 4.4 %collective-permute-start.3 = (bf16[272,128]{1,0:T(8,128)(2,1)S(1)}, bf16[272,128]{1,0:T(8,128)(2,1)S(1)}, u32[]{:S(2)}, u32[]{:S(2)}) collective-permute-start(bf16[272,128]{1,0:T(8,128)(2,1)S(1)} %shard_map.116.refs_0_), channel_id=1, source_target_pairs={{0,2},{2,0},{1,3},{3,1},{4,6},{6,4},{5,7},{7,5},{8,10},{10,8},{9,1... | collective-permute-start | bytes 208904 | tf_op jit(solution)/shard_map/ppermute | solution.py:18
  16.4 9.4 %collective-permute-start.4 = (bf16[384,128]{1,0:T(8,128)(2,1)S(1)}, bf16[384,128]{1,0:T(8,128)(2,1)S(1)}, u32[]{:S(2)}, u32[]{:S(2)}) collective-permute-start(bf16[384,128]{1,0:T(8,128)(2,1)S(1)} %get-tuple-element.79), channel_id=1, source_target_pairs={{0,8},{4,12},{8,0},{12,4},{1,9},{5,13},{9,1},{13,5},{2,10},{6,14},... | collective-permute-start | bytes 294920 | tf_op jit(solution)/shard_map/ppermute | solution.py:18
  17.6 8.2 %collective-permute-start.5 = (bf16[384,128]{1,0:T(8,128)(2,1)S(1)}, bf16[384,128]{1,0:T(8,128)(2,1)S(1)}, u32[]{:S(2)}, u32[]{:S(2)}) collective-permute-start(bf16[384,128]{1,0:T(8,128)(2,1)S(1)} %get-tuple-element.80), channel_id=1, source_target_pairs={{0,4},{4,0},{8,12},{12,8},{1,5},{5,1},{9,13},{13,9},{2,6},{6,2},{1... | collective-permute-start | bytes 294920 | tf_op jit(solution)/shard_map/ppermute | solution.py:18
  19.2 6.5 %collective-permute-start.6 = (bf16[256,128]{1,0:T(8,128)(2,1)S(1)}, bf16[256,128]{1,0:T(8,128)(2,1)S(1)}, u32[]{:S(2)}, u32[]{:S(2)}) collective-permute-start(bf16[256,128]{1,0:T(8,128)(2,1)S(1)} %get-tuple-element.81), channel_id=1, source_target_pairs={{0,12},{4,8},{8,4},{12,0},{1,13},{5,9},{9,5},{13,1},{2,14},{6,10},... | collective-permute-start | bytes 196616 | tf_op jit(solution)/shard_map/ppermute | solution.py:18
  26.9 1.5 %collective-permute-start.7 = (bf16[768,128]{1,0:T(8,128)(2,1)S(1)}, bf16[768,128]{1,0:T(8,128)(2,1)S(1)}, u32[]{:S(2)}, u32[]{:S(2)}) collective-permute-start(bf16[768,128]{1,0:T(8,128)(2,1)S(1)} %get-tuple-element.92.refs_0_), channel_id=1, source_target_pairs={{0,1},{1,0},{2,3},{3,2},{4,5},{5,4},{6,7},{7,6},{8,9},{9,8},{10,11... | collective-permute-start | bytes 589832 | tf_op jit(solution)/shard_map/ppermute | solution.py:18
  29.9 5.1 %collective-permute-start.8 = (bf16[128,128]{1,0:T(8,128)(2,1)S(1)}, bf16[128,128]{1,0:T(8,128)(2,1)S(1)}, u32[]{:S(2)}, u32[]{:S(2)}) collective-permute-start(bf16[128,128]{1,0:T(8,128)(2,1)S(1)} %get-tuple-element.101), channel_id=1, source_target_pairs={{0,8},{4,12},{8,0},{12,4},{1,9},{5,13},{9,1},{13,5},{2,10},{6,14},... | collective-permute-start | bytes 98312 | tf_op jit(solution)/shard_map/ppermute | solution.py:18
  31.3 4.0 %collective-permute-start.9 = (bf16[128,128]{1,0:T(8,128)(2,1)S(1)}, bf16[128,128]{1,0:T(8,128)(2,1)S(1)}, u32[]{:S(2)}, u32[]{:S(2)}) collective-permute-start(bf16[128,128]{1,0:T(8,128)(2,1)S(1)} %get-tuple-element.102), channel_id=1, source_target_pairs={{0,4},{4,0},{8,12},{12,8},{1,5},{5,1},{9,13},{13,9},{2,6},{6,2},{1... | collective-permute-start | bytes 98312 | tf_op jit(solution)/shard_map/ppermute | solution.py:18
  35.4 1.3 %collective-permute-start.10 = (bf16[256,128]{1,0:T(8,128)(2,1)S(1)}, bf16[256,128]{1,0:T(8,128)(2,1)S(1)}, u32[]{:S(2)}, u32[]{:S(2)}) collective-permute-start(bf16[256,128]{1,0:T(8,128)(2,1)S(1)} %get-tuple-element.105), channel_id=1, source_target_pairs={{0,1},{1,0},{2,3},{3,2},{4,5},{5,4},{6,7},{7,6},{8,9},{9,8},{10,11... | collective-permute-start | bytes 196616 | tf_op jit(solution)/shard_map/ppermute | solution.py:18
  36.8 4.3 %collective-permute-start.11 = (bf16[256,128]{1,0:T(8,128)(2,1)S(1)}, bf16[256,128]{1,0:T(8,128)(2,1)S(1)}, u32[]{:S(2)}, u32[]{:S(2)}) collective-permute-start(bf16[256,128]{1,0:T(8,128)(2,1)S(1)} %shard_map.123.refs_0_), channel_id=1, source_target_pairs={{0,2},{2,0},{1,3},{3,1},{4,6},{6,4},{5,7},{7,5},{8,10},{10,8},{9,1... | collective-permute-start | bytes 196616 | tf_op jit(solution)/shard_map/ppermute | solution.py:18
  41.8 6.0 %collective-permute-start.12 = (bf16[256,128]{1,0:T(8,128)(2,1)S(1)}, bf16[256,128]{1,0:T(8,128)(2,1)S(1)}, u32[]{:S(2)}, u32[]{:S(2)}) collective-permute-start(bf16[256,128]{1,0:T(8,128)(2,1)S(1)} %get-tuple-element.112), channel_id=1, source_target_pairs={{0,8},{4,12},{8,0},{12,4},{1,9},{5,13},{9,1},{13,5},{2,10},{6,14},... | collective-permute-start | bytes 196616 | tf_op jit(solution)/shard_map/ppermute | solution.py:18
  43.4 4.7 %collective-permute-start.13 = (bf16[256,128]{1,0:T(8,128)(2,1)S(1)}, bf16[256,128]{1,0:T(8,128)(2,1)S(1)}, u32[]{:S(2)}, u32[]{:S(2)}) collective-permute-start(bf16[256,128]{1,0:T(8,128)(2,1)S(1)} %get-tuple-element.113), channel_id=1, source_target_pairs={{0,4},{4,0},{8,12},{12,8},{1,5},{5,1},{9,13},{13,9},{2,6},{6,2},{1... | collective-permute-start | bytes 196616 | tf_op jit(solution)/shard_map/ppermute | solution.py:18
  48.1 1.3 %collective-permute-start.14 = (bf16[256,128]{1,0:T(8,128)(2,1)S(1)}, bf16[256,128]{1,0:T(8,128)(2,1)S(1)}, u32[]{:S(2)}, u32[]{:S(2)}) collective-permute-start(bf16[256,128]{1,0:T(8,128)(2,1)S(1)} %shard_map.126.refs_0_), channel_id=1, source_target_pairs={{0,1},{1,0},{2,3},{3,2},{4,5},{5,4},{6,7},{7,6},{8,9},{9,8},{10,11... | collective-permute-start | bytes 196616 | tf_op jit(solution)/shard_map/ppermute | solution.py:18
  50.2 5.1 %collective-permute-start.15 = (bf16[128,128]{1,0:T(8,128)(2,1)S(1)}, bf16[128,128]{1,0:T(8,128)(2,1)S(1)}, u32[]{:S(2)}, u32[]{:S(2)}) collective-permute-start(bf16[128,128]{1,0:T(8,128)(2,1)S(1)} %get-tuple-element.118), channel_id=1, source_target_pairs={{0,8},{4,12},{8,0},{12,4},{1,9},{5,13},{9,1},{13,5},{2,10},{6,14},... | collective-permute-start | bytes 98312 | tf_op jit(solution)/shard_map/ppermute | solution.py:18
  51.3 4.3 %collective-permute-start.16 = (bf16[128,128]{1,0:T(8,128)(2,1)S(1)}, bf16[128,128]{1,0:T(8,128)(2,1)S(1)}, u32[]{:S(2)}, u32[]{:S(2)}) collective-permute-start(bf16[128,128]{1,0:T(8,128)(2,1)S(1)} %get-tuple-element.119), channel_id=1, source_target_pairs={{0,4},{4,0},{8,12},{12,8},{1,5},{5,1},{9,13},{13,9},{2,6},{6,2},{1... | collective-permute-start | bytes 98312 | tf_op jit(solution)/shard_map/ppermute | solution.py:18

commit v8 on v7

--- a/solution.py
+++ b/solution.py
@@ -184,15 +184,15 @@
                 half = pre_of(b, e)
                 up = 1.0 + jnp.tanh(half)
                 active = half * up
-                if edge < slope_ref.shape[0]:
+                if slope_ref is not None:
                     slope_ref[edge] = (up + active * (2.0 - up)).astype(BF16)
                 total = active if total is None else total + active
             sum_scr[rows_of(b), :] = total.astype(BF16)
         half = node + mm(sum_scr[...], fold)
         up = 1.0 + jnp.tanh(half)
         hidden = half * up
-        kept = node_slope_ref.shape[0]
-        node_slope_ref[...] = (0.5 * (up + hidden * (2.0 - up))).astype(BF16)[0:kept, :]
+        if slope_ref is not None:
+            node_slope_ref[...] = (0.5 * (up + hidden * (2.0 - up))).astype(BF16)
         return hidden.astype(BF16)
 
     def senders_into(own, halos, layer, w_ref, send_scr):
@@ -320,10 +320,10 @@
     layer_scratch = [pltpu.VMEM((everyone,) + tile, BF16), pltpu.VMEM(fine, BF16)]
 
     def first_layer(s_ref, g0, g1, h_ref, recv, node, sender, pick, w_ref, fold_ref, info_ref, *rest):
-        first_ref, slope_ref, node_slope_ref, slots_ref, *sends, send_scr, sum_scr = rest
-        senders_into(sender, (g0[0:size, :], g1[0:size, :]), 0, w_ref, send_scr)
-        pre_of = fine_pre(s_ref, recv, pick, send_scr)
-        hidden = layer_forward(blocks, fold_ref[...], pre_of, node[...], slope_ref, node_slope_ref, sum_scr)
+        first_ref, slots_ref, send_ref, *sends, sum_scr = rest
+        senders_into(sender, (g0[0:size, :], g1[0:size, :]), 0, w_ref, send_ref)
+        pre_of = fine_pre(s_ref, recv, pick, send_ref)
+        hidden = layer_forward(blocks, fold_ref[...], pre_of, node[...], None, None, sum_scr)
         first_ref[...] = (h_ref[...].astype(F32) + mm(hidden, w_ref[0, 5])).astype(BF16)
         tail = info_ref[...].astype(F32) + g0[size:, :].astype(F32) + g1[size:, :].astype(F32)
         pooled_into(lambda b: first_ref[rows_of(b), :].astype(F32), s_ref, sends, tail)
@@ -331,17 +331,25 @@
             last = g[size:, :].astype(F32).astype(I32)[at_last : at_last + 1, :]
             slots_ref[r : r + 1, :] = last
 
-    first, slope0, node_slope0, halo_slots, *pool_sends = run(
+    first, halo_slots, senders0, *pool_sends = run(
         first_layer,
-        [(fine, BF16)] + slopes + [((8, features), I32)] + [((pool_rows, features), BF16)] * sub_size,
+        [(fine, BF16), ((8, features), I32), ((everyone,) + tile, BF16)] + [((pool_rows, features), BF16)] * sub_size,
         table, halo[0], halo[1], h0, recv0, node0, sender0, pick, w, fold0, info,
-        scratch=layer_scratch,
+        scratch=[pltpu.VMEM(fine, BF16)],
+    )
+
+    def first_slopes(s_ref, recv, node, send_ref, pick, fold_ref, slope_ref, node_slope_ref, sum_scr):
+        pre_of = fine_pre(s_ref, recv, pick, send_ref)
+        layer_forward(blocks, fold_ref[...], pre_of, node[...], slope_ref, node_slope_ref, sum_scr)
+
+    slope0, node_slope0 = run(
+        first_slopes, slopes, table, recv0, node0, senders0, pick, fold0, scratch=[pltpu.VMEM(fine, BF16)]
     )
 
     pool_in = reduced(pool_sends)
 
     def coarse_begin(s_ref, first_ref, *refs):
-        parts, (start_ref, divisor_ref, infos_ref, other, out0, out1) = refs[:pair_size], refs[pair_size:]
+        parts, (start_ref, inverse_ref, infos_ref, other, out0, out1) = refs[:pair_size], refs[pair_size:]
         total = parts[0][0:at_tail, :].astype(F32)
         tails = [part[at_tail:, :].astype(F32) for part in parts]
         counts = tails[0][at_last : at_last + 1, :]
@@ -349,9 +357,9 @@
             total = total + part[0:at_tail, :].astype(F32)
             counts = counts + tail[at_last : at_last + 1, :]
         for q in range(held):
-            divisor_ref[q : q + 1, :] = jnp.broadcast_to(jnp.maximum(counts[:, q : q + 1], 1.0), (1, features))
+            inverse_ref[q : q + 1, :] = jnp.broadcast_to(1.0 / jnp.maximum(counts[:, q : q + 1], 1.0), (1, features))
         for q in range(held):
-            start = (total[q * size : (q + 1) * size, :] / divisor_ref[q : q + 1, :]).astype(BF16)
+            start = (total[q * size : (q + 1) * size, :] * inverse_ref[q : q + 1, :]).astype(BF16)
             for out in (start_ref, other, out0, out1):
                 out[rows_of(q), :] = start
         for r, out in zip(ORDER, (out0, out1)):
@@ -361,7 +369,7 @@
         for mask, tail in enumerate(tails):
             infos_ref[pair ^ mask] = tail
 
-    coarse_start, divisor, infos, other_send, *halo_sends = run(
+    coarse_start, inverse, infos, other_send, *halo_sends = run(
         coarse_begin,
         [(wide, BF16), ((8, features), F32), ((held, TAIL, features), F32), (wide, BF16)]
         + [((halo_rows, features), BF16)] * rounds,
@@ -417,10 +425,11 @@
         scratch=[pltpu.VMEM(wide, F32), pltpu.VMEM(wide, BF16)],
     )
 
-    def coarse_layer(other_ref, g0, g1, h_ref, pre, node, far_pick, w_ref, join_ref, bias_ref, fold_ref, end_ref, slope_ref, node_slope_ref, sum_scr):
+    def coarse_layer(other_ref, g0, g1, h_ref, pre, node, far_pick, w_ref, join_ref, bias_ref, fold_ref, end_ref, arrived_ref, sum_scr):
         halos = [g[0:at_tail, :] for _, g in sorted(zip(ORDER, (g0, g1)))]
         states = [h_ref[...]] + halos
         arrived = (0.5 * mm(jnp.concatenate(halos + [other_ref[...]], axis=0), w_ref[1, 1])).astype(BF16)
+        arrived_ref[...] = arrived[0 : rounds * held * size, :]
         rows_all = held * size
         third = arrived[rounds * rows_all :, :]
         arrived = [arrived[r * rows_all : (r + 1) * rows_all, :] for r in range(rounds)]
@@ -442,26 +451,46 @@
             return value if v == 0 else value + recvs[v][q * size : (q + 1) * size, :]
 
         hidden = layer_forward(
-            doms * held, fold_ref[0], pre_of, jnp.concatenate(nodes_all, axis=0), slope_ref, node_slope_ref, sum_scr
+            doms * held, fold_ref[0], pre_of, jnp.concatenate(nodes_all, axis=0), None, None, sum_scr
         )
         state = jnp.concatenate(states, axis=0).astype(F32)
         end_ref[...] = (state + mm(hidden, w_ref[1, 5])).astype(BF16)
-    coarse_end, slope1, node_slope1 = run(
+    coarse_end, coarse_arrived = run(
         coarse_layer,
-        [((doms * held * size, features), BF16), ((held * degree,) + tile, BF16), (wide, BF16)],
+        [((doms * held * size, features), BF16), ((rounds * held * size, features), BF16)],
         other, coarse_halo[0], coarse_halo[1], coarse_start, pre1, node1, coarse_far, w, joined, joined_bias, fold,
         scratch=[pltpu.VMEM((doms * held * size, features), BF16)],
     )
+
+    def coarse_slopes(arrived, pre, node, far_pick, fold_ref, slope_ref, node_slope_ref, sum_scr):
+        width = degree * size
+        picked = []
+        for q in range(held):
+            ats = [pl.ds((r * held + q) * size, size) for r in range(rounds)]
+            senders = jnp.concatenate([arrived[at, :] for at in ats], axis=0)
+            picked.append(mm(far_pick[q * width : (q + 1) * width, :], senders))
+
+        def pre_of(q, e):
+            return pre[q * degree + e] + picked[q][e * size : (e + 1) * size, :]
+
+        layer_forward(held, fold_ref[0], pre_of, node[...], slope_ref, node_slope_ref, sum_scr)
+
+    slope1, node_slope1 = run(
+        coarse_slopes,
+        [((held * degree,) + tile, BF16), (wide, BF16)],
+        coarse_arrived, pre1, node1, coarse_far, fold,
+        scratch=[pltpu.VMEM(wide, BF16)],
+    )
     coarse_ends = share(coarse_end)
 
-    back_out = [(tile, BF16)] * rounds + [(fine, BF16), (fine, BF16), (tiles, BF16)]
-    back_scratch = [pltpu.VMEM(fine, F32), pltpu.VMEM((everyone,) + tile, F32)]
+    back_out = [(tile, BF16)] * rounds + [(fine, BF16), (fine, BF16), ((everyone,) + tile, F32)]
+    back_scratch = [pltpu.VMEM(fine, F32)]
 
     def last_layer(s_ref, slots_ref, g0, g1, *refs):
         parts = refs[:sub_size]
         first_ref, pick, put, w_ref, join_ref, bias_ref, fold_ref, d_out = refs[sub_size : sub_size + 8]
-        (r0, r1, d_node, d_recv, d_send, hidden_ref, middle_ref,
-         lift_scr, own_scr, state_scr, send_scr, sum_scr, slope_scr, node_slope_scr, act_scr, acc_scr) = refs[sub_size + 8 :]
+        (r0, r1, d_node, d_recv, acc_scr, hidden_ref, state_scr,
+         lift_scr, own_scr, send_scr, sum_scr, slope_scr, node_slope_scr, act_scr) = refs[sub_size + 8 :]
         lift_into(parts, s_ref, lift_scr)
         for b in range(blocks):
             lifted = lift_scr[scalar(s_ref, at_pool + b)].astype(F32)
@@ -471,33 +500,30 @@
             state_scr[rows_of(blocks + r), :] = (g[at_tail:, :].astype(F32) + lifted).astype(BF16)
         senders = (0.5 * mm(state_scr[...], w_ref[2, 1])).astype(BF16)
         send_scr[...] = senders.reshape((everyone,) + tile)
-        middle = state_scr[0 : blocks * size, :]
-        middle_ref[...] = middle
-        own_scr[...] = mm(middle, join_ref[1]) + bias_ref[1:2, :]
+        own_scr[...] = mm(state_scr[0 : blocks * size, :], join_ref[1]) + bias_ref[1:2, :]
         recv, node = own_scr.at[:, 0:features], own_scr.at[:, features:]
         fold = fold_ref[1]
         pre_of = fine_pre(s_ref, recv, pick, send_scr)
         hidden_ref[...] = layer_forward(blocks, fold, pre_of, node[...], slope_scr, node_slope_scr, sum_scr)
         fine_backward(d_out[...], s_ref, fold, put, slope_scr, node_slope_scr, d_node, d_recv, act_scr, acc_scr)
         halo_grads_into((r0, r1), [acc_scr[blocks:].reshape(far_size, features)], 2, w_ref)
-        d_send[...] = acc_scr[0:blocks].astype(BF16)
 
     *halo_grads, d_node, d_recv, d_send, hidden2, middle = run(
         last_layer,
-        back_out + [(fine, BF16), (fine, BF16)],
+        back_out + [(fine, BF16), ((everyone * size, features), BF16)],
         table, halo_slots, *coarse_halo, *coarse_ends, first, pick, put, w, joined, joined_bias, fold, d_out2,
         scratch=[pltpu.VMEM((doms * slots,) + tile, BF16)]
-        + [pltpu.VMEM((blocks * size, 2 * features), F32), pltpu.VMEM((everyone * size, features), BF16)]
+        + [pltpu.VMEM((blocks * size, 2 * features), F32)]
         + layer_scratch + [pltpu.VMEM((edges,) + tile, BF16), pltpu.VMEM(fine, BF16)] + back_scratch,
     )
     returned = exchange(halo_grads)
 
     def last_own(cot_ref, d_node, d_recv, d_send, h_ref, hidden_ref, w_ref, grad_ref, out_ref):
-        grad_ref[...] = own_back(cot_ref[...].astype(F32), 2, w_ref, d_node[...], d_recv[...], d_send[...])
-        out_ref[...] = (h_ref[...].astype(F32) + mm(hidden_ref[...], w_ref[2, 5])).astype(BF16)
+        grad_ref[...] = own_back(cot_ref[...].astype(F32), 2, w_ref, d_node[...], d_recv[...], d_send[0:blocks].reshape(fine))
+        out_ref[...] = (h_ref[0 : blocks * size, :].astype(F32) + mm(hidden_ref[...], w_ref[2, 5])).astype(BF16)
 
     grad_own, out_nodes = run(
-        last_own, [(fine, F32), (fine, BF16)], cot, d_node, d_recv, d_send.reshape(fine), middle, hidden2, w
+        last_own, [(fine, F32), (fine, BF16)], cot, d_node, d_recv, d_send, middle, hidden2, w
     )
 
     def pool_grads(s_ref, r0, r1, own_ref, grad_ref, *sends):
@@ -555,19 +581,19 @@
 
     (coarse_grad,) = run(coarse_own, [(wide, F32)], coarse_grad, coarse_put, d_node, d_pre, w)
 
-    def scale(own_ref, r0, r1, divisor_ref, out_ref):
+    def scale(own_ref, r0, r1, inverse_ref, out_ref):
         for q in range(held):
             rows = rows_of(q)
             total = own_ref[rows, :] + r0[rows, :].astype(F32) + r1[rows, :].astype(F32)
-            out_ref[rows, :] = (total / divisor_ref[q : q + 1, :]).astype(BF16)
-
-    (scaled,) = run(scale, [(wide, BF16)], coarse_grad, *coarse_returned, divisor)
+            out_ref[rows, :] = (total * inverse_ref[q : q + 1, :]).astype(BF16)
+
+    (scaled,) = run(scale, [(wide, BF16)], coarse_grad, *coarse_returned, inverse)
     scaled_parts = share(scaled)
 
     def first_back(s_ref, *refs):
         parts = refs[:sub_size]
         middle_ref, put, slope_ref, node_slope_ref, w_ref, fold_ref = refs[sub_size : sub_size + 6]
-        r0, r1, d_node, d_recv, d_send, grad_ref, lift_scr, act_scr, acc_scr = refs[sub_size + 6 :]
+        r0, r1, d_node, d_recv, acc_scr, grad_ref, lift_scr, act_scr = refs[sub_size + 6 :]
         lift_into(parts, s_ref, lift_scr)
         for b in range(blocks):
             lifted = lift_scr[scalar(s_ref, at_pool + b)].astype(F32)
@@ -575,7 +601,6 @@
         d_out = mm_t(grad_ref[...].astype(BF16), w_ref[0, 5])
         fine_backward(d_out, s_ref, fold_ref[...], put, slope_ref, node_slope_ref, d_node, d_recv, act_scr, acc_scr)
         halo_grads_into((r0, r1), [acc_scr[blocks:].reshape(far_size, features)], 0, w_ref)
-        d_send[...] = acc_scr[0:blocks].astype(BF16)
 
     *halo_grads, d_node, d_recv, d_send, grad_first = run(
         first_back,
@@ -586,9 +611,9 @@
     returned = exchange(halo_grads)
 
     def first_own(first_ref, d_node, d_recv, d_send, w_ref, grad_ref):
-        grad_ref[...] = own_back(first_ref[...], 0, w_ref, d_node[...], d_recv[...], d_send[...])
-
-    (grad_own,) = run(first_own, [(fine, F32)], grad_first, d_node, d_recv, d_send.reshape(fine), w)
+        grad_ref[...] = own_back(first_ref[...], 0, w_ref, d_node[...], d_recv[...], d_send[0:blocks].reshape(fine))
+
+    (grad_own,) = run(first_own, [(fine, F32)], grad_first, d_node, d_recv, d_send, w)
 
     def finish(s_ref, r0, r1, own_ref, out_ref):
         out_ref[...] = own_ref[...]

time: 56.5 us -> 56.3 us (level)
  waiting for transfers between devices: 23.9 us -> 22.8 us
  Pallas kernels: 11.4 us -> 12.4 us
    ppermute x17, waiting for transfers between devices: 23.9 us -> 22.8 us  [swapped(): lax.ppermute(value, axis, [(source, source ^ mask) for source in range(si...]
    pallas_call x15 -> x17, Pallas kernels: 8.81 us -> 9.79 us  [run(): pl.pallas_call(kernel, out_shape=[jax.ShapeDtypeStruct(shape, dtype) for...]
  transfers between devices with their start and end apart: 17 -> 17, of which waited for: 14 -> 14; matrix products, arithmetic and copies ran while one was open for 0% -> 0% of each run, Pallas kernels for 8% -> 10%
where the time goes in v8:
time: 56.3 us; the launch traced here: 56.1 us
  waiting for transfers between devices  22.8 us (40%)
  starting transfers between devices  20.1 us (36%)
  Pallas kernels  12.4 us (22%)
  between operations  0.77 us (1%)
    ppermute x17, waiting for transfers between devices, swapped(): lax.ppermute(value, axis, [(source, source ^ mask) for source in range(si...  22.8 us
    ppermute x17, starting transfers between devices, swapped(): lax.ppermute(value, axis, [(source, source ^ mask) for source in range(si...  20.1 us
    pallas_call x17, Pallas kernels, run(): pl.pallas_call(kernel, out_shape=[jax.ShapeDtypeStruct(shape, dtype) for...  9.79 us
    pallas_call x2, Pallas kernels, run_hbm(): pl.pallas_call(kernel, out_shape=[pltpu.VMEM(shape, dtype) for shape, dty...  2.63 us
  transfers between devices with their start and end apart: 17, of which 14 were waited for; matrix products, arithmetic and copies ran while one was open for 0% of the time, Pallas kernels for 10%

profile of v8, /device:TPU:0, one launch (start us, length us, event | category | flops | bytes accessed | tf_op | source)
XLA Modules:
  0.0 56.1 jit_solution(10557336442337104717)
XLA Ops:
  0.6 0.9 %shard_map.113 = (bf16[512,128]{1,0:T(8,128)(2,1)S(1)}, bf16[16,128]{1,0:T(8,128)(2,1)S(1)}, bf16[144,128]{1,0:T(8,128)(2,1)S(1)}, bf16[144,128]{1,0:T(8,128)(2,1)S(1)}) custom-call(s32[1,2]{1,0:T(1,128)} %bitcast.12, s32[4,128]{1,0:T(4,128)} %bitcast.11, s32[1,4]{1,0:T(1,128)} %listed_in.1, s32[1,4]{1,0:T(1,128)} %bitcast.14, bf16[512,128]{1,0:T(8,128)(2,1)} %nodes_in.1), custom_call_target="tpu_custom_call" | custom-call | bytes 1048576 | tf_op jit(solution)/shard_map/pallas_call | solution.py:46
  1.6 4.1 %collective-permute-start = (bf16[144,128]{1,0:T(8,128)(2,1)S(1)}, bf16[144,128]{1,0:T(8,128)(2,1)S(1)}, u32[]{:S(2)}, u32[]{:S(2)}) collective-permute-start(bf16[144,128]{1,0:T(8,128)(2,1)S(1)} %get-tuple-element.68), channel_id=1, source_target_pairs={{0,8},{4,12},{8,0},{12,4},{1,9},{5,13},{9,1},{13,5},{2,10},{6,14},... | collective-permute-start | bytes 110600 | tf_op jit(solution)/shard_map/ppermute | solution.py:18
  5.7 1.6 %collective-permute-start.1 = (bf16[144,128]{1,0:T(8,128)(2,1)S(1)}, bf16[144,128]{1,0:T(8,128)(2,1)S(1)}, u32[]{:S(2)}, u32[]{:S(2)}) collective-permute-start(bf16[144,128]{1,0:T(8,128)(2,1)S(1)} %get-tuple-element.69), channel_id=1, source_target_pairs={{0,4},{4,0},{8,12},{12,8},{1,5},{5,1},{9,13},{13,9},{2,6},{6,2},{1... | collective-permute-start | bytes 110600 | tf_op jit(solution)/shard_map/ppermute | solution.py:18
  7.3 1.7 %shard_map.114 = (s32[16,128]{1,0:T(8,128)S(1)}, bf16[3,6,128,128]{3,2,1,0:T(8,128)(2,1)S(1)}, f32[3,2,128]{2,1,0:T(2,128)S(1)}, bf16[512,128]{1,0:T(8,128)(2,1)...) custom-call(s32[1,2]{1,0:T(1,128)} %bitcast.13, ...), custom_call_target="tpu_custom_call" | custom-call | bytes 1048576 | tf_op jit(solution)/shard_map/pallas_call | solution.py:46
  9.0 0.0 collective-permute-done.g0
  9.0 0.7 %collective-permute-done.1.g1 = bf16[144,128]{1,0:T(8,128)(2,1)S(1)} collective-permute-done((bf16[144,128]{1,0:T(8,128)(2,1)S(1)}, bf16[144,128]{1,0:T(8,128)(2,1)S(1)}, u32[]{:S(2)}, u32[]{:S(2)}) %collective-permute-start.1) | collective-permute-done | bytes 36896 | tf_op jit(solution)/shard_map/ppermute | solution.py:18
  9.6 0.8 %shard_map.115 = (bf16[512,128]{1,0:T(8,128)(2,1)S(1)}, s32[8,128]{1,0:T(8,128)S(1)}, bf16[6,128,128]{2,1,0:T(8,128)(2,1)S(1)}, bf16[272,128]{1,0:T(8,128)(2,1)S(1)}, bf16[272,128]{1,0:T(8,128)(2,1)S(1)}) custom-call(s32[24,128]{1,0:T(8,128)S(1)} %get-tuple-element.67.s_ref, bf16[144,128]{1,0:T(8,128)(2,1)S(1)} %collective-permute-done.g0, ...), custom_call_target="tpu_custom_call" | custom-call | bytes 1048576 | tf_op jit(solution)/shard_map/pallas_call | solution.py:34
  10.4 0.1 collective-permute-start.2
  10.5 1.2 %collective-permute-done.2.refs_1_ = bf16[272,128]{1,0:T(8,128)(2,1)S(1)} collective-permute-done((bf16[272,128]{1,0:T(8,128)(2,1)S(1)}, bf16[272,128]{1,0:T(8,128)(2,1)S(1)}, u32[]{:S(2)}, u32[]{:S(2)}) %collective-permute-start.2) | collective-permute-done | bytes 69664 | tf_op jit(solution)/shard_map/ppermute | solution.py:18
  11.8 1.6 %collective-permute-start.3 = (bf16[272,128]{1,0:T(8,128)(2,1)S(1)}, bf16[272,128]{1,0:T(8,128)(2,1)S(1)}, u32[]{:S(2)}, u32[]{:S(2)}) collective-permute-start(bf16[272,128]{1,0:T(8,128)(2,1)S(1)} %shard_map.116.refs_0_), channel_id=1, source_target_pairs={{0,2},{2,0},{1,3},{3,1},{4,6},{6,4},{5,7},{7,5},{8,10},{10,8},{9,1... | collective-permute-start | bytes 208904 | tf_op jit(solution)/shard_map/ppermute | solution.py:18
  13.4 2.8 %collective-permute-done.3.refs_1_ = bf16[272,128]{1,0:T(8,128)(2,1)S(1)} collective-permute-done((bf16[272,128]{1,0:T(8,128)(2,1)S(1)}, bf16[272,128]{1,0:T(8,128)(2,1)S(1)}, u32[]{:S(2)}, u32[]{:S(2)}) %collective-permute-start.3) | collective-permute-done | bytes 69664 | tf_op jit(solution)/shard_map/ppermute | solution.py:18
  16.2 0.1 shard_map.117
  16.3 1.2 %collective-permute-start.4 = (bf16[384,128]{1,0:T(8,128)(2,1)S(1)}, bf16[384,128]{1,0:T(8,128)(2,1)S(1)}, u32[]{:S(2)}, u32[]{:S(2)}) collective-permute-start(bf16[384,128]{1,0:T(8,128)(2,1)S(1)} %get-tuple-element.81), channel_id=1, source_target_pairs={{0,8},{4,12},{8,0},{12,4},{1,9},{5,13},{9,1},{13,5},{2,10},{6,14},... | collective-permute-start | bytes 294920 | tf_op jit(solution)/shard_map/ppermute | solution.py:18
  17.5 1.6 %collective-permute-start.5 = (bf16[384,128]{1,0:T(8,128)(2,1)S(1)}, bf16[384,128]{1,0:T(8,128)(2,1)S(1)}, u32[]{:S(2)}, u32[]{:S(2)}) collective-permute-start(bf16[384,128]{1,0:T(8,128)(2,1)S(1)} %get-tuple-element.82), channel_id=1, source_target_pairs={{0,4},{4,0},{8,12},{12,8},{1,5},{5,1},{9,13},{13,9},{2,6},{6,2},{1... | collective-permute-start | bytes 294920 | tf_op jit(solution)/shard_map/ppermute | solution.py:18
  19.1 1.6 %collective-permute-start.6 = (bf16[256,128]{1,0:T(8,128)(2,1)S(1)}, bf16[256,128]{1,0:T(8,128)(2,1)S(1)}, u32[]{:S(2)}, u32[]{:S(2)}) collective-permute-start(bf16[256,128]{1,0:T(8,128)(2,1)S(1)} %get-tuple-element.83), channel_id=1, source_target_pairs={{0,12},{4,8},{8,4},{12,0},{1,13},{5,9},{9,5},{13,1},{2,14},{6,10},... | collective-permute-start | bytes 196616 | tf_op jit(solution)/shard_map/ppermute | solution.py:18
  20.7 1.2 %shard_map.118 = (f32[24,128,128]{2,1,0:T(8,128)S(1)}, f32[256,128]{1,0:T(8,128)S(1)}, bf16[2,128,128]{2,1,0:T(8,128)(2,1)S(1)}, bf16[2,128,256]{2,1,0:T(8,128)(...) custom-call(bf16[256,128]{1,0:T(8,128)(2,1)S(1)} %get-tuple-element., ...), custom_call_target="tpu_custom_call" | custom-call | bytes 1048576 | tf_op jit(solution)/shard_map/pallas_call | solution.py:34
  21.9 3.8 %collective-permute-done.6.other_ref = bf16[256,128]{1,0:T(8,128)(2,1)S(1)} collective-permute-done((bf16[256,128]{1,0:T(8,128)(2,1)S(1)}, bf16[256,128]{1,0:T(8,128)(2,1)S(1)}, u32[]{:S(2)}, u32[]{:S(2)}) %collective-permute-start.6) | collective-permute-done | bytes 65568 | tf_op jit(solution)/shard_map/ppermute | solution.py:18
  25.7 0.0 collective-permute-done.4.g0
  25.7 0.0 collective-permute-done.5.g1
  25.7 1.1 %shard_map.119 = (bf16[768,128]{1,0:T(8,128)(2,1)S(1)}, bf16[512,128]{1,0:T(8,128)(2,1)S(1)}) custom-call(bf16[256,128]{1,0:T(8,128)(2,1)S(1)} %collective-permute-done.6.other_ref, bf16[384,128]{1,0:T(8,128)(2,1)S(1)} %collective-permute-done.4.g0, bf16[384,128]{1,0:T(8,128)(2,1)S(1)} %collective-permute-done.5.g1, ...), custom_call_target="tpu_custom_call" | custom-call | bytes 1048576 | tf_op jit(solution)/shard_map/pallas_call | solution.py:34
  26.8 0.1 collective-permute-start.7
  26.8 1.4 %collective-permute-done.7.refs_1_ = bf16[768,128]{1,0:T(8,128)(2,1)S(1)} collective-permute-done((bf16[768,128]{1,0:T(8,128)(2,1)S(1)}, bf16[768,128]{1,0:T(8,128)(2,1)S(1)}, u32[]{:S(2)}, u32[]{:S(2)}) %collective-permute-start.7) | collective-permute-done | bytes 196640 | tf_op jit(solution)/shard_map/ppermute | solution.py:18
  28.3 1.5 %shard_map.120 = (bf16[128,128]{1,0:T(8,128)(2,1)S(1)}, bf16[128,128]{1,0:T(8,128)(2,1)S(1)}, bf16[512,128]{1,0:T(8,128)(2,1)S(1)}, bf16[512,128]{1,0:T(8,128)(2...) custom-call(s32[24,128]{1,0:T(8,128)S(1)} %get-tuple-element.67.s_ref, ...), custom_call_target="tpu_custom_call" | custom-call | bytes 1048576 | tf_op jit(solution)/shard_map/pallas_call | solution.py:34
  29.7 1.4 %collective-permute-start.8 = (bf16[128,128]{1,0:T(8,128)(2,1)S(1)}, bf16[128,128]{1,0:T(8,128)(2,1)S(1)}, u32[]{:S(2)}, u32[]{:S(2)}) collective-permute-start(bf16[128,128]{1,0:T(8,128)(2,1)S(1)} %get-tuple-element.103), channel_id=1, source_target_pairs={{0,8},{4,12},{8,0},{12,4},{1,9},{5,13},{9,1},{13,5},{2,10},{6,14},... | collective-permute-start | bytes 98312 | tf_op jit(solution)/shard_map/ppermute | solution.py:18
  31.1 0.8 %collective-permute-start.9 = (bf16[128,128]{1,0:T(8,128)(2,1)S(1)}, bf16[128,128]{1,0:T(8,128)(2,1)S(1)}, u32[]{:S(2)}, u32[]{:S(2)}) collective-permute-start(bf16[128,128]{1,0:T(8,128)(2,1)S(1)} %get-tuple-element.104), channel_id=1, source_target_pairs={{0,4},{4,0},{8,12},{12,8},{1,5},{5,1},{9,13},{13,9},{2,6},{6,2},{1... | collective-permute-start | bytes 98312 | tf_op jit(solution)/shard_map/ppermute | solution.py:18
  31.9 1.0 %shard_map.121 = (f32[512,128]{1,0:T(8,128)S(1)}, bf16[512,128]{1,0:T(8,128)(2,1)}) custom-call(bf16[512,128]{1,0:T(8,128)(2,1)S(1)} %get-tuple-element.66.cot_ref, bf16[512,128]{1,0:T(8,128)(2,1)S(1)} %get-tuple-element.97.d_node, bf16[512,128]{1,0:T(8,128)(2,1)S(1)} %get-tuple-element.98.d_recv, f32[6,128,128]{2,1,0:T(8,128)S(1)} %get-tuple-element.99.d_send, ...), custom_call_target="tpu_custom_call" | custom-call | bytes 1048576 | tf_op jit(solution)/shard_map/pallas_call | solution.py:34
  32.9 1.9 %collective-permute-done.8.r0 = bf16[128,128]{1,0:T(8,128)(2,1)S(1)} collective-permute-done((bf16[128,128]{1,0:T(8,128)(2,1)S(1)}, bf16[128,128]{1,0:T(8,128)(2,1)S(1)}, u32[]{:S(2)}, u32[]{:S(2)}) %collective-permute-start.8) | collective-permute-done | bytes 32800 | tf_op jit(solution)/shard_map/ppermute | solution.py:18
  34.8 0.3 collective-permute-done.9.r1
  35.1 0.1 shard_map.122
  35.2 0.1 collective-permute-start.10
  35.3 1.2 %collective-permute-done.10.refs_1_ = bf16[256,128]{1,0:T(8,128)(2,1)S(1)} collective-permute-done((bf16[256,128]{1,0:T(8,128)(2,1)S(1)}, bf16[256,128]{1,0:T(8,128)(2,1)S(1)}, u32[]{:S(2)}, u32[]{:S(2)}) %collective-permute-start.10) | collective-permute-done | bytes 65568 | tf_op jit(solution)/shard_map/ppermute | solution.py:18
  36.6 1.5 %collective-permute-start.11 = (bf16[256,128]{1,0:T(8,128)(2,1)S(1)}, bf16[256,128]{1,0:T(8,128)(2,1)S(1)}, u32[]{:S(2)}, u32[]{:S(2)}) collective-permute-start(bf16[256,128]{1,0:T(8,128)(2,1)S(1)} %shard_map.123.refs_0_), channel_id=1, source_target_pairs={{0,2},{2,0},{1,3},{3,1},{4,6},{6,4},{5,7},{7,5},{8,10},{10,8},{9,1... | collective-permute-start | bytes 196616 | tf_op jit(solution)/shard_map/ppermute | solution.py:18
  38.1 0.5 shard_map.124
  38.6 2.3 %collective-permute-done.11.refs_1_ = bf16[256,128]{1,0:T(8,128)(2,1)S(1)} collective-permute-done((bf16[256,128]{1,0:T(8,128)(2,1)S(1)}, bf16[256,128]{1,0:T(8,128)(2,1)S(1)}, u32[]{:S(2)}, u32[]{:S(2)}) %collective-permute-start.11) | collective-permute-done | bytes 65568 | tf_op jit(solution)/shard_map/ppermute | solution.py:18
  40.9 0.7 %shard_map.125 = (bf16[256,128]{1,0:T(8,128)(2,1)S(1)}, bf16[256,128]{1,0:T(8,128)(2,1)S(1)}, f32[256,128]{1,0:T(8,128)S(1)}, bf16[256,128]{1,0:T(8,128)(2,1)S(1)}, bf16[1024,128]{1,0:T(8,128)(2,1)S(1)}) custom-call(bf16[256,128]{1,0:T(8,128)(2,1)S(1)} %shard_map.123.refs_0_, bf16[256,128]{1,0:T(8,128)(2,1)S(1)} %collective-permute-done.11.refs_1_, ...), custom_call_target="tpu_custom_call" | custom-call | bytes 1048576 | tf_op jit(solution)/shard_map/pallas_call | solution.py:34
  41.6 1.6 %collective-permute-start.12 = (bf16[256,128]{1,0:T(8,128)(2,1)S(1)}, bf16[256,128]{1,0:T(8,128)(2,1)S(1)}, u32[]{:S(2)}, u32[]{:S(2)}) collective-permute-start(bf16[256,128]{1,0:T(8,128)(2,1)S(1)} %get-tuple-element.115), channel_id=1, source_target_pairs={{0,8},{4,12},{8,0},{12,4},{1,9},{5,13},{9,1},{13,5},{2,10},{6,14},... | collective-permute-start | bytes 196616 | tf_op jit(solution)/shard_map/ppermute | solution.py:18
  43.2 0.8 %collective-permute-start.13 = (bf16[256,128]{1,0:T(8,128)(2,1)S(1)}, bf16[256,128]{1,0:T(8,128)(2,1)S(1)}, u32[]{:S(2)}, u32[]{:S(2)}) collective-permute-start(bf16[256,128]{1,0:T(8,128)(2,1)S(1)} %get-tuple-element.116), channel_id=1, source_target_pairs={{0,4},{4,0},{8,12},{12,8},{1,5},{5,1},{9,13},{13,9},{2,6},{6,2},{1... | collective-permute-start | bytes 196616 | tf_op jit(solution)/shard_map/ppermute | solution.py:18
  44.0 0.4 shard_map.126.own_ref
  44.4 3.2 %collective-permute-done.12.r0 = bf16[256,128]{1,0:T(8,128)(2,1)S(1)} collective-permute-done((bf16[256,128]{1,0:T(8,128)(2,1)S(1)}, bf16[256,128]{1,0:T(8,128)(2,1)S(1)}, u32[]{:S(2)}, u32[]{:S(2)}) %collective-permute-start.12) | collective-permute-done | bytes 65568 | tf_op jit(solution)/shard_map/ppermute | solution.py:18
  47.6 0.3 collective-permute-done.13.r1
  48.0 0.1 collective-permute-start.14
  48.0 0.7 %shard_map.128 = (bf16[16,128,128]{2,1,0:T(8,128)(2,1)S(1)}, bf16[512,128]{1,0:T(8,128)(2,1)S(1)}) custom-call(s32[24,128]{1,0:T(8,128)S(1)} %get-tuple-element.67.s_ref, f32[512,128]{1,0:T(8,128)S(1)} %get-tuple-element.70.recv, f32[512,128]{1,0:T(8,128)S(1)} %get-tuple-element.71.node, bf16[6,128,128]{2,1,0:T(8,128)(2,1)S(1)} %get-tuple-element.119.send_ref, ...), custom_call_target="tpu_custom_call" | custom-call | bytes 1048576 | tf_op jit(solution)/shard_map/pallas_call | solution.py:34
  48.7 0.6 %collective-permute-done.14.refs_1_ = bf16[256,128]{1,0:T(8,128)(2,1)S(1)} collective-permute-done((bf16[256,128]{1,0:T(8,128)(2,1)S(1)}, bf16[256,128]{1,0:T(8,128)(2,1)S(1)}, u32[]{:S(2)}, u32[]{:S(2)}) %collective-permute-start.14) | collective-permute-done | bytes 65568 | tf_op jit(solution)/shard_map/ppermute | solution.py:18
  49.3 0.8 %shard_map.129 = (bf16[128,128]{1,0:T(8,128)(2,1)S(1)}, bf16[128,128]{1,0:T(8,128)(2,1)S(1)}, bf16[512,128]{1,0:T(8,128)(2,1)S(1)}, bf16[512,128]{1,0:T(8,128)(2...) custom-call(s32[24,128]{1,0:T(8,128)S(1)} %get-tuple-element.67.s_ref, ...), custom_call_target="tpu_custom_call" | custom-call | bytes 1048576 | tf_op jit(solution)/shard_map/pallas_call | solution.py:34
  50.1 1.0 %collective-permute-start.15 = (bf16[128,128]{1,0:T(8,128)(2,1)S(1)}, bf16[128,128]{1,0:T(8,128)(2,1)S(1)}, u32[]{:S(2)}, u32[]{:S(2)}) collective-permute-start(bf16[128,128]{1,0:T(8,128)(2,1)S(1)} %get-tuple-element.122), channel_id=1, source_target_pairs={{0,8},{4,12},{8,0},{12,4},{1,9},{5,13},{9,1},{13,5},{2,10},{6,14},... | collective-permute-start | bytes 98312 | tf_op jit(solution)/shard_map/ppermute | solution.py:18
  51.1 1.0 %collective-permute-start.16 = (bf16[128,128]{1,0:T(8,128)(2,1)S(1)}, bf16[128,128]{1,0:T(8,128)(2,1)S(1)}, u32[]{:S(2)}, u32[]{:S(2)}) collective-permute-start(bf16[128,128]{1,0:T(8,128)(2,1)S(1)} %get-tuple-element.123), channel_id=1, source_target_pairs={{0,4},{4,0},{8,12},{12,8},{1,5},{5,1},{9,13},{13,9},{2,6},{6,2},{1... | collective-permute-start | bytes 98312 | tf_op jit(solution)/shard_map/ppermute | solution.py:18
  52.1 0.3 shard_map.130
  52.4 2.8 %collective-permute-done.15.r0 = bf16[128,128]{1,0:T(8,128)(2,1)S(1)} collective-permute-done((bf16[128,128]{1,0:T(8,128)(2,1)S(1)}, bf16[128,128]{1,0:T(8,128)(2,1)S(1)}, u32[]{:S(2)}, u32[]{:S(2)}) %collective-permute-start.15) | collective-permute-done | bytes 32800 | tf_op jit(solution)/shard_map/ppermute | solution.py:18
  55.2 0.1 collective-permute-done.16.r1
  55.3 0.7 %shard_map.131 = f32[4,128,128]{2,1,0:T(8,128)} custom-call(s32[24,128]{1,0:T(8,128)S(1)} %get-tuple-element.67.s_ref, bf16[128,128]{1,0:T(8,128)(2,1)S(1)} %collective-permute-done.15.r0, bf16[128,128]{1,0:T(8,128)(2,1)S(1)} %collective-permute-done.16.r1, f32[4,128,128]{2,1,0:T(8,128)S(1)} %bitcast.7), custom_call_target="tpu_custom_call" | custom-call | bytes 1048576 | tf_op jit(solution)/shard_map/pallas_call | solution.py:34
  (3 shorter events, 0.1 us)
Async XLA Ops:
  1.6 7.4 %collective-permute-start = (bf16[144,128]{1,0:T(8,128)(2,1)S(1)}, bf16[144,128]{1,0:T(8,128)(2,1)S(1)}, u32[]{:S(2)}, u32[]{:S(2)}) collective-permute-start(bf16[144,128]{1,0:T(8,128)(2,1)S(1)} %get-tuple-element.68), channel_id=1, source_target_pairs={{0,8},{4,12},{8,0},{12,4},{1,9},{5,13},{9,1},{13,5},{2,10},{6,14},... | collective-permute-start | bytes 110600 | tf_op jit(solution)/shard_map/ppermute | solution.py:18
  5.7 4.0 %collective-permute-start.1 = (bf16[144,128]{1,0:T(8,128)(2,1)S(1)}, bf16[144,128]{1,0:T(8,128)(2,1)S(1)}, u32[]{:S(2)}, u32[]{:S(2)}) collective-permute-start(bf16[144,128]{1,0:T(8,128)(2,1)S(1)} %get-tuple-element.69), channel_id=1, source_target_pairs={{0,4},{4,0},{8,12},{12,8},{1,5},{5,1},{9,13},{13,9},{2,6},{6,2},{1... | collective-permute-start | bytes 110600 | tf_op jit(solution)/shard_map/ppermute | solution.py:18
  10.4 1.3 %collective-permute-start.2 = (bf16[272,128]{1,0:T(8,128)(2,1)S(1)}, bf16[272,128]{1,0:T(8,128)(2,1)S(1)}, u32[]{:S(2)}, u32[]{:S(2)}) collective-permute-start(bf16[272,128]{1,0:T(8,128)(2,1)S(1)} %get-tuple-element.80), channel_id=1, source_target_pairs={{0,1},{1,0},{2,3},{3,2},{4,5},{5,4},{6,7},{7,6},{8,9},{9,8},{10,11... | collective-permute-start | bytes 208904 | tf_op jit(solution)/shard_map/ppermute | solution.py:18
  11.8 4.4 %collective-permute-start.3 = (bf16[272,128]{1,0:T(8,128)(2,1)S(1)}, bf16[272,128]{1,0:T(8,128)(2,1)S(1)}, u32[]{:S(2)}, u32[]{:S(2)}) collective-permute-start(bf16[272,128]{1,0:T(8,128)(2,1)S(1)} %shard_map.116.refs_0_), channel_id=1, source_target_pairs={{0,2},{2,0},{1,3},{3,1},{4,6},{6,4},{5,7},{7,5},{8,10},{10,8},{9,1... | collective-permute-start | bytes 208904 | tf_op jit(solution)/shard_map/ppermute | solution.py:18
  16.3 9.4 %collective-permute-start.4 = (bf16[384,128]{1,0:T(8,128)(2,1)S(1)}, bf16[384,128]{1,0:T(8,128)(2,1)S(1)}, u32[]{:S(2)}, u32[]{:S(2)}) collective-permute-start(bf16[384,128]{1,0:T(8,128)(2,1)S(1)} %get-tuple-element.81), channel_id=1, source_target_pairs={{0,8},{4,12},{8,0},{12,4},{1,9},{5,13},{9,1},{13,5},{2,10},{6,14},... | collective-permute-start | bytes 294920 | tf_op jit(solution)/shard_map/ppermute | solution.py:18
  17.5 8.2 %collective-permute-start.5 = (bf16[384,128]{1,0:T(8,128)(2,1)S(1)}, bf16[384,128]{1,0:T(8,128)(2,1)S(1)}, u32[]{:S(2)}, u32[]{:S(2)}) collective-permute-start(bf16[384,128]{1,0:T(8,128)(2,1)S(1)} %get-tuple-element.82), channel_id=1, source_target_pairs={{0,4},{4,0},{8,12},{12,8},{1,5},{5,1},{9,13},{13,9},{2,6},{6,2},{1... | collective-permute-start | bytes 294920 | tf_op jit(solution)/shard_map/ppermute | solution.py:18
  19.1 6.5 %collective-permute-start.6 = (bf16[256,128]{1,0:T(8,128)(2,1)S(1)}, bf16[256,128]{1,0:T(8,128)(2,1)S(1)}, u32[]{:S(2)}, u32[]{:S(2)}) collective-permute-start(bf16[256,128]{1,0:T(8,128)(2,1)S(1)} %get-tuple-element.83), channel_id=1, source_target_pairs={{0,12},{4,8},{8,4},{12,0},{1,13},{5,9},{9,5},{13,1},{2,14},{6,10},... | collective-permute-start | bytes 196616 | tf_op jit(solution)/shard_map/ppermute | solution.py:18
  26.8 1.5 %collective-permute-start.7 = (bf16[768,128]{1,0:T(8,128)(2,1)S(1)}, bf16[768,128]{1,0:T(8,128)(2,1)S(1)}, u32[]{:S(2)}, u32[]{:S(2)}) collective-permute-start(bf16[768,128]{1,0:T(8,128)(2,1)S(1)} %get-tuple-element.94.refs_0_), channel_id=1, source_target_pairs={{0,1},{1,0},{2,3},{3,2},{4,5},{5,4},{6,7},{7,6},{8,9},{9,8},{10,11... | collective-permute-start | bytes 589832 | tf_op jit(solution)/shard_map/ppermute | solution.py:18
  29.7 5.1 %collective-permute-start.8 = (bf16[128,128]{1,0:T(8,128)(2,1)S(1)}, bf16[128,128]{1,0:T(8,128)(2,1)S(1)}, u32[]{:S(2)}, u32[]{:S(2)}) collective-permute-start(bf16[128,128]{1,0:T(8,128)(2,1)S(1)} %get-tuple-element.103), channel_id=1, source_target_pairs={{0,8},{4,12},{8,0},{12,4},{1,9},{5,13},{9,1},{13,5},{2,10},{6,14},... | collective-permute-start | bytes 98312 | tf_op jit(solution)/shard_map/ppermute | solution.py:18
  31.1 4.0 %collective-permute-start.9 = (bf16[128,128]{1,0:T(8,128)(2,1)S(1)}, bf16[128,128]{1,0:T(8,128)(2,1)S(1)}, u32[]{:S(2)}, u32[]{:S(2)}) collective-permute-start(bf16[128,128]{1,0:T(8,128)(2,1)S(1)} %get-tuple-element.104), channel_id=1, source_target_pairs={{0,4},{4,0},{8,12},{12,8},{1,5},{5,1},{9,13},{13,9},{2,6},{6,2},{1... | collective-permute-start | bytes 98312 | tf_op jit(solution)/shard_map/ppermute | solution.py:18
  35.2 1.3 %collective-permute-start.10 = (bf16[256,128]{1,0:T(8,128)(2,1)S(1)}, bf16[256,128]{1,0:T(8,128)(2,1)S(1)}, u32[]{:S(2)}, u32[]{:S(2)}) collective-permute-start(bf16[256,128]{1,0:T(8,128)(2,1)S(1)} %get-tuple-element.107), channel_id=1, source_target_pairs={{0,1},{1,0},{2,3},{3,2},{4,5},{5,4},{6,7},{7,6},{8,9},{9,8},{10,11... | collective-permute-start | bytes 196616 | tf_op jit(solution)/shard_map/ppermute | solution.py:18
  36.6 4.3 %collective-permute-start.11 = (bf16[256,128]{1,0:T(8,128)(2,1)S(1)}, bf16[256,128]{1,0:T(8,128)(2,1)S(1)}, u32[]{:S(2)}, u32[]{:S(2)}) collective-permute-start(bf16[256,128]{1,0:T(8,128)(2,1)S(1)} %shard_map.123.refs_0_), channel_id=1, source_target_pairs={{0,2},{2,0},{1,3},{3,1},{4,6},{6,4},{5,7},{7,5},{8,10},{10,8},{9,1... | collective-permute-start | bytes 196616 | tf_op jit(solution)/shard_map/ppermute | solution.py:18
  41.6 6.0 %collective-permute-start.12 = (bf16[256,128]{1,0:T(8,128)(2,1)S(1)}, bf16[256,128]{1,0:T(8,128)(2,1)S(1)}, u32[]{:S(2)}, u32[]{:S(2)}) collective-permute-start(bf16[256,128]{1,0:T(8,128)(2,1)S(1)} %get-tuple-element.115), channel_id=1, source_target_pairs={{0,8},{4,12},{8,0},{12,4},{1,9},{5,13},{9,1},{13,5},{2,10},{6,14},... | collective-permute-start | bytes 196616 | tf_op jit(solution)/shard_map/ppermute | solution.py:18
  43.2 4.7 %collective-permute-start.13 = (bf16[256,128]{1,0:T(8,128)(2,1)S(1)}, bf16[256,128]{1,0:T(8,128)(2,1)S(1)}, u32[]{:S(2)}, u32[]{:S(2)}) collective-permute-start(bf16[256,128]{1,0:T(8,128)(2,1)S(1)} %get-tuple-element.116), channel_id=1, source_target_pairs={{0,4},{4,0},{8,12},{12,8},{1,5},{5,1},{9,13},{13,9},{2,6},{6,2},{1... | collective-permute-start | bytes 196616 | tf_op jit(solution)/shard_map/ppermute | solution.py:18
  48.0 1.3 %collective-permute-start.14 = (bf16[256,128]{1,0:T(8,128)(2,1)S(1)}, bf16[256,128]{1,0:T(8,128)(2,1)S(1)}, u32[]{:S(2)}, u32[]{:S(2)}) collective-permute-start(bf16[256,128]{1,0:T(8,128)(2,1)S(1)} %shard_map.127.refs_0_), channel_id=1, source_target_pairs={{0,1},{1,0},{2,3},{3,2},{4,5},{5,4},{6,7},{7,6},{8,9},{9,8},{10,11... | collective-permute-start | bytes 196616 | tf_op jit(solution)/shard_map/ppermute | solution.py:18
  50.1 5.1 %collective-permute-start.15 = (bf16[128,128]{1,0:T(8,128)(2,1)S(1)}, bf16[128,128]{1,0:T(8,128)(2,1)S(1)}, u32[]{:S(2)}, u32[]{:S(2)}) collective-permute-start(bf16[128,128]{1,0:T(8,128)(2,1)S(1)} %get-tuple-element.122), channel_id=1, source_target_pairs={{0,8},{4,12},{8,0},{12,4},{1,9},{5,13},{9,1},{13,5},{2,10},{6,14},... | collective-permute-start | bytes 98312 | tf_op jit(solution)/shard_map/ppermute | solution.py:18
  51.1 4.3 %collective-permute-start.16 = (bf16[128,128]{1,0:T(8,128)(2,1)S(1)}, bf16[128,128]{1,0:T(8,128)(2,1)S(1)}, u32[]{:S(2)}, u32[]{:S(2)}) collective-permute-start(bf16[128,128]{1,0:T(8,128)(2,1)S(1)} %get-tuple-element.123), channel_id=1, source_target_pairs={{0,4},{4,0},{8,12},{12,8},{1,5},{5,1},{9,13},{13,9},{2,6},{6,2},{1... | collective-permute-start | bytes 98312 | tf_op jit(solution)/shard_map/ppermute | solution.py:18

commit v9 on v8

--- a/solution.py
+++ b/solution.py
@@ -405,10 +405,9 @@
                     pre[edge] = picked + recv[rows_of(q), :] if v == 0 else picked
                     for i, source in enumerate([n for n in range(doms) if n != v]):
                         far_pick[rows_of(edge), i * size : (i + 1) * size] = (hit & (near == source)).astype(BF16)
-                    if v == 0:
-                        to = rows == around[e : e + 1, :]
-                        for r in range(doms):
-                            cput[q, r * size : (r + 1) * size, e * size : (e + 1) * size] = (to & (near == r)).astype(BF16)
+                    to = rows == around[at : at + 1, :]
+                    for r in range(doms):
+                        cput[tile_at, r * size : (r + 1) * size, e * size : (e + 1) * size] = (to & (near == r)).astype(BF16)
         for edge in range(edges):
             put[edge] = (rows == ends[edge : edge + 1, :]).astype(BF16)
 
@@ -418,18 +417,16 @@
         [
             ((coarse_edges,) + tile, F32), (wide, F32), ((2,) + tile, BF16),
             ((2, features, 2 * features), BF16), ((8, 2 * features), F32),
-            ((coarse_edges * size, far_size), BF16), ((held, size + far_size, degree * size), BF16),
+            ((coarse_edges * size, far_size), BF16), ((doms * held, doms * size, degree * size), BF16),
             ((edges, size, size), BF16), (fine, F32),
         ],
         coarse_start, w, bias, cot, infos, ends,
         scratch=[pltpu.VMEM(wide, F32), pltpu.VMEM(wide, BF16)],
     )
 
-    def coarse_layer(other_ref, g0, g1, h_ref, pre, node, far_pick, w_ref, join_ref, bias_ref, fold_ref, end_ref, arrived_ref, sum_scr):
+    def coarse_forward(other_ref, g0, g1, pre, node, far_pick, w_ref, join_ref, bias_ref, fold_ref, slope_ref, node_slope_ref, sum_scr):
         halos = [g[0:at_tail, :] for _, g in sorted(zip(ORDER, (g0, g1)))]
-        states = [h_ref[...]] + halos
         arrived = (0.5 * mm(jnp.concatenate(halos + [other_ref[...]], axis=0), w_ref[1, 1])).astype(BF16)
-        arrived_ref[...] = arrived[0 : rounds * held * size, :]
         rows_all = held * size
         third = arrived[rounds * rows_all :, :]
         arrived = [arrived[r * rows_all : (r + 1) * rows_all, :] for r in range(rounds)]
@@ -450,36 +447,33 @@
             value = pre[b * degree + e] + picked[b][e * size : (e + 1) * size, :]
             return value if v == 0 else value + recvs[v][q * size : (q + 1) * size, :]
 
-        hidden = layer_forward(
-            doms * held, fold_ref[0], pre_of, jnp.concatenate(nodes_all, axis=0), None, None, sum_scr
+        nodes_all = jnp.concatenate(nodes_all, axis=0)
+        return layer_forward(doms * held, fold_ref[0], pre_of, nodes_all, slope_ref, node_slope_ref, sum_scr)
+
+    def coarse_layer(other_ref, g0, g1, h_ref, pre, node, far_pick, w_ref, join_ref, bias_ref, fold_ref, end_ref, sum_scr):
+        hidden = coarse_forward(
+            other_ref, g0, g1, pre, node, far_pick, w_ref, join_ref, bias_ref, fold_ref, None, None, sum_scr
         )
-        state = jnp.concatenate(states, axis=0).astype(F32)
+        halos = [g[0:at_tail, :] for _, g in sorted(zip(ORDER, (g0, g1)))]
+        state = jnp.concatenate([h_ref[...]] + halos, axis=0).astype(F32)
         end_ref[...] = (state + mm(hidden, w_ref[1, 5])).astype(BF16)
-    coarse_end, coarse_arrived = run(
+
+    all_wide = (doms * held * size, features)
+    (coarse_end,) = run(
         coarse_layer,
-        [((doms * held * size, features), BF16), ((rounds * held * size, features), BF16)],
-        other, coarse_halo[0], coarse_halo[1], coarse_start, pre1, node1, coarse_far, w, joined, joined_bias, fold,
-        scratch=[pltpu.VMEM((doms * held * size, features), BF16)],
-    )
-
-    def coarse_slopes(arrived, pre, node, far_pick, fold_ref, slope_ref, node_slope_ref, sum_scr):
-        width = degree * size
-        picked = []
-        for q in range(held):
-            ats = [pl.ds((r * held + q) * size, size) for r in range(rounds)]
-            senders = jnp.concatenate([arrived[at, :] for at in ats], axis=0)
-            picked.append(mm(far_pick[q * width : (q + 1) * width, :], senders))
-
-        def pre_of(q, e):
-            return pre[q * degree + e] + picked[q][e * size : (e + 1) * size, :]
-
-        layer_forward(held, fold_ref[0], pre_of, node[...], slope_ref, node_slope_ref, sum_scr)
+        [(all_wide, BF16)],
+        other, *coarse_halo, coarse_start, pre1, node1, coarse_far, w, joined, joined_bias, fold,
+        scratch=[pltpu.VMEM(all_wide, BF16)],
+    )
+
+    def coarse_slopes(*refs):
+        coarse_forward(*refs)
 
     slope1, node_slope1 = run(
         coarse_slopes,
-        [((held * degree,) + tile, BF16), (wide, BF16)],
-        coarse_arrived, pre1, node1, coarse_far, fold,
-        scratch=[pltpu.VMEM(wide, BF16)],
+        [((coarse_edges,) + tile, BF16), (all_wide, BF16)],
+        other, *coarse_halo, pre1, node1, coarse_far, w, joined, joined_bias, fold,
+        scratch=[pltpu.VMEM(all_wide, BF16)],
     )
     coarse_ends = share(coarse_end)
 
@@ -516,78 +510,115 @@
         + [pltpu.VMEM((blocks * size, 2 * features), F32)]
         + layer_scratch + [pltpu.VMEM((edges,) + tile, BF16), pltpu.VMEM(fine, BF16)] + back_scratch,
     )
-    returned = exchange(halo_grads)
-
-    def last_own(cot_ref, d_node, d_recv, d_send, h_ref, hidden_ref, w_ref, grad_ref, out_ref):
-        grad_ref[...] = own_back(cot_ref[...].astype(F32), 2, w_ref, d_node[...], d_recv[...], d_send[0:blocks].reshape(fine))
+
+    def last_pool(s_ref, slots_ref, cot_ref, d_node, d_recv, d_send, g0, g1, w_ref, grad_ref, *outs):
+        grad_ref[...] = own_back(
+            cot_ref[...].astype(F32), 2, w_ref, d_node[...], d_recv[...], d_send[0:blocks].reshape(fine)
+        )
+        pooled_into(lambda b: grad_ref[rows_of(b), :], s_ref, outs)
+        sub = scalar(s_ref, at_sub)
+        for r, g in zip(ORDER, (g0, g1)):
+            slot = scalar(slots_ref, r)
+            for sub_mask, out in enumerate(outs):
+                for q in range(held):
+                    hit = (slot == q * sub_size + (sub ^ sub_mask)).astype(F32)
+                    out[rows_of((1 + r) * held + q), :] = (g[...].astype(F32) * hit).astype(BF16)
+
+    grad_own, *grad_sends = run(
+        last_pool,
+        [(fine, F32)] + [(all_wide, BF16)] * sub_size,
+        table, halo_slots, cot, d_node, d_recv, d_send, *halo_grads, w,
+    )
+    grad_parts = grad_sends[:1] + [swapped(piece, "sub", mask) for mask, piece in enumerate(grad_sends) if mask > 0]
+
+    def last_out(h_ref, hidden_ref, w_ref, out_ref):
         out_ref[...] = (h_ref[0 : blocks * size, :].astype(F32) + mm(hidden_ref[...], w_ref[2, 5])).astype(BF16)
 
-    grad_own, out_nodes = run(
-        last_own, [(fine, F32), (fine, BF16)], cot, d_node, d_recv, d_send, middle, hidden2, w
-    )
-
-    def pool_grads(s_ref, r0, r1, own_ref, grad_ref, *sends):
+    (out_nodes,) = run(last_out, [(fine, BF16)], middle, hidden2, w)
+
+    def coarse_back(*refs):
+        parts = refs[:sub_size]
+        g0, g1, put, slope_ref, node_slope_ref, w_ref, fold_ref = refs[sub_size : sub_size + 7]
+        other_ref, out0, out1, grad_ref, d_node, recv_ref, send_ref, act_scr, pre_scr = refs[sub_size + 7 :]
+        grad = parts[0][...].astype(F32)
+        for part in parts[1:]:
+            grad = grad + part[...].astype(F32)
+        rows_all, width = held * size, degree * size
+        grad_ref[...] = grad[0:rows_all, :]
+        node_backward(mm_t(grad.astype(BF16), w_ref[1, 5]), fold_ref[0], node_slope_ref, d_node, act_scr)
+        recvs = []
+        for b in range(doms * held):
+            total = None
+            for e in range(degree):
+                edge = b * degree + e
+                d_pre = act_scr[rows_of(b), :] * slope_ref[edge].astype(F32)
+                total = d_pre if total is None else total + d_pre
+                pre_scr[rows_of(edge), :] = d_pre.astype(BF16)
+            recvs.append(total.astype(BF16))
+        senders = []
+        for v in range(doms):
+            tiles_v = [mm(put[v * held + q], pre_scr[pl.ds((v * held + q) * width, width), :]) for q in range(held)]
+            senders.append(
+                [jnp.concatenate([t[n * size : (n + 1) * size, :] for t in tiles_v], axis=0) for n in range(doms)]
+            )
+        send_ref[...] = (senders[0][0] + senders[1][1] + senders[2][2]).astype(BF16)
+        recv_ref[...] = jnp.concatenate(recvs[:held], axis=0)
+        to_rounds = [senders[0][1] + senders[1][0], senders[0][2] + senders[2][0]]
+        to_other = senders[1][2] + senders[2][1]
+        sent = mm_t(jnp.concatenate(to_rounds + [to_other], axis=0).astype(BF16), w_ref[1, 1])
+        sums = (
+            grad[rows_all:, :]
+            + mm_t(jnp.concatenate(recvs[held:], axis=0), w_ref[1, 0])
+            + mm_t(d_node[rows_all:, :], w_ref[1, 3])
+            + sent[0 : rounds * rows_all, :]
+        ).astype(BF16)
+        other_ref[...] = sent[rounds * rows_all :, :].astype(BF16)
+        for r, g, out in zip(ORDER, (g0, g1), (out0, out1)):
+            out[0:at_tail, :] = sums[r * rows_all : (r + 1) * rows_all, :]
+            out[at_tail:, :] = g[...]
+
+    other_send, *coarse_sends, coarse_grad, d_node, d_recv, d_send = run(
+        coarse_back,
+        [(wide, BF16)] + [((halo_rows, features), BF16)] * rounds
+        + [(wide, F32), (all_wide, BF16), (wide, BF16), (wide, BF16)],
+        *grad_parts, *halo_grads, coarse_put, slope1, node_slope1, w, fold,
+        scratch=[pltpu.VMEM(all_wide, F32), pltpu.VMEM((coarse_edges * size, features), BF16)],
+    )
+    other = swapped(other_send, "dom", xor_bits[0] ^ xor_bits[1])
+    returned = exchange(coarse_sends)
+
+    def coarse_own(grad_ref, d_node, d_recv, d_send, w_ref, own_ref):
+        own_ref[...] = own_back(grad_ref[...], 1, w_ref, d_node[0 : held * size, :], d_recv[...], d_send[...])
+
+    (coarse_grad,) = run(coarse_own, [(wide, F32)], coarse_grad, d_node, d_recv, d_send, w)
+
+    def chip_sum(own_ref, other_ref, r0, r1, out_ref):
+        total = own_ref[...] + other_ref[...].astype(F32)
+        for r in (r0, r1):
+            total = total + r[0:at_tail, :].astype(F32)
+        out_ref[...] = total.astype(BF16)
+
+    (chip,) = run(chip_sum, [(wide, BF16)], coarse_grad, other, *returned)
+    chips = [chip] + [swapped(chip, "pair", mask) for mask in range(1, pair_size)]
+
+    def middle_grads(s_ref, own_ref, r0, r1, grad_ref):
         grad_ref[...] = own_ref[...]
         for r, arrived in zip(ORDER, (r0, r1)):
             at = scalar(s_ref, r)
-            grad_ref[at] = grad_ref[at] + arrived[...].astype(F32)
-        pooled_into(lambda b: grad_ref[b], s_ref, sends)
-
-    grad_middle, *grad_sends = run(
-        pool_grads,
-        [(tiles, F32)] + [(wide, BF16)] * sub_size,
-        table, returned[0], returned[1], grad_own.reshape(tiles),
-    )
-    grads_in = reduced(grad_sends)
-
-    def coarse_back(*refs):
-        parts = refs[:pair_size]
-        put, slope_ref, node_slope_ref, w_ref, fold_ref, r0, r1, grad_ref, d_node, d_pre, act_scr = refs[pair_size:]
-        grad = parts[0][...].astype(F32)
-        for part in parts[1:]:
-            grad = grad + part[...].astype(F32)
-        grad_ref[...] = grad
-        d_out = mm_t(grad.astype(BF16), w_ref[1, 5])
-        node_backward(d_out, fold_ref[0], node_slope_ref, d_node, act_scr)
-        for q in range(held):
-            for e in range(degree):
-                edge = q * degree + e
-                d_pre[rows_of(edge), :] = (act_scr[rows_of(q), :] * slope_ref[edge].astype(F32)).astype(BF16)
-        width = degree * size
-        grads = [mm(put[q, size:, :], d_pre[q * width : (q + 1) * width, :]) for q in range(held)]
-        halo_grads_into((r0, r1), grads, 1, w_ref)
-
-    *coarse_sends, coarse_grad, d_node, d_pre = run(
-        coarse_back,
-        [(wide, BF16)] * rounds + [(wide, F32), (wide, BF16), ((held * degree * size, features), BF16)],
-        *grads_in, coarse_put, slope1, node_slope1, w, fold,
-        scratch=[pltpu.VMEM(wide, F32)],
-    )
-    coarse_returned = exchange(coarse_sends)
-
-    def coarse_own(grad_ref, put, d_node, d_pre, w_ref, own_ref):
-        width = degree * size
-        d_send = [mm(put[q, 0:size, :], d_pre[q * width : (q + 1) * width, :]) for q in range(held)]
-        d_recv = []
-        for q in range(held):
-            total = None
-            for e in range(degree):
-                part = d_pre[rows_of(q * degree + e), :].astype(F32)
-                total = part if total is None else total + part
-            d_recv.append(total.astype(BF16))
-        own_ref[...] = own_back(
-            grad_ref[...], 1, w_ref, d_node[...], jnp.concatenate(d_recv, axis=0), jnp.concatenate(d_send, axis=0)
-        )
-
-    (coarse_grad,) = run(coarse_own, [(wide, F32)], coarse_grad, coarse_put, d_node, d_pre, w)
-
-    def scale(own_ref, r0, r1, inverse_ref, out_ref):
+            grad_ref[at] = grad_ref[at] + arrived[at_tail:, :].astype(F32)
+
+    (grad_middle,) = run(middle_grads, [(tiles, F32)], table, grad_own.reshape(tiles), *returned)
+
+    def scale(*refs):
+        parts, (inverse_ref, out_ref) = refs[:pair_size], refs[pair_size:]
         for q in range(held):
             rows = rows_of(q)
-            total = own_ref[rows, :] + r0[rows, :].astype(F32) + r1[rows, :].astype(F32)
+            total = parts[0][rows, :].astype(F32)
+            for part in parts[1:]:
+                total = total + part[rows, :].astype(F32)
             out_ref[rows, :] = (total * inverse_ref[q : q + 1, :]).astype(BF16)
 
-    (scaled,) = run(scale, [(wide, BF16)], coarse_grad, *coarse_returned, inverse)
+    (scaled,) = run(scale, [(wide, BF16)], *chips, inverse)
     scaled_parts = share(scaled)
 
     def first_back(s_ref, *refs):

time: 56.3 us -> 55.7 us (0.989)
  waiting for transfers between devices: 22.8 us -> 20 us
  Pallas kernels: 12.4 us -> 14 us
  starting transfers between devices: 20.1 us -> 20.7 us
    ppermute x17 -> x16, waiting for transfers between devices: 22.8 us -> 20 us  [swapped(): lax.ppermute(value, axis, [(source, source ^ mask) for source in range(si...]
    pallas_call x17 -> x18, Pallas kernels: 9.79 us -> 11.4 us  [run(): pl.pallas_call(kernel, out_shape=[jax.ShapeDtypeStruct(shape, dtype) for...]
    ppermute x17 -> x16, starting transfers between devices: 20.1 us -> 20.7 us  [swapped(): lax.ppermute(value, axis, [(source, source ^ mask) for source in range(si...]
  transfers between devices with their start and end apart: 17 -> 16, of which waited for: 14 -> 11; matrix products, arithmetic and copies ran while one was open for 0% -> 0% of each run, Pallas kernels for 10% -> 11%
where the time goes in v9:
time: 55.7 us; the launch traced here: 55.5 us
  starting transfers between devices  20.7 us (37%)
  waiting for transfers between devices  20 us (36%)
  Pallas kernels  14 us (25%)
  between operations  0.77 us (1%)
    ppermute x16, starting transfers between devices, swapped(): lax.ppermute(value, axis, [(source, source ^ mask) for source in range(si...  20.7 us
    ppermute x16, waiting for transfers between devices, swapped(): lax.ppermute(value, axis, [(source, source ^ mask) for source in range(si...  20 us
    pallas_call x18, Pallas kernels, run(): pl.pallas_call(kernel, out_shape=[jax.ShapeDtypeStruct(shape, dtype) for...  11.4 us
    pallas_call x2, Pallas kernels, run_hbm(): pl.pallas_call(kernel, out_shape=[pltpu.VMEM(shape, dtype) for shape, dty...  2.63 us
  transfers between devices with their start and end apart: 16, of which 11 were waited for; matrix products, arithmetic and copies ran while one was open for 0% of the time, Pallas kernels for 11%

profile of v9, /device:TPU:0, one launch (start us, length us, event | category | flops | bytes accessed | tf_op | source)
XLA Modules:
  0.0 55.5 jit_solution(7707881900458413053)
XLA Ops:
  0.6 0.9 %shard_map.113 = (bf16[512,128]{1,0:T(8,128)(2,1)S(1)}, bf16[16,128]{1,0:T(8,128)(2,1)S(1)}, bf16[144,128]{1,0:T(8,128)(2,1)S(1)}, bf16[144,128]{1,0:T(8,128)(2,1)S(1)}) custom-call(s32[1,2]{1,0:T(1,128)} %bitcast.12, s32[4,128]{1,0:T(4,128)} %bitcast.11, s32[1,4]{1,0:T(1,128)} %listed_in.1, s32[1,4]{1,0:T(1,128)} %bitcast.14, bf16[512,128]{1,0:T(8,128)(2,1)} %nodes_in.1), custom_call_target="tpu_custom_call" | custom-call | bytes 1048576 | tf_op jit(solution)/shard_map/pallas_call | solution.py:46
  1.6 4.1 %collective-permute-start = (bf16[144,128]{1,0:T(8,128)(2,1)S(1)}, bf16[144,128]{1,0:T(8,128)(2,1)S(1)}, u32[]{:S(2)}, u32[]{:S(2)}) collective-permute-start(bf16[144,128]{1,0:T(8,128)(2,1)S(1)} %get-tuple-element.65), channel_id=1, source_target_pairs={{0,8},{4,12},{8,0},{12,4},{1,9},{5,13},{9,1},{13,5},{2,10},{6,14},... | collective-permute-start | bytes 110600 | tf_op jit(solution)/shard_map/ppermute | solution.py:18
  5.7 1.6 %collective-permute-start.1 = (bf16[144,128]{1,0:T(8,128)(2,1)S(1)}, bf16[144,128]{1,0:T(8,128)(2,1)S(1)}, u32[]{:S(2)}, u32[]{:S(2)}) collective-permute-start(bf16[144,128]{1,0:T(8,128)(2,1)S(1)} %get-tuple-element.66), channel_id=1, source_target_pairs={{0,4},{4,0},{8,12},{12,8},{1,5},{5,1},{9,13},{13,9},{2,6},{6,2},{1... | collective-permute-start | bytes 110600 | tf_op jit(solution)/shard_map/ppermute | solution.py:18
  7.3 1.7 %shard_map.114 = (s32[16,128]{1,0:T(8,128)S(1)}, bf16[3,6,128,128]{3,2,1,0:T(8,128)(2,1)S(1)}, f32[3,2,128]{2,1,0:T(2,128)S(1)}, bf16[512,128]{1,0:T(8,128)(2,1)...) custom-call(s32[1,2]{1,0:T(1,128)} %bitcast.13, ...), custom_call_target="tpu_custom_call" | custom-call | bytes 1048576 | tf_op jit(solution)/shard_map/pallas_call | solution.py:46
  9.0 0.0 collective-permute-done.g0
  9.0 0.7 %collective-permute-done.1.g1 = bf16[144,128]{1,0:T(8,128)(2,1)S(1)} collective-permute-done((bf16[144,128]{1,0:T(8,128)(2,1)S(1)}, bf16[144,128]{1,0:T(8,128)(2,1)S(1)}, u32[]{:S(2)}, u32[]{:S(2)}) %collective-permute-start.1) | collective-permute-done | bytes 36896 | tf_op jit(solution)/shard_map/ppermute | solution.py:18
  9.6 0.8 %shard_map.115 = (bf16[512,128]{1,0:T(8,128)(2,1)S(1)}, s32[8,128]{1,0:T(8,128)S(1)}, bf16[6,128,128]{2,1,0:T(8,128)(2,1)S(1)}, bf16[272,128]{1,0:T(8,128)(2,1)S(1)}, bf16[272,128]{1,0:T(8,128)(2,1)S(1)}) custom-call(s32[24,128]{1,0:T(8,128)S(1)} %get-tuple-element.64.s_ref, bf16[144,128]{1,0:T(8,128)(2,1)S(1)} %collective-permute-done.g0, ...), custom_call_target="tpu_custom_call" | custom-call | bytes 1048576 | tf_op jit(solution)/shard_map/pallas_call | solution.py:34
  10.4 0.1 collective-permute-start.2
  10.5 1.2 %collective-permute-done.2.refs_1_ = bf16[272,128]{1,0:T(8,128)(2,1)S(1)} collective-permute-done((bf16[272,128]{1,0:T(8,128)(2,1)S(1)}, bf16[272,128]{1,0:T(8,128)(2,1)S(1)}, u32[]{:S(2)}, u32[]{:S(2)}) %collective-permute-start.2) | collective-permute-done | bytes 69664 | tf_op jit(solution)/shard_map/ppermute | solution.py:18
  11.8 1.6 %collective-permute-start.3 = (bf16[272,128]{1,0:T(8,128)(2,1)S(1)}, bf16[272,128]{1,0:T(8,128)(2,1)S(1)}, u32[]{:S(2)}, u32[]{:S(2)}) collective-permute-start(bf16[272,128]{1,0:T(8,128)(2,1)S(1)} %shard_map.116.refs_0_), channel_id=1, source_target_pairs={{0,2},{2,0},{1,3},{3,1},{4,6},{6,4},{5,7},{7,5},{8,10},{10,8},{9,1... | collective-permute-start | bytes 208904 | tf_op jit(solution)/shard_map/ppermute | solution.py:18
  13.4 2.8 %collective-permute-done.3.refs_1_ = bf16[272,128]{1,0:T(8,128)(2,1)S(1)} collective-permute-done((bf16[272,128]{1,0:T(8,128)(2,1)S(1)}, bf16[272,128]{1,0:T(8,128)(2,1)S(1)}, u32[]{:S(2)}, u32[]{:S(2)}) %collective-permute-start.3) | collective-permute-done | bytes 69664 | tf_op jit(solution)/shard_map/ppermute | solution.py:18
  16.2 0.1 shard_map.117
  16.3 1.2 %collective-permute-start.4 = (bf16[384,128]{1,0:T(8,128)(2,1)S(1)}, bf16[384,128]{1,0:T(8,128)(2,1)S(1)}, u32[]{:S(2)}, u32[]{:S(2)}) collective-permute-start(bf16[384,128]{1,0:T(8,128)(2,1)S(1)} %get-tuple-element.78), channel_id=1, source_target_pairs={{0,8},{4,12},{8,0},{12,4},{1,9},{5,13},{9,1},{13,5},{2,10},{6,14},... | collective-permute-start | bytes 294920 | tf_op jit(solution)/shard_map/ppermute | solution.py:18
  17.5 1.6 %collective-permute-start.5 = (bf16[384,128]{1,0:T(8,128)(2,1)S(1)}, bf16[384,128]{1,0:T(8,128)(2,1)S(1)}, u32[]{:S(2)}, u32[]{:S(2)}) collective-permute-start(bf16[384,128]{1,0:T(8,128)(2,1)S(1)} %get-tuple-element.79), channel_id=1, source_target_pairs={{0,4},{4,0},{8,12},{12,8},{1,5},{5,1},{9,13},{13,9},{2,6},{6,2},{1... | collective-permute-start | bytes 294920 | tf_op jit(solution)/shard_map/ppermute | solution.py:18
  19.1 1.6 %collective-permute-start.6 = (bf16[256,128]{1,0:T(8,128)(2,1)S(1)}, bf16[256,128]{1,0:T(8,128)(2,1)S(1)}, u32[]{:S(2)}, u32[]{:S(2)}) collective-permute-start(bf16[256,128]{1,0:T(8,128)(2,1)S(1)} %get-tuple-element.80), channel_id=1, source_target_pairs={{0,12},{4,8},{8,4},{12,0},{1,13},{5,9},{9,5},{13,1},{2,14},{6,10},... | collective-permute-start | bytes 196616 | tf_op jit(solution)/shard_map/ppermute | solution.py:18
  20.7 1.6 %shard_map.118 = (f32[24,128,128]{2,1,0:T(8,128)S(1)}, f32[256,128]{1,0:T(8,128)S(1)}, bf16[2,128,128]{2,1,0:T(8,128)(2,1)S(1)}, bf16[2,128,256]{2,1,0:T(8,128)(...) custom-call(bf16[256,128]{1,0:T(8,128)(2,1)S(1)} %get-tuple-element., ...), custom_call_target="tpu_custom_call" | custom-call | bytes 1048576 | tf_op jit(solution)/shard_map/pallas_call | solution.py:34
  22.3 3.4 %collective-permute-done.6.other_ref.refs_0_ = bf16[256,128]{1,0:T(8,128)(2,1)S(1)} collective-permute-done((bf16[256,128]{1,0:T(8,128)(2,1)S(1)}, bf16[256,128]{1,0:T(8,128)(2,1)S(1)}, u32[]{:S(2)}, u32[]{:S(2)}) %collective-permute-start.6) | collective-permute-done | bytes 65568 | tf_op jit(solution)/shard_map/ppermute | solution.py:18
  25.7 0.0 collective-permute-done.4.g0.refs_1_
  25.7 0.0 collective-permute-done.5.g1.refs_2_
  25.7 1.1 %shard_map.119.refs_0_ = bf16[768,128]{1,0:T(8,128)(2,1)S(1)} custom-call(bf16[256,128]{1,0:T(8,128)(2,1)S(1)} %collective-permute-done.6.other_ref.refs_0_, bf16[384,128]{1,0:T(8,128)(2,1)S(1)} %collective-permute-done.4.g0.refs_1_, bf16[384,128]{1,0:T(8,128)(2,1)S(1)} %collective-permute-done.5.g1.refs_2_, bf16[256,128]{1,0:T(8,128)(2,1)S(1)} %get-tuple-element.81.h_ref, ...), custom_call_target="tpu_custom_call" | custom-call | bytes 1048576 | tf_op jit(solution)/shard_map/pallas_call | solution.py:34
  26.7 0.1 collective-permute-start.7
  26.8 1.4 %collective-permute-done.7.refs_1_ = bf16[768,128]{1,0:T(8,128)(2,1)S(1)} collective-permute-done((bf16[768,128]{1,0:T(8,128)(2,1)S(1)}, bf16[768,128]{1,0:T(8,128)(2,1)S(1)}, u32[]{:S(2)}, u32[]{:S(2)}) %collective-permute-start.7) | collective-permute-done | bytes 196640 | tf_op jit(solution)/shard_map/ppermute | solution.py:18
  28.2 1.5 %shard_map.120 = (bf16[128,128]{1,0:T(8,128)(2,1)S(1)}, bf16[128,128]{1,0:T(8,128)(2,1)S(1)}, bf16[512,128]{1,0:T(8,128)(2,1)S(1)}, bf16[512,128]{1,0:T(8,128)(2...) custom-call(s32[24,128]{1,0:T(8,128)S(1)} %get-tuple-element.64.s_ref, ...), custom_call_target="tpu_custom_call" | custom-call | bytes 1048576 | tf_op jit(solution)/shard_map/pallas_call | solution.py:34
  29.7 0.3 shard_map.122
  30.1 0.2 collective-permute-start.8
  30.3 1.0 %shard_map.123 = (bf16[24,128,128]{2,1,0:T(8,128)(2,1)S(1)}, bf16[768,128]{1,0:T(8,128)(2,1)S(1)}) custom-call(bf16[256,128]{1,0:T(8,128)(2,1)S(1)} %collective-permute-done.6.other_ref.refs_0_, bf16[384,128]{1,0:T(8,128)(2,1)S(1)} %collective-permute-done.4.g0.refs_1_, bf16[384,128]{1,0:T(8,128)(2,1)S(1)} %collective-permute-done.5.g1.refs_2_, ...), custom_call_target="tpu_custom_call" | custom-call | bytes 1048576 | tf_op jit(solution)/shard_map/pallas_call | solution.py:34
  31.3 0.2 collective-permute-done.8.refs_1_
  31.6 1.3 %shard_map.124 = (bf16[256,128]{1,0:T(8,128)(2,1)S(1)}, bf16[384,128]{1,0:T(8,128)(2,1)S(1)}, bf16[384,128]{1,0:T(8,128)(2,1)S(1)}, f32[256,128]{1,0:T(8,128)S(1...) custom-call(bf16[768,128]{1,0:T(8,128)(2,1)S(1)} %get-tuple-element.101.refs_0_, ...), custom_call_target="tpu_custom_call" | custom-call | bytes 1048576 | tf_op jit(solution)/shard_map/pallas_call | solution.py:34
  32.9 1.4 %collective-permute-start.10 = (bf16[384,128]{1,0:T(8,128)(2,1)S(1)}, bf16[384,128]{1,0:T(8,128)(2,1)S(1)}, u32[]{:S(2)}, u32[]{:S(2)}) collective-permute-start(bf16[384,128]{1,0:T(8,128)(2,1)S(1)} %get-tuple-element.111), channel_id=1, source_target_pairs={{0,8},{4,12},{8,0},{12,4},{1,9},{5,13},{9,1},{13,5},{2,10},{6,14},... | collective-permute-start | bytes 294920 | tf_op jit(solution)/shard_map/ppermute | solution.py:18
  34.3 0.8 %collective-permute-start.11 = (bf16[384,128]{1,0:T(8,128)(2,1)S(1)}, bf16[384,128]{1,0:T(8,128)(2,1)S(1)}, u32[]{:S(2)}, u32[]{:S(2)}) collective-permute-start(bf16[384,128]{1,0:T(8,128)(2,1)S(1)} %get-tuple-element.112), channel_id=1, source_target_pairs={{0,4},{4,0},{8,12},{12,8},{1,5},{5,1},{9,13},{13,9},{2,6},{6,2},{1... | collective-permute-start | bytes 294920 | tf_op jit(solution)/shard_map/ppermute | solution.py:18
  35.1 2.3 %collective-permute-start.9 = (bf16[256,128]{1,0:T(8,128)(2,1)S(1)}, bf16[256,128]{1,0:T(8,128)(2,1)S(1)}, u32[]{:S(2)}, u32[]{:S(2)}) collective-permute-start(bf16[256,128]{1,0:T(8,128)(2,1)S(1)} %get-tuple-element.110), channel_id=1, source_target_pairs={{0,12},{4,8},{8,4},{12,0},{1,13},{5,9},{9,5},{13,1},{2,14},{6,10},... | collective-permute-start | bytes 196616 | tf_op jit(solution)/shard_map/ppermute | solution.py:18
  37.4 0.2 shard_map.125.own_ref
  37.6 5.0 %collective-permute-done.9.other_ref = bf16[256,128]{1,0:T(8,128)(2,1)S(1)} collective-permute-done((bf16[256,128]{1,0:T(8,128)(2,1)S(1)}, bf16[256,128]{1,0:T(8,128)(2,1)S(1)}, u32[]{:S(2)}, u32[]{:S(2)}) %collective-permute-start.9) | collective-permute-done | bytes 65568 | tf_op jit(solution)/shard_map/ppermute | solution.py:18
  42.6 0.0 collective-permute-done.10.r0
  42.6 0.0 collective-permute-done.11.r1
  42.7 1.6 %collective-permute-start.12 = (bf16[256,128]{1,0:T(8,128)(2,1)S(1)}, bf16[256,128]{1,0:T(8,128)(2,1)S(1)}, u32[]{:S(2)}, u32[]{:S(2)}) collective-permute-start(bf16[256,128]{1,0:T(8,128)(2,1)S(1)} %shard_map.126.refs_0_), channel_id=1, source_target_pairs={{0,2},{2,0},{1,3},{3,1},{4,6},{6,4},{5,7},{7,5},{8,10},{10,8},{9,1... | collective-permute-start | bytes 196616 | tf_op jit(solution)/shard_map/ppermute | solution.py:18
  44.2 2.8 %collective-permute-done.12.refs_1_ = bf16[256,128]{1,0:T(8,128)(2,1)S(1)} collective-permute-done((bf16[256,128]{1,0:T(8,128)(2,1)S(1)}, bf16[256,128]{1,0:T(8,128)(2,1)S(1)}, u32[]{:S(2)}, u32[]{:S(2)}) %collective-permute-start.12) | collective-permute-done | bytes 65568 | tf_op jit(solution)/shard_map/ppermute | solution.py:18
  47.0 0.1 collective-permute-start.13
  47.1 0.7 %shard_map.129 = (bf16[16,128,128]{2,1,0:T(8,128)(2,1)S(1)}, bf16[512,128]{1,0:T(8,128)(2,1)S(1)}) custom-call(s32[24,128]{1,0:T(8,128)S(1)} %get-tuple-element.64.s_ref, f32[512,128]{1,0:T(8,128)S(1)} %get-tuple-element.67.recv, f32[512,128]{1,0:T(8,128)S(1)} %get-tuple-element.68.node, bf16[6,128,128]{2,1,0:T(8,128)(2,1)S(1)} %get-tuple-element.115.send_ref, ...), custom_call_target="tpu_custom_call" | custom-call | bytes 1048576 | tf_op jit(solution)/shard_map/pallas_call | solution.py:34
  47.8 0.1 shard_map.128.refs_2_
  47.9 0.5 collective-permute-done.13.refs_1_
  48.4 0.8 %shard_map.130 = (bf16[128,128]{1,0:T(8,128)(2,1)S(1)}, bf16[128,128]{1,0:T(8,128)(2,1)S(1)}, bf16[512,128]{1,0:T(8,128)(2,1)S(1)}, bf16[512,128]{1,0:T(8,128)(2...) custom-call(s32[24,128]{1,0:T(8,128)S(1)} %get-tuple-element.64.s_ref, ...), custom_call_target="tpu_custom_call" | custom-call | bytes 1048576 | tf_op jit(solution)/shard_map/pallas_call | solution.py:34
  49.2 1.7 %collective-permute-start.14 = (bf16[128,128]{1,0:T(8,128)(2,1)S(1)}, bf16[128,128]{1,0:T(8,128)(2,1)S(1)}, u32[]{:S(2)}, u32[]{:S(2)}) collective-permute-start(bf16[128,128]{1,0:T(8,128)(2,1)S(1)} %get-tuple-element.118), channel_id=1, source_target_pairs={{0,8},{4,12},{8,0},{12,4},{1,9},{5,13},{9,1},{13,5},{2,10},{6,14},... | collective-permute-start | bytes 98312 | tf_op jit(solution)/shard_map/ppermute | solution.py:18
  50.9 0.9 %collective-permute-start.15 = (bf16[128,128]{1,0:T(8,128)(2,1)S(1)}, bf16[128,128]{1,0:T(8,128)(2,1)S(1)}, u32[]{:S(2)}, u32[]{:S(2)}) collective-permute-start(bf16[128,128]{1,0:T(8,128)(2,1)S(1)} %get-tuple-element.119), channel_id=1, source_target_pairs={{0,4},{4,0},{8,12},{12,8},{1,5},{5,1},{9,13},{13,9},{2,6},{6,2},{1... | collective-permute-start | bytes 98312 | tf_op jit(solution)/shard_map/ppermute | solution.py:18
  51.8 0.8 %shard_map.121 = bf16[512,128]{1,0:T(8,128)(2,1)} custom-call(bf16[768,128]{1,0:T(8,128)(2,1)S(1)} %get-tuple-element.94.h_ref, bf16[512,128]{1,0:T(8,128)(2,1)S(1)} %get-tuple-element.95.hidden_ref, bf16[3,6,128,128]{3,2,1,0:T(8,128)(2,1)S(1)} %get-tuple-element.71.w_ref.refs_5_.refs_6_.refs_7_), custom_call_target="tpu_custom_call" | custom-call | bytes 1048576 | tf_op jit(solution)/shard_map/pallas_call | solution.py:34
  52.6 0.3 shard_map.131
  52.9 1.5 %collective-permute-done.14.r0 = bf16[128,128]{1,0:T(8,128)(2,1)S(1)} collective-permute-done((bf16[128,128]{1,0:T(8,128)(2,1)S(1)}, bf16[128,128]{1,0:T(8,128)(2,1)S(1)}, u32[]{:S(2)}, u32[]{:S(2)}) %collective-permute-start.14) | collective-permute-done | bytes 32800 | tf_op jit(solution)/shard_map/ppermute | solution.py:18
  54.4 0.4 collective-permute-done.15.r1
  54.8 0.7 %shard_map.132 = f32[4,128,128]{2,1,0:T(8,128)} custom-call(s32[24,128]{1,0:T(8,128)S(1)} %get-tuple-element.64.s_ref, bf16[128,128]{1,0:T(8,128)(2,1)S(1)} %collective-permute-done.14.r0, bf16[128,128]{1,0:T(8,128)(2,1)S(1)} %collective-permute-done.15.r1, f32[4,128,128]{2,1,0:T(8,128)S(1)} %bitcast.7), custom_call_target="tpu_custom_call" | custom-call | bytes 1048576 | tf_op jit(solution)/shard_map/pallas_call | solution.py:34
  (3 shorter events, 0.1 us)
Async XLA Ops:
  1.6 7.4 %collective-permute-start = (bf16[144,128]{1,0:T(8,128)(2,1)S(1)}, bf16[144,128]{1,0:T(8,128)(2,1)S(1)}, u32[]{:S(2)}, u32[]{:S(2)}) collective-permute-start(bf16[144,128]{1,0:T(8,128)(2,1)S(1)} %get-tuple-element.65), channel_id=1, source_target_pairs={{0,8},{4,12},{8,0},{12,4},{1,9},{5,13},{9,1},{13,5},{2,10},{6,14},... | collective-permute-start | bytes 110600 | tf_op jit(solution)/shard_map/ppermute | solution.py:18
  5.7 4.0 %collective-permute-start.1 = (bf16[144,128]{1,0:T(8,128)(2,1)S(1)}, bf16[144,128]{1,0:T(8,128)(2,1)S(1)}, u32[]{:S(2)}, u32[]{:S(2)}) collective-permute-start(bf16[144,128]{1,0:T(8,128)(2,1)S(1)} %get-tuple-element.66), channel_id=1, source_target_pairs={{0,4},{4,0},{8,12},{12,8},{1,5},{5,1},{9,13},{13,9},{2,6},{6,2},{1... | collective-permute-start | bytes 110600 | tf_op jit(solution)/shard_map/ppermute | solution.py:18
  10.4 1.3 %collective-permute-start.2 = (bf16[272,128]{1,0:T(8,128)(2,1)S(1)}, bf16[272,128]{1,0:T(8,128)(2,1)S(1)}, u32[]{:S(2)}, u32[]{:S(2)}) collective-permute-start(bf16[272,128]{1,0:T(8,128)(2,1)S(1)} %get-tuple-element.77), channel_id=1, source_target_pairs={{0,1},{1,0},{2,3},{3,2},{4,5},{5,4},{6,7},{7,6},{8,9},{9,8},{10,11... | collective-permute-start | bytes 208904 | tf_op jit(solution)/shard_map/ppermute | solution.py:18
  11.8 4.4 %collective-permute-start.3 = (bf16[272,128]{1,0:T(8,128)(2,1)S(1)}, bf16[272,128]{1,0:T(8,128)(2,1)S(1)}, u32[]{:S(2)}, u32[]{:S(2)}) collective-permute-start(bf16[272,128]{1,0:T(8,128)(2,1)S(1)} %shard_map.116.refs_0_), channel_id=1, source_target_pairs={{0,2},{2,0},{1,3},{3,1},{4,6},{6,4},{5,7},{7,5},{8,10},{10,8},{9,1... | collective-permute-start | bytes 208904 | tf_op jit(solution)/shard_map/ppermute | solution.py:18
  16.3 9.4 %collective-permute-start.4 = (bf16[384,128]{1,0:T(8,128)(2,1)S(1)}, bf16[384,128]{1,0:T(8,128)(2,1)S(1)}, u32[]{:S(2)}, u32[]{:S(2)}) collective-permute-start(bf16[384,128]{1,0:T(8,128)(2,1)S(1)} %get-tuple-element.78), channel_id=1, source_target_pairs={{0,8},{4,12},{8,0},{12,4},{1,9},{5,13},{9,1},{13,5},{2,10},{6,14},... | collective-permute-start | bytes 294920 | tf_op jit(solution)/shard_map/ppermute | solution.py:18
  17.5 8.2 %collective-permute-start.5 = (bf16[384,128]{1,0:T(8,128)(2,1)S(1)}, bf16[384,128]{1,0:T(8,128)(2,1)S(1)}, u32[]{:S(2)}, u32[]{:S(2)}) collective-permute-start(bf16[384,128]{1,0:T(8,128)(2,1)S(1)} %get-tuple-element.79), channel_id=1, source_target_pairs={{0,4},{4,0},{8,12},{12,8},{1,5},{5,1},{9,13},{13,9},{2,6},{6,2},{1... | collective-permute-start | bytes 294920 | tf_op jit(solution)/shard_map/ppermute | solution.py:18
  19.1 6.5 %collective-permute-start.6 = (bf16[256,128]{1,0:T(8,128)(2,1)S(1)}, bf16[256,128]{1,0:T(8,128)(2,1)S(1)}, u32[]{:S(2)}, u32[]{:S(2)}) collective-permute-start(bf16[256,128]{1,0:T(8,128)(2,1)S(1)} %get-tuple-element.80), channel_id=1, source_target_pairs={{0,12},{4,8},{8,4},{12,0},{1,13},{5,9},{9,5},{13,1},{2,14},{6,10},... | collective-permute-start | bytes 196616 | tf_op jit(solution)/shard_map/ppermute | solution.py:18
  26.7 1.5 %collective-permute-start.7 = (bf16[768,128]{1,0:T(8,128)(2,1)S(1)}, bf16[768,128]{1,0:T(8,128)(2,1)S(1)}, u32[]{:S(2)}, u32[]{:S(2)}) collective-permute-start(bf16[768,128]{1,0:T(8,128)(2,1)S(1)} %shard_map.119.refs_0_), channel_id=1, source_target_pairs={{0,1},{1,0},{2,3},{3,2},{4,5},{5,4},{6,7},{7,6},{8,9},{9,8},{10,11... | collective-permute-start | bytes 589832 | tf_op jit(solution)/shard_map/ppermute | solution.py:18
  30.1 1.5 %collective-permute-start.8 = (bf16[768,128]{1,0:T(8,128)(2,1)S(1)}, bf16[768,128]{1,0:T(8,128)(2,1)S(1)}, u32[]{:S(2)}, u32[]{:S(2)}) collective-permute-start(bf16[768,128]{1,0:T(8,128)(2,1)S(1)} %get-tuple-element.102), channel_id=1, source_target_pairs={{0,1},{1,0},{2,3},{3,2},{4,5},{5,4},{6,7},{7,6},{8,9},{9,8},{10,11... | collective-permute-start | bytes 589832 | tf_op jit(solution)/shard_map/ppermute | solution.py:18
  32.9 9.7 %collective-permute-start.10 = (bf16[384,128]{1,0:T(8,128)(2,1)S(1)}, bf16[384,128]{1,0:T(8,128)(2,1)S(1)}, u32[]{:S(2)}, u32[]{:S(2)}) collective-permute-start(bf16[384,128]{1,0:T(8,128)(2,1)S(1)} %get-tuple-element.111), channel_id=1, source_target_pairs={{0,8},{4,12},{8,0},{12,4},{1,9},{5,13},{9,1},{13,5},{2,10},{6,14},... | collective-permute-start | bytes 294920 | tf_op jit(solution)/shard_map/ppermute | solution.py:18
  34.3 8.3 %collective-permute-start.11 = (bf16[384,128]{1,0:T(8,128)(2,1)S(1)}, bf16[384,128]{1,0:T(8,128)(2,1)S(1)}, u32[]{:S(2)}, u32[]{:S(2)}) collective-permute-start(bf16[384,128]{1,0:T(8,128)(2,1)S(1)} %get-tuple-element.112), channel_id=1, source_target_pairs={{0,4},{4,0},{8,12},{12,8},{1,5},{5,1},{9,13},{13,9},{2,6},{6,2},{1... | collective-permute-start | bytes 294920 | tf_op jit(solution)/shard_map/ppermute | solution.py:18
  35.1 7.5 %collective-permute-start.9 = (bf16[256,128]{1,0:T(8,128)(2,1)S(1)}, bf16[256,128]{1,0:T(8,128)(2,1)S(1)}, u32[]{:S(2)}, u32[]{:S(2)}) collective-permute-start(bf16[256,128]{1,0:T(8,128)(2,1)S(1)} %get-tuple-element.110), channel_id=1, source_target_pairs={{0,12},{4,8},{8,4},{12,0},{1,13},{5,9},{9,5},{13,1},{2,14},{6,10},... | collective-permute-start | bytes 196616 | tf_op jit(solution)/shard_map/ppermute | solution.py:18
  42.7 4.3 %collective-permute-start.12 = (bf16[256,128]{1,0:T(8,128)(2,1)S(1)}, bf16[256,128]{1,0:T(8,128)(2,1)S(1)}, u32[]{:S(2)}, u32[]{:S(2)}) collective-permute-start(bf16[256,128]{1,0:T(8,128)(2,1)S(1)} %shard_map.126.refs_0_), channel_id=1, source_target_pairs={{0,2},{2,0},{1,3},{3,1},{4,6},{6,4},{5,7},{7,5},{8,10},{10,8},{9,1... | collective-permute-start | bytes 196616 | tf_op jit(solution)/shard_map/ppermute | solution.py:18
  47.0 1.3 %collective-permute-start.13 = (bf16[256,128]{1,0:T(8,128)(2,1)S(1)}, bf16[256,128]{1,0:T(8,128)(2,1)S(1)}, u32[]{:S(2)}, u32[]{:S(2)}) collective-permute-start(bf16[256,128]{1,0:T(8,128)(2,1)S(1)} %shard_map.127.refs_0_), channel_id=1, source_target_pairs={{0,1},{1,0},{2,3},{3,2},{4,5},{5,4},{6,7},{7,6},{8,9},{9,8},{10,11... | collective-permute-start | bytes 196616 | tf_op jit(solution)/shard_map/ppermute | solution.py:18
  49.2 5.2 %collective-permute-start.14 = (bf16[128,128]{1,0:T(8,128)(2,1)S(1)}, bf16[128,128]{1,0:T(8,128)(2,1)S(1)}, u32[]{:S(2)}, u32[]{:S(2)}) collective-permute-start(bf16[128,128]{1,0:T(8,128)(2,1)S(1)} %get-tuple-element.118), channel_id=1, source_target_pairs={{0,8},{4,12},{8,0},{12,4},{1,9},{5,13},{9,1},{13,5},{2,10},{6,14},... | collective-permute-start | bytes 98312 | tf_op jit(solution)/shard_map/ppermute | solution.py:18
  50.9 3.9 %collective-permute-start.15 = (bf16[128,128]{1,0:T(8,128)(2,1)S(1)}, bf16[128,128]{1,0:T(8,128)(2,1)S(1)}, u32[]{:S(2)}, u32[]{:S(2)}) collective-permute-start(bf16[128,128]{1,0:T(8,128)(2,1)S(1)} %get-tuple-element.119), channel_id=1, source_target_pairs={{0,4},{4,0},{8,12},{12,8},{1,5},{5,1},{9,13},{13,9},{2,6},{6,2},{1... | collective-permute-start | bytes 98312 | tf_op jit(solution)/shard_map/ppermute | solution.py:18

commit v10 on v9

--- a/solution.py
+++ b/solution.py
@@ -406,8 +406,8 @@
                     for i, source in enumerate([n for n in range(doms) if n != v]):
                         far_pick[rows_of(edge), i * size : (i + 1) * size] = (hit & (near == source)).astype(BF16)
                     to = rows == around[at : at + 1, :]
-                    for r in range(doms):
-                        cput[tile_at, r * size : (r + 1) * size, e * size : (e + 1) * size] = (to & (near == r)).astype(BF16)
+                    for i, source in enumerate([n for n in range(doms) if n != v] + [v]):
+                        cput[tile_at, i * size : (i + 1) * size, e * size : (e + 1) * size] = (to & (near == source)).astype(BF16)
         for edge in range(edges):
             put[edge] = (rows == ends[edge : edge + 1, :]).astype(BF16)
 
@@ -482,9 +482,9 @@
 
     def last_layer(s_ref, slots_ref, g0, g1, *refs):
         parts = refs[:sub_size]
-        first_ref, pick, put, w_ref, join_ref, bias_ref, fold_ref, d_out = refs[sub_size : sub_size + 8]
-        (r0, r1, d_node, d_recv, acc_scr, hidden_ref, state_scr,
-         lift_scr, own_scr, send_scr, sum_scr, slope_scr, node_slope_scr, act_scr) = refs[sub_size + 8 :]
+        first_ref, cot_ref, pick, put, w_ref, join_ref, bias_ref, fold_ref, d_out = refs[sub_size : sub_size + 9]
+        r0, r1, hidden_ref, state_scr, grad_ref, *outs = refs[sub_size + 9 : 2 * sub_size + 14]
+        (d_node, d_recv, acc_scr, lift_scr, own_scr, send_scr, sum_scr, slope_scr, node_slope_scr, act_scr) = refs[2 * sub_size + 14 :]
         lift_into(parts, s_ref, lift_scr)
         for b in range(blocks):
             lifted = lift_scr[scalar(s_ref, at_pool + b)].astype(F32)
@@ -501,34 +501,29 @@
         hidden_ref[...] = layer_forward(blocks, fold, pre_of, node[...], slope_scr, node_slope_scr, sum_scr)
         fine_backward(d_out[...], s_ref, fold, put, slope_scr, node_slope_scr, d_node, d_recv, act_scr, acc_scr)
         halo_grads_into((r0, r1), [acc_scr[blocks:].reshape(far_size, features)], 2, w_ref)
-
-    *halo_grads, d_node, d_recv, d_send, hidden2, middle = run(
-        last_layer,
-        back_out + [(fine, BF16), ((everyone * size, features), BF16)],
-        table, halo_slots, *coarse_halo, *coarse_ends, first, pick, put, w, joined, joined_bias, fold, d_out2,
-        scratch=[pltpu.VMEM((doms * slots,) + tile, BF16)]
-        + [pltpu.VMEM((blocks * size, 2 * features), F32)]
-        + layer_scratch + [pltpu.VMEM((edges,) + tile, BF16), pltpu.VMEM(fine, BF16)] + back_scratch,
-    )
-
-    def last_pool(s_ref, slots_ref, cot_ref, d_node, d_recv, d_send, g0, g1, w_ref, grad_ref, *outs):
         grad_ref[...] = own_back(
-            cot_ref[...].astype(F32), 2, w_ref, d_node[...], d_recv[...], d_send[0:blocks].reshape(fine)
+            cot_ref[...].astype(F32), 2, w_ref, d_node[...], d_recv[...], acc_scr[0:blocks].reshape(fine)
         )
         pooled_into(lambda b: grad_ref[rows_of(b), :], s_ref, outs)
         sub = scalar(s_ref, at_sub)
-        for r, g in zip(ORDER, (g0, g1)):
+        for r, g in zip(ORDER, (r0, r1)):
             slot = scalar(slots_ref, r)
             for sub_mask, out in enumerate(outs):
                 for q in range(held):
                     hit = (slot == q * sub_size + (sub ^ sub_mask)).astype(F32)
                     out[rows_of((1 + r) * held + q), :] = (g[...].astype(F32) * hit).astype(BF16)
 
-    grad_own, *grad_sends = run(
-        last_pool,
-        [(fine, F32)] + [(all_wide, BF16)] * sub_size,
-        table, halo_slots, cot, d_node, d_recv, d_send, *halo_grads, w,
-    )
+    rest = run(
+        last_layer,
+        [(tile, BF16)] * rounds + [(fine, BF16), ((everyone * size, features), BF16), (fine, F32)] + [(all_wide, BF16)] * sub_size,
+        table, halo_slots, *coarse_halo, *coarse_ends, first, cot, pick, put, w, joined, joined_bias, fold, d_out2,
+        scratch=[pltpu.VMEM(fine, BF16), pltpu.VMEM(fine, BF16), pltpu.VMEM((everyone,) + tile, F32)]
+        + [pltpu.VMEM((doms * slots,) + tile, BF16)]
+        + [pltpu.VMEM((blocks * size, 2 * features), F32)]
+        + layer_scratch + [pltpu.VMEM((edges,) + tile, BF16), pltpu.VMEM(fine, BF16)] + back_scratch,
+    )
+
+    halo_grads, (hidden2, middle, grad_own), grad_sends = rest[:rounds], rest[rounds : rounds + 3], list(rest[rounds + 3 :])
     grad_parts = grad_sends[:1] + [swapped(piece, "sub", mask) for mask, piece in enumerate(grad_sends) if mask > 0]
 
     def last_out(h_ref, hidden_ref, w_ref, out_ref):
@@ -539,7 +534,7 @@
     def coarse_back(*refs):
         parts = refs[:sub_size]
         g0, g1, put, slope_ref, node_slope_ref, w_ref, fold_ref = refs[sub_size : sub_size + 7]
-        other_ref, out0, out1, grad_ref, d_node, recv_ref, send_ref, act_scr, pre_scr = refs[sub_size + 7 :]
+        other_ref, out0, out1, grad_ref, d_node, pre_ref, act_scr = refs[sub_size + 7 :]
         grad = parts[0][...].astype(F32)
         for part in parts[1:]:
             grad = grad + part[...].astype(F32)
@@ -552,23 +547,25 @@
             for e in range(degree):
                 edge = b * degree + e
                 d_pre = act_scr[rows_of(b), :] * slope_ref[edge].astype(F32)
-                total = d_pre if total is None else total + d_pre
-                pre_scr[rows_of(edge), :] = d_pre.astype(BF16)
-            recvs.append(total.astype(BF16))
+                if b >= held:
+                    total = d_pre if total is None else total + d_pre
+                pre_ref[rows_of(edge), :] = d_pre.astype(BF16)
+            if b >= held:
+                recvs.append(total.astype(BF16))
         senders = []
         for v in range(doms):
-            tiles_v = [mm(put[v * held + q], pre_scr[pl.ds((v * held + q) * width, width), :]) for q in range(held)]
+            tiles_v = [
+                mm(put[v * held + q, 0:far_size, :], pre_ref[pl.ds((v * held + q) * width, width), :]) for q in range(held)
+            ]
             senders.append(
-                [jnp.concatenate([t[n * size : (n + 1) * size, :] for t in tiles_v], axis=0) for n in range(doms)]
+                [jnp.concatenate([t[n * size : (n + 1) * size, :] for t in tiles_v], axis=0) for n in range(rounds)]
             )
-        send_ref[...] = (senders[0][0] + senders[1][1] + senders[2][2]).astype(BF16)
-        recv_ref[...] = jnp.concatenate(recvs[:held], axis=0)
-        to_rounds = [senders[0][1] + senders[1][0], senders[0][2] + senders[2][0]]
-        to_other = senders[1][2] + senders[2][1]
+        to_rounds = [senders[0][0] + senders[1][0], senders[0][1] + senders[2][0]]
+        to_other = senders[1][1] + senders[2][1]
         sent = mm_t(jnp.concatenate(to_rounds + [to_other], axis=0).astype(BF16), w_ref[1, 1])
         sums = (
             grad[rows_all:, :]
-            + mm_t(jnp.concatenate(recvs[held:], axis=0), w_ref[1, 0])
+            + mm_t(jnp.concatenate(recvs, axis=0), w_ref[1, 0])
             + mm_t(d_node[rows_all:, :], w_ref[1, 3])
             + sent[0 : rounds * rows_all, :]
         ).astype(BF16)
@@ -577,20 +574,37 @@
             out[0:at_tail, :] = sums[r * rows_all : (r + 1) * rows_all, :]
             out[at_tail:, :] = g[...]
 
-    other_send, *coarse_sends, coarse_grad, d_node, d_recv, d_send = run(
+    other_send, *coarse_sends, coarse_grad, d_node, d_pre = run(
         coarse_back,
         [(wide, BF16)] + [((halo_rows, features), BF16)] * rounds
-        + [(wide, F32), (all_wide, BF16), (wide, BF16), (wide, BF16)],
+        + [(wide, F32), (all_wide, BF16), ((coarse_edges * size, features), BF16)],
         *grad_parts, *halo_grads, coarse_put, slope1, node_slope1, w, fold,
-        scratch=[pltpu.VMEM(all_wide, F32), pltpu.VMEM((coarse_edges * size, features), BF16)],
+        scratch=[pltpu.VMEM(all_wide, F32)],
     )
     other = swapped(other_send, "dom", xor_bits[0] ^ xor_bits[1])
     returned = exchange(coarse_sends)
 
-    def coarse_own(grad_ref, d_node, d_recv, d_send, w_ref, own_ref):
-        own_ref[...] = own_back(grad_ref[...], 1, w_ref, d_node[0 : held * size, :], d_recv[...], d_send[...])
-
-    (coarse_grad,) = run(coarse_own, [(wide, F32)], coarse_grad, d_node, d_recv, d_send, w)
+    def coarse_own(grad_ref, put, d_node, d_pre, w_ref, own_ref):
+        width = degree * size
+        d_send, d_recv = [], []
+        for q in range(held):
+            total = None
+            for v in range(doms):
+                at = v * held + q
+                part = mm(put[at, far_size:, :], d_pre[pl.ds(at * width, width), :])
+                total = part if total is None else total + part
+            d_send.append(total)
+            total = None
+            for e in range(degree):
+                part = d_pre[rows_of(q * degree + e), :].astype(F32)
+                total = part if total is None else total + part
+            d_recv.append(total.astype(BF16))
+        own_ref[...] = own_back(
+            grad_ref[...], 1, w_ref, d_node[0 : held * size, :],
+            jnp.concatenate(d_recv, axis=0), jnp.concatenate(d_send, axis=0),
+        )
+
+    (coarse_grad,) = run(coarse_own, [(wide, F32)], coarse_grad, coarse_put, d_node, d_pre, w)
 
     def chip_sum(own_ref, other_ref, r0, r1, out_ref):
         total = own_ref[...] + other_ref[...].astype(F32)

time: 55.7 us -> 55.4 us (level)
    pallas_call x18 -> x17, Pallas kernels: 11.4 us -> 11.4 us  [run(): pl.pallas_call(kernel, out_shape=[jax.ShapeDtypeStruct(shape, dtype) for...]
  transfers between devices with their start and end apart: 16 -> 16, of which waited for: 11 -> 11; matrix products, arithmetic and copies ran while one was open for 0% -> 0% of each run, Pallas kernels for 11% -> 12%
where the time goes in v10:
time: 55.4 us; the launch traced here: 55.2 us
  starting transfers between devices  20.7 us (37%)
  waiting for transfers between devices  19.7 us (36%)
  Pallas kernels  14.1 us (25%)
  between operations  0.76 us (1%)
    ppermute x16, starting transfers between devices, swapped(): lax.ppermute(value, axis, [(source, source ^ mask) for source in range(si...  20.7 us
    ppermute x16, waiting for transfers between devices, swapped(): lax.ppermute(value, axis, [(source, source ^ mask) for source in range(si...  19.7 us
    pallas_call x17, Pallas kernels, run(): pl.pallas_call(kernel, out_shape=[jax.ShapeDtypeStruct(shape, dtype) for...  11.4 us
    pallas_call x2, Pallas kernels, run_hbm(): pl.pallas_call(kernel, out_shape=[pltpu.VMEM(shape, dtype) for shape, dty...  2.63 us
  transfers between devices with their start and end apart: 16, of which 11 were waited for; matrix products, arithmetic and copies ran while one was open for 0% of the time, Pallas kernels for 12%

profile of v10, /device:TPU:0, one launch (start us, length us, event | category | flops | bytes accessed | tf_op | source)
XLA Modules:
  0.0 55.2 jit_solution(1692077468535415672)
XLA Ops:
  0.6 0.9 %shard_map.113 = (bf16[512,128]{1,0:T(8,128)(2,1)S(1)}, bf16[16,128]{1,0:T(8,128)(2,1)S(1)}, bf16[144,128]{1,0:T(8,128)(2,1)S(1)}, bf16[144,128]{1,0:T(8,128)(2,1)S(1)}) custom-call(s32[1,2]{1,0:T(1,128)} %bitcast.12, s32[4,128]{1,0:T(4,128)} %bitcast.11, s32[1,4]{1,0:T(1,128)} %listed_in.1, s32[1,4]{1,0:T(1,128)} %bitcast.14, bf16[512,128]{1,0:T(8,128)(2,1)} %nodes_in.1), custom_call_target="tpu_custom_call" | custom-call | bytes 1048576 | tf_op jit(solution)/shard_map/pallas_call | solution.py:46
  1.6 4.1 %collective-permute-start = (bf16[144,128]{1,0:T(8,128)(2,1)S(1)}, bf16[144,128]{1,0:T(8,128)(2,1)S(1)}, u32[]{:S(2)}, u32[]{:S(2)}) collective-permute-start(bf16[144,128]{1,0:T(8,128)(2,1)S(1)} %get-tuple-element.61), channel_id=1, source_target_pairs={{0,8},{4,12},{8,0},{12,4},{1,9},{5,13},{9,1},{13,5},{2,10},{6,14},... | collective-permute-start | bytes 110600 | tf_op jit(solution)/shard_map/ppermute | solution.py:18
  5.7 1.6 %collective-permute-start.1 = (bf16[144,128]{1,0:T(8,128)(2,1)S(1)}, bf16[144,128]{1,0:T(8,128)(2,1)S(1)}, u32[]{:S(2)}, u32[]{:S(2)}) collective-permute-start(bf16[144,128]{1,0:T(8,128)(2,1)S(1)} %get-tuple-element.62), channel_id=1, source_target_pairs={{0,4},{4,0},{8,12},{12,8},{1,5},{5,1},{9,13},{13,9},{2,6},{6,2},{1... | collective-permute-start | bytes 110600 | tf_op jit(solution)/shard_map/ppermute | solution.py:18
  7.3 1.7 %shard_map.114 = (s32[16,128]{1,0:T(8,128)S(1)}, bf16[3,6,128,128]{3,2,1,0:T(8,128)(2,1)S(1)}, f32[3,2,128]{2,1,0:T(2,128)S(1)}, bf16[512,128]{1,0:T(8,128)(2,1)...) custom-call(s32[1,2]{1,0:T(1,128)} %bitcast.13, ...), custom_call_target="tpu_custom_call" | custom-call | bytes 1048576 | tf_op jit(solution)/shard_map/pallas_call | solution.py:46
  9.0 0.0 collective-permute-done.g0
  9.0 0.7 %collective-permute-done.1.g1 = bf16[144,128]{1,0:T(8,128)(2,1)S(1)} collective-permute-done((bf16[144,128]{1,0:T(8,128)(2,1)S(1)}, bf16[144,128]{1,0:T(8,128)(2,1)S(1)}, u32[]{:S(2)}, u32[]{:S(2)}) %collective-permute-start.1) | collective-permute-done | bytes 36896 | tf_op jit(solution)/shard_map/ppermute | solution.py:18
  9.6 0.8 %shard_map.115 = (bf16[512,128]{1,0:T(8,128)(2,1)S(1)}, s32[8,128]{1,0:T(8,128)S(1)}, bf16[6,128,128]{2,1,0:T(8,128)(2,1)S(1)}, bf16[272,128]{1,0:T(8,128)(2,1)S(1)}, bf16[272,128]{1,0:T(8,128)(2,1)S(1)}) custom-call(s32[24,128]{1,0:T(8,128)S(1)} %get-tuple-element.60.s_ref, bf16[144,128]{1,0:T(8,128)(2,1)S(1)} %collective-permute-done.g0, ...), custom_call_target="tpu_custom_call" | custom-call | bytes 1048576 | tf_op jit(solution)/shard_map/pallas_call | solution.py:34
  10.4 0.1 collective-permute-start.2
  10.5 1.2 %collective-permute-done.2.refs_1_ = bf16[272,128]{1,0:T(8,128)(2,1)S(1)} collective-permute-done((bf16[272,128]{1,0:T(8,128)(2,1)S(1)}, bf16[272,128]{1,0:T(8,128)(2,1)S(1)}, u32[]{:S(2)}, u32[]{:S(2)}) %collective-permute-start.2) | collective-permute-done | bytes 69664 | tf_op jit(solution)/shard_map/ppermute | solution.py:18
  11.8 1.6 %collective-permute-start.3 = (bf16[272,128]{1,0:T(8,128)(2,1)S(1)}, bf16[272,128]{1,0:T(8,128)(2,1)S(1)}, u32[]{:S(2)}, u32[]{:S(2)}) collective-permute-start(bf16[272,128]{1,0:T(8,128)(2,1)S(1)} %shard_map.116.refs_0_), channel_id=1, source_target_pairs={{0,2},{2,0},{1,3},{3,1},{4,6},{6,4},{5,7},{7,5},{8,10},{10,8},{9,1... | collective-permute-start | bytes 208904 | tf_op jit(solution)/shard_map/ppermute | solution.py:18
  13.4 2.8 %collective-permute-done.3.refs_1_ = bf16[272,128]{1,0:T(8,128)(2,1)S(1)} collective-permute-done((bf16[272,128]{1,0:T(8,128)(2,1)S(1)}, bf16[272,128]{1,0:T(8,128)(2,1)S(1)}, u32[]{:S(2)}, u32[]{:S(2)}) %collective-permute-start.3) | collective-permute-done | bytes 69664 | tf_op jit(solution)/shard_map/ppermute | solution.py:18
  16.2 0.1 shard_map.117
  16.3 1.2 %collective-permute-start.4 = (bf16[384,128]{1,0:T(8,128)(2,1)S(1)}, bf16[384,128]{1,0:T(8,128)(2,1)S(1)}, u32[]{:S(2)}, u32[]{:S(2)}) collective-permute-start(bf16[384,128]{1,0:T(8,128)(2,1)S(1)} %get-tuple-element.74), channel_id=1, source_target_pairs={{0,8},{4,12},{8,0},{12,4},{1,9},{5,13},{9,1},{13,5},{2,10},{6,14},... | collective-permute-start | bytes 294920 | tf_op jit(solution)/shard_map/ppermute | solution.py:18
  17.5 1.6 %collective-permute-start.5 = (bf16[384,128]{1,0:T(8,128)(2,1)S(1)}, bf16[384,128]{1,0:T(8,128)(2,1)S(1)}, u32[]{:S(2)}, u32[]{:S(2)}) collective-permute-start(bf16[384,128]{1,0:T(8,128)(2,1)S(1)} %get-tuple-element.75), channel_id=1, source_target_pairs={{0,4},{4,0},{8,12},{12,8},{1,5},{5,1},{9,13},{13,9},{2,6},{6,2},{1... | collective-permute-start | bytes 294920 | tf_op jit(solution)/shard_map/ppermute | solution.py:18
  19.1 1.6 %collective-permute-start.6 = (bf16[256,128]{1,0:T(8,128)(2,1)S(1)}, bf16[256,128]{1,0:T(8,128)(2,1)S(1)}, u32[]{:S(2)}, u32[]{:S(2)}) collective-permute-start(bf16[256,128]{1,0:T(8,128)(2,1)S(1)} %get-tuple-element.76), channel_id=1, source_target_pairs={{0,12},{4,8},{8,4},{12,0},{1,13},{5,9},{9,5},{13,1},{2,14},{6,10},... | collective-permute-start | bytes 196616 | tf_op jit(solution)/shard_map/ppermute | solution.py:18
  20.7 1.6 %shard_map.118 = (f32[24,128,128]{2,1,0:T(8,128)S(1)}, f32[256,128]{1,0:T(8,128)S(1)}, bf16[2,128,128]{2,1,0:T(8,128)(2,1)S(1)}, bf16[2,128,256]{2,1,0:T(8,128)(...) custom-call(bf16[256,128]{1,0:T(8,128)(2,1)S(1)} %get-tuple-element., ...), custom_call_target="tpu_custom_call" | custom-call | bytes 1048576 | tf_op jit(solution)/shard_map/pallas_call | solution.py:34
  22.3 3.4 %collective-permute-done.6.other_ref.refs_0_ = bf16[256,128]{1,0:T(8,128)(2,1)S(1)} collective-permute-done((bf16[256,128]{1,0:T(8,128)(2,1)S(1)}, bf16[256,128]{1,0:T(8,128)(2,1)S(1)}, u32[]{:S(2)}, u32[]{:S(2)}) %collective-permute-start.6) | collective-permute-done | bytes 65568 | tf_op jit(solution)/shard_map/ppermute | solution.py:18
  25.7 0.0 collective-permute-done.4.g0.refs_1_
  25.7 0.0 collective-permute-done.5.g1.refs_2_
  25.7 1.1 %shard_map.119.refs_0_ = bf16[768,128]{1,0:T(8,128)(2,1)S(1)} custom-call(bf16[256,128]{1,0:T(8,128)(2,1)S(1)} %collective-permute-done.6.other_ref.refs_0_, bf16[384,128]{1,0:T(8,128)(2,1)S(1)} %collective-permute-done.4.g0.refs_1_, bf16[384,128]{1,0:T(8,128)(2,1)S(1)} %collective-permute-done.5.g1.refs_2_, bf16[256,128]{1,0:T(8,128)(2,1)S(1)} %get-tuple-element.77.h_ref, ...), custom_call_target="tpu_custom_call" | custom-call | bytes 1048576 | tf_op jit(solution)/shard_map/pallas_call | solution.py:34
  26.7 0.1 collective-permute-start.7
  26.8 1.4 %collective-permute-done.7.refs_1_ = bf16[768,128]{1,0:T(8,128)(2,1)S(1)} collective-permute-done((bf16[768,128]{1,0:T(8,128)(2,1)S(1)}, bf16[768,128]{1,0:T(8,128)(2,1)S(1)}, u32[]{:S(2)}, u32[]{:S(2)}) %collective-permute-start.7) | collective-permute-done | bytes 196640 | tf_op jit(solution)/shard_map/ppermute | solution.py:18
  28.2 1.7 %shard_map.120 = (bf16[128,128]{1,0:T(8,128)(2,1)S(1)}, bf16[128,128]{1,0:T(8,128)(2,1)S(1)}, bf16[512,128]{1,0:T(8,128)(2,1)S(1)}, bf16[768,128]{1,0:T(8,128)(2...) custom-call(s32[24,128]{1,0:T(8,128)S(1)} %get-tuple-element.60.s_ref, ...), custom_call_target="tpu_custom_call" | custom-call | bytes 1048576 | tf_op jit(solution)/shard_map/pallas_call | solution.py:34
  30.0 0.2 collective-permute-start.8
  30.2 1.1 %shard_map.122 = (bf16[24,128,128]{2,1,0:T(8,128)(2,1)S(1)}, bf16[768,128]{1,0:T(8,128)(2,1)S(1)}) custom-call(bf16[256,128]{1,0:T(8,128)(2,1)S(1)} %collective-permute-done.6.other_ref.refs_0_, bf16[384,128]{1,0:T(8,128)(2,1)S(1)} %collective-permute-done.4.g0.refs_1_, bf16[384,128]{1,0:T(8,128)(2,1)S(1)} %collective-permute-done.5.g1.refs_2_, ...), custom_call_target="tpu_custom_call" | custom-call | bytes 1048576 | tf_op jit(solution)/shard_map/pallas_call | solution.py:34
  31.2 0.2 collective-permute-done.8.refs_1_
  31.5 1.1 %shard_map.123 = (bf16[256,128]{1,0:T(8,128)(2,1)S(1)}, bf16[384,128]{1,0:T(8,128)(2,1)S(1)}, bf16[384,128]{1,0:T(8,128)(2,1)S(1)}, f32[256,128]{1,0:T(8,128)S(1...) custom-call(bf16[768,128]{1,0:T(8,128)(2,1)S(1)} %get-tuple-element.92.refs_0_, ...), custom_call_target="tpu_custom_call" | custom-call | bytes 1048576 | tf_op jit(solution)/shard_map/pallas_call | solution.py:34
  32.6 1.4 %collective-permute-start.10 = (bf16[384,128]{1,0:T(8,128)(2,1)S(1)}, bf16[384,128]{1,0:T(8,128)(2,1)S(1)}, u32[]{:S(2)}, u32[]{:S(2)}) collective-permute-start(bf16[384,128]{1,0:T(8,128)(2,1)S(1)} %get-tuple-element.103), channel_id=1, source_target_pairs={{0,8},{4,12},{8,0},{12,4},{1,9},{5,13},{9,1},{13,5},{2,10},{6,14},... | collective-permute-start | bytes 294920 | tf_op jit(solution)/shard_map/ppermute | solution.py:18
  34.0 0.8 %collective-permute-start.11 = (bf16[384,128]{1,0:T(8,128)(2,1)S(1)}, bf16[384,128]{1,0:T(8,128)(2,1)S(1)}, u32[]{:S(2)}, u32[]{:S(2)}) collective-permute-start(bf16[384,128]{1,0:T(8,128)(2,1)S(1)} %get-tuple-element.104), channel_id=1, source_target_pairs={{0,4},{4,0},{8,12},{12,8},{1,5},{5,1},{9,13},{13,9},{2,6},{6,2},{1... | collective-permute-start | bytes 294920 | tf_op jit(solution)/shard_map/ppermute | solution.py:18
  34.8 2.3 %collective-permute-start.9 = (bf16[256,128]{1,0:T(8,128)(2,1)S(1)}, bf16[256,128]{1,0:T(8,128)(2,1)S(1)}, u32[]{:S(2)}, u32[]{:S(2)}) collective-permute-start(bf16[256,128]{1,0:T(8,128)(2,1)S(1)} %get-tuple-element.102), channel_id=1, source_target_pairs={{0,12},{4,8},{8,4},{12,0},{1,13},{5,9},{9,5},{13,1},{2,14},{6,10},... | collective-permute-start | bytes 196616 | tf_op jit(solution)/shard_map/ppermute | solution.py:18
  37.1 0.6 %shard_map.124.own_ref = f32[256,128]{1,0:T(8,128)S(1)} custom-call(f32[256,128]{1,0:T(8,128)S(1)} %get-tuple-element.99.grad_ref, bf16[6,384,512]{2,1,0:T(8,128)(2,1)S(1)} %get-tuple-element.96.refs_4_.put, bf16[768,128]{1,0:T(8,128)(2,1)S(1)} %get-tuple-element.100.d_node, bf16[3072,128]{1,0:T(8,128)(2,1)S(1)} %get-tuple-element.101.d_pre, ...), custom_call_target="tpu_custom_call" | custom-call | bytes 1048576 | tf_op jit(solution)/shard_map/pallas_call | solution.py:34
  37.6 4.7 %collective-permute-done.9.other_ref = bf16[256,128]{1,0:T(8,128)(2,1)S(1)} collective-permute-done((bf16[256,128]{1,0:T(8,128)(2,1)S(1)}, bf16[256,128]{1,0:T(8,128)(2,1)S(1)}, u32[]{:S(2)}, u32[]{:S(2)}) %collective-permute-start.9) | collective-permute-done | bytes 65568 | tf_op jit(solution)/shard_map/ppermute | solution.py:18
  42.4 0.0 collective-permute-done.10.r0
  42.4 0.0 collective-permute-done.11.r1
  42.4 1.5 %collective-permute-start.12 = (bf16[256,128]{1,0:T(8,128)(2,1)S(1)}, bf16[256,128]{1,0:T(8,128)(2,1)S(1)}, u32[]{:S(2)}, u32[]{:S(2)}) collective-permute-start(bf16[256,128]{1,0:T(8,128)(2,1)S(1)} %shard_map.125.refs_0_), channel_id=1, source_target_pairs={{0,2},{2,0},{1,3},{3,1},{4,6},{6,4},{5,7},{7,5},{8,10},{10,8},{9,1... | collective-permute-start | bytes 196616 | tf_op jit(solution)/shard_map/ppermute | solution.py:18
  44.0 2.8 %collective-permute-done.12.refs_1_ = bf16[256,128]{1,0:T(8,128)(2,1)S(1)} collective-permute-done((bf16[256,128]{1,0:T(8,128)(2,1)S(1)}, bf16[256,128]{1,0:T(8,128)(2,1)S(1)}, u32[]{:S(2)}, u32[]{:S(2)}) %collective-permute-start.12) | collective-permute-done | bytes 65568 | tf_op jit(solution)/shard_map/ppermute | solution.py:18
  46.8 0.1 collective-permute-start.13
  46.8 0.7 %shard_map.128 = (bf16[16,128,128]{2,1,0:T(8,128)(2,1)S(1)}, bf16[512,128]{1,0:T(8,128)(2,1)S(1)}) custom-call(s32[24,128]{1,0:T(8,128)S(1)} %get-tuple-element.60.s_ref, f32[512,128]{1,0:T(8,128)S(1)} %get-tuple-element.63.recv, f32[512,128]{1,0:T(8,128)S(1)} %get-tuple-element.64.node, bf16[6,128,128]{2,1,0:T(8,128)(2,1)S(1)} %get-tuple-element.107.send_ref, ...), custom_call_target="tpu_custom_call" | custom-call | bytes 1048576 | tf_op jit(solution)/shard_map/pallas_call | solution.py:34
  47.5 0.1 shard_map.127.refs_2_
  47.6 0.5 collective-permute-done.13.refs_1_
  48.1 0.8 %shard_map.129 = (bf16[128,128]{1,0:T(8,128)(2,1)S(1)}, bf16[128,128]{1,0:T(8,128)(2,1)S(1)}, bf16[512,128]{1,0:T(8,128)(2,1)S(1)}, bf16[512,128]{1,0:T(8,128)(2...) custom-call(s32[24,128]{1,0:T(8,128)S(1)} %get-tuple-element.60.s_ref, ...), custom_call_target="tpu_custom_call" | custom-call | bytes 1048576 | tf_op jit(solution)/shard_map/pallas_call | solution.py:34
  48.9 1.7 %collective-permute-start.14 = (bf16[128,128]{1,0:T(8,128)(2,1)S(1)}, bf16[128,128]{1,0:T(8,128)(2,1)S(1)}, u32[]{:S(2)}, u32[]{:S(2)}) collective-permute-start(bf16[128,128]{1,0:T(8,128)(2,1)S(1)} %get-tuple-element.110), channel_id=1, source_target_pairs={{0,8},{4,12},{8,0},{12,4},{1,9},{5,13},{9,1},{13,5},{2,10},{6,14},... | collective-permute-start | bytes 98312 | tf_op jit(solution)/shard_map/ppermute | solution.py:18
  50.6 0.9 %collective-permute-start.15 = (bf16[128,128]{1,0:T(8,128)(2,1)S(1)}, bf16[128,128]{1,0:T(8,128)(2,1)S(1)}, u32[]{:S(2)}, u32[]{:S(2)}) collective-permute-start(bf16[128,128]{1,0:T(8,128)(2,1)S(1)} %get-tuple-element.111), channel_id=1, source_target_pairs={{0,4},{4,0},{8,12},{12,8},{1,5},{5,1},{9,13},{13,9},{2,6},{6,2},{1... | collective-permute-start | bytes 98312 | tf_op jit(solution)/shard_map/ppermute | solution.py:18
  51.5 0.8 %shard_map.121 = bf16[512,128]{1,0:T(8,128)(2,1)} custom-call(bf16[768,128]{1,0:T(8,128)(2,1)S(1)} %get-tuple-element.90.h_ref, bf16[512,128]{1,0:T(8,128)(2,1)S(1)} %get-tuple-element.91.hidden_ref, bf16[3,6,128,128]{3,2,1,0:T(8,128)(2,1)S(1)} %get-tuple-element.67.w_ref.refs_6_.refs_7_), custom_call_target="tpu_custom_call" | custom-call | bytes 1048576 | tf_op jit(solution)/shard_map/pallas_call | solution.py:34
  52.3 0.3 shard_map.130
  52.6 1.5 %collective-permute-done.14.r0 = bf16[128,128]{1,0:T(8,128)(2,1)S(1)} collective-permute-done((bf16[128,128]{1,0:T(8,128)(2,1)S(1)}, bf16[128,128]{1,0:T(8,128)(2,1)S(1)}, u32[]{:S(2)}, u32[]{:S(2)}) %collective-permute-start.14) | collective-permute-done | bytes 32800 | tf_op jit(solution)/shard_map/ppermute | solution.py:18
  54.1 0.4 collective-permute-done.15.r1
  54.5 0.7 %shard_map.131 = f32[4,128,128]{2,1,0:T(8,128)} custom-call(s32[24,128]{1,0:T(8,128)S(1)} %get-tuple-element.60.s_ref, bf16[128,128]{1,0:T(8,128)(2,1)S(1)} %collective-permute-done.14.r0, bf16[128,128]{1,0:T(8,128)(2,1)S(1)} %collective-permute-done.15.r1, f32[4,128,128]{2,1,0:T(8,128)S(1)} %bitcast.7), custom_call_target="tpu_custom_call" | custom-call | bytes 1048576 | tf_op jit(solution)/shard_map/pallas_call | solution.py:34
  (3 shorter events, 0.1 us)
Async XLA Ops:
  1.6 7.4 %collective-permute-start = (bf16[144,128]{1,0:T(8,128)(2,1)S(1)}, bf16[144,128]{1,0:T(8,128)(2,1)S(1)}, u32[]{:S(2)}, u32[]{:S(2)}) collective-permute-start(bf16[144,128]{1,0:T(8,128)(2,1)S(1)} %get-tuple-element.61), channel_id=1, source_target_pairs={{0,8},{4,12},{8,0},{12,4},{1,9},{5,13},{9,1},{13,5},{2,10},{6,14},... | collective-permute-start | bytes 110600 | tf_op jit(solution)/shard_map/ppermute | solution.py:18
  5.7 4.0 %collective-permute-start.1 = (bf16[144,128]{1,0:T(8,128)(2,1)S(1)}, bf16[144,128]{1,0:T(8,128)(2,1)S(1)}, u32[]{:S(2)}, u32[]{:S(2)}) collective-permute-start(bf16[144,128]{1,0:T(8,128)(2,1)S(1)} %get-tuple-element.62), channel_id=1, source_target_pairs={{0,4},{4,0},{8,12},{12,8},{1,5},{5,1},{9,13},{13,9},{2,6},{6,2},{1... | collective-permute-start | bytes 110600 | tf_op jit(solution)/shard_map/ppermute | solution.py:18
  10.4 1.3 %collective-permute-start.2 = (bf16[272,128]{1,0:T(8,128)(2,1)S(1)}, bf16[272,128]{1,0:T(8,128)(2,1)S(1)}, u32[]{:S(2)}, u32[]{:S(2)}) collective-permute-start(bf16[272,128]{1,0:T(8,128)(2,1)S(1)} %get-tuple-element.73), channel_id=1, source_target_pairs={{0,1},{1,0},{2,3},{3,2},{4,5},{5,4},{6,7},{7,6},{8,9},{9,8},{10,11... | collective-permute-start | bytes 208904 | tf_op jit(solution)/shard_map/ppermute | solution.py:18
  11.8 4.4 %collective-permute-start.3 = (bf16[272,128]{1,0:T(8,128)(2,1)S(1)}, bf16[272,128]{1,0:T(8,128)(2,1)S(1)}, u32[]{:S(2)}, u32[]{:S(2)}) collective-permute-start(bf16[272,128]{1,0:T(8,128)(2,1)S(1)} %shard_map.116.refs_0_), channel_id=1, source_target_pairs={{0,2},{2,0},{1,3},{3,1},{4,6},{6,4},{5,7},{7,5},{8,10},{10,8},{9,1... | collective-permute-start | bytes 208904 | tf_op jit(solution)/shard_map/ppermute | solution.py:18
  16.3 9.4 %collective-permute-start.4 = (bf16[384,128]{1,0:T(8,128)(2,1)S(1)}, bf16[384,128]{1,0:T(8,128)(2,1)S(1)}, u32[]{:S(2)}, u32[]{:S(2)}) collective-permute-start(bf16[384,128]{1,0:T(8,128)(2,1)S(1)} %get-tuple-element.74), channel_id=1, source_target_pairs={{0,8},{4,12},{8,0},{12,4},{1,9},{5,13},{9,1},{13,5},{2,10},{6,14},... | collective-permute-start | bytes 294920 | tf_op jit(solution)/shard_map/ppermute | solution.py:18
  17.5 8.2 %collective-permute-start.5 = (bf16[384,128]{1,0:T(8,128)(2,1)S(1)}, bf16[384,128]{1,0:T(8,128)(2,1)S(1)}, u32[]{:S(2)}, u32[]{:S(2)}) collective-permute-start(bf16[384,128]{1,0:T(8,128)(2,1)S(1)} %get-tuple-element.75), channel_id=1, source_target_pairs={{0,4},{4,0},{8,12},{12,8},{1,5},{5,1},{9,13},{13,9},{2,6},{6,2},{1... | collective-permute-start | bytes 294920 | tf_op jit(solution)/shard_map/ppermute | solution.py:18
  19.1 6.5 %collective-permute-start.6 = (bf16[256,128]{1,0:T(8,128)(2,1)S(1)}, bf16[256,128]{1,0:T(8,128)(2,1)S(1)}, u32[]{:S(2)}, u32[]{:S(2)}) collective-permute-start(bf16[256,128]{1,0:T(8,128)(2,1)S(1)} %get-tuple-element.76), channel_id=1, source_target_pairs={{0,12},{4,8},{8,4},{12,0},{1,13},{5,9},{9,5},{13,1},{2,14},{6,10},... | collective-permute-start | bytes 196616 | tf_op jit(solution)/shard_map/ppermute | solution.py:18
  26.7 1.5 %collective-permute-start.7 = (bf16[768,128]{1,0:T(8,128)(2,1)S(1)}, bf16[768,128]{1,0:T(8,128)(2,1)S(1)}, u32[]{:S(2)}, u32[]{:S(2)}) collective-permute-start(bf16[768,128]{1,0:T(8,128)(2,1)S(1)} %shard_map.119.refs_0_), channel_id=1, source_target_pairs={{0,1},{1,0},{2,3},{3,2},{4,5},{5,4},{6,7},{7,6},{8,9},{9,8},{10,11... | collective-permute-start | bytes 589832 | tf_op jit(solution)/shard_map/ppermute | solution.py:18
  30.0 1.5 %collective-permute-start.8 = (bf16[768,128]{1,0:T(8,128)(2,1)S(1)}, bf16[768,128]{1,0:T(8,128)(2,1)S(1)}, u32[]{:S(2)}, u32[]{:S(2)}) collective-permute-start(bf16[768,128]{1,0:T(8,128)(2,1)S(1)} %get-tuple-element.93), channel_id=1, source_target_pairs={{0,1},{1,0},{2,3},{3,2},{4,5},{5,4},{6,7},{7,6},{8,9},{9,8},{10,11... | collective-permute-start | bytes 589832 | tf_op jit(solution)/shard_map/ppermute | solution.py:18
  32.6 9.7 %collective-permute-start.10 = (bf16[384,128]{1,0:T(8,128)(2,1)S(1)}, bf16[384,128]{1,0:T(8,128)(2,1)S(1)}, u32[]{:S(2)}, u32[]{:S(2)}) collective-permute-start(bf16[384,128]{1,0:T(8,128)(2,1)S(1)} %get-tuple-element.103), channel_id=1, source_target_pairs={{0,8},{4,12},{8,0},{12,4},{1,9},{5,13},{9,1},{13,5},{2,10},{6,14},... | collective-permute-start | bytes 294920 | tf_op jit(solution)/shard_map/ppermute | solution.py:18
  34.0 8.3 %collective-permute-start.11 = (bf16[384,128]{1,0:T(8,128)(2,1)S(1)}, bf16[384,128]{1,0:T(8,128)(2,1)S(1)}, u32[]{:S(2)}, u32[]{:S(2)}) collective-permute-start(bf16[384,128]{1,0:T(8,128)(2,1)S(1)} %get-tuple-element.104), channel_id=1, source_target_pairs={{0,4},{4,0},{8,12},{12,8},{1,5},{5,1},{9,13},{13,9},{2,6},{6,2},{1... | collective-permute-start | bytes 294920 | tf_op jit(solution)/shard_map/ppermute | solution.py:18
  34.8 7.6 %collective-permute-start.9 = (bf16[256,128]{1,0:T(8,128)(2,1)S(1)}, bf16[256,128]{1,0:T(8,128)(2,1)S(1)}, u32[]{:S(2)}, u32[]{:S(2)}) collective-permute-start(bf16[256,128]{1,0:T(8,128)(2,1)S(1)} %get-tuple-element.102), channel_id=1, source_target_pairs={{0,12},{4,8},{8,4},{12,0},{1,13},{5,9},{9,5},{13,1},{2,14},{6,10},... | collective-permute-start | bytes 196616 | tf_op jit(solution)/shard_map/ppermute | solution.py:18
  42.4 4.3 %collective-permute-start.12 = (bf16[256,128]{1,0:T(8,128)(2,1)S(1)}, bf16[256,128]{1,0:T(8,128)(2,1)S(1)}, u32[]{:S(2)}, u32[]{:S(2)}) collective-permute-start(bf16[256,128]{1,0:T(8,128)(2,1)S(1)} %shard_map.125.refs_0_), channel_id=1, source_target_pairs={{0,2},{2,0},{1,3},{3,1},{4,6},{6,4},{5,7},{7,5},{8,10},{10,8},{9,1... | collective-permute-start | bytes 196616 | tf_op jit(solution)/shard_map/ppermute | solution.py:18
  46.8 1.3 %collective-permute-start.13 = (bf16[256,128]{1,0:T(8,128)(2,1)S(1)}, bf16[256,128]{1,0:T(8,128)(2,1)S(1)}, u32[]{:S(2)}, u32[]{:S(2)}) collective-permute-start(bf16[256,128]{1,0:T(8,128)(2,1)S(1)} %shard_map.126.refs_0_), channel_id=1, source_target_pairs={{0,1},{1,0},{2,3},{3,2},{4,5},{5,4},{6,7},{7,6},{8,9},{9,8},{10,11... | collective-permute-start | bytes 196616 | tf_op jit(solution)/shard_map/ppermute | solution.py:18
  48.9 5.2 %collective-permute-start.14 = (bf16[128,128]{1,0:T(8,128)(2,1)S(1)}, bf16[128,128]{1,0:T(8,128)(2,1)S(1)}, u32[]{:S(2)}, u32[]{:S(2)}) collective-permute-start(bf16[128,128]{1,0:T(8,128)(2,1)S(1)} %get-tuple-element.110), channel_id=1, source_target_pairs={{0,8},{4,12},{8,0},{12,4},{1,9},{5,13},{9,1},{13,5},{2,10},{6,14},... | collective-permute-start | bytes 98312 | tf_op jit(solution)/shard_map/ppermute | solution.py:18
  50.6 3.9 %collective-permute-start.15 = (bf16[128,128]{1,0:T(8,128)(2,1)S(1)}, bf16[128,128]{1,0:T(8,128)(2,1)S(1)}, u32[]{:S(2)}, u32[]{:S(2)}) collective-permute-start(bf16[128,128]{1,0:T(8,128)(2,1)S(1)} %get-tuple-element.111), channel_id=1, source_target_pairs={{0,4},{4,0},{8,12},{12,8},{1,5},{5,1},{9,13},{13,9},{2,6},{6,2},{1... | collective-permute-start | bytes 98312 | tf_op jit(solution)/shard_map/ppermute | solution.py:18

commit v11 on v10

--- a/solution.py
+++ b/solution.py
@@ -356,8 +356,9 @@
         for part, tail in zip(parts[1:], tails[1:]):
             total = total + part[0:at_tail, :].astype(F32)
             counts = counts + tail[at_last : at_last + 1, :]
+        inverses = 1.0 / jnp.maximum(counts, 1.0)
         for q in range(held):
-            inverse_ref[q : q + 1, :] = jnp.broadcast_to(1.0 / jnp.maximum(counts[:, q : q + 1], 1.0), (1, features))
+            inverse_ref[q : q + 1, :] = jnp.broadcast_to(inverses[:, q : q + 1], (1, features))
         for q in range(held):
             start = (total[q * size : (q + 1) * size, :] * inverse_ref[q : q + 1, :]).astype(BF16)
             for out in (start_ref, other, out0, out1):
@@ -510,8 +511,8 @@
             slot = scalar(slots_ref, r)
             for sub_mask, out in enumerate(outs):
                 for q in range(held):
-                    hit = (slot == q * sub_size + (sub ^ sub_mask)).astype(F32)
-                    out[rows_of((1 + r) * held + q), :] = (g[...].astype(F32) * hit).astype(BF16)
+                    hit = slot == q * sub_size + (sub ^ sub_mask)
+                    out[rows_of((1 + r) * held + q), :] = jnp.where(hit, g[...], jnp.zeros(tile, BF16))
 
     rest = run(
         last_layer,

time: 55.4 us -> 55.5 us (level)
  no operation moved by 1% of the time
where the time goes in v11:
time: 55.5 us; the launch traced here: 55.2 us
  starting transfers between devices  20.7 us (37%)
  waiting for transfers between devices  19.7 us (35%)
  Pallas kernels  14.1 us (25%)
  between operations  0.76 us (1%)
    ppermute x16, starting transfers between devices, swapped(): lax.ppermute(value, axis, [(source, source ^ mask) for source in range(si...  20.7 us
    ppermute x16, waiting for transfers between devices, swapped(): lax.ppermute(value, axis, [(source, source ^ mask) for source in range(si...  19.7 us
    pallas_call x17, Pallas kernels, run(): pl.pallas_call(kernel, out_shape=[jax.ShapeDtypeStruct(shape, dtype) for...  11.5 us
    pallas_call x2, Pallas kernels, run_hbm(): pl.pallas_call(kernel, out_shape=[pltpu.VMEM(shape, dtype) for shape, dty...  2.63 us
  transfers between devices with their start and end apart: 16, of which 11 were waited for; matrix products, arithmetic and copies ran while one was open for 0% of the time, Pallas kernels for 12%

profile of v11, /device:TPU:0, one launch (start us, length us, event | category | flops | bytes accessed | tf_op | source)
XLA Modules:
  0.0 55.2 jit_solution(13285059360996090945)
XLA Ops:
  0.6 0.9 %shard_map.113 = (bf16[512,128]{1,0:T(8,128)(2,1)S(1)}, bf16[16,128]{1,0:T(8,128)(2,1)S(1)}, bf16[144,128]{1,0:T(8,128)(2,1)S(1)}, bf16[144,128]{1,0:T(8,128)(2,1)S(1)}) custom-call(s32[1,2]{1,0:T(1,128)} %bitcast.12, s32[4,128]{1,0:T(4,128)} %bitcast.11, s32[1,4]{1,0:T(1,128)} %listed_in.1, s32[1,4]{1,0:T(1,128)} %bitcast.14, bf16[512,128]{1,0:T(8,128)(2,1)} %nodes_in.1), custom_call_target="tpu_custom_call" | custom-call | bytes 1048576 | tf_op jit(solution)/shard_map/pallas_call | solution.py:46
  1.6 4.1 %collective-permute-start = (bf16[144,128]{1,0:T(8,128)(2,1)S(1)}, bf16[144,128]{1,0:T(8,128)(2,1)S(1)}, u32[]{:S(2)}, u32[]{:S(2)}) collective-permute-start(bf16[144,128]{1,0:T(8,128)(2,1)S(1)} %get-tuple-element.61), channel_id=1, source_target_pairs={{0,8},{4,12},{8,0},{12,4},{1,9},{5,13},{9,1},{13,5},{2,10},{6,14},... | collective-permute-start | bytes 110600 | tf_op jit(solution)/shard_map/ppermute | solution.py:18
  5.7 1.6 %collective-permute-start.1 = (bf16[144,128]{1,0:T(8,128)(2,1)S(1)}, bf16[144,128]{1,0:T(8,128)(2,1)S(1)}, u32[]{:S(2)}, u32[]{:S(2)}) collective-permute-start(bf16[144,128]{1,0:T(8,128)(2,1)S(1)} %get-tuple-element.62), channel_id=1, source_target_pairs={{0,4},{4,0},{8,12},{12,8},{1,5},{5,1},{9,13},{13,9},{2,6},{6,2},{1... | collective-permute-start | bytes 110600 | tf_op jit(solution)/shard_map/ppermute | solution.py:18
  7.3 1.7 %shard_map.114 = (s32[16,128]{1,0:T(8,128)S(1)}, bf16[3,6,128,128]{3,2,1,0:T(8,128)(2,1)S(1)}, f32[3,2,128]{2,1,0:T(2,128)S(1)}, bf16[512,128]{1,0:T(8,128)(2,1)...) custom-call(s32[1,2]{1,0:T(1,128)} %bitcast.13, ...), custom_call_target="tpu_custom_call" | custom-call | bytes 1048576 | tf_op jit(solution)/shard_map/pallas_call | solution.py:46
  9.0 0.0 collective-permute-done.g0
  9.0 0.7 %collective-permute-done.1.g1 = bf16[144,128]{1,0:T(8,128)(2,1)S(1)} collective-permute-done((bf16[144,128]{1,0:T(8,128)(2,1)S(1)}, bf16[144,128]{1,0:T(8,128)(2,1)S(1)}, u32[]{:S(2)}, u32[]{:S(2)}) %collective-permute-start.1) | collective-permute-done | bytes 36896 | tf_op jit(solution)/shard_map/ppermute | solution.py:18
  9.6 0.8 %shard_map.115 = (bf16[512,128]{1,0:T(8,128)(2,1)S(1)}, s32[8,128]{1,0:T(8,128)S(1)}, bf16[6,128,128]{2,1,0:T(8,128)(2,1)S(1)}, bf16[272,128]{1,0:T(8,128)(2,1)S(1)}, bf16[272,128]{1,0:T(8,128)(2,1)S(1)}) custom-call(s32[24,128]{1,0:T(8,128)S(1)} %get-tuple-element.60.s_ref, bf16[144,128]{1,0:T(8,128)(2,1)S(1)} %collective-permute-done.g0, ...), custom_call_target="tpu_custom_call" | custom-call | bytes 1048576 | tf_op jit(solution)/shard_map/pallas_call | solution.py:34
  10.4 0.1 collective-permute-start.2
  10.5 1.2 %collective-permute-done.2.refs_1_ = bf16[272,128]{1,0:T(8,128)(2,1)S(1)} collective-permute-done((bf16[272,128]{1,0:T(8,128)(2,1)S(1)}, bf16[272,128]{1,0:T(8,128)(2,1)S(1)}, u32[]{:S(2)}, u32[]{:S(2)}) %collective-permute-start.2) | collective-permute-done | bytes 69664 | tf_op jit(solution)/shard_map/ppermute | solution.py:18
  11.8 1.6 %collective-permute-start.3 = (bf16[272,128]{1,0:T(8,128)(2,1)S(1)}, bf16[272,128]{1,0:T(8,128)(2,1)S(1)}, u32[]{:S(2)}, u32[]{:S(2)}) collective-permute-start(bf16[272,128]{1,0:T(8,128)(2,1)S(1)} %shard_map.116.refs_0_), channel_id=1, source_target_pairs={{0,2},{2,0},{1,3},{3,1},{4,6},{6,4},{5,7},{7,5},{8,10},{10,8},{9,1... | collective-permute-start | bytes 208904 | tf_op jit(solution)/shard_map/ppermute | solution.py:18
  13.4 2.8 %collective-permute-done.3.refs_1_ = bf16[272,128]{1,0:T(8,128)(2,1)S(1)} collective-permute-done((bf16[272,128]{1,0:T(8,128)(2,1)S(1)}, bf16[272,128]{1,0:T(8,128)(2,1)S(1)}, u32[]{:S(2)}, u32[]{:S(2)}) %collective-permute-start.3) | collective-permute-done | bytes 69664 | tf_op jit(solution)/shard_map/ppermute | solution.py:18
  16.2 0.1 shard_map.117
  16.3 1.2 %collective-permute-start.4 = (bf16[384,128]{1,0:T(8,128)(2,1)S(1)}, bf16[384,128]{1,0:T(8,128)(2,1)S(1)}, u32[]{:S(2)}, u32[]{:S(2)}) collective-permute-start(bf16[384,128]{1,0:T(8,128)(2,1)S(1)} %get-tuple-element.74), channel_id=1, source_target_pairs={{0,8},{4,12},{8,0},{12,4},{1,9},{5,13},{9,1},{13,5},{2,10},{6,14},... | collective-permute-start | bytes 294920 | tf_op jit(solution)/shard_map/ppermute | solution.py:18
  17.5 1.6 %collective-permute-start.5 = (bf16[384,128]{1,0:T(8,128)(2,1)S(1)}, bf16[384,128]{1,0:T(8,128)(2,1)S(1)}, u32[]{:S(2)}, u32[]{:S(2)}) collective-permute-start(bf16[384,128]{1,0:T(8,128)(2,1)S(1)} %get-tuple-element.75), channel_id=1, source_target_pairs={{0,4},{4,0},{8,12},{12,8},{1,5},{5,1},{9,13},{13,9},{2,6},{6,2},{1... | collective-permute-start | bytes 294920 | tf_op jit(solution)/shard_map/ppermute | solution.py:18
  19.1 1.6 %collective-permute-start.6 = (bf16[256,128]{1,0:T(8,128)(2,1)S(1)}, bf16[256,128]{1,0:T(8,128)(2,1)S(1)}, u32[]{:S(2)}, u32[]{:S(2)}) collective-permute-start(bf16[256,128]{1,0:T(8,128)(2,1)S(1)} %get-tuple-element.76), channel_id=1, source_target_pairs={{0,12},{4,8},{8,4},{12,0},{1,13},{5,9},{9,5},{13,1},{2,14},{6,10},... | collective-permute-start | bytes 196616 | tf_op jit(solution)/shard_map/ppermute | solution.py:18
  20.7 1.6 %shard_map.118 = (f32[24,128,128]{2,1,0:T(8,128)S(1)}, f32[256,128]{1,0:T(8,128)S(1)}, bf16[2,128,128]{2,1,0:T(8,128)(2,1)S(1)}, bf16[2,128,256]{2,1,0:T(8,128)(...) custom-call(bf16[256,128]{1,0:T(8,128)(2,1)S(1)} %get-tuple-element., ...), custom_call_target="tpu_custom_call" | custom-call | bytes 1048576 | tf_op jit(solution)/shard_map/pallas_call | solution.py:34
  22.3 3.4 %collective-permute-done.6.other_ref.refs_0_ = bf16[256,128]{1,0:T(8,128)(2,1)S(1)} collective-permute-done((bf16[256,128]{1,0:T(8,128)(2,1)S(1)}, bf16[256,128]{1,0:T(8,128)(2,1)S(1)}, u32[]{:S(2)}, u32[]{:S(2)}) %collective-permute-start.6) | collective-permute-done | bytes 65568 | tf_op jit(solution)/shard_map/ppermute | solution.py:18
  25.7 0.0 collective-permute-done.4.g0.refs_1_
  25.7 0.0 collective-permute-done.5.g1.refs_2_
  25.7 1.1 %shard_map.119.refs_0_ = bf16[768,128]{1,0:T(8,128)(2,1)S(1)} custom-call(bf16[256,128]{1,0:T(8,128)(2,1)S(1)} %collective-permute-done.6.other_ref.refs_0_, bf16[384,128]{1,0:T(8,128)(2,1)S(1)} %collective-permute-done.4.g0.refs_1_, bf16[384,128]{1,0:T(8,128)(2,1)S(1)} %collective-permute-done.5.g1.refs_2_, bf16[256,128]{1,0:T(8,128)(2,1)S(1)} %get-tuple-element.77.h_ref, ...), custom_call_target="tpu_custom_call" | custom-call | bytes 1048576 | tf_op jit(solution)/shard_map/pallas_call | solution.py:34
  26.7 0.1 collective-permute-start.7
  26.8 1.4 %collective-permute-done.7.refs_1_ = bf16[768,128]{1,0:T(8,128)(2,1)S(1)} collective-permute-done((bf16[768,128]{1,0:T(8,128)(2,1)S(1)}, bf16[768,128]{1,0:T(8,128)(2,1)S(1)}, u32[]{:S(2)}, u32[]{:S(2)}) %collective-permute-start.7) | collective-permute-done | bytes 196640 | tf_op jit(solution)/shard_map/ppermute | solution.py:18
  28.2 1.7 %shard_map.120 = (bf16[128,128]{1,0:T(8,128)(2,1)S(1)}, bf16[128,128]{1,0:T(8,128)(2,1)S(1)}, bf16[512,128]{1,0:T(8,128)(2,1)S(1)}, bf16[768,128]{1,0:T(8,128)(2...) custom-call(s32[24,128]{1,0:T(8,128)S(1)} %get-tuple-element.60.s_ref, ...), custom_call_target="tpu_custom_call" | custom-call | bytes 1048576 | tf_op jit(solution)/shard_map/pallas_call | solution.py:34
  30.0 0.2 collective-permute-start.8
  30.2 1.1 %shard_map.122 = (bf16[24,128,128]{2,1,0:T(8,128)(2,1)S(1)}, bf16[768,128]{1,0:T(8,128)(2,1)S(1)}) custom-call(bf16[256,128]{1,0:T(8,128)(2,1)S(1)} %collective-permute-done.6.other_ref.refs_0_, bf16[384,128]{1,0:T(8,128)(2,1)S(1)} %collective-permute-done.4.g0.refs_1_, bf16[384,128]{1,0:T(8,128)(2,1)S(1)} %collective-permute-done.5.g1.refs_2_, ...), custom_call_target="tpu_custom_call" | custom-call | bytes 1048576 | tf_op jit(solution)/shard_map/pallas_call | solution.py:34
  31.3 0.2 collective-permute-done.8.refs_1_
  31.5 1.1 %shard_map.123 = (bf16[256,128]{1,0:T(8,128)(2,1)S(1)}, bf16[384,128]{1,0:T(8,128)(2,1)S(1)}, bf16[384,128]{1,0:T(8,128)(2,1)S(1)}, f32[256,128]{1,0:T(8,128)S(1...) custom-call(bf16[768,128]{1,0:T(8,128)(2,1)S(1)} %get-tuple-element.92.refs_0_, ...), custom_call_target="tpu_custom_call" | custom-call | bytes 1048576 | tf_op jit(solution)/shard_map/pallas_call | solution.py:34
  32.6 1.4 %collective-permute-start.10 = (bf16[384,128]{1,0:T(8,128)(2,1)S(1)}, bf16[384,128]{1,0:T(8,128)(2,1)S(1)}, u32[]{:S(2)}, u32[]{:S(2)}) collective-permute-start(bf16[384,128]{1,0:T(8,128)(2,1)S(1)} %get-tuple-element.103), channel_id=1, source_target_pairs={{0,8},{4,12},{8,0},{12,4},{1,9},{5,13},{9,1},{13,5},{2,10},{6,14},... | collective-permute-start | bytes 294920 | tf_op jit(solution)/shard_map/ppermute | solution.py:18
  34.1 0.8 %collective-permute-start.11 = (bf16[384,128]{1,0:T(8,128)(2,1)S(1)}, bf16[384,128]{1,0:T(8,128)(2,1)S(1)}, u32[]{:S(2)}, u32[]{:S(2)}) collective-permute-start(bf16[384,128]{1,0:T(8,128)(2,1)S(1)} %get-tuple-element.104), channel_id=1, source_target_pairs={{0,4},{4,0},{8,12},{12,8},{1,5},{5,1},{9,13},{13,9},{2,6},{6,2},{1... | collective-permute-start | bytes 294920 | tf_op jit(solution)/shard_map/ppermute | solution.py:18
  34.8 2.3 %collective-permute-start.9 = (bf16[256,128]{1,0:T(8,128)(2,1)S(1)}, bf16[256,128]{1,0:T(8,128)(2,1)S(1)}, u32[]{:S(2)}, u32[]{:S(2)}) collective-permute-start(bf16[256,128]{1,0:T(8,128)(2,1)S(1)} %get-tuple-element.102), channel_id=1, source_target_pairs={{0,12},{4,8},{8,4},{12,0},{1,13},{5,9},{9,5},{13,1},{2,14},{6,10},... | collective-permute-start | bytes 196616 | tf_op jit(solution)/shard_map/ppermute | solution.py:18
  37.1 0.6 %shard_map.124.own_ref = f32[256,128]{1,0:T(8,128)S(1)} custom-call(f32[256,128]{1,0:T(8,128)S(1)} %get-tuple-element.99.grad_ref, bf16[6,384,512]{2,1,0:T(8,128)(2,1)S(1)} %get-tuple-element.96.refs_4_.put, bf16[768,128]{1,0:T(8,128)(2,1)S(1)} %get-tuple-element.100.d_node, bf16[3072,128]{1,0:T(8,128)(2,1)S(1)} %get-tuple-element.101.d_pre, ...), custom_call_target="tpu_custom_call" | custom-call | bytes 1048576 | tf_op jit(solution)/shard_map/pallas_call | solution.py:34
  37.7 4.7 %collective-permute-done.9.other_ref = bf16[256,128]{1,0:T(8,128)(2,1)S(1)} collective-permute-done((bf16[256,128]{1,0:T(8,128)(2,1)S(1)}, bf16[256,128]{1,0:T(8,128)(2,1)S(1)}, u32[]{:S(2)}, u32[]{:S(2)}) %collective-permute-start.9) | collective-permute-done | bytes 65568 | tf_op jit(solution)/shard_map/ppermute | solution.py:18
  42.4 0.0 collective-permute-done.10.r0
  42.4 0.0 collective-permute-done.11.r1
  42.4 1.5 %collective-permute-start.12 = (bf16[256,128]{1,0:T(8,128)(2,1)S(1)}, bf16[256,128]{1,0:T(8,128)(2,1)S(1)}, u32[]{:S(2)}, u32[]{:S(2)}) collective-permute-start(bf16[256,128]{1,0:T(8,128)(2,1)S(1)} %shard_map.125.refs_0_), channel_id=1, source_target_pairs={{0,2},{2,0},{1,3},{3,1},{4,6},{6,4},{5,7},{7,5},{8,10},{10,8},{9,1... | collective-permute-start | bytes 196616 | tf_op jit(solution)/shard_map/ppermute | solution.py:18
  44.0 2.8 %collective-permute-done.12.refs_1_ = bf16[256,128]{1,0:T(8,128)(2,1)S(1)} collective-permute-done((bf16[256,128]{1,0:T(8,128)(2,1)S(1)}, bf16[256,128]{1,0:T(8,128)(2,1)S(1)}, u32[]{:S(2)}, u32[]{:S(2)}) %collective-permute-start.12) | collective-permute-done | bytes 65568 | tf_op jit(solution)/shard_map/ppermute | solution.py:18
  46.8 0.1 collective-permute-start.13
  46.9 0.7 %shard_map.128 = (bf16[16,128,128]{2,1,0:T(8,128)(2,1)S(1)}, bf16[512,128]{1,0:T(8,128)(2,1)S(1)}) custom-call(s32[24,128]{1,0:T(8,128)S(1)} %get-tuple-element.60.s_ref, f32[512,128]{1,0:T(8,128)S(1)} %get-tuple-element.63.recv, f32[512,128]{1,0:T(8,128)S(1)} %get-tuple-element.64.node, bf16[6,128,128]{2,1,0:T(8,128)(2,1)S(1)} %get-tuple-element.107.send_ref, ...), custom_call_target="tpu_custom_call" | custom-call | bytes 1048576 | tf_op jit(solution)/shard_map/pallas_call | solution.py:34
  47.5 0.1 shard_map.127.refs_2_
  47.6 0.5 collective-permute-done.13.refs_1_
  48.1 0.8 %shard_map.129 = (bf16[128,128]{1,0:T(8,128)(2,1)S(1)}, bf16[128,128]{1,0:T(8,128)(2,1)S(1)}, bf16[512,128]{1,0:T(8,128)(2,1)S(1)}, bf16[512,128]{1,0:T(8,128)(2...) custom-call(s32[24,128]{1,0:T(8,128)S(1)} %get-tuple-element.60.s_ref, ...), custom_call_target="tpu_custom_call" | custom-call | bytes 1048576 | tf_op jit(solution)/shard_map/pallas_call | solution.py:34
  48.9 1.7 %collective-permute-start.14 = (bf16[128,128]{1,0:T(8,128)(2,1)S(1)}, bf16[128,128]{1,0:T(8,128)(2,1)S(1)}, u32[]{:S(2)}, u32[]{:S(2)}) collective-permute-start(bf16[128,128]{1,0:T(8,128)(2,1)S(1)} %get-tuple-element.110), channel_id=1, source_target_pairs={{0,8},{4,12},{8,0},{12,4},{1,9},{5,13},{9,1},{13,5},{2,10},{6,14},... | collective-permute-start | bytes 98312 | tf_op jit(solution)/shard_map/ppermute | solution.py:18
  50.6 0.9 %collective-permute-start.15 = (bf16[128,128]{1,0:T(8,128)(2,1)S(1)}, bf16[128,128]{1,0:T(8,128)(2,1)S(1)}, u32[]{:S(2)}, u32[]{:S(2)}) collective-permute-start(bf16[128,128]{1,0:T(8,128)(2,1)S(1)} %get-tuple-element.111), channel_id=1, source_target_pairs={{0,4},{4,0},{8,12},{12,8},{1,5},{5,1},{9,13},{13,9},{2,6},{6,2},{1... | collective-permute-start | bytes 98312 | tf_op jit(solution)/shard_map/ppermute | solution.py:18
  51.5 0.8 %shard_map.121 = bf16[512,128]{1,0:T(8,128)(2,1)} custom-call(bf16[768,128]{1,0:T(8,128)(2,1)S(1)} %get-tuple-element.90.h_ref, bf16[512,128]{1,0:T(8,128)(2,1)S(1)} %get-tuple-element.91.hidden_ref, bf16[3,6,128,128]{3,2,1,0:T(8,128)(2,1)S(1)} %get-tuple-element.67.w_ref.refs_6_.refs_7_), custom_call_target="tpu_custom_call" | custom-call | bytes 1048576 | tf_op jit(solution)/shard_map/pallas_call | solution.py:34
  52.3 0.3 shard_map.130
  52.6 1.5 %collective-permute-done.14.r0 = bf16[128,128]{1,0:T(8,128)(2,1)S(1)} collective-permute-done((bf16[128,128]{1,0:T(8,128)(2,1)S(1)}, bf16[128,128]{1,0:T(8,128)(2,1)S(1)}, u32[]{:S(2)}, u32[]{:S(2)}) %collective-permute-start.14) | collective-permute-done | bytes 32800 | tf_op jit(solution)/shard_map/ppermute | solution.py:18
  54.1 0.4 collective-permute-done.15.r1
  54.5 0.8 %shard_map.131 = f32[4,128,128]{2,1,0:T(8,128)} custom-call(s32[24,128]{1,0:T(8,128)S(1)} %get-tuple-element.60.s_ref, bf16[128,128]{1,0:T(8,128)(2,1)S(1)} %collective-permute-done.14.r0, bf16[128,128]{1,0:T(8,128)(2,1)S(1)} %collective-permute-done.15.r1, f32[4,128,128]{2,1,0:T(8,128)S(1)} %bitcast.7), custom_call_target="tpu_custom_call" | custom-call | bytes 1048576 | tf_op jit(solution)/shard_map/pallas_call | solution.py:34
  (3 shorter events, 0.1 us)
Async XLA Ops:
  1.6 7.4 %collective-permute-start = (bf16[144,128]{1,0:T(8,128)(2,1)S(1)}, bf16[144,128]{1,0:T(8,128)(2,1)S(1)}, u32[]{:S(2)}, u32[]{:S(2)}) collective-permute-start(bf16[144,128]{1,0:T(8,128)(2,1)S(1)} %get-tuple-element.61), channel_id=1, source_target_pairs={{0,8},{4,12},{8,0},{12,4},{1,9},{5,13},{9,1},{13,5},{2,10},{6,14},... | collective-permute-start | bytes 110600 | tf_op jit(solution)/shard_map/ppermute | solution.py:18
  5.7 4.0 %collective-permute-start.1 = (bf16[144,128]{1,0:T(8,128)(2,1)S(1)}, bf16[144,128]{1,0:T(8,128)(2,1)S(1)}, u32[]{:S(2)}, u32[]{:S(2)}) collective-permute-start(bf16[144,128]{1,0:T(8,128)(2,1)S(1)} %get-tuple-element.62), channel_id=1, source_target_pairs={{0,4},{4,0},{8,12},{12,8},{1,5},{5,1},{9,13},{13,9},{2,6},{6,2},{1... | collective-permute-start | bytes 110600 | tf_op jit(solution)/shard_map/ppermute | solution.py:18
  10.4 1.3 %collective-permute-start.2 = (bf16[272,128]{1,0:T(8,128)(2,1)S(1)}, bf16[272,128]{1,0:T(8,128)(2,1)S(1)}, u32[]{:S(2)}, u32[]{:S(2)}) collective-permute-start(bf16[272,128]{1,0:T(8,128)(2,1)S(1)} %get-tuple-element.73), channel_id=1, source_target_pairs={{0,1},{1,0},{2,3},{3,2},{4,5},{5,4},{6,7},{7,6},{8,9},{9,8},{10,11... | collective-permute-start | bytes 208904 | tf_op jit(solution)/shard_map/ppermute | solution.py:18
  11.8 4.4 %collective-permute-start.3 = (bf16[272,128]{1,0:T(8,128)(2,1)S(1)}, bf16[272,128]{1,0:T(8,128)(2,1)S(1)}, u32[]{:S(2)}, u32[]{:S(2)}) collective-permute-start(bf16[272,128]{1,0:T(8,128)(2,1)S(1)} %shard_map.116.refs_0_), channel_id=1, source_target_pairs={{0,2},{2,0},{1,3},{3,1},{4,6},{6,4},{5,7},{7,5},{8,10},{10,8},{9,1... | collective-permute-start | bytes 208904 | tf_op jit(solution)/shard_map/ppermute | solution.py:18
  16.3 9.4 %collective-permute-start.4 = (bf16[384,128]{1,0:T(8,128)(2,1)S(1)}, bf16[384,128]{1,0:T(8,128)(2,1)S(1)}, u32[]{:S(2)}, u32[]{:S(2)}) collective-permute-start(bf16[384,128]{1,0:T(8,128)(2,1)S(1)} %get-tuple-element.74), channel_id=1, source_target_pairs={{0,8},{4,12},{8,0},{12,4},{1,9},{5,13},{9,1},{13,5},{2,10},{6,14},... | collective-permute-start | bytes 294920 | tf_op jit(solution)/shard_map/ppermute | solution.py:18
  17.5 8.2 %collective-permute-start.5 = (bf16[384,128]{1,0:T(8,128)(2,1)S(1)}, bf16[384,128]{1,0:T(8,128)(2,1)S(1)}, u32[]{:S(2)}, u32[]{:S(2)}) collective-permute-start(bf16[384,128]{1,0:T(8,128)(2,1)S(1)} %get-tuple-element.75), channel_id=1, source_target_pairs={{0,4},{4,0},{8,12},{12,8},{1,5},{5,1},{9,13},{13,9},{2,6},{6,2},{1... | collective-permute-start | bytes 294920 | tf_op jit(solution)/shard_map/ppermute | solution.py:18
  19.1 6.5 %collective-permute-start.6 = (bf16[256,128]{1,0:T(8,128)(2,1)S(1)}, bf16[256,128]{1,0:T(8,128)(2,1)S(1)}, u32[]{:S(2)}, u32[]{:S(2)}) collective-permute-start(bf16[256,128]{1,0:T(8,128)(2,1)S(1)} %get-tuple-element.76), channel_id=1, source_target_pairs={{0,12},{4,8},{8,4},{12,0},{1,13},{5,9},{9,5},{13,1},{2,14},{6,10},... | collective-permute-start | bytes 196616 | tf_op jit(solution)/shard_map/ppermute | solution.py:18
  26.7 1.5 %collective-permute-start.7 = (bf16[768,128]{1,0:T(8,128)(2,1)S(1)}, bf16[768,128]{1,0:T(8,128)(2,1)S(1)}, u32[]{:S(2)}, u32[]{:S(2)}) collective-permute-start(bf16[768,128]{1,0:T(8,128)(2,1)S(1)} %shard_map.119.refs_0_), channel_id=1, source_target_pairs={{0,1},{1,0},{2,3},{3,2},{4,5},{5,4},{6,7},{7,6},{8,9},{9,8},{10,11... | collective-permute-start | bytes 589832 | tf_op jit(solution)/shard_map/ppermute | solution.py:18
  30.0 1.5 %collective-permute-start.8 = (bf16[768,128]{1,0:T(8,128)(2,1)S(1)}, bf16[768,128]{1,0:T(8,128)(2,1)S(1)}, u32[]{:S(2)}, u32[]{:S(2)}) collective-permute-start(bf16[768,128]{1,0:T(8,128)(2,1)S(1)} %get-tuple-element.93), channel_id=1, source_target_pairs={{0,1},{1,0},{2,3},{3,2},{4,5},{5,4},{6,7},{7,6},{8,9},{9,8},{10,11... | collective-permute-start | bytes 589832 | tf_op jit(solution)/shard_map/ppermute | solution.py:18
  32.6 9.7 %collective-permute-start.10 = (bf16[384,128]{1,0:T(8,128)(2,1)S(1)}, bf16[384,128]{1,0:T(8,128)(2,1)S(1)}, u32[]{:S(2)}, u32[]{:S(2)}) collective-permute-start(bf16[384,128]{1,0:T(8,128)(2,1)S(1)} %get-tuple-element.103), channel_id=1, source_target_pairs={{0,8},{4,12},{8,0},{12,4},{1,9},{5,13},{9,1},{13,5},{2,10},{6,14},... | collective-permute-start | bytes 294920 | tf_op jit(solution)/shard_map/ppermute | solution.py:18
  34.1 8.3 %collective-permute-start.11 = (bf16[384,128]{1,0:T(8,128)(2,1)S(1)}, bf16[384,128]{1,0:T(8,128)(2,1)S(1)}, u32[]{:S(2)}, u32[]{:S(2)}) collective-permute-start(bf16[384,128]{1,0:T(8,128)(2,1)S(1)} %get-tuple-element.104), channel_id=1, source_target_pairs={{0,4},{4,0},{8,12},{12,8},{1,5},{5,1},{9,13},{13,9},{2,6},{6,2},{1... | collective-permute-start | bytes 294920 | tf_op jit(solution)/shard_map/ppermute | solution.py:18
  34.8 7.6 %collective-permute-start.9 = (bf16[256,128]{1,0:T(8,128)(2,1)S(1)}, bf16[256,128]{1,0:T(8,128)(2,1)S(1)}, u32[]{:S(2)}, u32[]{:S(2)}) collective-permute-start(bf16[256,128]{1,0:T(8,128)(2,1)S(1)} %get-tuple-element.102), channel_id=1, source_target_pairs={{0,12},{4,8},{8,4},{12,0},{1,13},{5,9},{9,5},{13,1},{2,14},{6,10},... | collective-permute-start | bytes 196616 | tf_op jit(solution)/shard_map/ppermute | solution.py:18
  42.4 4.3 %collective-permute-start.12 = (bf16[256,128]{1,0:T(8,128)(2,1)S(1)}, bf16[256,128]{1,0:T(8,128)(2,1)S(1)}, u32[]{:S(2)}, u32[]{:S(2)}) collective-permute-start(bf16[256,128]{1,0:T(8,128)(2,1)S(1)} %shard_map.125.refs_0_), channel_id=1, source_target_pairs={{0,2},{2,0},{1,3},{3,1},{4,6},{6,4},{5,7},{7,5},{8,10},{10,8},{9,1... | collective-permute-start | bytes 196616 | tf_op jit(solution)/shard_map/ppermute | solution.py:18
  46.8 1.3 %collective-permute-start.13 = (bf16[256,128]{1,0:T(8,128)(2,1)S(1)}, bf16[256,128]{1,0:T(8,128)(2,1)S(1)}, u32[]{:S(2)}, u32[]{:S(2)}) collective-permute-start(bf16[256,128]{1,0:T(8,128)(2,1)S(1)} %shard_map.126.refs_0_), channel_id=1, source_target_pairs={{0,1},{1,0},{2,3},{3,2},{4,5},{5,4},{6,7},{7,6},{8,9},{9,8},{10,11... | collective-permute-start | bytes 196616 | tf_op jit(solution)/shard_map/ppermute | solution.py:18
  48.9 5.2 %collective-permute-start.14 = (bf16[128,128]{1,0:T(8,128)(2,1)S(1)}, bf16[128,128]{1,0:T(8,128)(2,1)S(1)}, u32[]{:S(2)}, u32[]{:S(2)}) collective-permute-start(bf16[128,128]{1,0:T(8,128)(2,1)S(1)} %get-tuple-element.110), channel_id=1, source_target_pairs={{0,8},{4,12},{8,0},{12,4},{1,9},{5,13},{9,1},{13,5},{2,10},{6,14},... | collective-permute-start | bytes 98312 | tf_op jit(solution)/shard_map/ppermute | solution.py:18
  50.6 3.9 %collective-permute-start.15 = (bf16[128,128]{1,0:T(8,128)(2,1)S(1)}, bf16[128,128]{1,0:T(8,128)(2,1)S(1)}, u32[]{:S(2)}, u32[]{:S(2)}) collective-permute-start(bf16[128,128]{1,0:T(8,128)(2,1)S(1)} %get-tuple-element.111), channel_id=1, source_target_pairs={{0,4},{4,0},{8,12},{12,8},{1,5},{5,1},{9,13},{13,9},{2,6},{6,2},{1... | collective-permute-start | bytes 98312 | tf_op jit(solution)/shard_map/ppermute | solution.py:18
